TPU v7x, 32 devices: a whole 2x2x4 slice. The times are simulated.
32 devices in a mesh: dp: 4 (over y, core), expert: 8 (over z, x).
Axes of the slice: x: 2, y: 2, z: 4, core: 2. Of those that a mesh axis runs over, the one named last changes fastest.
Arguments:
- layer_input: bfloat16 [8192, 1536], P(('dp', 'expert')), may hold values from -6 to 6
- cotangent: float32 [8192, 1536], P(('dp', 'expert')), may hold values from -6 to 6
- lengths: int32 [32], P(('dp', 'expert')), may hold values from 64 to 256, as said below
- routes_a: int32 [8192, 6], P(('dp', 'expert')), may hold values from 0 to 15, all different within a row; in each aligned block of 128 rows (0 to 127, 128 to 255, ...) at most 60 rows name the same one
- routes_b: int32 [8192, 6], P(('dp', 'expert')), may hold values from 0 to 15, all different within a row; in each aligned block of 128 rows (0 to 127, 128 to 255, ...) at most 60 rows name the same one
- mixer_in: bfloat16 [1536, 6448], P(('dp', 'expert')), may hold values from -0.15625 to 0.15625
- mixer_out: bfloat16 [1536, 3072], P(('dp', 'expert')), may hold values from -0.109375 to 0.109375
- router_a: bfloat16 [1536, 16], P(('dp', 'expert')), may hold values from -0.078125 to 0.078125
- shared_in_a: bfloat16 [1536, 2048], P(('dp', 'expert')), may hold values from -0.15625 to 0.15625
- shared_out_a: bfloat16 [1536, 1024], P(('dp', 'expert')), may hold values from -0.1875 to 0.1875
- expert_in_a: bfloat16 [16, 1536, 1024], P('expert', 'dp'), may hold values from -0.15625 to 0.15625
- expert_out_a: bfloat16 [16, 1536, 512], P('expert', 'dp'), may hold values from -0.25 to 0.25
- attn_qkv: bfloat16 [1536, 2560], P(('dp', 'expert')), may hold values from -0.15625 to 0.15625
- attn_out: bfloat16 [1536, 1536], P(('dp', 'expert')), may hold values from -0.4375 to 0.4375
- router_b: bfloat16 [1536, 16], P(('dp', 'expert')), may hold values from -0.078125 to 0.078125
- shared_in_b: bfloat16 [1536, 2048], P(('dp', 'expert')), may hold values from -0.15625 to 0.15625
- shared_out_b: bfloat16 [1536, 1024], P(('dp', 'expert')), may hold values from -0.1875 to 0.1875
- expert_in_b: bfloat16 [16, 1536, 1024], P('expert', 'dp'), may hold values from -0.15625 to 0.15625
- expert_out_b: bfloat16 [16, 1536, 512], P('expert', 'dp'), may hold values from -0.25 to 0.25
- norm_gains: float32 [4, 1536], replicated, may hold values from 0.5 to 1.5
- mixer_gain: float32 [3072], replicated, may hold values from 0.5 to 1.5
- conv_weight: float32 [4, 3328], replicated, may hold values from -3 to 3
- conv_bias: float32 [3328], replicated, may hold values from -3 to 3
- decay_log: float32 [48], replicated, may hold values from -4.5 to 0.5
- step_bias: float32 [48], replicated, may hold values from -4 to -0.5
- skip_gain: float32 [48], replicated, may hold values from 0.5 to 1.5
Outputs:
- layer_output: float32 [8192, 1536], P(('dp', 'expert'))
- input_grad: float32 [8192, 1536], P(('dp', 'expert'))
- grad_mixer_in: float32 [1536, 6448], P(('dp', 'expert'))
- grad_mixer_out: float32 [1536, 3072], P(('dp', 'expert'))
- grad_router_a: float32 [1536, 16], P(('dp', 'expert'))
- grad_shared_in_a: float32 [1536, 2048], P(('dp', 'expert'))
- grad_shared_out_a: float32 [1536, 1024], P(('dp', 'expert'))
- grad_expert_in_a: float32 [16, 1536, 1024], P('expert', 'dp')
- grad_expert_out_a: float32 [16, 1536, 512], P('expert', 'dp')
- grad_attn_qkv: float32 [1536, 2560], P(('dp', 'expert'))
- grad_attn_out: float32 [1536, 1536], P(('dp', 'expert'))
- grad_router_b: float32 [1536, 16], P(('dp', 'expert'))
- grad_shared_in_b: float32 [1536, 2048], P(('dp', 'expert'))
- grad_shared_out_b: float32 [1536, 1024], P(('dp', 'expert'))
- grad_expert_in_b: float32 [16, 1536, 1024], P('expert', 'dp')
- grad_expert_out_b: float32 [16, 1536, 512], P('expert', 'dp')
- grad_norm_gains: float32 [4, 1536], replicated
- grad_mixer_gain: float32 [3072], replicated
- grad_conv_weight: float32 [4, 3328], replicated
- grad_conv_bias: float32 [3328], replicated
- grad_decay_log: float32 [48], replicated
- grad_step_bias: float32 [48], replicated
- grad_skip_gain: float32 [48], replicated
Inputs may be any that keep to these rules, and one draw needn't show every extreme that they name: `routes_a`: in each aligned block of 128 rows, no expert is named by more than 60 rows. `routes_b`: in each aligned block of 128 rows, no expert is named by more than 60 rows. `lengths`: some slot has exactly 256 valid tokens and some exactly 64.
All inputs are finite; a program needn't handle non-finite values.
Results may differ from a plain program's by a relative error of at most 0.023.
Values may be sent and summed in bfloat16 or wider, within the bound.
A program may use at most 448 MiB of HBM per device.

v0:
```python
import jax
import jax.numpy as jnp
from jax import lax
from jax.sharding import PartitionSpec as P

MHEADS = 48
MHDIM = 64
NSTATE = 128
KCONV = 4
AHEADS = 12
KVHEADS = 4
AHDIM = 128
TOP = 6
MICRO = 2
SLOT_LEN = 256
DI = 3072
CONVCH = 3328
QD = 1536
KVD = 512
QKV = 2560


EPS = 1e-05
HIGH = lax.Precision.HIGHEST
FLOAT = jnp.float32
BRAIN = jnp.bfloat16


def matmul(left, right):
    return jnp.dot(left, right, preferred_element_type=FLOAT)


def matmul_nt(left, right):
    return lax.dot_general(left, right, (((1,), (1,)), ((), ())), preferred_element_type=FLOAT)


def matmul_tn(left, right):
    return lax.dot_general(left, right, (((0,), (0,)), ((), ())), preferred_element_type=FLOAT)


def silu_of(values):
    return values * jax.nn.sigmoid(values)


def softplus_of(values):
    return jnp.log1p(jnp.exp(values))


def rms_norm(values, norm_gain):
    return values * lax.rsqrt(jnp.mean(values * values, axis=-1, keepdims=True) + EPS) * norm_gain


def softmax_of(scores):
    largest = jnp.max(scores, axis=-1, keepdims=True)
    raised = jnp.exp(scores - largest)
    return raised / jnp.sum(raised, axis=-1, keepdims=True)


def swiglu(gate_up):
    half_width = gate_up.shape[-1] // 2
    return silu_of(gate_up[..., :half_width]) * gate_up[..., half_width:]


def carry_mix(inputs, decay_rate, skip_gain):
    heads_in, b_rows, c_rows, step_size, state = inputs
    length = heads_in.shape[0]
    log_decay = jnp.cumsum(step_size * decay_rate, axis=0)
    spread = log_decay[:, None, :] - log_decay[None, :, :]
    causal = (jnp.arange(length)[:, None] >= jnp.arange(length)[None, :])[:, :, None]
    decay_mat = jnp.where(causal, jnp.exp(jnp.where(causal, spread, 0.0)), 0.0)
    intersection = jnp.dot(c_rows, b_rows.T, precision=HIGH, preferred_element_type=FLOAT)
    mixing = intersection[:, :, None] * decay_mat * step_size[None, :, :]
    mixed_heads = jnp.einsum("tsh,shp->thp", mixing, heads_in, precision=HIGH)
    from_state = (
        jnp.einsum("tn,hpn->thp", c_rows, state, precision=HIGH) * jnp.exp(log_decay)[:, :, None]
    )
    total_decay = log_decay[-1]
    weight_in = jnp.exp(total_decay[None, :] - log_decay) * step_size
    new_state = jnp.exp(total_decay)[:, None, None] * state + jnp.einsum(
        "sh,shp,sn->hpn", weight_in, heads_in, b_rows, precision=HIGH
    )
    return (mixed_heads + from_state + skip_gain[None, :, None] * heads_in, new_state)


def mixer_segment(projected, tail, state, params):
    slot_count, length = (projected.shape[0], projected.shape[1])
    gate_part = projected[..., :DI]
    conv_part = projected[..., DI : DI + CONVCH]
    step_raw = projected[..., DI + CONVCH :]
    padded = jnp.concatenate([tail, conv_part], axis=1)
    conv_out = params["conv_bias"] + padded[:, 0:length] * params["conv_weight"][0]
    for tap_index in range(1, KCONV):
        conv_out = (
            conv_out + padded[:, tap_index : tap_index + length] * params["conv_weight"][tap_index]
        )
    new_tail = padded[:, length:]
    conv_out = silu_of(conv_out)
    heads_in = conv_out[..., :DI].reshape(slot_count, length, MHEADS, MHDIM)
    b_rows = conv_out[..., DI : DI + NSTATE]
    c_rows = conv_out[..., DI + NSTATE :]
    step_size = softplus_of(step_raw + params["step_bias"])
    decay_rate = -jnp.exp(params["decay_log"])
    skip_gain = params["skip_gain"]
    mixed_heads, new_state = lax.map(
        lambda inputs: carry_mix(inputs, decay_rate, skip_gain),
        (heads_in, b_rows, c_rows, step_size, state),
    )
    gated_out = mixed_heads.reshape(slot_count, length, DI) * silu_of(gate_part)
    return (rms_norm(gated_out, params["mixer_gain"]), new_tail, new_state)


def route_weights(logits, routes, valid_rows):
    chosen = jnp.take_along_axis(logits, routes, axis=1)
    return softmax_of(chosen) * valid_rows[:, None]


def to_experts(buffer):
    return lax.all_to_all(buffer, "expert", split_axis=0, concat_axis=0, tiled=True)


def from_experts(buffer):
    return lax.all_to_all(buffer, "expert", split_axis=0, concat_axis=0, tiled=True)


def fetch_expert(expert_in, expert_out):
    return (
        lax.all_gather(expert_in, "dp", axis=1, tiled=True),
        lax.all_gather(expert_out, "dp", axis=1, tiled=True),
    )


def fetch_first(
    mixer_in, mixer_out, router_a, shared_in_a, shared_out_a, expert_in_a, expert_out_a
):
    layer = (
        lax.all_gather(mixer_in, ("dp", "expert"), axis=0, tiled=True),
        lax.all_gather(mixer_out, ("dp", "expert"), axis=0, tiled=True),
        lax.all_gather(router_a, ("dp", "expert"), axis=0, tiled=True),
        lax.all_gather(shared_in_a, ("dp", "expert"), axis=0, tiled=True),
        lax.all_gather(shared_out_a, ("dp", "expert"), axis=0, tiled=True),
    )
    return (layer, fetch_expert(expert_in_a, expert_out_a))


def fetch_second(
    attn_qkv, attn_out, router_b, shared_in_b, shared_out_b, expert_in_b, expert_out_b
):
    layer = (
        lax.all_gather(attn_qkv, ("dp", "expert"), axis=0, tiled=True),
        lax.all_gather(attn_out, ("dp", "expert"), axis=0, tiled=True),
        lax.all_gather(router_b, ("dp", "expert"), axis=0, tiled=True),
        lax.all_gather(shared_in_b, ("dp", "expert"), axis=0, tiled=True),
        lax.all_gather(shared_out_b, ("dp", "expert"), axis=0, tiled=True),
    )
    return (layer, fetch_expert(expert_in_b, expert_out_b))


def routing_slots(routes, valid_rows, experts, capacity):
    flat_routes = routes.reshape(-1)
    live_pairs = (jnp.repeat(valid_rows, TOP) > 0).astype(jnp.int32)
    onehot = (flat_routes[:, None] == jnp.arange(experts)[None, :]).astype(jnp.int32) * live_pairs[
        :, None
    ]
    position = jnp.sum((jnp.cumsum(onehot, axis=0) - 1) * onehot, axis=1)
    return jnp.where(live_pairs > 0, flat_routes * capacity + position, experts * capacity)


def scatter_pairs(pair_rows, slot_index, experts, capacity):
    width = pair_rows.shape[-1]
    buffer = (
        jnp.zeros((experts * capacity, width), BRAIN).at[slot_index].set(pair_rows, mode="drop")
    )
    groups = lax.axis_size("expert")
    return buffer.reshape(groups, experts // groups, capacity, width)


def collect_pairs(buffer, slot_index):
    flat_rows = buffer.reshape(-1, buffer.shape[-1])
    return jnp.take(flat_rows, slot_index, axis=0, mode="fill", fill_value=0)


def mixer_forward(hidden, norm_gain, mixer_in, mixer_out, small_params, slot_count, tail, state):
    normed, norm_back = jax.vjp(rms_norm, hidden, norm_gain)
    normed_low = normed.astype(BRAIN)
    projected = matmul(normed_low, mixer_in).reshape(slot_count, hidden.shape[0] // slot_count, -1)
    (mixer_norm, new_tail, new_state), core_back = jax.vjp(
        mixer_segment, projected, tail, state, small_params
    )
    mixed_low = mixer_norm.reshape(hidden.shape[0], -1).astype(BRAIN)
    output = hidden + matmul_nt(mixed_low, mixer_out)
    return (
        output,
        new_tail,
        new_state,
        (norm_back, normed_low, core_back, mixed_low, mixer_norm.shape),
    )


def mixer_backward(grad_out, grad_tail, grad_state, saved_mix, mixer_in, mixer_out):
    norm_back, normed_low, core_back, mixed_low, mixed_shape = saved_mix
    grad_low = grad_out.astype(BRAIN)
    grad_mixer_out = matmul_tn(grad_low, mixed_low)
    grad_mixed = matmul(grad_low, mixer_out).reshape(mixed_shape)
    grad_proj, grad_prev_tail, grad_prev_state, grad_small = core_back(
        (grad_mixed, grad_tail, grad_state)
    )
    grad_proj = grad_proj.reshape(normed_low.shape[0], -1).astype(BRAIN)
    grad_mixer_in = matmul_tn(normed_low, grad_proj)
    grad_hidden, grad_gain = norm_back(matmul_nt(grad_proj, mixer_in))
    return (
        grad_out + grad_hidden,
        grad_gain,
        (grad_mixer_in, grad_mixer_out),
        grad_small,
        grad_prev_tail,
        grad_prev_state,
    )


def moe_forward(
    hidden,
    routes,
    valid_rows,
    norm_gain,
    router,
    shared_in,
    shared_out,
    expert_in,
    expert_out,
    slot_count,
):
    experts = router.shape[1]
    row_count = hidden.shape[0]
    capacity = slot_count * (SLOT_LEN // MICRO * TOP // experts * 5 // 4)
    normed, norm_back = jax.vjp(rms_norm, hidden, norm_gain)
    normed_low = normed.astype(BRAIN)
    logits = matmul(normed_low, router)
    weights, gate_back = jax.vjp(lambda scores: route_weights(scores, routes, valid_rows), logits)
    slot_index = routing_slots(routes, valid_rows, experts, capacity)
    received = to_experts(
        scatter_pairs(jnp.repeat(normed_low, TOP, axis=0), slot_index, experts, capacity)
    )
    gate_up = jnp.einsum("secd,edf->secf", received, expert_in, preferred_element_type=FLOAT)
    inner_act, inner_back = jax.vjp(swiglu, gate_up)
    inner_low = inner_act.astype(BRAIN)
    result = jnp.einsum(
        "secf,edf->secd", inner_low, expert_out, preferred_element_type=FLOAT
    ).astype(BRAIN)
    returned = (
        collect_pairs(from_experts(result), slot_index).astype(FLOAT).reshape(row_count, TOP, -1)
    )
    routed = jnp.sum(weights[:, :, None] * returned, axis=1)
    shared_mid, shared_back = jax.vjp(swiglu, matmul(normed_low, shared_in))
    shared_low = shared_mid.astype(BRAIN)
    output = hidden + routed + matmul_nt(shared_low, shared_out)
    return (
        output,
        (
            norm_back,
            normed_low,
            gate_back,
            weights,
            slot_index,
            received,
            inner_back,
            inner_low,
            returned,
            shared_back,
            shared_low,
        ),
    )


def moe_backward(grad_out, saved_moe, router, shared_in, shared_out, expert_in, expert_out):
    (
        norm_back,
        normed_low,
        gate_back,
        weights,
        slot_index,
        received,
        inner_back,
        inner_low,
        returned,
        shared_back,
        shared_low,
    ) = saved_moe
    experts = router.shape[1]
    capacity = received.shape[2]
    row_count = grad_out.shape[0]
    grad_low = grad_out.astype(BRAIN)
    grad_shared_out = matmul_tn(grad_low, shared_low)
    grad_shared_gu = shared_back(matmul(grad_low, shared_out))[0].astype(BRAIN)
    grad_shared_in = matmul_tn(normed_low, grad_shared_gu)
    grad_normed = matmul_nt(grad_shared_gu, shared_in)
    pair_grads = (
        (weights[:, :, None] * grad_out[:, None, :]).astype(BRAIN).reshape(row_count * TOP, -1)
    )
    grad_result = to_experts(scatter_pairs(pair_grads, slot_index, experts, capacity))
    grad_weights = jnp.sum(returned * grad_out[:, None, :], axis=2)
    grad_inner = jnp.einsum("secd,edf->secf", grad_result, expert_out, preferred_element_type=FLOAT)
    grad_expert_out = jnp.einsum(
        "secd,secf->edf", grad_result, inner_low, preferred_element_type=FLOAT
    )
    grad_gate_up = inner_back(grad_inner)[0].astype(BRAIN)
    grad_expert_in = jnp.einsum(
        "secd,secf->edf", received, grad_gate_up, preferred_element_type=FLOAT
    )
    grad_received = jnp.einsum(
        "secf,edf->secd", grad_gate_up, expert_in, preferred_element_type=FLOAT
    ).astype(BRAIN)
    grad_pairs = (
        collect_pairs(from_experts(grad_received), slot_index)
        .astype(FLOAT)
        .reshape(row_count, TOP, -1)
    )
    grad_normed = grad_normed + jnp.sum(grad_pairs, axis=1)
    grad_logits = gate_back(grad_weights)[0].astype(BRAIN)
    grad_router = matmul_tn(normed_low, grad_logits)
    grad_normed = grad_normed + matmul_nt(grad_logits, router)
    grad_hidden, grad_gain = norm_back(grad_normed)
    return (
        grad_out + grad_hidden,
        grad_gain,
        (grad_router, grad_shared_in, grad_shared_out),
        (grad_expert_in, grad_expert_out),
    )


def causal_mask(length, offset, total):
    return (jnp.arange(length) + offset)[:, None] >= jnp.arange(total)[None, :]


def attention_forward(
    hidden, norm_gain, attn_qkv, attn_out, slot_count, earlier_keys, earlier_values
):
    row_count = hidden.shape[0]
    length = row_count // slot_count
    normed, norm_back = jax.vjp(rms_norm, hidden, norm_gain)
    normed_low = normed.astype(BRAIN)
    qkv_low = matmul(normed_low, attn_qkv).astype(BRAIN).reshape(slot_count, length, QKV)
    queries = qkv_low[..., :QD].reshape(slot_count, length, KVHEADS, AHEADS // KVHEADS, AHDIM)
    key_rows = qkv_low[..., QD : QD + KVD].reshape(slot_count, length, KVHEADS, AHDIM)
    value_rows = qkv_low[..., QD + KVD :].reshape(slot_count, length, KVHEADS, AHDIM)
    all_keys = jnp.concatenate(earlier_keys + [key_rows], axis=1)
    all_values = jnp.concatenate(earlier_values + [value_rows], axis=1)
    offset = len(earlier_keys) * length
    mask = causal_mask(length, offset, all_keys.shape[1])
    raw_scores = jnp.einsum("stkgd,sukd->skgtu", queries, all_keys, preferred_element_type=FLOAT)
    scores = jnp.where(mask, raw_scores * AHDIM ** (-0.5), -1e30)
    largest = jnp.max(scores, axis=-1, keepdims=True)
    log_total = largest + jnp.log(jnp.sum(jnp.exp(scores - largest), axis=-1, keepdims=True))
    attn_probs = jnp.exp(scores - log_total)
    attended = jnp.einsum(
        "skgtu,sukd->stkgd", attn_probs.astype(BRAIN), all_values, preferred_element_type=FLOAT
    )
    mixed_low = attended.astype(BRAIN).reshape(row_count, QD)
    output = hidden + matmul_nt(mixed_low, attn_out)
    return (
        output,
        key_rows,
        value_rows,
        (norm_back, normed_low, queries, all_keys, all_values, log_total, mixed_low, offset),
    )


def attention_backward(grad_out, saved_attn, attn_qkv, attn_out, later_keys, later_values):
    norm_back, normed_low, queries, all_keys, all_values, log_total, mixed_low, offset = saved_attn
    row_count = grad_out.shape[0]
    length = queries.shape[1]
    grad_low = grad_out.astype(BRAIN)
    grad_attn_out = matmul_tn(grad_low, mixed_low)
    grad_mixed = matmul(grad_low, attn_out).astype(BRAIN).reshape(queries.shape)
    score_scale = AHDIM ** (-0.5)
    mask = causal_mask(length, offset, all_keys.shape[1])
    raw_scores = jnp.einsum("stkgd,sukd->skgtu", queries, all_keys, preferred_element_type=FLOAT)
    scores = jnp.where(mask, raw_scores * score_scale, -1e30)
    attn_probs = jnp.exp(scores - log_total)
    grad_probs = jnp.einsum(
        "stkgd,sukd->skgtu", grad_mixed, all_values, preferred_element_type=FLOAT
    )
    grad_values_all = jnp.einsum(
        "skgtu,stkgd->sukd", attn_probs.astype(BRAIN), grad_mixed, preferred_element_type=FLOAT
    )
    inner_sum = jnp.sum(attn_probs * grad_probs, axis=-1, keepdims=True)
    grad_raw = (attn_probs * (grad_probs - inner_sum) * score_scale).astype(BRAIN)
    grad_queries = jnp.einsum("skgtu,sukd->stkgd", grad_raw, all_keys, preferred_element_type=FLOAT)
    grad_keys_all = jnp.einsum("skgtu,stkgd->sukd", grad_raw, queries, preferred_element_type=FLOAT)
    own_keys = grad_keys_all[:, offset:] + later_keys
    own_values = grad_values_all[:, offset:] + later_values
    earlier_count = offset // length
    earlier_keys = [
        grad_keys_all[:, index * length : (index + 1) * length] for index in range(earlier_count)
    ]
    earlier_values = [
        grad_values_all[:, index * length : (index + 1) * length] for index in range(earlier_count)
    ]
    grad_qkv = jnp.concatenate(
        [
            grad_queries.reshape(row_count, QD),
            own_keys.reshape(row_count, KVD),
            own_values.reshape(row_count, KVD),
        ],
        axis=1,
    ).astype(BRAIN)
    grad_attn_qkv = matmul_tn(normed_low, grad_qkv)
    grad_hidden, grad_gain = norm_back(matmul_nt(grad_qkv, attn_qkv))
    return (
        grad_out + grad_hidden,
        grad_gain,
        (grad_attn_qkv, grad_attn_out),
        earlier_keys,
        earlier_values,
    )


def add_into(totals, update):
    return update if totals is None else jax.tree.map(jnp.add, totals, update)


def per_device(
    layer_input,
    cotangent,
    lengths,
    routes_a,
    routes_b,
    mixer_in,
    mixer_out,
    router_a,
    shared_in_a,
    shared_out_a,
    expert_in_a,
    expert_out_a,
    attn_qkv,
    attn_out,
    router_b,
    shared_in_b,
    shared_out_b,
    expert_in_b,
    expert_out_b,
    norm_gains,
    mixer_gain,
    conv_weight,
    conv_bias,
    decay_log,
    step_bias,
    skip_gain,
):
    small_params = {
        "conv_weight": conv_weight,
        "conv_bias": conv_bias,
        "decay_log": decay_log,
        "step_bias": step_bias,
        "skip_gain": skip_gain,
        "mixer_gain": mixer_gain,
    }
    slot_count = lengths.shape[0]
    seg_len = SLOT_LEN // MICRO
    positions = jnp.arange(slot_count * SLOT_LEN)
    valid_all = (positions % SLOT_LEN < jnp.repeat(lengths, SLOT_LEN)).astype(FLOAT)

    def take_seg(array, index):
        shaped = array.reshape((slot_count, MICRO, seg_len) + array.shape[1:])
        return shaped[:, index].reshape((slot_count * seg_len,) + array.shape[1:])

    def first_weights():
        return fetch_first(
            mixer_in, mixer_out, router_a, shared_in_a, shared_out_a, expert_in_a, expert_out_a
        )

    def second_weights():
        return fetch_second(
            attn_qkv, attn_out, router_b, shared_in_b, shared_out_b, expert_in_b, expert_out_b
        )

    tail = jnp.zeros((slot_count, conv_weight.shape[0] - 1, conv_weight.shape[1]), FLOAT)
    state = jnp.zeros((slot_count, MHEADS, MHDIM, NSTATE), FLOAT)
    key_list = []
    value_list = []
    saved_all = []
    outputs = []
    for micro_index in range(MICRO):
        first = first_weights()
        second = second_weights()
        (w_mix_in, w_mix_out, w_router_a, w_shared_in_a, w_shared_out_a), (
            w_exp_in_a,
            w_exp_out_a,
        ) = first
        (w_qkv, w_attn_out, w_router_b, w_shared_in_b, w_shared_out_b), (
            w_exp_in_b,
            w_exp_out_b,
        ) = second
        hidden = take_seg(layer_input, micro_index).astype(FLOAT)
        valid_rows = take_seg(valid_all, micro_index)
        routes_one = take_seg(routes_a, micro_index)
        routes_two = take_seg(routes_b, micro_index)
        after_mixer, tail, state, saved_mix = mixer_forward(
            hidden, norm_gains[0], w_mix_in, w_mix_out, small_params, slot_count, tail, state
        )
        after_moe, saved_moe_a = moe_forward(
            after_mixer,
            routes_one,
            valid_rows,
            norm_gains[1],
            w_router_a,
            w_shared_in_a,
            w_shared_out_a,
            w_exp_in_a,
            w_exp_out_a,
            slot_count,
        )
        after_attention, key_rows, value_rows, saved_attn = attention_forward(
            after_moe,
            norm_gains[2],
            w_qkv,
            w_attn_out,
            slot_count,
            list(key_list),
            list(value_list),
        )
        key_list.append(key_rows)
        value_list.append(value_rows)
        final_rows, saved_moe_b = moe_forward(
            after_attention,
            routes_two,
            valid_rows,
            norm_gains[3],
            w_router_b,
            w_shared_in_b,
            w_shared_out_b,
            w_exp_in_b,
            w_exp_out_b,
            slot_count,
        )
        outputs.append(final_rows.reshape(slot_count, seg_len, -1))
        saved_all.append((saved_mix, saved_moe_a, saved_attn, saved_moe_b, valid_rows))
    key_grads = [jnp.zeros((slot_count, seg_len, KVHEADS, AHDIM), FLOAT) for index in range(MICRO)]
    value_grads = [
        jnp.zeros((slot_count, seg_len, KVHEADS, AHDIM), FLOAT) for index in range(MICRO)
    ]
    grads_mid = [None] * MICRO
    second_dense = None
    second_expert = None
    second_gains = None
    for micro_index in reversed(range(MICRO)):
        second = second_weights()
        (w_qkv, w_attn_out, w_router_b, w_shared_in_b, w_shared_out_b), (
            w_exp_in_b,
            w_exp_out_b,
        ) = second
        saved_mix, saved_moe_a, saved_attn, saved_moe_b, valid_rows = saved_all[micro_index]
        out_grad = take_seg(cotangent, micro_index) * valid_rows[:, None]
        grad_third, gain_four, dense_four, expert_four = moe_backward(
            out_grad,
            saved_moe_b,
            w_router_b,
            w_shared_in_b,
            w_shared_out_b,
            w_exp_in_b,
            w_exp_out_b,
        )
        grad_second, gain_three, attn_grads, earlier_keys, earlier_values = attention_backward(
            grad_third,
            saved_attn,
            w_qkv,
            w_attn_out,
            key_grads[micro_index],
            value_grads[micro_index],
        )
        for index in range(micro_index):
            key_grads[index] = earlier_keys[index]
            value_grads[index] = earlier_values[index]
        grads_mid[micro_index] = grad_second
        second_dense = add_into(
            second_dense,
            (attn_grads[0], attn_grads[1], dense_four[0], dense_four[1], dense_four[2]),
        )
        second_expert = add_into(second_expert, expert_four)
        second_gains = add_into(second_gains, (gain_three, gain_four))
    grad_tail = jnp.zeros_like(tail)
    grad_state = jnp.zeros_like(state)
    grads_in = [None] * MICRO
    first_dense = None
    first_expert = None
    first_gains = None
    small_total = None
    for micro_index in reversed(range(MICRO)):
        first = first_weights()
        (w_mix_in, w_mix_out, w_router_a, w_shared_in_a, w_shared_out_a), (
            w_exp_in_a,
            w_exp_out_a,
        ) = first
        saved_mix, saved_moe_a, saved_attn, saved_moe_b, valid_rows = saved_all[micro_index]
        grad_first, gain_two, dense_two, expert_two = moe_backward(
            grads_mid[micro_index],
            saved_moe_a,
            w_router_a,
            w_shared_in_a,
            w_shared_out_a,
            w_exp_in_a,
            w_exp_out_a,
        )
        grad_start, gain_one, mix_grads, grad_small, grad_tail, grad_state = mixer_backward(
            grad_first, grad_tail, grad_state, saved_mix, w_mix_in, w_mix_out
        )
        grads_in[micro_index] = grad_start.reshape(slot_count, seg_len, -1)
        first_dense = add_into(
            first_dense, (mix_grads[0], mix_grads[1], dense_two[0], dense_two[1], dense_two[2])
        )
        first_expert = add_into(first_expert, expert_two)
        first_gains = add_into(first_gains, (gain_one, gain_two))
        small_total = add_into(small_total, grad_small)
    dense_shards = (
        lax.psum_scatter(first_dense[0], ("dp", "expert"), scatter_dimension=0, tiled=True),
        lax.psum_scatter(first_dense[1], ("dp", "expert"), scatter_dimension=0, tiled=True),
        lax.psum_scatter(first_dense[2], ("dp", "expert"), scatter_dimension=0, tiled=True),
        lax.psum_scatter(first_dense[3], ("dp", "expert"), scatter_dimension=0, tiled=True),
        lax.psum_scatter(first_dense[4], ("dp", "expert"), scatter_dimension=0, tiled=True),
        lax.psum_scatter(second_dense[0], ("dp", "expert"), scatter_dimension=0, tiled=True),
        lax.psum_scatter(second_dense[1], ("dp", "expert"), scatter_dimension=0, tiled=True),
        lax.psum_scatter(second_dense[2], ("dp", "expert"), scatter_dimension=0, tiled=True),
        lax.psum_scatter(second_dense[3], ("dp", "expert"), scatter_dimension=0, tiled=True),
        lax.psum_scatter(second_dense[4], ("dp", "expert"), scatter_dimension=0, tiled=True),
    )
    expert_shards = (
        lax.psum_scatter(
            first_expert[0].astype(jnp.bfloat16), "dp", scatter_dimension=1, tiled=True
        ).astype(jnp.float32),
        lax.psum_scatter(
            first_expert[1].astype(jnp.bfloat16), "dp", scatter_dimension=1, tiled=True
        ).astype(jnp.float32),
        lax.psum_scatter(
            second_expert[0].astype(jnp.bfloat16), "dp", scatter_dimension=1, tiled=True
        ).astype(jnp.float32),
        lax.psum_scatter(
            second_expert[1].astype(jnp.bfloat16), "dp", scatter_dimension=1, tiled=True
        ).astype(jnp.float32),
    )
    first_dense_shards = dense_shards[0:5]
    second_dense_shards = dense_shards[5:10]
    first_expert_shards = expert_shards[0:2]
    second_expert_shards = expert_shards[2:4]
    gain_total = jnp.stack([first_gains[0], first_gains[1], second_gains[0], second_gains[1]])
    small_sums = lax.psum(
        (
            gain_total,
            small_total["mixer_gain"],
            small_total["conv_weight"],
            small_total["conv_bias"],
            small_total["decay_log"],
            small_total["step_bias"],
            small_total["skip_gain"],
        ),
        ("dp", "expert"),
    )
    layer_output = jnp.stack(outputs, axis=1).reshape(slot_count * SLOT_LEN, -1)
    input_grad = jnp.stack(grads_in, axis=1).reshape(slot_count * SLOT_LEN, -1)
    return (
        layer_output,
        input_grad,
        first_dense_shards[0],
        first_dense_shards[1],
        first_dense_shards[2],
        first_dense_shards[3],
        first_dense_shards[4],
        first_expert_shards[0],
        first_expert_shards[1],
        second_dense_shards[0],
        second_dense_shards[1],
        second_dense_shards[2],
        second_dense_shards[3],
        second_dense_shards[4],
        second_expert_shards[0],
        second_expert_shards[1],
        small_sums[0],
        small_sums[1],
        small_sums[2],
        small_sums[3],
        small_sums[4],
        small_sums[5],
        small_sums[6],
    )


def solution(mesh):
    return jax.shard_map(
        per_device,
        mesh=mesh,
        in_specs=(
            P(("dp", "expert"), None),
            P(("dp", "expert"), None),
            P(("dp", "expert")),
            P(("dp", "expert"), None),
            P(("dp", "expert"), None),
            P(("dp", "expert"), None),
            P(("dp", "expert"), None),
            P(("dp", "expert"), None),
            P(("dp", "expert"), None),
            P(("dp", "expert"), None),
            P("expert", "dp", None),
            P("expert", "dp", None),
            P(("dp", "expert"), None),
            P(("dp", "expert"), None),
            P(("dp", "expert"), None),
            P(("dp", "expert"), None),
            P(("dp", "expert"), None),
            P("expert", "dp", None),
            P("expert", "dp", None),
            P(),
            P(),
            P(),
            P(),
            P(),
            P(),
            P(),
        ),
        out_specs=(
            P(("dp", "expert"), None),
            P(("dp", "expert"), None),
            P(("dp", "expert"), None),
            P(("dp", "expert"), None),
            P(("dp", "expert"), None),
            P(("dp", "expert"), None),
            P(("dp", "expert"), None),
            P("expert", "dp", None),
            P("expert", "dp", None),
            P(("dp", "expert"), None),
            P(("dp", "expert"), None),
            P(("dp", "expert"), None),
            P(("dp", "expert"), None),
            P(("dp", "expert"), None),
            P("expert", "dp", None),
            P("expert", "dp", None),
            P(),
            P(),
            P(),
            P(),
            P(),
            P(),
            P(),
        ),
        check_vma=False,
    )
```

profile of v0, /device:TPU:16, one launch (start us, length us, event | category | flops | bytes accessed | tf_op | source)
XLA Modules:
  0.0 3646.7 jit_solution(15218195779839435069)
XLA Ops:
  23.6 117.7 %all-gather.15.cloned.1.call-done = bf16[1536,6448]{1,0:T(8,128)(2,1)} async-done(((bf16[48,6448]{1,0:T(8,128)(2,1)}), bf16[1536,6448]{1,0:T(8,128)(2,1)}) %all-gather.15.cloned.1.call-update) | async-done | bytes 19808272 | tf_op jit(solution)/shard_map/all_gather | solution.py:136
  141.3 8.4 convolution_bitcast_fusion.1
  162.7 8.5 fusion.147
  196.8 9.2 fusion.166
  245.5 8.0 scatter_custom_fusion
  282.8 7.9 scatter_custom_fusion.2
  301.6 37.1 %all-to-all-done = bf16[8,2,60,1536]{3,1,2,0:T(2,128)(2,1)} async-done(((bf16[8,2,60,1536]{3,1,2,0:T(2,128)(2,1)}), bf16[8,2,60,1536]{3,1,2,0:T(2,128)(2,1)}, u32[]{:S(2)}, u32[]{:S(2)}) %all-to-all-start) | async-done | bytes 2949152 | tf_op jit(solution)/shard_map/all_to_all | solution.py:118
  338.7 8.1 all-to-all-start.4
  365.2 69.8 %all-to-all-done.4 = bf16[8,2,60,1536]{3,1,2,0:T(2,128)(2,1)} async-done(((bf16[8,2,60,1536]{3,1,2,0:T(2,128)(2,1)}), bf16[8,2,60,1536]{3,1,2,0:T(2,128)(2,1)}, u32[]{:S(2)}, u32[]{:S(2)}) %all-to-all-start.4) | async-done | bytes 2949152 | tf_op jit(solution)/shard_map/all_to_all | solution.py:118
  435.0 7.7 all-to-all-start.1
  443.4 122.5 %all-gather = bf16[32,48,16]{1,2,0:T(8,128)(2,1)S(1)} all-gather(bf16[1,48,16]{1,2,0:T(8,128)(2,1)S(1)} %bitcast.1007), channel_id=1, replica_groups=mesh['dp'=4,'expert'=8] {'dp','expert'}, dimensions={0}, use_global_device_ids=true | all-gather | bytes 50688 | tf_op jit(solution)/shard_map/all_gather | solution.py:138
  567.1 65.2 %all-gather.1 = bf16[32,48,16]{1,2,0:T(8,128)(2,1)S(1)} all-gather(bf16[1,48,16]{1,2,0:T(8,128)(2,1)S(1)} %bitcast.1008), channel_id=1, replica_groups=mesh['dp'=4,'expert'=8] {'dp','expert'}, dimensions={0}, use_global_device_ids=true | all-gather | bytes 50688 | tf_op jit(solution)/shard_map/all_gather | solution.py:151
  665.6 10.6 all-to-all-start.5
  797.9 13.2 scatter_custom_fusion.4
  837.7 8.8 scatter_custom_fusion.1
  857.4 34.9 all-to-all-done.8
  892.3 8.0 all-to-all-start.2
  910.7 13.2 scatter_custom_fusion.5
  934.7 28.1 all-to-all-done.2
  962.8 7.7 all-to-all-start.10
  978.5 8.8 scatter_custom_fusion.3
  998.2 35.0 all-to-all-done.10
  1041.7 9.1 fusion.118
  1050.8 8.8 bitcast_multiply_fusion.11
  1067.0 58.5 %all-to-all-done.6 = bf16[8,2,60,1536]{3,1,2,0:T(2,128)(2,1)} async-done(((bf16[8,2,60,1536]{3,1,2,0:T(2,128)(2,1)}), bf16[8,2,60,1536]{3,1,2,0:T(2,128)(2,1)}, u32[]{:S(2)}, u32[]{:S(2)}) %all-to-all-start.6) | async-done | bytes 2949152 | tf_op jit(solution)/shard_map/all_to_all | solution.py:118
  1125.6 8.0 all-to-all-start.3
  1133.6 7.8 fusion.41
  1146.0 50.6 %all-to-all-done.3 = bf16[8,2,60,1536]{3,1,2,0:T(2,128)(2,1)} async-done(((bf16[8,2,60,1536]{3,1,2,0:T(2,128)(2,1)}), bf16[8,2,60,1536]{3,1,2,0:T(2,128)(2,1)}, u32[]{:S(2)}, u32[]{:S(2)}) %all-to-all-start.3) | async-done | bytes 2949152 | tf_op jit(solution)/shard_map/all_to_all | solution.py:122
  1225.9 47.2 %all-to-all-done.9 = bf16[8,2,60,1536]{3,1,2,0:T(2,128)(2,1)} async-done(((bf16[8,2,60,1536]{3,1,2,0:T(2,128)(2,1)}), bf16[8,2,60,1536]{3,1,2,0:T(2,128)(2,1)}, u32[]{:S(2)}, u32[]{:S(2)}) %all-to-all-start.9) | async-done | bytes 2949152 | tf_op jit(solution)/shard_map/all_to_all | solution.py:122
  1273.1 8.0 all-to-all-start.7
  1302.2 49.8 %all-to-all-done.7 = bf16[8,2,60,1536]{3,1,2,0:T(2,128)(2,1)} async-done(((bf16[8,2,60,1536]{3,1,2,0:T(2,128)(2,1)}), bf16[8,2,60,1536]{3,1,2,0:T(2,128)(2,1)}, u32[]{:S(2)}, u32[]{:S(2)}) %all-to-all-start.7) | async-done | bytes 2949152 | tf_op jit(solution)/shard_map/all_to_all | solution.py:122
  1460.7 36.6 %scatter_fusion.1 = f32[128,16]{0,1:T(8,128)S(1)} fusion(f32[128,16]{0,1:T(8,128)S(1)} %broadcast_in_dim.469.clone, s32[768]{0:T(1024)S(1)} %reshape.1950, f32[768]{0:T(1024)S(1)} %reshape.1952), kind=kCustom, calls=%fused_computation.21 | custom fusion | flops 768 | bytes 15360 | tf_op jit(solution)/shard_map/transpose(jvp(jit(take_along_axis)))/scatter-add | solution.py:113
  1502.7 36.8 %scatter_fusion = f32[128,16]{0,1:T(8,128)S(1)} fusion(f32[128,16]{0,1:T(8,128)S(1)} %broadcast_in_dim.469.clone.1, s32[768]{0:T(1024)S(1)} %reshape.1944, f32[768]{0:T(1024)S(1)} %reshape.1946), kind=kCustom, calls=%fused_computation.20 | custom fusion | flops 768 | bytes 15360 | tf_op jit(solution)/shard_map/transpose(jvp(jit(take_along_axis)))/scatter-add | solution.py:113
  1599.0 36.6 %scatter_fusion.3 = f32[128,16]{0,1:T(8,128)S(1)} fusion(f32[128,16]{0,1:T(8,128)S(1)} %broadcast_in_dim.469.clone.2, s32[768]{0:T(1024)S(1)} %copy-done.9, f32[768]{0:T(1024)S(1)} %reshape.1964), kind=kCustom, calls=%fused_computation.23 | custom fusion | flops 768 | bytes 15360 | tf_op jit(solution)/shard_map/transpose(jvp(jit(take_along_axis)))/scatter-add | solution.py:113
  1635.9 36.6 %scatter_fusion.2 = f32[128,16]{0,1:T(8,128)S(1)} fusion(f32[128,16]{0,1:T(8,128)S(1)} %broadcast_in_dim.469.clone.3, s32[768]{0:T(1024)S(1)} %copy-done.8, f32[768]{0:T(1024)S(1)} %reshape.1958), kind=kCustom, calls=%fused_computation.22 | custom fusion | flops 768 | bytes 15360 | tf_op jit(solution)/shard_map/transpose(jvp(jit(take_along_axis)))/scatter-add | solution.py:113
  1681.7 11.4 fusion.88
  1693.1 12.4 fusion
  1706.5 13.7 scatter_custom_fusion.7
  1734.1 13.2 scatter_custom_fusion.6
  1754.8 44.7 %all-to-all-done.14 = bf16[8,2,60,1536]{3,1,2,0:T(2,128)(2,1)} async-done(((bf16[8,2,60,1536]{3,1,2,0:T(2,128)(2,1)}), bf16[8,2,60,1536]{3,1,2,0:T(2,128)(2,1)}, u32[]{:S(2)}, u32[]{:S(2)}) %all-to-all-start.14) | async-done | bytes 2949152 | tf_op jit(solution)/shard_map/all_to_all | solution.py:118
  1813.4 56.6 %all-to-all-done.12 = bf16[8,2,60,1536]{3,1,2,0:T(2,128)(2,1)S(1)} async-done(((bf16[8,2,60,1536]{3,1,2,0:T(2,128)(2,1)}), bf16[8,2,60,1536]{3,1,2,0:T(2,128)(2,1)S(1)}, u32[]{:S(2)}, u32[]{:S(2)}) %all-to-all-start.12) | async-done | bytes 2949152 | tf_op jit(solution)/shard_map/all_to_all | solution.py:118
  1877.1 9.1 bitcast_multiply_fusion.7
  1890.5 10.7 fusion.91
  1901.2 10.1 fusion.1
  1940.0 7.7 all-to-all-start.13
  1947.7 7.9 fusion.44
  1960.3 49.9 %all-to-all-done.13 = bf16[8,2,60,1536]{3,1,2,0:T(2,128)(2,1)S(1)} async-done(((bf16[8,2,60,1536]{3,1,2,0:T(2,128)(2,1)}), bf16[8,2,60,1536]{3,1,2,0:T(2,128)(2,1)S(1)}, u32[]{:S(2)}, u32[]{:S(2)}) %all-to-all-start.13) | async-done | bytes 2949152 | tf_op jit(solution)/shard_map/all_to_all | solution.py:122
  2064.2 17.9 all-to-all-done.15
  2178.6 10.1 fusion.151
  2238.4 12.6 fusion.506
  2251.1 12.5 fusion.254
  2268.2 9.0 convolution_add_fusion.3
  2292.4 8.0 convolution_add_fusion.1
  2301.6 8.1 fusion.331
  2309.7 12.1 convolution_add_fusion.2
  2323.0 18.9 fusion.309
  2341.9 30.8 convolution_add_fusion
  2415.5 15.8 reduce-scatter.25.cloned.1.call-done
  2431.4 132.9 %all-reduce.52.cloned.1.call-done = (f32[4,1536]{1,0:T(4,128)}, f32[3072]{0:T(1024)}, f32[4,3328]{1,0:T(4,128)}, f32[3328]{0:T(1024)}, f32[48]{0:T(128)}, /*index=5*/f32[48]{0:T(128)}, f32[48]{0:T(128)}) async-done(((f32[4,1536]{1,0:T(4,128)}, f32[3072]{0:T(1024)}, f32[4,3328]{1,0:T(4,128)}, f32[3328]{0:T(1024)}, f32[48]{0:T(128)}, /*index=5*/f32[48]{0:T(128)}, f32[48]{0:T(128)}), (f32[4,1536]{1,0:T(4,128)}, ...) | async-done | bytes 104016 | tf_op jit(solution)/shard_map/psum | solution.py:644
  2564.3 141.7 %reduce-scatter.33.cloned.1.call-done = f32[48,1536]{1,0:T(8,128)} async-done(((f32[1536,1536]{1,0:T(8,128)}), f32[48,1536]{1,0:T(8,128)}) %reduce-scatter.33.cloned.1.call-update) | async-done | bytes 294928 | tf_op jit(solution)/shard_map/reduce_scatter | solution.py:620
  2705.9 161.4 %reduce-scatter.23.cloned.1.call-done = f32[48,2048]{1,0:T(8,128)} async-done(((f32[1536,2048]{1,0:T(8,128)}), f32[48,2048]{1,0:T(8,128)}) %reduce-scatter.23.cloned.1.call-update) | async-done | bytes 393232 | tf_op jit(solution)/shard_map/reduce_scatter | solution.py:617
  2867.3 177.2 %reduce-scatter.31.cloned.1.call-done = f32[48,2560]{1,0:T(8,128)} async-done(((f32[1536,2560]{1,0:T(8,128)}), f32[48,2560]{1,0:T(8,128)}) %reduce-scatter.31.cloned.1.call-update) | async-done | bytes 491536 | tf_op jit(solution)/shard_map/reduce_scatter | solution.py:619
  3044.5 213.6 %reduce-scatter.21.cloned.1.call-done = f32[48,3072]{1,0:T(8,128)} async-done(((f32[1536,3072]{1,0:T(8,128)}), f32[48,3072]{1,0:T(8,128)}) %reduce-scatter.21.cloned.1.call-update) | async-done | bytes 589840 | tf_op jit(solution)/shard_map/reduce_scatter | solution.py:615
  3258.1 372.5 %reduce-scatter.19.cloned.1.call-done = f32[48,6448]{1,0:T(8,128)} async-done(((f32[1536,6448]{1,0:T(8,128)}), f32[48,6448]{1,0:T(8,128)}) %reduce-scatter.19.cloned.1.call-update) | async-done | bytes 1238032 | tf_op jit(solution)/shard_map/reduce_scatter | solution.py:614
  (1430 shorter events, 989.4 us)
Async XLA Ops:
  7.2 134.1 %all-gather.15.cloned.1.call-start = ((), (), s32[]{:S(2)}) async-start(), calls=%async_computation.30 | async-start | bytes 20680704 | tf_op jit(solution)/shard_map/all_gather | solution.py:136
  8.0 217.1 %all-gather.17.cloned.1.call-start = ((), (), s32[]{:S(2)}) async-start(), calls=%async_computation.31 | async-start | bytes 9732096 | tf_op jit(solution)/shard_map/all_gather | solution.py:137
  8.7 338.1 %all-gather.19.cloned.1.call-start = ((), (), s32[]{:S(2)}) async-start(), calls=%async_computation.32 | async-start | bytes 7864320 | tf_op jit(solution)/shard_map/all_gather | solution.py:127
  9.5 347.0 %all-gather.21.cloned.1.call-start = ((), (), s32[]{:S(2)}) async-start(), calls=%async_computation.33 | async-start | bytes 3932160 | tf_op jit(solution)/shard_map/all_gather | solution.py:128
  10.1 679.2 %all-gather.23.cloned.1.call-start = ((), (), s32[]{:S(2)}) async-start(), calls=%async_computation.34 | async-start | bytes 6488064 | tf_op jit(solution)/shard_map/all_gather | solution.py:139
  10.6 711.8 %all-gather.25.cloned.1.call-start = ((), (), s32[]{:S(2)}) async-start(), calls=%async_computation.35 | async-start | bytes 3244032 | tf_op jit(solution)/shard_map/all_gather | solution.py:140
  11.2 714.5 %all-gather.27.cloned.1.call-start = ((), (), s32[]{:S(2)}) async-start(), calls=%async_computation.36 | async-start | bytes 8110080 | tf_op jit(solution)/shard_map/all_gather | solution.py:149
  12.1 137.7 %copy-start.151 = (s32[256,6]{1,0:T(8,128)}, s32[256,6]{1,0:T(8,128)S(1)}, u32[]{:S(2)}) copy-start(s32[256,6]{1,0:T(8,128)S(1)} %copy.673) | copy-start | bytes 18436
  13.3 619.3 %copy-start.149 = (s32[256,6]{1,0:T(8,128)}, s32[256,6]{1,0:T(8,128)S(1)}, u32[]{:S(2)}) copy-start(s32[256,6]{1,0:T(8,128)S(1)} %copy.685) | copy-start | bytes 18436
  14.2 135.6 %copy-start.272 = (s32[768]{0:T(1024)}, s32[768]{0:T(1024)S(1)}, u32[]{:S(2)}) copy-start(s32[768]{0:T(1024)S(1)} %eq.138) | copy-start | bytes 9220
  15.8 134.0 %copy-start.274 = (s32[768]{0:T(1024)}, s32[768]{0:T(1024)S(1)}, u32[]{:S(2)}) copy-start(s32[768]{0:T(1024)S(1)} %convert_element_type.405) | copy-start | bytes 9220
  16.1 133.7 %copy-start.326 = (f32[128]{0:T(128)}, f32[128]{0:T(128)S(1)}, u32[]{:S(2)}) copy-start(f32[128]{0:T(128)S(1)} %fusion.460) | copy-start | bytes 1540
  16.8 134.4 %copy-start.200 = (f32[1536]{0:T(1024)}, f32[1536]{0:T(1024)S(1)}, u32[]{:S(2)}) copy-start(f32[1536]{0:T(1024)S(1)} %get-tuple-element.733) | copy-start | bytes 18436
  16.8 222.0 %copy-start.250 = (f32[1536]{0:T(1024)}, f32[1536]{0:T(1024)S(1)}, u32[]{:S(2)}) copy-start(f32[1536]{0:T(1024)S(1)} %get-tuple-element.732) | copy-start | bytes 18436
  16.8 134.4 %copy-start.315 = (f32[128]{0:T(128)}, f32[128]{0:T(128)S(1)}, u32[]{:S(2)}) copy-start(f32[128]{0:T(128)S(1)} %fusion.465) | copy-start | bytes 1540
  16.8 144.2 %copy-start.367 = (f32[48]{0:T(128)}, f32[48]{0:T(128)S(1)}, u32[]{:S(2)}) copy-start(f32[48]{0:T(128)S(1)} %exponential_negate_fusion) | copy-start | bytes 580
  17.6 145.1 %copy-start.245 = (f32[3328]{0:T(1024)}, f32[3328]{0:T(1024)S(1)}, u32[]{:S(2)}) copy-start(f32[3328]{0:T(1024)S(1)} %get-tuple-element.727) | copy-start | bytes 39940
  239.6 449.7 %copy-start.56 = (bf16[128,1536]{1,0:T(8,128)(2,1)}, bf16[128,1536]{1,0:T(8,128)(2,1)S(1)}, u32[]{:S(2)}) copy-start(bf16[128,1536]{1,0:T(8,128)(2,1)S(1)} %get-tuple-element.906) | copy-start | bytes 1179652
  239.6 453.8 %copy-start.62 = (bf16[128,1536]{1,0:T(8,128)(2,1)}, bf16[128,1536]{1,0:T(8,128)(2,1)S(1)}, u32[]{:S(2)}) copy-start(bf16[128,1536]{1,0:T(8,128)(2,1)S(1)} %get-tuple-element.905) | copy-start | bytes 1179652
  264.5 74.3 %all-to-all-start = ((bf16[8,2,60,1536]{3,1,2,0:T(2,128)(2,1)}), bf16[8,2,60,1536]{3,1,2,0:T(2,128)(2,1)}, u32[]{:S(2)}, u32[]{:S(2)}) async-start(bf16[8,2,60,1536]{3,1,2,0:T(2,128)(2,1)} %copy.676), calls=%async_computation | async-start | bytes 5898240 | tf_op jit(solution)/shard_map/all_to_all | solution.py:118
  338.7 96.2 %all-to-all-start.4 = ((bf16[8,2,60,1536]{3,1,2,0:T(2,128)(2,1)}), bf16[8,2,60,1536]{3,1,2,0:T(2,128)(2,1)}, u32[]{:S(2)}, u32[]{:S(2)}) async-start(bf16[8,2,60,1536]{3,1,2,0:T(2,128)(2,1)} %copy.701), calls=%async_computation.4 | async-start | bytes 5898240 | tf_op jit(solution)/shard_map/all_to_all | solution.py:118
  365.2 200.9 %copy-start.152 = (s32[256,6]{1,0:T(8,128)S(1)}, s32[256,6]{1,0:T(8,128)}, u32[]{:S(2)}) copy-start(s32[256,6]{1,0:T(8,128)} %copy-done.151) | copy-start | bytes 18436
  365.2 201.9 %copy-start.361 = (bf16[48,16]{0,1:T(8,128)(2,1)S(1)}, bf16[48,16]{0,1:T(8,128)(2,1)}, u32[]{:S(2)}) copy-start(bf16[48,16]{0,1:T(8,128)(2,1)} %param.44) | copy-start | bytes 4612
  435.0 230.6 %all-to-all-start.1 = ((bf16[8,2,60,1536]{3,1,2,0:T(2,128)(2,1)}), bf16[8,2,60,1536]{3,1,2,0:T(2,128)(2,1)}, u32[]{:S(2)}, u32[]{:S(2)}) async-start(bf16[8,2,60,1536]{3,1,2,0:T(2,128)(2,1)} %copy.678), calls=%async_computation.1 | async-start | bytes 5898240 | tf_op jit(solution)/shard_map/all_to_all | solution.py:122
  442.7 190.8 %copy-start.364 = (f32[1,2,128]{2,1,0:T(2,128)S(1)}, f32[1,2,128]{2,1,0:T(2,128)}, u32[]{:S(2)}) copy-start(f32[1,2,128]{2,1,0:T(2,128)} %copy-done.363) | copy-start | bytes 3076
  442.7 332.3 %all-gather.29.cloned.1.call-start = ((), (), s32[]{:S(2)}) async-start(), calls=%async_computation.37 | async-start | bytes 4866048 | tf_op jit(solution)/shard_map/all_gather | solution.py:150
  632.6 158.8 %copy-start.171 = (bf16[1536,16]{0,1:T(8,128)(2,1)}, bf16[1536,16]{0,1:T(8,128)(2,1)S(1)}, u32[]{:S(2)}) copy-start(bf16[1536,16]{0,1:T(8,128)(2,1)S(1)} %reshape.1979) | copy-start | bytes 147460
  665.6 73.4 %all-to-all-start.5 = ((bf16[8,2,60,1536]{3,1,2,0:T(2,128)(2,1)}), bf16[8,2,60,1536]{3,1,2,0:T(2,128)(2,1)}, u32[]{:S(2)}, u32[]{:S(2)}) async-start(bf16[8,2,60,1536]{3,1,2,0:T(2,128)(2,1)} %copy.703), calls=%async_computation.5 | async-start | bytes 5898240 | tf_op jit(solution)/shard_map/all_to_all | solution.py:122
  785.9 498.7 %copy-start.65 = (bf16[128,1536]{1,0:T(8,128)(2,1)}, bf16[128,1536]{1,0:T(8,128)(2,1)S(1)}, u32[]{:S(2)}) copy-start(bf16[128,1536]{1,0:T(8,128)(2,1)S(1)} %get-tuple-element.903) | copy-start | bytes 1179652
  785.9 503.6 %copy-start.59 = (bf16[128,1536]{1,0:T(8,128)(2,1)}, bf16[128,1536]{1,0:T(8,128)(2,1)S(1)}, u32[]{:S(2)}) copy-start(bf16[128,1536]{1,0:T(8,128)(2,1)S(1)} %get-tuple-element.904) | copy-start | bytes 1179652
  797.6 486.4 %copy-start.358 = (f32[128]{0:T(128)}, f32[128]{0:T(128)S(1)}, u32[]{:S(2)}) copy-start(f32[128]{0:T(128)S(1)} %fusion.442) | copy-start | bytes 1540
  822.0 70.2 %all-to-all-start.8 = ((bf16[8,2,60,1536]{3,1,2,0:T(2,128)(2,1)}), bf16[8,2,60,1536]{3,1,2,0:T(2,128)(2,1)}, u32[]{:S(2)}, u32[]{:S(2)}) async-start(bf16[8,2,60,1536]{3,1,2,0:T(2,128)(2,1)} %copy.717), calls=%async_computation.8 | async-start | bytes 5898240 | tf_op jit(solution)/shard_map/all_to_all | solution.py:118
  829.8 211.9 %all-gather.31.cloned.1.call-start = ((), (), s32[]{:S(2)}) async-start(), calls=%async_computation.38 | async-start | bytes 7864320 | tf_op jit(solution)/shard_map/all_gather | solution.py:127
  892.3 70.5 %all-to-all-start.2 = ((bf16[8,2,60,1536]{3,1,2,0:T(2,128)(2,1)}), bf16[8,2,60,1536]{3,1,2,0:T(2,128)(2,1)}, u32[]{:S(2)}, u32[]{:S(2)}) async-start(bf16[8,2,60,1536]{3,1,2,0:T(2,128)(2,1)} %copy.688), calls=%async_computation.2 | async-start | bytes 5898240 | tf_op jit(solution)/shard_map/all_to_all | solution.py:118
  910.4 449.3 %copy-start.356 = (f32[128]{0:T(128)}, f32[128]{0:T(128)S(1)}, u32[]{:S(2)}) copy-start(f32[128]{0:T(128)S(1)} %fusion.444) | copy-start | bytes 1540
  962.8 70.4 %all-to-all-start.10 = ((bf16[8,2,60,1536]{3,1,2,0:T(2,128)(2,1)}), bf16[8,2,60,1536]{3,1,2,0:T(2,128)(2,1)}, u32[]{:S(2)}, u32[]{:S(2)}) async-start(bf16[8,2,60,1536]{3,1,2,0:T(2,128)(2,1)} %copy.727), calls=%async_computation.10 | async-start | bytes 5898240 | tf_op jit(solution)/shard_map/all_to_all | solution.py:118
  970.5 80.2 %all-gather.33.cloned.1.call-start = ((), (), s32[]{:S(2)}) async-start(), calls=%async_computation.39 | async-start | bytes 3932160 | tf_op jit(solution)/shard_map/all_gather | solution.py:128
  1033.2 92.3 %all-to-all-start.6 = ((bf16[8,2,60,1536]{3,1,2,0:T(2,128)(2,1)}), bf16[8,2,60,1536]{3,1,2,0:T(2,128)(2,1)}, u32[]{:S(2)}, u32[]{:S(2)}) async-start(bf16[8,2,60,1536]{3,1,2,0:T(2,128)(2,1)} %copy.713), calls=%async_computation.6 | async-start | bytes 5898240 | tf_op jit(solution)/shard_map/all_to_all | solution.py:118
  1040.9 243.7 %all-gather.35.cloned.1.call-start = ((), (), s32[]{:S(2)}) async-start(), calls=%async_computation.40 | async-start | bytes 6488064 | tf_op jit(solution)/shard_map/all_gather | solution.py:152
  1125.6 71.0 %all-to-all-start.3 = ((bf16[8,2,60,1536]{3,1,2,0:T(2,128)(2,1)}), bf16[8,2,60,1536]{3,1,2,0:T(2,128)(2,1)}, u32[]{:S(2)}, u32[]{:S(2)}) async-start(bf16[8,2,60,1536]{3,1,2,0:T(2,128)(2,1)} %copy.690), calls=%async_computation.3 | async-start | bytes 5898240 | tf_op jit(solution)/shard_map/all_to_all | solution.py:122
  1196.6 76.5 %all-to-all-start.9 = ((bf16[8,2,60,1536]{3,1,2,0:T(2,128)(2,1)}), bf16[8,2,60,1536]{3,1,2,0:T(2,128)(2,1)}, u32[]{:S(2)}, u32[]{:S(2)}) async-start(bf16[8,2,60,1536]{3,1,2,0:T(2,128)(2,1)} %copy.719), calls=%async_computation.9 | async-start | bytes 5898240 | tf_op jit(solution)/shard_map/all_to_all | solution.py:122
  1204.3 156.0 %all-gather.37.cloned.1.call-start = ((), (), s32[]{:S(2)}) async-start(), calls=%async_computation.41 | async-start | bytes 3244032 | tf_op jit(solution)/shard_map/all_gather | solution.py:153
  1273.1 78.9 %all-to-all-start.7 = ((bf16[8,2,60,1536]{3,1,2,0:T(2,128)(2,1)}), bf16[8,2,60,1536]{3,1,2,0:T(2,128)(2,1)}, u32[]{:S(2)}, u32[]{:S(2)}) async-start(bf16[8,2,60,1536]{3,1,2,0:T(2,128)(2,1)} %copy.715), calls=%async_computation.7 | async-start | bytes 5898240 | tf_op jit(solution)/shard_map/all_to_all | solution.py:122
  1352.0 75.8 %all-to-all-start.11 = ((bf16[8,2,60,1536]{3,1,2,0:T(2,128)(2,1)}), bf16[8,2,60,1536]{3,1,2,0:T(2,128)(2,1)}, u32[]{:S(2)}, u32[]{:S(2)}) async-start(bf16[8,2,60,1536]{3,1,2,0:T(2,128)(2,1)} %copy.729), calls=%async_computation.11 | async-start | bytes 5898240 | tf_op jit(solution)/shard_map/all_to_all | solution.py:122
  1359.7 1039.1 %reduce-scatter.45.cloned.1.call-start = ((), (), s32[]{:S(2)}) async-start(), calls=%async_computation.55 | async-start | bytes 811008
  1364.4 175.2 %copy-start.137 = (f32[128,1024]{1,0:T(8,128)}, f32[128,1024]{1,0:T(8,128)S(1)}, u32[]{:S(2)}) copy-start(f32[128,1024]{1,0:T(8,128)S(1)} %get-tuple-element.838) | copy-start | bytes 1572868
  1599.0 801.3 %reduce-scatter.43.cloned.1.call-start = ((), (), s32[]{:S(2)}) async-start(), calls=%async_computation.54 | async-start | bytes 811008
  1673.9 727.7 %reduce-scatter.41.cloned.1.call-start = ((), (), s32[]{:S(2)}) async-start(), calls=%async_computation.53 | async-start | bytes 3932160 | tf_op jit(solution)/shard_map/reduce_scatter | solution.py:635
  1681.4 722.8 %reduce-scatter.39.cloned.1.call-start = ((), (), s32[]{:S(2)}) async-start(), calls=%async_computation.52 | async-start | bytes 7864320 | tf_op jit(solution)/shard_map/reduce_scatter | solution.py:632
  1727.6 71.8 %all-to-all-start.14 = ((bf16[8,2,60,1536]{3,1,2,0:T(2,128)(2,1)}), bf16[8,2,60,1536]{3,1,2,0:T(2,128)(2,1)}, u32[]{:S(2)}, u32[]{:S(2)}) async-start(bf16[8,2,60,1536]{3,1,2,0:T(2,128)(2,1)} %copy.743), calls=%async_computation.14 | async-start | bytes 5898240 | tf_op jit(solution)/shard_map/all_to_all | solution.py:118
  1799.4 70.6 %all-to-all-start.12 = ((bf16[8,2,60,1536]{3,1,2,0:T(2,128)(2,1)}), bf16[8,2,60,1536]{3,1,2,0:T(2,128)(2,1)S(1)}, u32[]{:S(2)}, u32[]{:S(2)}) async-start(bf16[8,2,60,1536]{3,1,2,0:T(2,128)(2,1)} %copy.737), calls=%async_computation.12 | async-start | bytes 5898240 | tf_op jit(solution)/shard_map/all_to_all | solution.py:118
  1806.6 603.0 %reduce-scatter.29.cloned.1.call-start = ((), (), s32[]{:S(2)}) async-start(), calls=%async_computation.47 | async-start | bytes 3932160 | tf_op jit(solution)/shard_map/reduce_scatter | solution.py:629
  1876.8 535.3 %reduce-scatter.27.cloned.1.call-start = ((), (), s32[]{:S(2)}) async-start(), calls=%async_computation.46 | async-start | bytes 7864320 | tf_op jit(solution)/shard_map/reduce_scatter | solution.py:626
  1911.4 504.2 %reduce-scatter.37.cloned.1.call-start = ((), (), s32[]{:S(2)}) async-start(), calls=%async_computation.51 | async-start | bytes 6488064 | tf_op jit(solution)/shard_map/reduce_scatter | solution.py:623
  1917.4 498.2 %reduce-scatter.35.cloned.1.call-start = ((), (), s32[]{:S(2)}) async-start(), calls=%async_computation.50 | async-start | bytes 12976128 | tf_op jit(solution)/shard_map/reduce_scatter | solution.py:622
  1940.0 70.2 %all-to-all-start.13 = ((bf16[8,2,60,1536]{3,1,2,0:T(2,128)(2,1)}), bf16[8,2,60,1536]{3,1,2,0:T(2,128)(2,1)S(1)}, u32[]{:S(2)}, u32[]{:S(2)}) async-start(bf16[8,2,60,1536]{3,1,2,0:T(2,128)(2,1)} %copy.739), calls=%async_computation.13 | async-start | bytes 5898240 | tf_op jit(solution)/shard_map/all_to_all | solution.py:122
  2011.8 70.3 %all-to-all-start.15 = ((bf16[8,2,60,1536]{3,1,2,0:T(2,128)(2,1)}), bf16[8,2,60,1536]{3,1,2,0:T(2,128)(2,1)}, u32[]{:S(2)}, u32[]{:S(2)}) async-start(bf16[8,2,60,1536]{3,1,2,0:T(2,128)(2,1)} %copy.745), calls=%async_computation.15 | async-start | bytes 5898240 | tf_op jit(solution)/shard_map/all_to_all | solution.py:122
  2019.4 412.0 %reduce-scatter.25.cloned.1.call-start = ((), (), s32[]{:S(2)}) async-start(), calls=%async_computation.45 | async-start | bytes 6488064 | tf_op jit(solution)/shard_map/reduce_scatter | solution.py:618
  2033.5 530.8 %all-reduce.52.cloned.1.call-start = ((), (), s32[]{:S(2)}) async-start(), calls=%async_computation.56 | async-start | bytes 216064 | tf_op jit(solution)/shard_map/psum | solution.py:644
  2268.2 437.8 %reduce-scatter.33.cloned.1.call-start = ((), (), s32[]{:S(2)}) async-start(), calls=%async_computation.49 | async-start | bytes 9732096 | tf_op jit(solution)/shard_map/reduce_scatter | solution.py:620
  2277.3 590.0 %reduce-scatter.23.cloned.1.call-start = ((), (), s32[]{:S(2)}) async-start(), calls=%async_computation.44 | async-start | bytes 12976128 | tf_op jit(solution)/shard_map/reduce_scatter | solution.py:617
  2287.8 756.7 %reduce-scatter.31.cloned.1.call-start = ((), (), s32[]{:S(2)}) async-start(), calls=%async_computation.48 | async-start | bytes 16220160 | tf_op jit(solution)/shard_map/reduce_scatter | solution.py:619
  2300.5 957.6 %reduce-scatter.21.cloned.1.call-start = ((), (), s32[]{:S(2)}) async-start(), calls=%async_computation.43 | async-start | bytes 19464192 | tf_op jit(solution)/shard_map/reduce_scatter | solution.py:615
  2321.9 1308.8 %reduce-scatter.19.cloned.1.call-start = ((), (), s32[]{:S(2)}) async-start(), calls=%async_computation.42 | async-start | bytes 41361408 | tf_op jit(solution)/shard_map/reduce_scatter | solution.py:614
  (406 other events, 4255.6 us)
Sparse Core Ops, SparseCore 0:
  11.0 130.2 all-gather.14
  144.3 80.6 all-gather.16
  226.6 45.5 all-gather.18
  273.7 28.5 all-gather.20
  305.1 123.8 all-gather.22
  431.8 102.7 all-gather.24
  537.6 76.3 all-gather.26
  617.0 63.2 all-gather.28
  832.1 47.2 all-gather.30
  972.6 29.3 all-gather.32
  1044.7 93.3 all-gather.34
  1207.8 106.8 all-gather.36
  1599.1 95.2 reduce-scatter.44
  1699.4 112.2 reduce-scatter.42
  1814.1 52.1 reduce-scatter.40
  1868.8 58.3 reduce-scatter.38
  1930.2 37.9 reduce-scatter.28
  1970.7 58.3 reduce-scatter.26
  2035.3 113.8 reduce-scatter.36
  2156.7 154.7 reduce-scatter.34
  2317.8 113.5 reduce-scatter.24
  2439.5 124.7 all-reduce.51
  2571.7 134.1 reduce-scatter.32
  2712.4 154.8 reduce-scatter.22
  2874.9 169.5 reduce-scatter.30
  3052.5 205.5 reduce-scatter.20
  3266.1 364.5 reduce-scatter.18
where the time goes:
time: 3660 us; the launch traced here: 3650 us
  waiting for transfers between devices  1930 us (53%)
  matrix products  529 us (14%)
  local copies, waits for them, and re-layouts  479 us (13%)
  other arithmetic  374 us (10%)
  blocking collectives  188 us (5%)
  starting transfers between devices  127 us (3%)
    reduce_scatter x1, waiting for transfers between devices, per_device(): lax.psum_scatter(first_dense[0], ('dp', 'expert'), scatter_dimension=0, t...  373 us
    all_to_all x8, waiting for transfers between devices, to_experts(): lax.all_to_all(buffer, 'expert', split_axis=0, concat_axis=0, tiled=True)  365 us
    all_to_all x8, waiting for transfers between devices, from_experts(): lax.all_to_all(buffer, 'expert', split_axis=0, concat_axis=0, tiled=True)  222 us
    reduce_scatter x1, waiting for transfers between devices, per_device(): lax.psum_scatter(first_dense[1], ('dp', 'expert'), scatter_dimension=0, t...  214 us
    reduce_scatter x1, waiting for transfers between devices, per_device(): lax.psum_scatter(second_dense[0], ('dp', 'expert'), scatter_dimension=0,...  177 us
    reduce_scatter x1, waiting for transfers between devices, per_device(): lax.psum_scatter(first_dense[3], ('dp', 'expert'), scatter_dimension=0, t...  161 us
    scatter-add x6, other arithmetic, route_weights(): chosen = jnp.take_along_axis(logits, routes, axis=1)  148 us
    reduce_scatter x1, waiting for transfers between devices, per_device(): lax.psum_scatter(second_dense[1], ('dp', 'expert'), scatter_dimension=0,...  142 us
  transfers between devices with their start and end apart: 43, of which 23 were waited for; matrix products, arithmetic and copies ran while one was open for 31% of the time, Pallas kernels for 0%

commit v1 on v0

v1 whole, which is shorter than its diff:
```python
import functools

import jax
import jax.numpy as jnp
from jax import lax
from jax.experimental import pallas as pl
from jax.experimental.pallas import tpu as pltpu
from jax.sharding import PartitionSpec as P

MHEADS = 48
MHDIM = 64
NSTATE = 128
KCONV = 4
AHEADS = 12
KVHEADS = 4
AHDIM = 128
SLOT_LEN = 256
HALF = 128
CAP = 60
DI = 3072
CONVCH = 3328
QD = 1536
KVD = 512
QKV = 2560

EPS = 1e-05
HIGH = lax.Precision.HIGHEST
FLOAT = jnp.float32
BRAIN = jnp.bfloat16
MESH = pl.DeviceIdType.MESH
BOTH = ("dp", "expert")
PICKED = SLOT_LEN // HALF * 64
MIB = 2**20


def matmul(left, right):
    return jnp.dot(left, right, preferred_element_type=FLOAT)


def matmul_nt(left, right):
    return lax.dot_general(left, right, (((1,), (1,)), ((), ())), preferred_element_type=FLOAT)


def matmul_tn(left, right):
    return lax.dot_general(left, right, (((0,), (0,)), ((), ())), preferred_element_type=FLOAT)


def silu_of(values):
    return values * jax.nn.sigmoid(values)


def softplus_of(values):
    return jnp.log1p(jnp.exp(values))


def rms_norm(values, norm_gain):
    return values * lax.rsqrt(jnp.mean(values * values, axis=-1, keepdims=True) + EPS) * norm_gain


def whole_spec(shape):
    return pl.BlockSpec(shape, lambda *at: (0,) * len(shape), pipeline_mode=pl.Buffered(1))


def expert_place(group):
    me = lax.axis_index("expert")
    return me // 2, lax.rem(me, 2)

def greet(z, x, line):
    barrier = pltpu.get_barrier_semaphore()
    def hello(device):
        pl.semaphore_signal(barrier, inc=1, device_id={"expert": device}, device_id_type=MESH)
    hello(2 * z + 1 - x)
    @pl.when(z > 0)
    def _():
        hello(2 * (z - 1) + x)
    @pl.when(z < line - 1)
    def _():
        hello(2 * (z + 1) + x)
    pl.semaphore_wait(barrier, 1 + jnp.where(z > 0, 1, 0) + jnp.where(z < line - 1, 1, 0))

def spread_kernel(count, group, *refs):
    ins, outs = refs[:count], refs[count:2 * count]
    up_sems, down_sems, cross_sems, recv_sems, own_sems = refs[2 * count:]
    line = group // 2
    z, x = expert_place(group)
    greet(z, x, line)

    def copy(i, src, place, sem, device):
        return pltpu.make_async_remote_copy(
            src_ref=src, dst_ref=outs[i].at[place], send_sem=sem, recv_sem=recv_sems.at[i, place],
            device_id={"expert": device}, device_id_type=MESH)

    def moves(i, s, rising):
        zz = z - s if rising else z + s
        place = 2 * zz + x
        src = ins[i] if s == 0 else outs[i].at[place]
        up = copy(i, src, place, up_sems.at[i, s], 2 * (z + 1) + x)
        down = copy(i, src, place, down_sems.at[i, s], 2 * (z - 1) + x)
        cross = copy(i, src, place, cross_sems.at[i, zz], 2 * z + 1 - x)
        return up, down, cross

    for i in range(count):
        pltpu.make_async_copy(ins[i], outs[i].at[2 * z + x], own_sems.at[i]).start()
    for s in range(line):
        for rising in (True, False) if s else (True,):
            valid = (z - s >= 0) if rising else (z + s < line)
            @pl.when(valid)
            def _():
                for i in range(count):
                    up, down, cross = moves(i, s, rising)
                    if s:
                        cross.wait_recv()
                    if rising:
                        pl.when(z < line - 1)(up.start)
                    if not rising or s == 0:
                        pl.when(z > 0)(down.start)
                    cross.start()
    for i in range(count):
        for zz in range(line):
            place = 2 * zz + 1 - x
            copy(i, ins[i], place, own_sems.at[i], 2 * z + 1 - x).wait_recv()
        pltpu.make_async_copy(ins[i], outs[i].at[2 * z + x], own_sems.at[i]).wait()
    for s in range(line):
        for rising in (True, False) if s else (True,):
            valid = (z - s >= 0) if rising else (z + s < line)
            @pl.when(valid)
            def _():
                for i in range(count):
                    up, down, cross = moves(i, s, rising)
                    if rising:
                        pl.when(z < line - 1)(up.wait_send)
                    if not rising or s == 0:
                        pl.when(z > 0)(down.wait_send)
                    cross.wait_send()

def spread(arrays, group, number):
    n = len(arrays); line = group // 2
    return pl.pallas_call(
        functools.partial(spread_kernel, n, group),
        out_shape=[jax.ShapeDtypeStruct((group,) + a.shape, a.dtype) for a in arrays],
        in_specs=[pl.BlockSpec(memory_space=pl.ANY)] * n,
        out_specs=[pl.BlockSpec(memory_space=pl.ANY)] * n,
        scratch_shapes=[
            pltpu.SemaphoreType.DMA((n, line)), pltpu.SemaphoreType.DMA((n, line)),
            pltpu.SemaphoreType.DMA((n, line)), pltpu.SemaphoreType.DMA((n, group)),
            pltpu.SemaphoreType.DMA((n,))],
        compiler_params=pltpu.CompilerParams(collective_id=number, has_side_effects=True),
        name="spread%d" % number,
    )(*arrays)

def gather_sum_kernel(count, group, *refs):
    ins, outs = refs[:count], refs[count:2 * count]
    line = group // 2
    bufs = refs[2 * count:2 * count + 4 * count]
    own_sems, cross_send, cross_recv, up_send, up_recv, down_send, down_recv = refs[6 * count:]
    held = [bufs[4 * i] for i in range(count)]
    crossed = [bufs[4 * i + 1] for i in range(count)]
    below = [bufs[4 * i + 2] for i in range(count)]
    above = [bufs[4 * i + 3] for i in range(count)]
    z, x = expert_place(group)
    greet(z, x, line)

    def own(i, d):
        return pltpu.make_async_copy(ins[i].at[2 * d + x], held[i].at[d], own_sems.at[i, d])

    def cross(i, d):
        return pltpu.make_async_remote_copy(
            src_ref=ins[i].at[2 * d + 1 - x], dst_ref=crossed[i].at[d], send_sem=cross_send.at[i, d],
            recv_sem=cross_recv.at[i, d], device_id={"expert": 2 * z + 1 - x}, device_id_type=MESH)

    def rise(i, d):
        return pltpu.make_async_remote_copy(
            src_ref=held[i].at[d], dst_ref=below[i].at[d], send_sem=up_send.at[i, d],
            recv_sem=up_recv.at[i, d], device_id={"expert": 2 * (z + 1) + x}, device_id_type=MESH)

    def fall(i, d):
        return pltpu.make_async_remote_copy(
            src_ref=held[i].at[d], dst_ref=above[i].at[d], send_sem=down_send.at[i, d],
            recv_sem=down_recv.at[i, d], device_id={"expert": 2 * (z - 1) + x}, device_id_type=MESH)

    def order(act):
        for k in range(line):
            pl.when(line - 1 - k > z)(functools.partial(act, line - 1 - k))
            pl.when(k < z)(functools.partial(act, k))
        for k in range(line):
            pl.when(k == z)(functools.partial(act, k))

    def start_cross(d):
        for i in range(count):
            cross(i, d).start()

    def start_own(d):
        for i in range(count):
            own(i, d).start()
    order(start_cross)
    order(start_own)

    def add_rows(i, d, target, sources):
        rows = held[i].shape[1]
        step = min(rows, 16)
        def body(j, carry):
            at = pl.ds(pl.multiple_of(j * step, step), step)
            total = held[i][d, at].astype(FLOAT)
            for source in sources:
                total = total + source[i][d, at].astype(FLOAT)
            if target is None:
                held[i][d, at] = total.astype(held[i].dtype)
            else:
                target[i][at] = total.astype(target[i].dtype)
            return carry
        lax.fori_loop(0, rows // step, body, 0)

    def ready(i, d):
        own(i, d).wait()
        cross(i, d).wait_recv()

    for k in range(line - 1):
        d = line - 1 - k
        @pl.when(d > z)
        def _():
            for i in range(count):
                ready(i, d)
                @pl.when(z > 0)
                def _():
                    rise(i, d).wait_recv()
                    add_rows(i, d, None, [crossed, below])
                @pl.when(z == 0)
                def _():
                    add_rows(i, d, None, [crossed])
                rise(i, d).start()
        d = k
        @pl.when(d < z)
        def _():
            for i in range(count):
                ready(i, d)
                @pl.when(z < line - 1)
                def _():
                    fall(i, d).wait_recv()
                    add_rows(i, d, None, [crossed, above])
                @pl.when(z == line - 1)
                def _():
                    add_rows(i, d, None, [crossed])
                fall(i, d).start()
    for d in range(line):
        @pl.when(d == z)
        def _():
            for i in range(count):
                ready(i, d)
                if d == 0:
                    fall(i, d).wait_recv()
                    add_rows(i, d, outs, [crossed, above])
                elif d == line - 1:
                    rise(i, d).wait_recv()
                    add_rows(i, d, outs, [crossed, below])
                else:
                    fall(i, d).wait_recv()
                    rise(i, d).wait_recv()
                    add_rows(i, d, outs, [crossed, below, above])
    for d in range(line):
        for i in range(count):
            cross(i, d).wait_send()
            pl.when(d > z)(rise(i, d).wait_send)
            pl.when(d < z)(fall(i, d).wait_send)

def gather_sum(arrays, group, number):
    n = len(arrays); line = group // 2
    scratch = []
    for a in arrays:
        scratch += [pltpu.VMEM((line,) + a.shape[1:], a.dtype)] * 4
    return pl.pallas_call(
        functools.partial(gather_sum_kernel, n, group),
        out_shape=[jax.ShapeDtypeStruct(a.shape[1:], FLOAT) for a in arrays],
        in_specs=[pl.BlockSpec(memory_space=pl.ANY)] * n,
        out_specs=[pl.BlockSpec(memory_space=pltpu.VMEM)] * n,
        scratch_shapes=scratch + [pltpu.SemaphoreType.DMA((n, line))] * 7,
        compiler_params=pltpu.CompilerParams(collective_id=number, has_side_effects=True, vmem_limit_bytes=40 * 2**20),
        name="gather_sum%d" % number,
    )(*arrays)


def swap_sum_kernel(steps, value_ref, out_ref, totals, landed, send_sems, recv_sems):
    barrier = pltpu.get_barrier_semaphore()

    def partner(axis, bit):
        me = lax.axis_index(axis)
        return {axis: me + bit * (1 - 2 * lax.rem(me // bit, 2))}

    for axis, bit in steps:
        pl.semaphore_signal(barrier, inc=1, device_id=partner(axis, bit), device_id_type=MESH)
    pl.semaphore_wait(barrier, len(steps))
    totals[0] = value_ref[...]
    for step, (axis, bit) in enumerate(steps):
        copy = pltpu.make_async_remote_copy(
            src_ref=totals.at[step],
            dst_ref=landed.at[step],
            send_sem=send_sems.at[step],
            recv_sem=recv_sems.at[step],
            device_id=partner(axis, bit),
            device_id_type=MESH,
        )
        copy.start()
        copy.wait()
        totals[step + 1] = totals[step] + landed[step]
    out_ref[...] = totals[len(steps)]


def swap_sum(value, number):
    steps = []
    for axis in BOTH:
        bit = 1
        while bit < lax.axis_size(axis):
            steps.append((axis, bit))
            bit *= 2
    vmem = pl.BlockSpec(memory_space=pltpu.VMEM)
    return pl.pallas_call(
        functools.partial(swap_sum_kernel, steps),
        out_shape=jax.ShapeDtypeStruct(value.shape, FLOAT),
        in_specs=[vmem],
        out_specs=vmem,
        scratch_shapes=[
            pltpu.VMEM((len(steps) + 1,) + value.shape, FLOAT),
            pltpu.VMEM((len(steps),) + value.shape, FLOAT),
            pltpu.SemaphoreType.DMA((len(steps),)),
            pltpu.SemaphoreType.DMA((len(steps),)),
        ],
        compiler_params=pltpu.CompilerParams(collective_id=number, has_side_effects=True),
        name="swap_sum",
    )(value)


def state_setup(step_ref, rate_ref, step_t_ref, rate_t_ref, b_ref, c_ref, cum, cum_t, cross):
    length = step_ref.shape[0]
    down = lax.broadcasted_iota(jnp.int32, (length, length), 0)
    along = lax.broadcasted_iota(jnp.int32, (length, length), 1)
    lower = jnp.where(down >= along, 1.0, 0.0)
    upper = jnp.where(down <= along, 1.0, 0.0)
    cum[...] = jnp.dot(
        lower, step_ref[...] * rate_ref[...], precision=HIGH, preferred_element_type=FLOAT
    )
    cum_t[...] = jnp.dot(
        step_t_ref[...] * rate_t_ref[...], upper, precision=HIGH, preferred_element_type=FLOAT
    )
    cross[...] = lax.dot_general(
        c_ref[...], b_ref[...], (((1,), (1,)), ((), ())), precision=HIGH, preferred_element_type=FLOAT
    )


def decay_of(head, cum, cum_t):
    length, heads = cum.shape
    lane = lax.broadcasted_iota(jnp.int32, (length, heads), 1)
    column = jnp.sum(jnp.where(lane == head, cum[...], 0.0), axis=1, keepdims=True)
    spread_out = column - cum_t[pl.ds(head, 1), :]
    down = lax.broadcasted_iota(jnp.int32, (length, length), 0)
    along = lax.broadcasted_iota(jnp.int32, (length, length), 1)
    return jnp.exp(jnp.where(down >= along, spread_out, -1e30))


def state_forward_kernel(
    x_ref, b_ref, c_ref, step_ref, rate_ref, step_t_ref, rate_t_ref, skip_ref, y_ref, cum, cum_t, cross
):
    pair = pl.program_id(0)

    @pl.when(pair == 0)
    def _():
        state_setup(step_ref, rate_ref, step_t_ref, rate_t_ref, b_ref, c_ref, cum, cum_t, cross)

    values = x_ref[...]
    values_low = values.astype(BRAIN)
    total = values * skip_ref[...]
    side = lax.broadcasted_iota(jnp.int32, values.shape, 1) // MHDIM
    for j in range(2):
        head = 2 * pair + j
        mixing = cross[...] * decay_of(head, cum, cum_t) * step_t_ref[pl.ds(head, 1), :]
        part = jnp.dot(mixing.astype(BRAIN), values_low, preferred_element_type=FLOAT)
        total = total + jnp.where(side == j, part, 0.0)
    y_ref[...] = total


def state_specs(length):
    column = lambda place: pl.BlockSpec((length, NSTATE), place)
    return [
        column(lambda i: (0, i)),
        column(lambda i: (0, DI // NSTATE)),
        column(lambda i: (0, DI // NSTATE + 1)),
        whole_spec((length, MHEADS)),
        whole_spec((1, MHEADS)),
        whole_spec((MHEADS, length)),
        whole_spec((MHEADS, 1)),
        pl.BlockSpec((1, 2 * MHDIM), lambda i: (0, i)),
    ]


def state_operands(conv_out, step_size, decay_rate, skip_gain):
    return (
        conv_out,
        conv_out,
        conv_out,
        step_size,
        decay_rate[None, :],
        step_size.T,
        decay_rate[:, None],
        jnp.repeat(skip_gain, MHDIM)[None, :],
    )


def state_forward(conv_out, step_size, decay_rate, skip_gain):
    length = conv_out.shape[0]
    return pl.pallas_call(
        state_forward_kernel,
        grid=(MHEADS // 2,),
        out_shape=jax.ShapeDtypeStruct((length, DI), FLOAT),
        in_specs=state_specs(length),
        out_specs=pl.BlockSpec((length, 2 * MHDIM), lambda i: (0, i)),
        scratch_shapes=[
            pltpu.VMEM((length, MHEADS), FLOAT),
            pltpu.VMEM((MHEADS, length), FLOAT),
            pltpu.VMEM((length, length), FLOAT),
        ],
        compiler_params=pltpu.CompilerParams(vmem_limit_bytes=32 * MIB),
        name="state_forward",
    )(*state_operands(conv_out, step_size, decay_rate, skip_gain))


def state_backward_kernel(
    x_ref, b_ref, c_ref, step_ref, rate_ref, step_t_ref, rate_t_ref, skip_ref, dy_ref,
    dx_ref, db_ref, dc_ref, row_ref, column_ref, cum, cum_t, cross, dcross,
):
    pair = pl.program_id(0)

    @pl.when(pair == 0)
    def _():
        state_setup(step_ref, rate_ref, step_t_ref, rate_t_ref, b_ref, c_ref, cum, cum_t, cross)
        dcross[...] = jnp.zeros_like(dcross)
        row_ref[...] = jnp.zeros_like(row_ref)

    values_low = x_ref[...].astype(BRAIN)
    grads = dy_ref[...]
    total = grads * skip_ref[...]
    side = lax.broadcasted_iota(jnp.int32, grads.shape, 1) // MHDIM
    lane = lax.broadcasted_iota(jnp.int32, row_ref.shape, 1)
    for j in range(2):
        head = 2 * pair + j
        steps = step_t_ref[pl.ds(head, 1), :]
        decay = decay_of(head, cum, cum_t)
        own = jnp.where(side == j, grads, 0.0).astype(BRAIN)
        mixing = cross[...] * decay
        total = total + matmul_tn((mixing * steps).astype(BRAIN), own)
        dmix = matmul_nt(own, values_low)
        dcross[...] += dmix * decay * steps
        weighed = dmix * mixing
        column_ref[pl.ds(head, 1), :] = jnp.sum(weighed, axis=0, keepdims=True)
        row_sum = jnp.sum(weighed * steps, axis=1, keepdims=True)
        row_ref[...] += jnp.where(lane == head, row_sum, 0.0)
    dx_ref[...] = total

    @pl.when(pair == pl.num_programs(0) - 1)
    def _():
        dc_ref[...] = jnp.dot(dcross[...], b_ref[...], precision=HIGH, preferred_element_type=FLOAT)
        db_ref[...] = lax.dot_general(
            dcross[...], c_ref[...], (((0,), (0,)), ((), ())), precision=HIGH, preferred_element_type=FLOAT
        )


def state_backward(conv_out, step_size, decay_rate, skip_gain, grad_mixed):
    length = conv_out.shape[0]
    pair_block = pl.BlockSpec((length, 2 * MHDIM), lambda i: (0, i))
    dx, db, dc, row_sums, column_sums = pl.pallas_call(
        state_backward_kernel,
        grid=(MHEADS // 2,),
        out_shape=[
            jax.ShapeDtypeStruct((length, DI), FLOAT),
            jax.ShapeDtypeStruct((length, NSTATE), FLOAT),
            jax.ShapeDtypeStruct((length, NSTATE), FLOAT),
            jax.ShapeDtypeStruct((length, MHEADS), FLOAT),
            jax.ShapeDtypeStruct((MHEADS, length), FLOAT),
        ],
        in_specs=state_specs(length) + [pair_block],
        out_specs=[
            pair_block,
            pl.BlockSpec((length, NSTATE), lambda i: (0, 0)),
            pl.BlockSpec((length, NSTATE), lambda i: (0, 0)),
            pl.BlockSpec((length, MHEADS), lambda i: (0, 0)),
            pl.BlockSpec((MHEADS, length), lambda i: (0, 0)),
        ],
        scratch_shapes=[
            pltpu.VMEM((length, MHEADS), FLOAT),
            pltpu.VMEM((MHEADS, length), FLOAT),
            pltpu.VMEM((length, length), FLOAT),
            pltpu.VMEM((length, length), FLOAT),
        ],
        compiler_params=pltpu.CompilerParams(vmem_limit_bytes=32 * MIB),
        name="state_backward",
    )(*state_operands(conv_out, step_size, decay_rate, skip_gain), grad_mixed)
    column_sums = column_sums.T
    dcum = row_sums - column_sums * step_size
    places = jnp.arange(length)
    upper = (places[:, None] <= places[None, :]).astype(FLOAT)
    drate_step = jnp.dot(upper, dcum, precision=HIGH, preferred_element_type=FLOAT)
    grad_step = column_sums + drate_step * decay_rate
    grad_decay_log = jnp.sum(drate_step * step_size, axis=0) * decay_rate
    return dx, db, dc, grad_step, grad_decay_log


def convolve(conv_in, conv_weight, conv_bias):
    length = conv_in.shape[0]
    padded = jnp.pad(conv_in, ((KCONV - 1, 0), (0, 0)))
    total = conv_bias + padded[0:length] * conv_weight[0]
    for tap in range(1, KCONV):
        total = total + padded[tap : tap + length] * conv_weight[tap]
    return silu_of(total)


def gated_norm(mixed, gate_z, mixer_gain):
    return rms_norm(mixed * silu_of(gate_z), mixer_gain)


def step_of(step_raw, step_bias):
    return softplus_of(step_raw + step_bias)


def mixer_forward(hidden, norm_gain, mixer_in, mixer_out, small):
    normed, norm_back = jax.vjp(rms_norm, hidden, norm_gain)
    normed_low = normed.astype(BRAIN)
    projected = matmul(normed_low, mixer_in)
    gate_z = projected[:, :DI]
    conv_in = projected[:, DI : DI + CONVCH]
    step_raw = projected[:, DI + CONVCH :]
    conv_out, conv_back = jax.vjp(convolve, conv_in, small["conv_weight"], small["conv_bias"])
    step_size, step_back = jax.vjp(step_of, step_raw, small["step_bias"])
    decay_rate = -jnp.exp(small["decay_log"])
    mixed = state_forward(conv_out, step_size, decay_rate, small["skip_gain"])
    mixer_norm, gated_back = jax.vjp(gated_norm, mixed, gate_z, small["mixer_gain"])
    mixer_low = mixer_norm.astype(BRAIN)
    output = hidden + matmul_nt(mixer_low, mixer_out)
    saved = (norm_back, normed_low, conv_out, conv_back, step_size, step_back, decay_rate, gated_back, mixer_low)
    return output, saved


def mixer_backward(grad_out, saved, mixer_in, mixer_out, small):
    norm_back, normed_low, conv_out, conv_back, step_size, step_back, decay_rate, gated_back, mixer_low = saved
    grad_low = grad_out.astype(BRAIN)
    grad_mixer_out = matmul_tn(grad_low, mixer_low).astype(BRAIN)
    grad_mixed, grad_gate, grad_mixer_gain = gated_back(matmul(grad_low, mixer_out))
    dx, db, dc, grad_step, grad_decay_log = state_backward(
        conv_out, step_size, decay_rate, small["skip_gain"], grad_mixed
    )
    grad_skip = jnp.sum(jnp.sum(grad_mixed * conv_out[:, :DI], axis=0).reshape(MHEADS, MHDIM), axis=1)
    grad_conv_in, grad_conv_weight, grad_conv_bias = conv_back(jnp.concatenate([dx, db, dc], axis=1))
    grad_step_raw, grad_step_bias = step_back(grad_step)
    grad_proj = jnp.concatenate([grad_gate, grad_conv_in, grad_step_raw], axis=1).astype(BRAIN)
    grad_mixer_in = matmul_tn(normed_low, grad_proj).astype(BRAIN)
    grad_hidden, grad_gain = norm_back(matmul_nt(grad_proj, mixer_in))
    grad_small = (
        grad_mixer_gain, grad_conv_weight, grad_conv_bias, grad_decay_log, grad_step_bias, grad_skip
    )
    return grad_out + grad_hidden, grad_gain, grad_mixer_in, grad_mixer_out, grad_small


def pick_rows(gates):
    tokens = gates.shape[1]
    down = lax.broadcasted_iota(jnp.int32, (tokens, tokens), 0)
    along = lax.broadcasted_iota(jnp.int32, (tokens, tokens), 1)
    upper = jnp.where(down <= along, 1.0, 0.0).astype(BRAIN)
    live = jnp.where(gates != 0.0, 1.0, 0.0)
    place = jnp.dot(
        jnp.broadcast_to(live, (8, tokens)).astype(BRAIN), upper, preferred_element_type=FLOAT
    )[0:1] - 1.0
    ranks = lax.broadcasted_iota(jnp.int32, (PICKED, tokens), 0).astype(FLOAT)
    return (ranks == place) & (live > 0.0)


def expert_forward_kernel(x_ref, g_ref, in_ref, out_ref, sin_ref, sout_ref, y_ref, xe_ref, gu_ref, sgu_ref):
    rows = x_ref[0]
    shared_gu = jnp.dot(rows, sin_ref[...], preferred_element_type=FLOAT)
    half = shared_gu.shape[1] // 2
    shared_mid = (silu_of(shared_gu[:, :half]) * shared_gu[:, half:]).astype(BRAIN)
    sgu_ref[0] = shared_gu.astype(sgu_ref.dtype)
    total = matmul_nt(shared_mid, sout_ref[...])
    for e in range(in_ref.shape[0]):
        gates = g_ref[0, e : e + 1, :]
        hit = pick_rows(gates)
        picked = jnp.dot(
            jnp.where(hit, 1.0, 0.0).astype(BRAIN), rows, preferred_element_type=FLOAT
        ).astype(BRAIN)
        gate_up = jnp.dot(picked, in_ref[e], preferred_element_type=FLOAT)
        width = gate_up.shape[1] // 2
        inner = (silu_of(gate_up[:, :width]) * gate_up[:, width:]).astype(BRAIN)
        result = matmul_nt(inner, out_ref[e]).astype(BRAIN)
        total = total + matmul_tn(jnp.where(hit, gates, 0.0).astype(BRAIN), result)
        xe_ref[e, 0] = picked
        gu_ref[e, 0] = gate_up.astype(gu_ref.dtype)
    y_ref[0] = total.astype(y_ref.dtype)


def expert_forward(rows, gates, expert_in, expert_out, shared_in, shared_out):
    group, tokens, width = rows.shape
    local = expert_in.shape[0]
    inner = expert_in.shape[2]
    by_slot = lambda *shape: pl.BlockSpec((1,) + shape, lambda s: (s,) + (0,) * len(shape))
    by_pair = lambda *shape: pl.BlockSpec((local, 1) + shape, lambda s: (0, s) + (0,) * len(shape))
    return pl.pallas_call(
        expert_forward_kernel,
        grid=(group,),
        out_shape=[
            jax.ShapeDtypeStruct(rows.shape, BRAIN),
            jax.ShapeDtypeStruct((local, group, PICKED, width), BRAIN),
            jax.ShapeDtypeStruct((local, group, PICKED, inner), BRAIN),
            jax.ShapeDtypeStruct((group, tokens, shared_in.shape[1]), BRAIN),
        ],
        in_specs=[
            by_slot(tokens, width),
            by_slot(local, tokens),
            whole_spec(expert_in.shape),
            whole_spec(expert_out.shape),
            whole_spec(shared_in.shape),
            whole_spec(shared_out.shape),
        ],
        out_specs=[
            by_slot(tokens, width),
            by_pair(PICKED, width),
            by_pair(PICKED, inner),
            by_slot(tokens, shared_in.shape[1]),
        ],
        compiler_params=pltpu.CompilerParams(vmem_limit_bytes=52 * MIB),
        name="expert_forward",
    )(rows, gates, expert_in, expert_out, shared_in, shared_out)


def swiglu_back(gate, up, grad):
    sig = jax.nn.sigmoid(gate)
    act = gate * sig
    return grad * up * (sig + act * (1.0 - sig)), grad * act, act * up


def expert_backward_kernel(
    d_ref, g_ref, gu_ref, sgu_ref, in_ref, out_ref, sin_ref, sout_ref,
    dx_ref, dg_ref, dgu_ref, dres_ref, mid_ref, dsgu_ref, smid_ref,
):
    grads = d_ref[0]
    shared_gu = sgu_ref[0].astype(FLOAT)
    half = shared_gu.shape[1] // 2
    dmid = jnp.dot(grads, sout_ref[...], preferred_element_type=FLOAT)
    dgate, dup, shared_mid = swiglu_back(shared_gu[:, :half], shared_gu[:, half:], dmid)
    shared_d = jnp.concatenate([dgate, dup], axis=1).astype(BRAIN)
    dsgu_ref[0] = shared_d
    smid_ref[0] = shared_mid.astype(BRAIN)
    total = matmul_nt(shared_d, sin_ref[...])
    for e in range(in_ref.shape[0]):
        gates = g_ref[0, e : e + 1, :]
        hit = pick_rows(gates)
        chosen = jnp.where(hit, 1.0, 0.0).astype(BRAIN)
        weight = jnp.sum(jnp.where(hit, gates, 0.0), axis=1, keepdims=True)
        picked = jnp.dot(chosen, grads, preferred_element_type=FLOAT)
        dres_ref[e, 0] = (picked * weight).astype(BRAIN)
        raw = jnp.dot(picked.astype(BRAIN), out_ref[e], preferred_element_type=FLOAT)
        gate_up = gu_ref[e, 0].astype(FLOAT)
        width = gate_up.shape[1] // 2
        dgate, dup, inner = swiglu_back(gate_up[:, :width], gate_up[:, width:], raw * weight)
        inner_low = inner.astype(BRAIN)
        mid_ref[e, 0] = inner_low
        dweight = jnp.sum(raw * inner_low.astype(FLOAT), axis=1, keepdims=True)
        dg_ref[0, e : e + 1, :] = jnp.sum(jnp.where(hit, dweight, 0.0), axis=0, keepdims=True)
        dgu = jnp.concatenate([dgate, dup], axis=1).astype(BRAIN)
        dgu_ref[e, 0] = dgu
        back = matmul_nt(dgu, in_ref[e]).astype(BRAIN)
        total = total + matmul_tn(chosen, back)
    dx_ref[0] = total.astype(dx_ref.dtype)


def expert_backward(grads, gates, gate_up, shared_gu, expert_in, expert_out, shared_in, shared_out):
    group, tokens, width = grads.shape
    local = expert_in.shape[0]
    inner = expert_in.shape[2]
    by_slot = lambda *shape: pl.BlockSpec((1,) + shape, lambda s: (s,) + (0,) * len(shape))
    by_pair = lambda *shape: pl.BlockSpec((local, 1) + shape, lambda s: (0, s) + (0,) * len(shape))
    return pl.pallas_call(
        expert_backward_kernel,
        grid=(group,),
        out_shape=[
            jax.ShapeDtypeStruct(grads.shape, BRAIN),
            jax.ShapeDtypeStruct((group, local, tokens), FLOAT),
            jax.ShapeDtypeStruct((local, group, PICKED, inner), BRAIN),
            jax.ShapeDtypeStruct((local, group, PICKED, width), BRAIN),
            jax.ShapeDtypeStruct((local, group, PICKED, inner // 2), BRAIN),
            jax.ShapeDtypeStruct(shared_gu.shape, BRAIN),
            jax.ShapeDtypeStruct(shared_gu.shape[:2] + (shared_gu.shape[2] // 2,), BRAIN),
        ],
        in_specs=[
            by_slot(tokens, width),
            by_slot(local, tokens),
            by_pair(PICKED, inner),
            by_slot(tokens, shared_gu.shape[2]),
            whole_spec(expert_in.shape),
            whole_spec(expert_out.shape),
            whole_spec(shared_in.shape),
            whole_spec(shared_out.shape),
        ],
        out_specs=[
            by_slot(tokens, width),
            by_slot(local, tokens),
            by_pair(PICKED, inner),
            by_pair(PICKED, width),
            by_pair(PICKED, inner // 2),
            by_slot(tokens, shared_gu.shape[2]),
            by_slot(tokens, shared_gu.shape[2] // 2),
        ],
        compiler_params=pltpu.CompilerParams(vmem_limit_bytes=52 * MIB),
        name="expert_backward",
    )(grads, gates, gate_up, shared_gu, expert_in, expert_out, shared_in, shared_out)


def moe_forward(hidden, routes, valid, norm_gain, weights):
    router, shared_in, shared_out, expert_in, expert_out = weights
    group = lax.axis_size("expert")
    local = expert_in.shape[0]
    normed, norm_back = jax.vjp(rms_norm, hidden, norm_gain)
    normed_low = normed.astype(BRAIN)
    logits = matmul(normed_low, router)
    chosen = jnp.any(routes[:, :, None] == jnp.arange(router.shape[1])[None, None, :], axis=1)
    largest = jnp.max(jnp.where(chosen, logits, -jnp.inf), axis=1, keepdims=True)
    raised = jnp.where(chosen, jnp.exp(jnp.where(chosen, logits - largest, 0.0)), 0.0)
    probs = raised / jnp.sum(raised, axis=1, keepdims=True)
    gates = probs * valid[:, None]
    rows_all, gates_all = spread([normed_low, gates.T], group, 1)
    own_gates = lax.dynamic_slice_in_dim(gates_all, lax.axis_index("expert") * local, local, axis=1)
    partial, picked, gate_up, shared_gu = expert_forward(
        rows_all, own_gates, expert_in, expert_out, shared_in, shared_out
    )
    output = hidden + gather_sum([partial], group, 2)[0]
    return output, (norm_back, normed_low, probs, rows_all, own_gates, picked, gate_up, shared_gu)


def moe_backward(grad_out, saved, valid, weights):
    norm_back, normed_low, probs, rows_all, own_gates, picked, gate_up, shared_gu = saved
    router, shared_in, shared_out, expert_in, expert_out = weights
    group = lax.axis_size("expert")
    local, width, inner = expert_in.shape
    grads_all = spread([grad_out.astype(BRAIN)], group, 3)[0]
    partial, dgates, dgate_up, dresult, middle, dshared, shared_mid = expert_backward(
        grads_all, own_gates, gate_up, shared_gu, expert_in, expert_out, shared_in, shared_out
    )
    placed = lax.dynamic_update_slice_in_dim(
        jnp.zeros((group, probs.shape[1], probs.shape[0]), FLOAT),
        dgates,
        lax.axis_index("expert") * local,
        axis=1,
    )
    grad_normed, grad_gates = gather_sum([partial, placed], group, 4)
    rows_of = lambda array: array.reshape(local, -1, array.shape[-1])
    by_expert = lambda left, right: lax.dot_general(
        rows_of(left), rows_of(right), (((1,), (1,)), ((0,), (0,))), preferred_element_type=FLOAT
    ).astype(BRAIN)
    grad_expert_in = by_expert(picked, dgate_up)
    grad_expert_out = by_expert(dresult, middle)
    flat = lambda array: array.reshape(-1, array.shape[-1])
    grad_shared_in = matmul_tn(flat(rows_all), flat(dshared)).astype(BRAIN)
    grad_shared_out = matmul_tn(flat(grads_all), flat(shared_mid)).astype(BRAIN)
    grad_probs = grad_gates.T * valid[:, None]
    grad_logits = probs * (grad_probs - jnp.sum(probs * grad_probs, axis=1, keepdims=True))
    logits_low = grad_logits.astype(BRAIN)
    grad_router = matmul_tn(normed_low, logits_low).astype(BRAIN)
    grad_hidden, grad_gain = norm_back(grad_normed + matmul_nt(logits_low, router))
    return (
        grad_out + grad_hidden,
        grad_gain,
        grad_router,
        grad_shared_in,
        grad_shared_out,
        grad_expert_in,
        grad_expert_out,
    )


def attend_scores(query, key_rows):
    length = query.shape[0]
    down = lax.broadcasted_iota(jnp.int32, (length, length), 0)
    along = lax.broadcasted_iota(jnp.int32, (length, length), 1)
    scores = jnp.where(down >= along, matmul_nt(query, key_rows) * AHDIM ** (-0.5), -1e30)
    raised = jnp.exp(scores - jnp.max(scores, axis=1, keepdims=True))
    return raised / jnp.sum(raised, axis=1, keepdims=True)


def attention_forward_kernel(q_ref, k_ref, v_ref, o_ref):
    for j in range(AHEADS // KVHEADS):
        part = slice(j * AHDIM, (j + 1) * AHDIM)
        probs = attend_scores(q_ref[:, part], k_ref[...])
        o_ref[:, part] = matmul(probs.astype(BRAIN), v_ref[...]).astype(BRAIN)


def attention_specs(length):
    queries = pl.BlockSpec((length, QD // KVHEADS), lambda h: (0, h))
    keys = pl.BlockSpec((length, AHDIM), lambda h: (0, QD // AHDIM + h))
    values = pl.BlockSpec((length, AHDIM), lambda h: (0, (QD + KVD) // AHDIM + h))
    return [queries, keys, values]


def attention_core(qkv):
    length = qkv.shape[0]
    specs = attention_specs(length)
    return pl.pallas_call(
        attention_forward_kernel,
        grid=(KVHEADS,),
        out_shape=jax.ShapeDtypeStruct((length, QD), BRAIN),
        in_specs=specs,
        out_specs=specs[0],
        compiler_params=pltpu.CompilerParams(vmem_limit_bytes=32 * MIB),
        name="attention_forward",
    )(qkv, qkv, qkv)


def attention_backward_kernel(q_ref, k_ref, v_ref, d_ref, dq_ref, dk_ref, dv_ref):
    keys = k_ref[...]
    values = v_ref[...]
    dkeys = jnp.zeros(keys.shape, FLOAT)
    dvalues = jnp.zeros(keys.shape, FLOAT)
    for j in range(AHEADS // KVHEADS):
        part = slice(j * AHDIM, (j + 1) * AHDIM)
        query = q_ref[:, part]
        grads = d_ref[:, part]
        probs = attend_scores(query, keys)
        dprobs = matmul_nt(grads, values)
        dvalues = dvalues + matmul_tn(probs.astype(BRAIN), grads)
        inner = jnp.sum(probs * dprobs, axis=1, keepdims=True)
        draw = (probs * (dprobs - inner) * AHDIM ** (-0.5)).astype(BRAIN)
        dq_ref[:, part] = matmul(draw, keys).astype(BRAIN)
        dkeys = dkeys + matmul_tn(draw, query)
    dk_ref[...] = dkeys.astype(BRAIN)
    dv_ref[...] = dvalues.astype(BRAIN)


def attention_core_back(qkv, grads):
    length = qkv.shape[0]
    specs = attention_specs(length)
    head_block = pl.BlockSpec((length, AHDIM), lambda h: (0, h))
    return pl.pallas_call(
        attention_backward_kernel,
        grid=(KVHEADS,),
        out_shape=[
            jax.ShapeDtypeStruct((length, QD), BRAIN),
            jax.ShapeDtypeStruct((length, KVD), BRAIN),
            jax.ShapeDtypeStruct((length, KVD), BRAIN),
        ],
        in_specs=specs + [specs[0]],
        out_specs=[specs[0], head_block, head_block],
        compiler_params=pltpu.CompilerParams(vmem_limit_bytes=32 * MIB),
        name="attention_backward",
    )(qkv, qkv, qkv, grads)


def attention_forward(hidden, norm_gain, attn_qkv, attn_out):
    normed, norm_back = jax.vjp(rms_norm, hidden, norm_gain)
    normed_low = normed.astype(BRAIN)
    qkv = matmul(normed_low, attn_qkv).astype(BRAIN)
    attended = attention_core(qkv)
    output = hidden + matmul_nt(attended, attn_out)
    return output, (norm_back, normed_low, qkv, attended)


def attention_backward(grad_out, saved, attn_qkv, attn_out):
    norm_back, normed_low, qkv, attended = saved
    grad_low = grad_out.astype(BRAIN)
    grad_attn_out = matmul_tn(grad_low, attended).astype(BRAIN)
    grad_attended = matmul(grad_low, attn_out).astype(BRAIN)
    grad_qkv = jnp.concatenate(attention_core_back(qkv, grad_attended), axis=1)
    grad_attn_qkv = matmul_tn(normed_low, grad_qkv).astype(BRAIN)
    grad_hidden, grad_gain = norm_back(matmul_nt(grad_qkv, attn_qkv))
    return grad_out + grad_hidden, grad_gain, grad_attn_qkv, grad_attn_out


def gather_dense(array):
    return lax.all_gather(array, BOTH, axis=0, tiled=True)


def gather_expert(array):
    return lax.all_gather(array, "dp", axis=1, tiled=True)


def scatter_dense(array):
    return lax.psum_scatter(array, BOTH, scatter_dimension=0, tiled=True).astype(FLOAT)


def scatter_expert(array):
    return lax.psum_scatter(array, "dp", scatter_dimension=1, tiled=True).astype(FLOAT)


def shared_columns(shared):
    group = lax.axis_size("expert")
    rows = shared[0].shape[0]
    pieces = []
    for shared_in, shared_out in zip(shared[0::2], shared[1::2]):
        half = shared_in.shape[1] // 2
        pieces += [shared_in[:, :half], shared_in[:, half:], shared_out]
    cut = [piece.reshape(rows, group, -1) for piece in pieces]
    return jnp.transpose(jnp.concatenate(cut, axis=2), (1, 0, 2))


def gather_shared(shared):
    group = lax.axis_size("expert")
    mine = lax.all_to_all(shared_columns(shared), "expert", split_axis=0, concat_axis=0, tiled=True)
    mine = mine.reshape(-1, mine.shape[2])
    whole = lax.all_gather(mine, "dp", axis=0, tiled=True)
    part = shared[1].shape[1] // group
    return [
        whole[:, 0 : 2 * part],
        whole[:, 2 * part : 3 * part],
        whole[:, 3 * part : 5 * part],
        whole[:, 5 * part :],
    ]


def scatter_shared(grads):
    group = lax.axis_size("expert")
    rows = lax.psum_scatter(jnp.concatenate(grads, axis=1), "dp", scatter_dimension=0, tiled=True)
    rows = rows.reshape(group, -1, rows.shape[1])
    own = lax.all_to_all(rows, "expert", split_axis=0, concat_axis=0, tiled=True).astype(FLOAT)
    part = own.shape[2] // 6

    def columns(index):
        piece = jnp.transpose(own[:, :, index * part : (index + 1) * part], (1, 0, 2))
        return piece.reshape(piece.shape[0], -1)

    return [
        jnp.concatenate([columns(0), columns(1)], axis=1),
        columns(2),
        jnp.concatenate([columns(3), columns(4)], axis=1),
        columns(5),
    ]


def per_device(
    layer_input, cotangent, lengths, routes_a, routes_b,
    mixer_in, mixer_out, router_a, shared_in_a, shared_out_a, expert_in_a, expert_out_a,
    attn_qkv, attn_out, router_b, shared_in_b, shared_out_b, expert_in_b, expert_out_b,
    norm_gains, mixer_gain, conv_weight, conv_bias, decay_log, step_bias, skip_gain,
):
    small = {
        "conv_weight": conv_weight,
        "conv_bias": conv_bias,
        "decay_log": decay_log,
        "step_bias": step_bias,
        "skip_gain": skip_gain,
        "mixer_gain": mixer_gain,
    }
    assert lengths.shape[0] == 1 and layer_input.shape[0] == SLOT_LEN
    valid = (jnp.arange(SLOT_LEN) < lengths[0]).astype(FLOAT)
    w_mixer_in = gather_dense(mixer_in)
    w_mixer_out = gather_dense(mixer_out)
    w_routers = gather_dense(jnp.concatenate([router_a, router_b], axis=1))
    experts = router_a.shape[1]
    w_shared = gather_shared([shared_in_a, shared_out_a, shared_in_b, shared_out_b])
    weights_a = (
        w_routers[:, :experts], w_shared[0], w_shared[1], gather_expert(expert_in_a), gather_expert(expert_out_a)
    )
    w_qkv = gather_dense(attn_qkv)
    w_attn_out = gather_dense(attn_out)
    weights_b = (
        w_routers[:, experts:], w_shared[2], w_shared[3], gather_expert(expert_in_b), gather_expert(expert_out_b)
    )
    hidden = layer_input.astype(FLOAT)
    hidden, saved_mix = mixer_forward(hidden, norm_gains[0], w_mixer_in, w_mixer_out, small)
    hidden, saved_a = moe_forward(hidden, routes_a, valid, norm_gains[1], weights_a)
    hidden, saved_attn = attention_forward(hidden, norm_gains[2], w_qkv, w_attn_out)
    layer_output, saved_b = moe_forward(hidden, routes_b, valid, norm_gains[3], weights_b)
    grad = cotangent * valid[:, None]
    grad, gain_four, d_router_b, d_shared_in_b, d_shared_out_b, d_in_b, d_out_b = moe_backward(
        grad, saved_b, valid, weights_b
    )
    d_in_b, d_out_b = scatter_expert(d_in_b), scatter_expert(d_out_b)
    grad, gain_three, d_qkv, d_attn_out = attention_backward(grad, saved_attn, w_qkv, w_attn_out)
    d_qkv, d_attn_out = scatter_dense(d_qkv), scatter_dense(d_attn_out)
    grad, gain_two, d_router_a, d_shared_in_a, d_shared_out_a, d_in_a, d_out_a = moe_backward(
        grad, saved_a, valid, weights_a
    )
    d_in_a, d_out_a = scatter_expert(d_in_a), scatter_expert(d_out_a)
    d_shared = scatter_shared([d_shared_in_a, d_shared_out_a, d_shared_in_b, d_shared_out_b])
    d_routers = scatter_dense(jnp.concatenate([d_router_a, d_router_b], axis=1))
    grad, gain_one, d_mixer_in, d_mixer_out, grad_small = mixer_backward(
        grad, saved_mix, w_mixer_in, w_mixer_out, small
    )
    d_mixer_out = scatter_dense(d_mixer_out)
    d_mixer_in = scatter_dense(d_mixer_in)
    parts = [jnp.stack([gain_one, gain_two, gain_three, gain_four])] + list(grad_small)
    flat = jnp.concatenate([part.reshape(-1) for part in parts])
    padded = jnp.pad(flat, (0, -flat.shape[0] % 1024)).reshape(-1, 128)
    summed = swap_sum(padded, 5).reshape(-1)
    sums = []
    place = 0
    for part in parts:
        sums.append(summed[place : place + part.size].reshape(part.shape))
        place += part.size
    return (
        layer_output, grad,
        d_mixer_in, d_mixer_out, d_routers[:, :experts], d_shared[0], d_shared[1], d_in_a, d_out_a,
        d_qkv, d_attn_out, d_routers[:, experts:], d_shared[2], d_shared[3], d_in_b, d_out_b,
        *sums,
    )


def solution(mesh):
    rows = P(BOTH, None)
    expert = P("expert", "dp", None)
    first = (rows, rows, rows, rows, rows, expert, expert)
    second = (rows, rows, rows, rows, rows, expert, expert)
    return jax.shard_map(
        per_device,
        mesh=mesh,
        in_specs=(rows, rows, P(BOTH), rows, rows) + first + second + (P(),) * 7,
        out_specs=(rows, rows) + first + second + (P(),) * 7,
        check_vma=False,
    )
```

time: 3660 us -> 2000 us (0.55)
  waiting for transfers between devices: 1930 us -> 767 us
  Pallas kernels: 0 us -> 858 us
  local copies, waits for them, and re-layouts: 479 us -> 54.5 us
  matrix products: 529 us -> 140 us
  other arithmetic: 374 us -> 60.2 us
  starting transfers between devices: 127 us -> 11.2 us
  blocking collectives: 188 us -> 84.8 us
    pallas_call x0 -> x17, Pallas kernels: none -> 858 us  [the longest x4 328 us: gather_sum(): pl.pallas_call(functools.partial(gather_sum_kernel, n, group), out_shape=...]
    all_to_all x16 -> x1, waiting for transfers between devices: 587 us -> 11.8 us  [scatter_shared(): lax.all_to_all(rows, 'expert', split_axis=0, concat_axis=0, tiled=True)]
    reduce_scatter x12 -> x9, waiting for transfers between devices: 1080 us -> 688 us  [the longest x4 494 us: scatter_dense(): lax.psum_scatter(array, BOTH, scatter_dimension=0, tiled=True).astype(FLOAT)]
    dot_general x58 -> x5, matrix products: 261 us -> 42.9 us  [the longest x4 40.9 us: moe_backward(): lax.dot_general(rows_of(left), rows_of(right), (((1,), (1,)), ((0,), (0,)...]
    reshape x44 -> x17, local copies, waits for them, and re-layouts: 184 us -> 3.52 us  [the longest x3 1.43 us: columns(): return piece.reshape(piece.shape[0], -1)]
    scatter-add x6 -> x0, other arithmetic: 148 us -> none  [route_weights(): chosen = jnp.take_along_axis(logits, routes, axis=1)]
    psum x1 -> x0, waiting for transfers between devices: 133 us -> none  [per_device(): lax.psum((gain_total, small_total['mixer_gain'], small_total['conv_weight...]
    all_gather x2 -> x1, blocking collectives: 188 us -> 64.4 us  [gather_dense(): return lax.all_gather(array, BOTH, axis=0, tiled=True)]
  transfers between devices with their start and end apart: 43 -> 20, of which waited for: 23 -> 12; matrix products, arithmetic and copies ran while one was open for 31% -> 10% of each run, Pallas kernels for 0% -> 26%
where the time goes in v1:
time: 2000 us; the launch traced here: 1990 us
  Pallas kernels  858 us (43%)
  waiting for transfers between devices  767 us (38%)
  matrix products  140 us (7%)
  blocking collectives  84.8 us (4%)
  other arithmetic  60.2 us (3%)
  local copies, waits for them, and re-layouts  54.5 us (3%)
    reduce_scatter x4, waiting for transfers between devices, scatter_dense(): lax.psum_scatter(array, BOTH, scatter_dimension=0, tiled=True).astype(FLOAT)  494 us
    pallas_call x4, Pallas kernels, gather_sum(): pl.pallas_call(functools.partial(gather_sum_kernel, n, group), out_shape=...  328 us
    pallas_call x4, Pallas kernels, spread(): pl.pallas_call(functools.partial(spread_kernel, n, group), out_shape=[jax...  321 us
    reduce_scatter x4, waiting for transfers between devices, scatter_expert(): lax.psum_scatter(array, 'dp', scatter_dimension=1, tiled=True).astype(FLOAT)  194 us
    pallas_call x2, Pallas kernels, expert_backward(): pl.pallas_call(expert_backward_kernel, grid=(group,), out_shape=[jax.Shap...  79.4 us
    pallas_call x2, Pallas kernels, expert_forward(): pl.pallas_call(expert_forward_kernel, grid=(group,), out_shape=[jax.Shape...  65.8 us
    all_gather x1, blocking collectives, gather_dense(): return lax.all_gather(array, BOTH, axis=0, tiled=True)  64.4 us
    all_gather x4, waiting for transfers between devices, gather_dense(): return lax.all_gather(array, BOTH, axis=0, tiled=True)  62.5 us
  transfers between devices with their start and end apart: 20, of which 12 were waited for; matrix products, arithmetic and copies ran while one was open for 10% of the time, Pallas kernels for 26%

profile of v1, /device:TPU:16, one launch (start us, length us, event | category | flops | bytes accessed | tf_op | source)
XLA Modules:
  0.0 1992.6 jit_solution(9960366944441185501)
XLA Ops:
  10.3 20.4 %all_to_all.10 = bf16[8,48,768]{2,1,0:T(8,128)(2,1)} all-to-all(bf16[8,48,768]{2,1,0:T(8,128)(2,1)S(1)} %bitcast.198), channel_id=1, replica_groups=mesh['dp'=4,'expert'=8] {'expert'}, dimensions={0} | all-to-all | bytes 1179648 | tf_op jit(solution)/shard_map/all_to_all | solution.py:899
  38.5 64.4 %all-gather = bf16[32,48,32]{1,2,0:T(8,128)(2,1)S(1)} all-gather(bf16[1,48,32]{1,2,0:T(8,128)(2,1)S(1)} %maximum_bitcast_fusion), channel_id=1, replica_groups=mesh['dp'=4,'expert'=8] {'dp','expert'}, dimensions={0}, use_global_device_ids=true | all-gather | bytes 101376 | tf_op jit(solution)/shard_map/all_gather | solution.py:871
  104.3 118.4 %spread3.2.d_ref = bf16[8,256,1536]{2,1,0:T(8,128)(2,1)} custom-call(bf16[256,1536]{1,0:T(8,128)(2,1)} %multiply_convert_fusion.4.refs_0_), custom_call_target="tpu_custom_call" | custom-call | tf_op jit(solution)/shard_map/spread3/pallas_call | solution.py:138
  226.4 6.9 all-gather.11.cloned.1.call-done
  233.4 9.8 fusion.33
  248.2 8.3 fusion.3
  256.5 9.3 state_forward.1
  265.8 5.6 multiply_reduce_fusion.6
  271.5 50.3 %all-gather.13.cloned.1.call-done = bf16[1536,3072]{1,0:T(8,128)(2,1)} async-done(((bf16[48,3072]{1,0:T(8,128)(2,1)}), bf16[1536,3072]{1,0:T(8,128)(2,1)}) %all-gather.13.cloned.1.call-update) | async-done | bytes 9437200 | tf_op jit(solution)/shard_map/all_gather | solution.py:871
  321.8 6.4 multiply_reduce_fusion.15
  330.6 74.1 %spread1.2 = (bf16[8,256,1536]{2,1,0:T(8,128)(2,1)}, f32[8,16,256]{2,1,0:T(8,128)}) custom-call(bf16[256,1536]{1,0:T(8,128)(2,1)} %copy-done.46, f32[16,256]{1,0:T(8,128)} %fusion.62.refs_1_), custom_call_target="tpu_custom_call" | custom-call | tf_op jit(solution)/shard_map/spread1/pallas_call | solution.py:138
  405.6 33.0 %expert_forward.2 = (bf16[8,256,1536]{2,1,0:T(8,128)(2,1)}, bf16[2,8,128,1536]{3,2,1,0:T(8,128)(2,1)}, bf16[2,8,128,1024]{3,2,1,0:T(8,128)(2,1)}, bf16[8,256,256]{2,1,0:T(8,128)(2,1)}) custom-call(bf16[8,256,1536]{2,1,0:T(8,128)(2,1)} %get-tuple-element.61.x_ref, f32[8,2,256]{2,1,0:T(2,128)S(1)} %constant_dynamic-slice_fusion.1.g_ref, ...), custom_call_target="tpu_custom_call" | custom-call | tf_op jit(solution)/shard_map/expert_forward/pallas_call | solution.py:601
  438.6 2.8 copy-done.7
  441.4 102.4 %gather_sum2.2 = f32[256,1536]{1,0:T(8,128)S(1)} custom-call(bf16[8,256,1536]{2,1,0:T(8,128)(2,1)S(1)} %copy-done.7), custom_call_target="tpu_custom_call" | custom-call | tf_op jit(solution)/shard_map/gather_sum2/pallas_call | solution.py:270
  545.1 6.0 convolution_convert_fusion.6.q_ref.k_ref.v_ref
  551.1 4.6 attention_forward.1
  556.6 5.2 all-gather.23.cloned.1.call-done
  561.8 4.6 multiply_reduce_fusion.13
  569.6 74.1 %spread1.3 = (bf16[8,256,1536]{2,1,0:T(8,128)(2,1)}, f32[8,16,256]{2,1,0:T(8,128)}) custom-call(bf16[256,1536]{1,0:T(8,128)(2,1)} %copy-done.48, f32[16,256]{1,0:T(8,128)} %fusion.58.refs_1_), custom_call_target="tpu_custom_call" | custom-call | tf_op jit(solution)/shard_map/spread1/pallas_call | solution.py:138
  645.7 32.9 %expert_forward.3 = (bf16[8,256,1536]{2,1,0:T(8,128)(2,1)}, bf16[2,8,128,1536]{3,2,1,0:T(8,128)(2,1)}, bf16[2,8,128,1024]{3,2,1,0:T(8,128)(2,1)}, bf16[8,256,256]{2,1,0:T(8,128)(2,1)}) custom-call(bf16[8,256,1536]{2,1,0:T(8,128)(2,1)} %get-tuple-element.64.x_ref, f32[8,2,256]{2,1,0:T(2,128)S(1)} %constant_dynamic-slice_fusion.g_ref, ...), custom_call_target="tpu_custom_call" | custom-call | tf_op jit(solution)/shard_map/expert_forward/pallas_call | solution.py:601
  678.5 2.8 copy-done.8
  681.3 75.9 %gather_sum2.3 = f32[256,1536]{1,0:T(8,128)S(1)} custom-call(bf16[8,256,1536]{2,1,0:T(8,128)(2,1)S(1)} %copy-done.8), custom_call_target="tpu_custom_call" | custom-call | tf_op jit(solution)/shard_map/gather_sum2/pallas_call | solution.py:270
  757.3 39.6 %expert_backward.2 = (bf16[8,256,1536]{2,1,0:T(8,128)(2,1)}, f32[8,2,256]{2,1,0:T(2,128)S(1)}, bf16[2,8,128,1024]{3,2,1,0:T(8,128)(2,1)}, bf16[2,8,128,1536]{3,2...) custom-call(bf16[8,256,1536]{2,1,0:T(8,128)(2,1)} %spread3.2.d_ref, ...), custom_call_target="tpu_custom_call" | custom-call | tf_op jit(solution)/shard_map/expert_backward/pallas_call | solution.py:676
  796.9 4.7 fusion.12
  801.6 5.7 fusion.10
  807.4 82.1 %gather_sum4.2 = (f32[256,1536]{1,0:T(8,128)S(1)}, f32[16,256]{1,0:T(8,128)S(1)}) custom-call(bf16[8,256,1536]{2,1,0:T(8,128)(2,1)S(1)} %bitcast.196, f32[8,16,256]{2,1,0:T(8,128)S(1)} %constant_dynamic-update-slice_fusion.7.refs_1_), custom_call_target="tpu_custom_call" | custom-call | tf_op jit(solution)/shard_map/gather_sum4/pallas_call | solution.py:270
  894.0 7.1 attention_backward.1
  901.2 3.0 multiply_reduce_fusion.8
  906.1 54.5 %spread3.3.d_ref = bf16[8,256,1536]{2,1,0:T(8,128)(2,1)} custom-call(bf16[256,1536]{1,0:T(8,128)(2,1)} %get-tuple-element.127.refs_0_), custom_call_target="tpu_custom_call" | custom-call | tf_op jit(solution)/shard_map/spread3/pallas_call | solution.py:138
  960.6 39.8 %expert_backward.3 = (bf16[8,256,1536]{2,1,0:T(8,128)(2,1)}, f32[8,2,256]{2,1,0:T(2,128)S(1)}, bf16[2,8,128,1024]{3,2,1,0:T(8,128)(2,1)}, bf16[2,8,128,1536]{3,2...) custom-call(bf16[8,256,1536]{2,1,0:T(8,128)(2,1)} %spread3.3.d_ref, ...), custom_call_target="tpu_custom_call" | custom-call | tf_op jit(solution)/shard_map/expert_backward/pallas_call | solution.py:676
  1001.6 4.7 fusion.9
  1006.5 2.5 copy.221
  1009.2 2.8 copy-done.6
  1011.9 67.8 %gather_sum4.3 = (f32[256,1536]{1,0:T(8,128)S(1)}, f32[16,256]{1,0:T(8,128)S(1)}) custom-call(bf16[8,256,1536]{2,1,0:T(8,128)(2,1)S(1)} %copy-done.6, f32[8,16,256]{2,1,0:T(8,128)S(1)} %constant_dynamic-update-slice_fusion.6.refs_1_), custom_call_target="tpu_custom_call" | custom-call | tf_op jit(solution)/shard_map/gather_sum4/pallas_call | solution.py:270
  1081.3 4.9 convolution_convert_fusion.3
  1086.7 8.6 convolution_convert_fusion.7
  1095.3 8.7 convolution_convert_fusion.8
  1105.5 6.8 convolution_convert_fusion.1
  1112.5 11.8 convolution_convert_fusion.4
  1124.4 11.8 convolution_convert_fusion.5
  1140.7 5.3 convolution_convert_fusion.2
  1146.2 8.8 multiply_reduce_fusion.4
  1155.1 5.0 fusion.7
  1160.1 16.4 state_backward.1
  1180.3 2.3 constant_dynamic-update-slice_fusion.5
  1184.7 4.8 multiply_reduce_fusion.2
  1192.9 10.3 convolution_convert_fusion
  1204.2 11.8 fusion.16
  1216.9 25.7 %swap_sum.1 = f32[208,128]{1,0:T(8,128)} custom-call(f32[208,128]{1,0:T(8,128)} %pad_bitcast_fusion.value_ref), custom_call_target="tpu_custom_call" | custom-call | tf_op jit(solution)/shard_map/swap_sum/pallas_call | solution.py:315
  1249.5 9.9 all-to-all-start.1
  1259.4 3.0 fusion.20
  1263.7 11.8 all-to-all-done.1
  1278.7 12.5 reduce-scatter.25.cloned.1.call-done
  1292.9 39.1 %reduce-scatter.29.cloned.1.call-done = bf16[2,384,512]{2,1,0:T(8,128)(2,1)} async-done(((bf16[2,1536,512]{2,1,0:T(8,128)(2,1)}), bf16[2,384,512]{2,1,0:T(8,128)(2,1)}) %reduce-scatter.29.cloned.1.call-update) | async-done | bytes 786448 | tf_op jit(solution)/shard_map/reduce_scatter | solution.py:883
  1332.0 2.5 convert_element_type.165
  1334.4 37.9 %reduce-scatter.21.cloned.1.call-done = bf16[2,384,512]{2,1,0:T(8,128)(2,1)} async-done(((bf16[2,1536,512]{2,1,0:T(8,128)(2,1)}), bf16[2,384,512]{2,1,0:T(8,128)(2,1)}) %reduce-scatter.21.cloned.1.call-update) | async-done | bytes 786448 | tf_op jit(solution)/shard_map/reduce_scatter | solution.py:883
  1372.4 2.5 convert_element_type.157
  1374.9 125.6 %reduce-scatter.23.cloned.1.call-done = bf16[48,2560]{1,0:T(8,128)(2,1)} async-done(((bf16[1536,2560]{1,0:T(8,128)(2,1)}), bf16[48,2560]{1,0:T(8,128)(2,1)}) %reduce-scatter.23.cloned.1.call-update) | async-done | bytes 245776 | tf_op jit(solution)/shard_map/reduce_scatter | solution.py:879
  1502.2 59.1 %reduce-scatter.27.cloned.1.call-done = bf16[2,384,1024]{2,1,0:T(8,128)(2,1)} async-done(((bf16[2,1536,1024]{2,1,0:T(8,128)(2,1)}), bf16[2,384,1024]{2,1,0:T(8,128)(2,1)}) %reduce-scatter.27.cloned.1.call-update) | async-done | bytes 1572880 | tf_op jit(solution)/shard_map/reduce_scatter | solution.py:883
  1561.4 3.5 convert_element_type.163
  1564.9 57.4 %reduce-scatter.19.cloned.1.call-done = bf16[2,384,1024]{2,1,0:T(8,128)(2,1)} async-done(((bf16[2,1536,1024]{2,1,0:T(8,128)(2,1)}), bf16[2,384,1024]{2,1,0:T(8,128)(2,1)}) %reduce-scatter.19.cloned.1.call-update) | async-done | bytes 1572880 | tf_op jit(solution)/shard_map/reduce_scatter | solution.py:883
  1622.3 3.5 convert_element_type.155
  1625.8 136.9 %reduce-scatter.17.cloned.1.call-done = bf16[48,3072]{1,0:T(8,128)(2,1)} async-done(((bf16[1536,3072]{1,0:T(8,128)(2,1)}), bf16[48,3072]{1,0:T(8,128)(2,1)}) %reduce-scatter.17.cloned.1.call-update) | async-done | bytes 294928 | tf_op jit(solution)/shard_map/reduce_scatter | solution.py:879
  1764.5 218.9 %reduce-scatter.15.cloned.1.call-done = bf16[48,6448]{1,0:T(8,128)(2,1)} async-done(((bf16[1536,6448]{1,0:T(8,128)(2,1)}), bf16[48,6448]{1,0:T(8,128)(2,1)}) %reduce-scatter.15.cloned.1.call-update) | async-done | bytes 619024 | tf_op jit(solution)/shard_map/reduce_scatter | solution.py:879
  (369 shorter events, 76.2 us)
Async XLA Ops:
  7.2 215.6 %all-gather.19.cloned.1.call-start = ((), (), s32[]{:S(2)}) async-start(), calls=%async_computation.16 | async-start | bytes 2949120 | tf_op jit(solution)/shard_map/all_gather | solution.py:901
  30.7 202.6 %all-gather.11.cloned.1.call-start = ((), (), s32[]{:S(2)}) async-start(), calls=%async_computation.12 | async-start | bytes 20680704 | tf_op jit(solution)/shard_map/all_gather | solution.py:871
  31.5 6.3 copy-start.82
  31.5 6.3 copy-start.83
  31.5 6.5 copy-start.92
  31.5 6.6 copy-start.74
  31.6 6.7 copy-start.72
  31.6 290.2 %all-gather.13.cloned.1.call-start = ((), (), s32[]{:S(2)}) async-start(), calls=%async_computation.13 | async-start | bytes 9732096 | tf_op jit(solution)/shard_map/all_gather | solution.py:871
  32.3 373.2 %all-gather.17.cloned.1.call-start = ((), (), s32[]{:S(2)}) async-start(), calls=%async_computation.15 | async-start | bytes 3932160 | tf_op jit(solution)/shard_map/all_gather | solution.py:875
  32.9 70.4 %copy-start.54 = (f32[256,1536]{1,0:T(8,128)S(1)}, f32[256,1536]{1,0:T(8,128)}, u32[]{:S(2)}) copy-start(f32[256,1536]{1,0:T(8,128)} %param.27) | copy-start | bytes 4718596
  32.9 372.7 %all-gather.15.cloned.1.call-start = ((), (), s32[]{:S(2)}) async-start(), calls=%async_computation.14 | async-start | bytes 7864320 | tf_op jit(solution)/shard_map/all_gather | solution.py:875
  33.5 511.6 %all-gather.21.cloned.1.call-start = ((), (), s32[]{:S(2)}) async-start(), calls=%async_computation.17 | async-start | bytes 8110080 | tf_op jit(solution)/shard_map/all_gather | solution.py:871
  34.1 527.7 %all-gather.23.cloned.1.call-start = ((), (), s32[]{:S(2)}) async-start(), calls=%async_computation.18 | async-start | bytes 4866048 | tf_op jit(solution)/shard_map/all_gather | solution.py:871
  34.8 609.8 %all-gather.27.cloned.1.call-start = ((), (), s32[]{:S(2)}) async-start(), calls=%async_computation.20 | async-start | bytes 3932160 | tf_op jit(solution)/shard_map/all_gather | solution.py:875
  35.6 609.1 %all-gather.25.cloned.1.call-start = ((), (), s32[]{:S(2)}) async-start(), calls=%async_computation.19 | async-start | bytes 7864320 | tf_op jit(solution)/shard_map/all_gather | solution.py:875
  36.3 1213.2 %reduce-scatter.33.cloned.1.call-start = ((), (), s32[]{:S(2)}) async-start(), calls=%async_computation.30 | async-start | bytes 2949120 | tf_op jit(solution)/shard_map/reduce_scatter | solution.py:913
  37.3 185.5 %copy-start.77 = (f32[256]{0:T(256)}, f32[256]{0:T(256)S(1)}, u32[]{:S(2)}) copy-start(f32[256]{0:T(256)S(1)} %fusion.21) | copy-start | bytes 3076
  37.3 196.1 %copy-start.70 = (f32[256]{0:T(256)}, f32[256]{0:T(256)S(1)}, u32[]{:S(2)}) copy-start(f32[256]{0:T(256)S(1)} %fusion.67) | copy-start | bytes 3076
  37.8 218.7 %copy-start.26 = (f32[1,48]{1,0:T(1,128)}, f32[1,48]{1,0:T(1,128)S(1)}, u32[]{:S(2)}) copy-start(f32[1,48]{1,0:T(1,128)S(1)} %get-tuple-element.163.rate_ref) | copy-start | bytes 580
  38.0 218.5 %copy-start.18 = (f32[48,1]{1,0:T(8,128)}, f32[48,1]{1,0:T(8,128)S(1)}, u32[]{:S(2)}) copy-start(f32[48,1]{1,0:T(8,128)S(1)} %copy.180.rate_t_ref) | copy-start | bytes 580
  38.2 218.3 %copy-start.24 = (f32[1,3072]{1,0:T(1,128)}, f32[1,3072]{1,0:T(1,128)S(1)}, u32[]{:S(2)}) copy-start(f32[1,3072]{1,0:T(1,128)S(1)} %broadcast_in_dim_reshape.4.skip_ref) | copy-start | bytes 36868
  38.3 195.1 %copy-start.59 = (f32[1536]{0:T(1024)}, f32[1536]{0:T(1024)S(1)}, u32[]{:S(2)}) copy-start(f32[1536]{0:T(1024)S(1)} %get-tuple-element.120) | copy-start | bytes 18436
  38.4 209.7 %copy-start.62 = (f32[3328]{0:T(1024)}, f32[3328]{0:T(1024)S(1)}, u32[]{:S(2)}) copy-start(f32[3328]{0:T(1024)S(1)} %get-tuple-element.114) | copy-start | bytes 39940
  38.4 209.7 %copy-start.64 = (f32[3328]{0:T(1024)}, f32[3328]{0:T(1024)S(1)}, u32[]{:S(2)}) copy-start(f32[3328]{0:T(1024)S(1)} %get-tuple-element.115) | copy-start | bytes 39940
  38.5 209.7 %copy-start.66 = (f32[3328]{0:T(1024)}, f32[3328]{0:T(1024)S(1)}, u32[]{:S(2)}) copy-start(f32[3328]{0:T(1024)S(1)} %get-tuple-element.116) | copy-start | bytes 39940
  38.5 209.7 %copy-start.68 = (f32[3328]{0:T(1024)}, f32[3328]{0:T(1024)S(1)}, u32[]{:S(2)}) copy-start(f32[3328]{0:T(1024)S(1)} %get-tuple-element.117) | copy-start | bytes 39940
  247.1 9.4 copy-start.16
  248.1 8.4 copy-start.13
  256.5 9.3 copy-start.2
  265.8 56.0 %copy-start.73 = (f32[3072]{0:T(1024)S(1)}, f32[3072]{0:T(1024)}, u32[]{:S(2)}) copy-start(f32[3072]{0:T(1024)} %param.46) | copy-start | bytes 36868
  271.5 56.7 %copy-start.79 = (f32[256]{0:T(256)}, f32[256]{0:T(256)S(1)}, u32[]{:S(2)}) copy-start(f32[256]{0:T(256)S(1)} %get-tuple-element.131) | copy-start | bytes 3076
  328.2 110.3 %copy-start.84 = (f32[256]{0:T(256)}, f32[256]{0:T(256)S(1)}, u32[]{:S(2)}) copy-start(f32[256]{0:T(256)S(1)} %get-tuple-element.165) | copy-start | bytes 3076
  441.4 102.4 %copy-start.36 = (f32[256,1536]{1,0:T(8,128)S(1)}, f32[256,1536]{1,0:T(8,128)}, u32[]{:S(2)}) copy-start(f32[256,1536]{1,0:T(8,128)} %copy-done.35) | copy-start | bytes 4718596
  807.4 82.2 %copy-start.44 = (f32[256,1536]{1,0:T(8,128)S(1)}, f32[256,1536]{1,0:T(8,128)}, u32[]{:S(2)}) copy-start(f32[256,1536]{1,0:T(8,128)} %copy-done.43) | copy-start | bytes 4718596
  807.4 85.2 %slice-start.4 = ((s8[4718592]{0:T(1024)(128)(4,1)}), s8[4194304]{0:T(1024)(128)(4,1)S(1)}, s32[]{:S(2)}) async-start(s8[4718592]{0:T(1024)(128)(4,1)} %bitcast.207), calls=%async_computation.35 | async-start | bytes 8388608
  890.9 10.3 slice-start.2
  892.6 11.7 copy-start.38
  892.6 8.6 slice-start.3
  894.0 7.2 copy-start.39
  960.6 39.8 %copy-start.34 = (bf16[8,256,1536]{2,1,0:T(8,128)(2,1)S(1)}, bf16[8,256,1536]{2,1,0:T(8,128)(2,1)}, u32[]{:S(2)}) copy-start(bf16[8,256,1536]{2,1,0:T(8,128)(2,1)} %spread3.3.d_ref) | copy-start | bytes 18874372
  1009.1 253.3 %reduce-scatter.31.cloned.1.call-start = ((), (), s32[]{:S(2)}) async-start(), calls=%async_computation.29 | async-start | bytes 405504
  1011.9 67.8 %copy-start.49 = (bf16[256,1536]{1,0:T(8,128)(2,1)S(1)}, bf16[256,1536]{1,0:T(8,128)(2,1)}, u32[]{:S(2)}) copy-start(bf16[256,1536]{1,0:T(8,128)(2,1)} %copy-done.48) | copy-start | bytes 2359300
  1011.9 68.1 %copy-start.47 = (bf16[256,1536]{1,0:T(8,128)(2,1)S(1)}, bf16[256,1536]{1,0:T(8,128)(2,1)}, u32[]{:S(2)}) copy-start(bf16[256,1536]{1,0:T(8,128)(2,1)} %copy-done.46) | copy-start | bytes 2359300
  1011.9 69.3 %copy-start.12 = (bf16[256,1536]{1,0:T(8,128)(2,1)S(1)}, bf16[256,1536]{1,0:T(8,128)(2,1)}, u32[]{:S(2)}) copy-start(bf16[256,1536]{1,0:T(8,128)(2,1)} %copy-done.11) | copy-start | bytes 2359300
  1081.2 210.1 %reduce-scatter.25.cloned.1.call-start = ((), (), s32[]{:S(2)}) async-start(), calls=%async_computation.26 | async-start | bytes 4866048 | tf_op jit(solution)/shard_map/reduce_scatter | solution.py:879
  1086.2 245.8 %reduce-scatter.29.cloned.1.call-start = ((), (), s32[]{:S(2)}) async-start(), calls=%async_computation.28 | async-start | bytes 3932160 | tf_op jit(solution)/shard_map/reduce_scatter | solution.py:883
  1095.3 277.1 %reduce-scatter.21.cloned.1.call-start = ((), (), s32[]{:S(2)}) async-start(), calls=%async_computation.24 | async-start | bytes 3932160 | tf_op jit(solution)/shard_map/reduce_scatter | solution.py:883
  1104.1 396.4 %reduce-scatter.23.cloned.1.call-start = ((), (), s32[]{:S(2)}) async-start(), calls=%async_computation.25 | async-start | bytes 8110080 | tf_op jit(solution)/shard_map/reduce_scatter | solution.py:879
  1112.3 449.1 %reduce-scatter.27.cloned.1.call-start = ((), (), s32[]{:S(2)}) async-start(), calls=%async_computation.27 | async-start | bytes 7864320 | tf_op jit(solution)/shard_map/reduce_scatter | solution.py:883
  1124.3 498.0 %reduce-scatter.19.cloned.1.call-start = ((), (), s32[]{:S(2)}) async-start(), calls=%async_computation.23 | async-start | bytes 7864320 | tf_op jit(solution)/shard_map/reduce_scatter | solution.py:883
  1136.2 626.5 %reduce-scatter.17.cloned.1.call-start = ((), (), s32[]{:S(2)}) async-start(), calls=%async_computation.22 | async-start | bytes 9732096 | tf_op jit(solution)/shard_map/reduce_scatter | solution.py:879
  1146.1 8.9 copy-start.80
  1146.1 8.9 copy-start.3
  1146.1 837.4 %reduce-scatter.15.cloned.1.call-start = ((), (), s32[]{:S(2)}) async-start(), calls=%async_computation.21 | async-start | bytes 20680704 | tf_op jit(solution)/shard_map/reduce_scatter | solution.py:879
  1146.1 8.8 copy-start.5
  1146.2 8.8 copy-start.32
  1160.1 22.6 %copy-start.91 = (f32[48]{0:T(128)S(1)}, f32[48]{0:T(128)}, u32[]{:S(2)}) copy-start(f32[48]{0:T(128)} %param.50) | copy-start | bytes 580
  1160.1 22.6 %copy-start.95 = (f32[48]{0:T(128)S(1)}, f32[48]{0:T(128)}, u32[]{:S(2)}) copy-start(f32[48]{0:T(128)} %get-tuple-element.162) | copy-start | bytes 580
  1204.2 12.0 copy-start.94
  1204.2 12.0 copy-start.76
  1204.2 55.2 %copy-start.78 = (f32[256]{0:T(256)S(1)}, f32[256]{0:T(256)}, u32[]{:S(2)}) copy-start(f32[256]{0:T(256)} %copy-done.77) | copy-start | bytes 3076
  1216.0 43.4 %copy-start.42 = (f32[256,1536]{1,0:T(8,128)S(1)}, f32[256,1536]{1,0:T(8,128)}, u32[]{:S(2)}) copy-start(f32[256,1536]{1,0:T(8,128)} %copy-done.41) | copy-start | bytes 4718596
  1249.5 26.0 %all-to-all-start.1 = ((bf16[8,48,768]{2,1,0:T(8,128)(2,1)}), bf16[8,48,768]{2,1,0:T(8,128)(2,1)S(1)}, u32[]{:S(2)}, u32[]{:S(2)}) async-start(bf16[8,48,768]{2,1,0:T(8,128)(2,1)} %bitcast.199), calls=%async_computation.3 | async-start | bytes 1179648 | tf_op jit(solution)/shard_map/all_to_all | solution.py:915
  1561.4 424.3 %copy-start.1 = (bf16[48,1024]{1,0:T(8,128)(2,1)S(1)}, bf16[48,1024]{1,0:T(8,128)(2,1)}, u32[]{:S(2)}) copy-start(bf16[48,1024]{1,0:T(8,128)(2,1)} %param.35) | copy-start | bytes 294916
  (60 other events, 183.0 us)
Sparse Core Ops, SparseCore 0:
  30.9 24.1 all-gather.18
  58.1 175.2 all-gather.10
  236.4 85.3 all-gather.12
  323.2 27.6 all-gather.16
  352.3 46.3 all-gather.14
  401.5 93.3 all-gather.20
  498.0 63.7 all-gather.22
  563.4 27.6 all-gather.26
  592.6 46.3 all-gather.24
  1009.2 34.5 reduce-scatter.32
  1081.3 92.9 reduce-scatter.30
  1179.6 111.5 reduce-scatter.24
  1293.9 37.9 reduce-scatter.28
  1334.3 37.9 reduce-scatter.20
  1378.8 121.6 reduce-scatter.22
  1502.9 58.4 reduce-scatter.26
  1563.9 58.3 reduce-scatter.18
  1628.1 134.5 reduce-scatter.16
  1770.3 213.1 reduce-scatter.14

commit v2 on v1

--- a/solution.py
+++ b/solution.py
@@ -61,122 +61,200 @@
     return pl.BlockSpec(shape, lambda *at: (0,) * len(shape), pipeline_mode=pl.Buffered(1))
 
 
-def expert_place(group):
-    me = lax.axis_index("expert")
-    return me // 2, lax.rem(me, 2)
-
-def greet(z, x, line):
+def places(group):
+    q = lax.axis_index("dp")
+    e = lax.axis_index("expert")
+    return q // 2, lax.rem(q, 2), e // 2, lax.rem(e, 2)
+
+
+def greet(peers):
     barrier = pltpu.get_barrier_semaphore()
-    def hello(device):
-        pl.semaphore_signal(barrier, inc=1, device_id={"expert": device}, device_id_type=MESH)
-    hello(2 * z + 1 - x)
-    @pl.when(z > 0)
-    def _():
-        hello(2 * (z - 1) + x)
-    @pl.when(z < line - 1)
-    def _():
-        hello(2 * (z + 1) + x)
-    pl.semaphore_wait(barrier, 1 + jnp.where(z > 0, 1, 0) + jnp.where(z < line - 1, 1, 0))
-
-def spread_kernel(count, group, *refs):
-    ins, outs = refs[:count], refs[count:2 * count]
-    up_sems, down_sems, cross_sems, recv_sems, own_sems = refs[2 * count:]
+    count = 0
+    for condition, device in peers:
+
+        def hello():
+            pl.semaphore_signal(barrier, inc=1, device_id=device, device_id_type=MESH)
+
+        if condition is None:
+            hello()
+            count = count + 1
+        else:
+            pl.when(condition)(hello)
+            count = count + jnp.where(condition, 1, 0)
+    pl.semaphore_wait(barrier, count)
+
+
+def line_peers(z, x, line):
+    return [
+        (None, {"expert": 2 * z + 1 - x}),
+        (z > 0, {"expert": 2 * (z - 1) + x}),
+        (z < line - 1, {"expert": 2 * (z + 1) + x}),
+    ]
+
+
+def remote(src, dst, send_sem, recv_sem, device):
+    return pltpu.make_async_remote_copy(
+        src_ref=src, dst_ref=dst, send_sem=send_sem, recv_sem=recv_sem, device_id=device, device_id_type=MESH
+    )
+
+
+def spread_kernel(count, wide, group, *refs):
+    total = count + wide
+    ins, outs = refs[:total], refs[total : 2 * total]
+    sems = refs[2 * total :]
+    up_sems, down_sems, cross_sems, recv_sems, own_sems = sems[:5]
     line = group // 2
-    z, x = expert_place(group)
-    greet(z, x, line)
+    y, c, z, x = places(group)
+    sibling, opposite = {"dp": 2 * y + 1 - c}, {"dp": 2 * (1 - y) + c}
+    greet(line_peers(z, x, line) + ([(None, sibling), (None, opposite)] if wide else []))
 
     def copy(i, src, place, sem, device):
-        return pltpu.make_async_remote_copy(
-            src_ref=src, dst_ref=outs[i].at[place], send_sem=sem, recv_sem=recv_sems.at[i, place],
-            device_id={"expert": device}, device_id_type=MESH)
+        return remote(src, outs[i].at[place], sem, recv_sems.at[i, place], {"expert": device})
 
     def moves(i, s, rising):
         zz = z - s if rising else z + s
         place = 2 * zz + x
         src = ins[i] if s == 0 else outs[i].at[place]
-        up = copy(i, src, place, up_sems.at[i, s], 2 * (z + 1) + x)
-        down = copy(i, src, place, down_sems.at[i, s], 2 * (z - 1) + x)
-        cross = copy(i, src, place, cross_sems.at[i, zz], 2 * z + 1 - x)
+        up = functools.partial(copy, i, src, place, up_sems.at[i, s], 2 * (z + 1) + x)
+        down = functools.partial(copy, i, src, place, down_sems.at[i, s], 2 * (z - 1) + x)
+        cross = functools.partial(copy, i, src, place, cross_sems.at[i, zz], 2 * z + 1 - x)
         return up, down, cross
 
-    for i in range(count):
-        pltpu.make_async_copy(ins[i], outs[i].at[2 * z + x], own_sems.at[i]).start()
-    for s in range(line):
-        for rising in (True, False) if s else (True,):
-            valid = (z - s >= 0) if rising else (z + s < line)
-            @pl.when(valid)
-            def _():
-                for i in range(count):
-                    up, down, cross = moves(i, s, rising)
-                    if s:
-                        cross.wait_recv()
-                    if rising:
-                        pl.when(z < line - 1)(up.start)
-                    if not rising or s == 0:
-                        pl.when(z > 0)(down.start)
-                    cross.start()
+    def steps(act):
+        for s in range(line):
+            for rising in (True, False) if s else (True,):
+                valid = (z - s >= 0) if rising else (z + s < line)
+
+                @pl.when(valid)
+                def _():
+                    for i in range(count):
+                        act(i, s, rising, *moves(i, s, rising))
+
+    def block(i, q):
+        rows = ins[i].shape[1]
+        return outs[i].at[:, pl.ds(pl.multiple_of(q * rows, rows), rows), :]
+
+    def wide_copy(i, kind):
+        wide_send, wide_recv = sems[5:]
+        own, other = 2 * y + c, 2 * (1 - y) + c
+        k = i - count
+        if kind == 0:
+            return remote(ins[i], block(i, own), wide_send.at[k, 0], wide_recv.at[k, 0], sibling)
+        if kind == 1:
+            return remote(ins[i], block(i, own), wide_send.at[k, 1], wide_recv.at[k, 1], opposite)
+        return remote(block(i, other), block(i, other), wide_send.at[k, 2], wide_recv.at[k, 2], sibling)
+
+    def own_copy(i):
+        place = outs[i].at[2 * z + x] if i < count else block(i, 2 * y + c)
+        return pltpu.make_async_copy(ins[i], place, own_sems.at[i])
+
+    def forward(i, s, rising, up, down, cross):
+        if s:
+            cross().wait_recv()
+        if rising:
+            pl.when(z < line - 1)(lambda: up().start())
+        if not rising or s == 0:
+            pl.when(z > 0)(lambda: down().start())
+        cross().start()
+
+    def settle(i, s, rising, up, down, cross):
+        if rising:
+            pl.when(z < line - 1)(lambda: up().wait_send())
+        if not rising or s == 0:
+            pl.when(z > 0)(lambda: down().wait_send())
+        cross().wait_send()
+
+    for i in range(count, total):
+        wide_copy(i, 1).start()
+        wide_copy(i, 0).start()
+    for i in range(total):
+        own_copy(i).start()
+    steps(forward)
+    for i in range(count, total):
+        wide_copy(i, 1).wait_recv()
+        wide_copy(i, 2).start()
     for i in range(count):
         for zz in range(line):
             place = 2 * zz + 1 - x
             copy(i, ins[i], place, own_sems.at[i], 2 * z + 1 - x).wait_recv()
-        pltpu.make_async_copy(ins[i], outs[i].at[2 * z + x], own_sems.at[i]).wait()
-    for s in range(line):
-        for rising in (True, False) if s else (True,):
-            valid = (z - s >= 0) if rising else (z + s < line)
-            @pl.when(valid)
-            def _():
-                for i in range(count):
-                    up, down, cross = moves(i, s, rising)
-                    if rising:
-                        pl.when(z < line - 1)(up.wait_send)
-                    if not rising or s == 0:
-                        pl.when(z > 0)(down.wait_send)
-                    cross.wait_send()
-
-def spread(arrays, group, number):
-    n = len(arrays); line = group // 2
+    steps(settle)
+    for i in range(count, total):
+        wide_copy(i, 0).wait()
+        wide_copy(i, 1).wait_send()
+        wide_copy(i, 2).wait()
+    for i in range(total):
+        own_copy(i).wait()
+
+
+def spread(arrays, wide, group, number):
+    n, w, line = len(arrays), len(wide), group // 2
+    split = lax.axis_size("dp")
+    dma = pltpu.SemaphoreType.DMA
+    any_spec = pl.BlockSpec(memory_space=pl.ANY)
+    shapes = [jax.ShapeDtypeStruct((group,) + a.shape, a.dtype) for a in arrays]
+    shapes += [jax.ShapeDtypeStruct((a.shape[0], split * a.shape[1], a.shape[2]), a.dtype) for a in wide]
     return pl.pallas_call(
-        functools.partial(spread_kernel, n, group),
-        out_shape=[jax.ShapeDtypeStruct((group,) + a.shape, a.dtype) for a in arrays],
-        in_specs=[pl.BlockSpec(memory_space=pl.ANY)] * n,
-        out_specs=[pl.BlockSpec(memory_space=pl.ANY)] * n,
-        scratch_shapes=[
-            pltpu.SemaphoreType.DMA((n, line)), pltpu.SemaphoreType.DMA((n, line)),
-            pltpu.SemaphoreType.DMA((n, line)), pltpu.SemaphoreType.DMA((n, group)),
-            pltpu.SemaphoreType.DMA((n,))],
+        functools.partial(spread_kernel, n, w, group),
+        out_shape=shapes,
+        in_specs=[any_spec] * (n + w),
+        out_specs=[any_spec] * (n + w),
+        scratch_shapes=[dma((n, line)), dma((n, line)), dma((n, line)), dma((n, group)), dma((n + w,))]
+        + ([dma((w, 3)), dma((w, 3))] if w else []),
         compiler_params=pltpu.CompilerParams(collective_id=number, has_side_effects=True),
         name="spread%d" % number,
-    )(*arrays)
-
-def gather_sum_kernel(count, group, *refs):
-    ins, outs = refs[:count], refs[count:2 * count]
+    )(*arrays, *wide)
+
+
+def add_blocks(target, sources, rows):
+    step = min(rows, 16)
+
+    def body(j, carry):
+        at = pl.ds(pl.multiple_of(j * step, step), step)
+
+        def view(item):
+            ref, lead, columns = item
+            return ref, tuple(lead) + (at,) + (() if columns is None else (columns,))
+
+        total = None
+        for item in sources:
+            ref, index = view(item)
+            value = ref[index].astype(FLOAT)
+            total = value if total is None else total + value
+        ref, index = view(target)
+        ref[index] = total.astype(ref.dtype)
+        return carry
+
+    lax.fori_loop(0, rows // step, body, 0)
+
+
+def gather_sum_kernel(count, wide, group, *refs):
+    total = count + wide
+    ins, outs = refs[:total], refs[total : 2 * total]
+    bufs = refs[2 * total : 2 * total + 4 * count + 3 * wide]
+    own_sems, cross_send, cross_recv, up_send, up_recv, down_send, down_recv = refs[2 * total + 4 * count + 3 * wide :][:7]
     line = group // 2
-    bufs = refs[2 * count:2 * count + 4 * count]
-    own_sems, cross_send, cross_recv, up_send, up_recv, down_send, down_recv = refs[6 * count:]
     held = [bufs[4 * i] for i in range(count)]
     crossed = [bufs[4 * i + 1] for i in range(count)]
     below = [bufs[4 * i + 2] for i in range(count)]
     above = [bufs[4 * i + 3] for i in range(count)]
-    z, x = expert_place(group)
-    greet(z, x, line)
+    y, c, z, x = places(group)
+    sibling, opposite = {"dp": 2 * y + 1 - c}, {"dp": 2 * (1 - y) + c}
+    greet(line_peers(z, x, line) + ([(None, sibling), (None, opposite)] if wide else []))
 
     def own(i, d):
         return pltpu.make_async_copy(ins[i].at[2 * d + x], held[i].at[d], own_sems.at[i, d])
 
     def cross(i, d):
-        return pltpu.make_async_remote_copy(
-            src_ref=ins[i].at[2 * d + 1 - x], dst_ref=crossed[i].at[d], send_sem=cross_send.at[i, d],
-            recv_sem=cross_recv.at[i, d], device_id={"expert": 2 * z + 1 - x}, device_id_type=MESH)
+        return remote(
+            ins[i].at[2 * d + 1 - x], crossed[i].at[d], cross_send.at[i, d], cross_recv.at[i, d],
+            {"expert": 2 * z + 1 - x},
+        )
 
     def rise(i, d):
-        return pltpu.make_async_remote_copy(
-            src_ref=held[i].at[d], dst_ref=below[i].at[d], send_sem=up_send.at[i, d],
-            recv_sem=up_recv.at[i, d], device_id={"expert": 2 * (z + 1) + x}, device_id_type=MESH)
+        return remote(held[i].at[d], below[i].at[d], up_send.at[i, d], up_recv.at[i, d], {"expert": 2 * (z + 1) + x})
 
     def fall(i, d):
-        return pltpu.make_async_remote_copy(
-            src_ref=held[i].at[d], dst_ref=above[i].at[d], send_sem=down_send.at[i, d],
-            recv_sem=down_recv.at[i, d], device_id={"expert": 2 * (z - 1) + x}, device_id_type=MESH)
+        return remote(held[i].at[d], above[i].at[d], down_send.at[i, d], down_recv.at[i, d], {"expert": 2 * (z - 1) + x})
 
     def order(act):
         for k in range(line):
@@ -185,30 +263,50 @@
         for k in range(line):
             pl.when(k == z)(functools.partial(act, k))
 
-    def start_cross(d):
+    def start_all(d):
         for i in range(count):
             cross(i, d).start()
-
-    def start_own(d):
-        for i in range(count):
             own(i, d).start()
-    order(start_cross)
-    order(start_own)
-
-    def add_rows(i, d, target, sources):
-        rows = held[i].shape[1]
-        step = min(rows, 16)
-        def body(j, carry):
-            at = pl.ds(pl.multiple_of(j * step, step), step)
-            total = held[i][d, at].astype(FLOAT)
-            for source in sources:
-                total = total + source[i][d, at].astype(FLOAT)
-            if target is None:
-                held[i][d, at] = total.astype(held[i].dtype)
-            else:
-                target[i][at] = total.astype(target[i].dtype)
-            return carry
-        lax.fori_loop(0, rows // step, body, 0)
+
+    order(start_all)
+
+    def wide_parts(i):
+        k = i - count
+        kept, landed, arrived = bufs[4 * count + 3 * k : 4 * count + 3 * k + 3]
+        wide_own, core_send, core_recv, side_send, side_recv = refs[-5:]
+        rows = ins[i].shape[1] // 4
+
+        def block(q):
+            return ins[i].at[:, pl.ds(pl.multiple_of(q * rows, rows), rows), :]
+
+        def load(h):
+            return pltpu.make_async_copy(block(2 * h + c), kept.at[h], wide_own.at[k, h])
+
+        def to_sibling(h):
+            return remote(block(2 * h + 1 - c), landed.at[h], core_send.at[k, h], core_recv.at[k, h], sibling)
+
+        def to_opposite():
+            return remote(kept.at[1 - y], arrived, side_send.at[k], side_recv.at[k], opposite)
+
+        return kept, landed, arrived, load, to_sibling, to_opposite, rows
+
+    for i in range(count, total):
+        load, to_sibling = wide_parts(i)[3:5]
+        for h in (1 - y, y):
+            to_sibling(h).start()
+            load(h).start()
+    for i in range(count, total):
+        kept, landed, arrived, load, to_sibling, to_opposite, rows = wide_parts(i)
+        h = 1 - y
+        load(h).wait()
+        to_sibling(h).wait_recv()
+        for e in range(ins[i].shape[0]):
+            add_blocks((kept, (h, e), None), [(kept, (h, e), None), (landed, (h, e), None)], rows)
+        to_opposite().start()
+
+    def add(i, d, final, sources):
+        target = (outs[i], (), None) if final else (held[i], (d,), None)
+        add_blocks(target, [(held[i], (d,), None)] + [(s[i], (d,), None) for s in sources], held[i].shape[1])
 
     def ready(i, d):
         own(i, d).wait()
@@ -216,116 +314,506 @@
 
     for k in range(line - 1):
         d = line - 1 - k
+
         @pl.when(d > z)
         def _():
             for i in range(count):
                 ready(i, d)
+
                 @pl.when(z > 0)
                 def _():
                     rise(i, d).wait_recv()
-                    add_rows(i, d, None, [crossed, below])
+                    add(i, d, False, [crossed, below])
+
                 @pl.when(z == 0)
                 def _():
-                    add_rows(i, d, None, [crossed])
+                    add(i, d, False, [crossed])
+
                 rise(i, d).start()
+
         d = k
+
         @pl.when(d < z)
         def _():
             for i in range(count):
                 ready(i, d)
+
                 @pl.when(z < line - 1)
                 def _():
                     fall(i, d).wait_recv()
-                    add_rows(i, d, None, [crossed, above])
+                    add(i, d, False, [crossed, above])
+
                 @pl.when(z == line - 1)
                 def _():
-                    add_rows(i, d, None, [crossed])
+                    add(i, d, False, [crossed])
+
                 fall(i, d).start()
+
+    for i in range(count, total):
+        kept, landed, arrived, load, to_sibling, to_opposite, rows = wide_parts(i)
+        load(y).wait()
+        to_sibling(y).wait_recv()
+        to_opposite().wait_recv()
+        for e in range(ins[i].shape[0]):
+            add_blocks(
+                (outs[i], (e,), None), [(kept, (y, e), None), (landed, (y, e), None), (arrived, (e,), None)], rows
+            )
     for d in range(line):
+
         @pl.when(d == z)
         def _():
             for i in range(count):
                 ready(i, d)
-                if d == 0:
+                if d < line - 1:
                     fall(i, d).wait_recv()
-                    add_rows(i, d, outs, [crossed, above])
-                elif d == line - 1:
+                if d > 0:
                     rise(i, d).wait_recv()
-                    add_rows(i, d, outs, [crossed, below])
-                else:
-                    fall(i, d).wait_recv()
-                    rise(i, d).wait_recv()
-                    add_rows(i, d, outs, [crossed, below, above])
+                add(i, d, True, [crossed] + ([below] if d > 0 else []) + ([above] if d < line - 1 else []))
+
     for d in range(line):
         for i in range(count):
             cross(i, d).wait_send()
-            pl.when(d > z)(rise(i, d).wait_send)
-            pl.when(d < z)(fall(i, d).wait_send)
-
-def gather_sum(arrays, group, number):
-    n = len(arrays); line = group // 2
+            pl.when(d > z)(lambda: rise(i, d).wait_send())
+            pl.when(d < z)(lambda: fall(i, d).wait_send())
+    for i in range(count, total):
+        to_sibling, to_opposite = wide_parts(i)[4:6]
+        for h in range(2):
+            to_sibling(h).wait_send()
+        to_opposite().wait_send()
+
+
+def gather_sum(arrays, wide, group, number):
+    n, w, line = len(arrays), len(wide), group // 2
+    dma = pltpu.SemaphoreType.DMA
     scratch = []
     for a in arrays:
         scratch += [pltpu.VMEM((line,) + a.shape[1:], a.dtype)] * 4
+    shapes = [jax.ShapeDtypeStruct(a.shape[1:], FLOAT) for a in arrays]
+    for a in wide:
+        part = (a.shape[0], a.shape[1] // 4, a.shape[2])
+        scratch += [pltpu.VMEM((2,) + part, a.dtype)] * 2 + [pltpu.VMEM(part, a.dtype)]
+        shapes.append(jax.ShapeDtypeStruct(part, FLOAT))
+    scratch += [dma((n, line))] * 7
+    if w:
+        scratch += [dma((w, 2))] * 3 + [dma((w,))] * 2
     return pl.pallas_call(
-        functools.partial(gather_sum_kernel, n, group),
-        out_shape=[jax.ShapeDtypeStruct(a.shape[1:], FLOAT) for a in arrays],
-        in_specs=[pl.BlockSpec(memory_space=pl.ANY)] * n,
-        out_specs=[pl.BlockSpec(memory_space=pltpu.VMEM)] * n,
-        scratch_shapes=scratch + [pltpu.SemaphoreType.DMA((n, line))] * 7,
-        compiler_params=pltpu.CompilerParams(collective_id=number, has_side_effects=True, vmem_limit_bytes=40 * 2**20),
+        functools.partial(gather_sum_kernel, n, w, group),
+        out_shape=shapes,
+        in_specs=[pl.BlockSpec(memory_space=pl.ANY)] * (n + w),
+        out_specs=[pl.BlockSpec(memory_space=pltpu.VMEM)] * (n + w),
+        scratch_shapes=scratch,
+        compiler_params=pltpu.CompilerParams(collective_id=number, has_side_effects=True, vmem_limit_bytes=52 * MIB),
         name="gather_sum%d" % number,
-    )(*arrays)
-
-
-def swap_sum_kernel(steps, value_ref, out_ref, totals, landed, send_sems, recv_sems):
-    barrier = pltpu.get_barrier_semaphore()
+    )(*arrays, *wide)
+
+
+def head_kernel(group, cut, mix_ref, router_ref, shared_ref, mix_out, router_out, shared_out, own_sems, send_sems, recv_sems, swap_send, swap_recv):
+    line = group // 2
+    y, c, z, x = places(group)
+    sibling, opposite = {"dp": 2 * y + 1 - c}, {"dp": 2 * (1 - y) + c}
+    rising, falling, across = {"expert": 2 * (z + 1) + x}, {"expert": 2 * (z - 1) + x}, {"expert": 2 * z + 1 - x}
+    me = 2 * z + x
+    peers = [(None, {"expert": lax.rem(me + k, group)}) for k in range(1, group)]
+    greet(peers + [(None, sibling), (None, opposite)])
+    width = mix_ref.shape[1]
+    pieces = [
+        (mix_ref, mix_out, pl.ds(0, cut)),
+        (mix_ref, mix_out, pl.ds(cut, width - cut)),
+        (router_ref, router_out, pl.ds(0, router_ref.shape[1])),
+    ]
+    first = (0, 2)
+    second = (1,)
+
+    def copy(p, yy, cc, zz, xx, way, device, own=False):
+        ref, out, columns = pieces[p]
+        place = (2 * yy + cc) * group + 2 * zz + xx
+        dst = out.at[place, :, columns]
+        src = ref.at[:, columns] if own else dst
+        slot = yy * group + 2 * zz + xx
+        return remote(src, dst, send_sems.at[p, slot, way], recv_sems.at[p, place], device)
+
+    def swap(k):
+        to = lax.rem(me + k, group)
+        return remote(shared_ref.at[to], shared_out.at[me], swap_send.at[k], swap_recv.at[me], {"expert": to})
+
+    def own_copy(i, ref, out):
+        return pltpu.make_async_copy(ref, out, own_sems.at[i])
+
+    owns = [
+        (mix_ref, mix_out.at[(2 * y + c) * group + me]),
+        (router_ref, router_out.at[(2 * y + c) * group + me]),
+        (shared_ref.at[me], shared_out.at[me]),
+    ]
+
+    def steps(act):
+        for s in range(line):
+            for up in (True, False) if s else (True,):
+                zz = z - s if up else z + s
+                valid = (z - s >= 0) if up else (z + s < line)
+
+                @pl.when(valid)
+                def _():
+                    act(s, up, zz)
+
+    def column_moves(p, s, up, zz):
+        own = s == 0
+        moves = []
+        if up:
+            moves.append((z < line - 1, functools.partial(copy, p, y, c, zz, x, 0, rising, own)))
+        if not up or own:
+            moves.append((z > 0, functools.partial(copy, p, y, c, zz, x, 1, falling, own)))
+        moves.append((None, functools.partial(copy, p, y, c, zz, x, 2, across, own)))
+        moves.append((None, functools.partial(copy, p, y, c, zz, x, 3, opposite, own)))
+        moves.append((None, functools.partial(copy, p, y, c, zz, x, 4, sibling, own)))
+        return moves
+
+    def later_moves(p, zz):
+        if p in first:
+            return [
+                ((y, x, 0), [(3, opposite), (4, sibling)], (y, 1 - x)),
+                ((y, x, 1), [(4, sibling)], (1 - y, x)),
+                ((y, x, 1), [(4, sibling)], (1 - y, 1 - x)),
+            ]
+        return [
+            ((y, x, 0), [(2, across), (4, sibling)], (1 - y, x)),
+            ((y, x, 1), [(4, sibling)], (y, 1 - x)),
+            ((y, x, 1), [(4, sibling)], (1 - y, 1 - x)),
+        ]
+
+    for p in range(3):
+        for condition, move in column_moves(p, 0, True, z):
+            if condition is None:
+                move().start()
+            else:
+                pl.when(condition)(lambda: move().start())
+    for k in range(1, group):
+        swap(k).start()
+    for i, (ref, out) in enumerate(owns):
+        own_copy(i, ref, out).start()
+
+    def column(s, up, zz):
+        if s == 0:
+            return
+        for p in range(3):
+            copy(p, y, c, zz, x, 4, sibling).wait_recv()
+            for condition, move in column_moves(p, s, up, zz):
+                if condition is None:
+                    move().start()
+                else:
+                    pl.when(condition)(lambda: move().start())
+
+    def later(phase, start):
+        def act(s, up, zz):
+            for p in range(3):
+                for (_, _, when), sends, (yy, xx) in later_moves(p, zz):
+                    if when != phase:
+                        continue
+                    if start:
+                        copy(p, yy, c, zz, xx, 4, sibling).wait_recv()
+                    for way, device in sends:
+                        item = copy(p, yy, c, zz, xx, way, device)
+                        if start:
+                            item.start()
+                        else:
+                            item.wait_send()
+
+        return act
+
+    steps(column)
+    steps(later(0, True))
+    steps(later(1, True))
+
+    def finish(s, up, zz):
+        for p in range(3):
+            for yy in range(2):
+                for xx in range(2):
+                    copy(p, yy, 1 - c, zz, xx, 4, sibling).wait_recv()
+
+    steps(finish)
+
+    def settle(s, up, zz):
+        for p in range(3):
+            for condition, move in column_moves(p, s, up, zz):
+                if condition is None:
+                    move().wait_send()
+                else:
+                    pl.when(condition)(lambda: move().wait_send())
+
+    steps(settle)
+    steps(later(0, False))
+    steps(later(1, False))
+    for k in range(1, group):
+        source = lax.rem(me + k, group)
+        remote(shared_ref.at[source], shared_out.at[source], swap_send.at[k], swap_recv.at[source], across).wait_recv()
+        swap(k).wait_send()
+    for i, (ref, out) in enumerate(owns):
+        own_copy(i, ref, out).wait()
+
+
+def half_columns(width):
+    return width // 256 * 128
+
+
+def head_exchange(mix, routers, shared, number):
+    group = lax.axis_size("expert")
+    total = 4 * group
+    dma = pltpu.SemaphoreType.DMA
+    any_spec = pl.BlockSpec(memory_space=pl.ANY)
+    return pl.pallas_call(
+        functools.partial(head_kernel, group, half_columns(mix.shape[1])),
+        out_shape=[
+            jax.ShapeDtypeStruct((total,) + mix.shape, mix.dtype),
+            jax.ShapeDtypeStruct((total,) + routers.shape, routers.dtype),
+            jax.ShapeDtypeStruct(shared.shape, shared.dtype),
+        ],
+        in_specs=[any_spec] * 3,
+        out_specs=[any_spec] * 3,
+        scratch_shapes=[dma((3,)), dma((3, 2 * group, 5)), dma((3, total)), dma((group,)), dma((group,))],
+        compiler_params=pltpu.CompilerParams(collective_id=number, has_side_effects=True),
+        name="head_exchange",
+    )(mix, routers, shared)
+
+
+def tail_kernel(group, cut, steps, *refs):
+    (mix_ref, router_ref, shared_ref, small_ref, mix_out, router_out, shared_out, small_out) = refs[:8]
+    bufs = refs[8:20]
+    totals, small_landed = refs[20:22]
+    (own_sems, core_send, core_recv, one_send, one_recv, two_send, two_recv, line_send, line_recv,
+     swap_send, swap_recv, small_send, small_recv, keep_sem) = refs[22:]
+    line = group // 2
+    y, c, z, x = places(group)
+    sibling, opposite = {"dp": 2 * y + 1 - c}, {"dp": 2 * (1 - y) + c}
+    rising, falling, across = {"expert": 2 * (z + 1) + x}, {"expert": 2 * (z - 1) + x}, {"expert": 2 * z + 1 - x}
+    me = 2 * z + x
 
     def partner(axis, bit):
-        me = lax.axis_index(axis)
-        return {axis: me + bit * (1 - 2 * lax.rem(me // bit, 2))}
-
-    for axis, bit in steps:
-        pl.semaphore_signal(barrier, inc=1, device_id=partner(axis, bit), device_id_type=MESH)
-    pl.semaphore_wait(barrier, len(steps))
-    totals[0] = value_ref[...]
-    for step, (axis, bit) in enumerate(steps):
-        copy = pltpu.make_async_remote_copy(
-            src_ref=totals.at[step],
-            dst_ref=landed.at[step],
-            send_sem=send_sems.at[step],
-            recv_sem=recv_sems.at[step],
-            device_id=partner(axis, bit),
-            device_id_type=MESH,
+        here = lax.axis_index(axis)
+        return {axis: here + bit * (1 - 2 * lax.rem(here // bit, 2))}
+
+    peers = [(None, {"expert": lax.rem(me + k, group)}) for k in range(1, group)]
+    greet(peers + [(None, sibling), (None, opposite)])
+
+    ins, outs = (mix_ref, router_ref), (mix_out, router_out)
+    held, landed, one, two, below, above = (bufs[0:2], bufs[2:4], bufs[4:6], bufs[6:8], bufs[8:10], bufs[10:12])
+    rows = mix_ref.shape[1]
+    width = mix_ref.shape[2]
+    pieces = [(0, pl.ds(0, cut), True), (0, pl.ds(cut, width - cut), False), (1, pl.ds(0, router_ref.shape[2]), True)]
+
+    def slot(yy, zz, xx):
+        return yy * group + 2 * zz + xx
+
+    def load(a, yy, zz, xx):
+        s = slot(yy, zz, xx)
+        return pltpu.make_async_copy(ins[a].at[(2 * yy + c) * group + 2 * zz + xx], held[a].at[s], own_sems.at[a, s])
+
+    def to_sibling(a, yy, zz, xx):
+        s = slot(yy, zz, xx)
+        return remote(
+            ins[a].at[(2 * yy + 1 - c) * group + 2 * zz + xx], landed[a].at[s], core_send.at[a, s], core_recv.at[a, s], sibling
         )
-        copy.start()
-        copy.wait()
-        totals[step + 1] = totals[step] + landed[step]
-    out_ref[...] = totals[len(steps)]
-
-
-def swap_sum(value, number):
+
+    def stage_one(p, zz, k):
+        a, columns, over_y = pieces[p]
+        s = slot(1 - y, zz, k) if over_y else slot(k, zz, 1 - x)
+        return remote(
+            held[a].at[s, :, columns], one[a].at[2 * zz + k, :, columns], one_send.at[p, 2 * zz + k],
+            one_recv.at[p, 2 * zz + k], opposite if over_y else across,
+        )
+
+    def stage_two(p, zz):
+        a, columns, over_y = pieces[p]
+        s = slot(y, zz, 1 - x) if over_y else slot(1 - y, zz, x)
+        return remote(
+            held[a].at[s, :, columns], two[a].at[zz, :, columns], two_send.at[p, zz], two_recv.at[p, zz],
+            across if over_y else opposite,
+        )
+
+    def rise(a, zz):
+        return remote(held[a].at[slot(y, zz, x)], below[a].at[zz], line_send.at[a, 0, zz], line_recv.at[a, 0, zz], rising)
+
+    def fall(a, zz):
+        return remote(held[a].at[slot(y, zz, x)], above[a].at[zz], line_send.at[a, 1, zz], line_recv.at[a, 1, zz], falling)
+
+    table = [sorted(range(line), key=lambda d: (-abs(d - k), d)) for k in range(line)]
+
+    def target(j):
+        return sum(jnp.where(z == k, table[k][j], 0) for k in range(line))
+
+    def swap(k):
+        to = lax.rem(me + k, group)
+        return remote(shared_ref.at[to], shared_out.at[me], swap_send.at[k], swap_recv.at[me], {"expert": to})
+
+    def small(step):
+        axis, bit = steps[step]
+        return remote(
+            totals.at[step], small_landed.at[step], small_send.at[step], small_recv.at[step], partner(axis, bit)
+        )
+
+    keep = pltpu.make_async_copy(shared_ref.at[me], shared_out.at[me], keep_sem)
+    keep.start()
+    corners = [(yy, xx) for yy in range(2) for xx in range(2)]
+    for j in range(line):
+        for a in range(2):
+            for yy, xx in corners:
+                to_sibling(a, yy, target(j), xx).start()
+                load(a, yy, target(j), xx).start()
+    for k in range(1, group):
+        swap(k).start()
+    totals[0] = small_ref[...]
+    small(0).start()
+
+    def advance(step):
+        if step < len(steps):
+            small(step).wait()
+            totals[step + 1] = totals[step] + small_landed[step]
+            if step + 1 < len(steps):
+                small(step + 1).start()
+
+    def phase_a(zz):
+        for a in range(2):
+            for yy, xx in corners:
+                s = slot(yy, zz, xx)
+                load(a, yy, zz, xx).wait()
+                to_sibling(a, yy, zz, xx).wait_recv()
+                add_blocks((held[a], (s,), None), [(held[a], (s,), None), (landed[a], (s,), None)], rows)
+        for p in range(3):
+            for k in range(2):
+                stage_one(p, zz, k).start()
+
+    def phase_b(zz):
+        for p, (a, columns, over_y) in enumerate(pieces):
+            for k in (1 - x, x) if over_y else (1 - y, y):
+                s = slot(y, zz, k) if over_y else slot(k, zz, x)
+                stage_one(p, zz, k).wait_recv()
+                add_blocks(
+                    (held[a], (s,), columns), [(held[a], (s,), columns), (one[a], (2 * zz + k,), columns)], rows
+                )
+            stage_two(p, zz).start()
+
+    def phase_c(zz):
+        s = slot(y, zz, x)
+        for p in range(3):
+            stage_two(p, zz).wait_recv()
+        for a in range(2):
+            base = [(held[a], (s,), None), (two[a], (zz,), None)]
+            low = (below[a], (zz,), None)
+            high = (above[a], (zz,), None)
+            kept = (held[a], (s,), None)
+
+            @pl.when(zz > z)
+            def _():
+                @pl.when(z > 0)
+                def _():
+                    rise(a, zz).wait_recv()
+                    add_blocks(kept, base + [low], rows)
+
+                @pl.when(z == 0)
+                def _():
+                    add_blocks(kept, base, rows)
+
+                rise(a, zz).start()
+
+            @pl.when(zz < z)
+            def _():
+                @pl.when(z < line - 1)
+                def _():
+                    fall(a, zz).wait_recv()
+                    add_blocks(kept, base + [high], rows)
+
+                @pl.when(z == line - 1)
+                def _():
+                    add_blocks(kept, base, rows)
+
+                fall(a, zz).start()
+
+    def phase_last():
+        s = slot(y, z, x)
+        for p in range(3):
+            stage_two(p, z).wait_recv()
+        for a in range(2):
+            base = [(held[a], (s,), None), (two[a], (z,), None)]
+            low = (below[a], (z,), None)
+            high = (above[a], (z,), None)
+            final = (outs[a], (), None)
+
+            @pl.when(z == 0)
+            def _():
+                fall(a, z).wait_recv()
+                add_blocks(final, base + [high], rows)
+
+            @pl.when(z == line - 1)
+            def _():
+                rise(a, z).wait_recv()
+                add_blocks(final, base + [low], rows)
+
+            @pl.when((z > 0) & (z < line - 1))
+            def _():
+                fall(a, z).wait_recv()
+                rise(a, z).wait_recv()
+                add_blocks(final, base + [low, high], rows)
+
+    for t in range(line + 2):
+        if t < line:
+            phase_a(target(t))
+        if 0 <= t - 1 < line:
+            phase_b(target(t - 1))
+        if 0 <= t - 2 < line - 1:
+            phase_c(target(t - 2))
+        if t - 2 == line - 1:
+            phase_last()
+        advance(t)
+    for step in range(line + 2, len(steps)):
+        advance(step)
+    small_out[...] = totals[len(steps)]
+    for k in range(1, group):
+        source = lax.rem(me + k, group)
+        remote(shared_ref.at[source], shared_out.at[source], swap_send.at[k], swap_recv.at[source], across).wait_recv()
+        swap(k).wait_send()
+    keep.wait()
+    for zz in range(line):
+        for a in range(2):
+            for yy, xx in corners:
+                to_sibling(a, yy, zz, xx).wait_send()
+            pl.when(zz > z)(lambda: rise(a, zz).wait_send())
+            pl.when(zz < z)(lambda: fall(a, zz).wait_send())
+        for p in range(3):
+            for k in range(2):
+                stage_one(p, zz, k).wait_send()
+            stage_two(p, zz).wait_send()
+
+
+def tail_exchange(mix, routers, shared, small, number):
+    group = lax.axis_size("expert")
+    line = group // 2
     steps = []
     for axis in BOTH:
         bit = 1
         while bit < lax.axis_size(axis):
             steps.append((axis, bit))
             bit *= 2
+    dma = pltpu.SemaphoreType.DMA
     vmem = pl.BlockSpec(memory_space=pltpu.VMEM)
+    any_spec = pl.BlockSpec(memory_space=pl.ANY)
+    scratch = []
+    for blocks in (2 * group, 2 * group, group, line, line, line):
+        scratch += [pltpu.VMEM((blocks,) + a.shape[1:], a.dtype) for a in (mix, routers)]
+    scratch += [pltpu.VMEM((len(steps) + 1,) + small.shape, FLOAT), pltpu.VMEM((len(steps),) + small.shape, FLOAT)]
+    scratch += [dma((2, 2 * group))] * 3 + [dma((3, group))] * 2 + [dma((3, line))] * 2 + [dma((2, 2, line))] * 2
+    scratch += [dma((group,))] * 2 + [dma((len(steps),))] * 2 + [dma]
     return pl.pallas_call(
-        functools.partial(swap_sum_kernel, steps),
-        out_shape=jax.ShapeDtypeStruct(value.shape, FLOAT),
-        in_specs=[vmem],
-        out_specs=vmem,
-        scratch_shapes=[
-            pltpu.VMEM((len(steps) + 1,) + value.shape, FLOAT),
-            pltpu.VMEM((len(steps),) + value.shape, FLOAT),
-            pltpu.SemaphoreType.DMA((len(steps),)),
-            pltpu.SemaphoreType.DMA((len(steps),)),
+        functools.partial(tail_kernel, group, half_columns(mix.shape[2]), steps),
+        out_shape=[
+            jax.ShapeDtypeStruct(mix.shape[1:], FLOAT),
+            jax.ShapeDtypeStruct(routers.shape[1:], FLOAT),
+            jax.ShapeDtypeStruct(shared.shape, shared.dtype),
+            jax.ShapeDtypeStruct(small.shape, FLOAT),
         ],
-        compiler_params=pltpu.CompilerParams(collective_id=number, has_side_effects=True),
-        name="swap_sum",
-    )(value)
+        in_specs=[any_spec, any_spec, any_spec, vmem],
+        out_specs=[vmem, vmem, any_spec, vmem],
+        scratch_shapes=scratch,
+        compiler_params=pltpu.CompilerParams(collective_id=number, has_side_effects=True, vmem_limit_bytes=56 * MIB),
+        name="tail_exchange",
+    )(mix, routers, shared, small)
 
 
 def state_setup(step_ref, rate_ref, step_t_ref, rate_t_ref, b_ref, c_ref, cum, cum_t, cross):
@@ -540,7 +1028,8 @@
     norm_back, normed_low, conv_out, conv_back, step_size, step_back, decay_rate, gated_back, mixer_low = saved
     grad_low = grad_out.astype(BRAIN)
     grad_mixer_out = matmul_tn(grad_low, mixer_low).astype(BRAIN)
-    grad_mixed, grad_gate, grad_mixer_gain = gated_back(matmul(grad_low, mixer_out))
+    grad_norm, grad_mixer_out = lax.optimization_barrier((matmul(grad_low, mixer_out), grad_mixer_out))
+    grad_mixed, grad_gate, grad_mixer_gain = gated_back(grad_norm)
     dx, db, dc, grad_step, grad_decay_log = state_backward(
         conv_out, step_size, decay_rate, small["skip_gain"], grad_mixed
     )
@@ -709,10 +1198,9 @@
     )(grads, gates, gate_up, shared_gu, expert_in, expert_out, shared_in, shared_out)
 
 
-def moe_forward(hidden, routes, valid, norm_gain, weights):
-    router, shared_in, shared_out, expert_in, expert_out = weights
+def moe_forward(hidden, routes, valid, norm_gain, router, pieces):
     group = lax.axis_size("expert")
-    local = expert_in.shape[0]
+    local = pieces[0].shape[0]
     normed, norm_back = jax.vjp(rms_norm, hidden, norm_gain)
     normed_low = normed.astype(BRAIN)
     logits = matmul(normed_low, router)
@@ -721,21 +1209,25 @@
     raised = jnp.where(chosen, jnp.exp(jnp.where(chosen, logits - largest, 0.0)), 0.0)
     probs = raised / jnp.sum(raised, axis=1, keepdims=True)
     gates = probs * valid[:, None]
-    rows_all, gates_all = spread([normed_low, gates.T], group, 1)
+    if lax.axis_size("dp") == 4:
+        rows_all, gates_all, expert_in, expert_out, shared = spread([normed_low, gates.T], pieces, group, 1)
+    else:
+        rows_all, gates_all = spread([normed_low, gates.T], [], group, 1)
+        expert_in, expert_out, shared = [lax.all_gather(p, "dp", axis=1, tiled=True) for p in pieces]
+    part = shared.shape[2] // 3
+    weights = (router, shared[0, :, : 2 * part], shared[0, :, 2 * part :], expert_in, expert_out)
     own_gates = lax.dynamic_slice_in_dim(gates_all, lax.axis_index("expert") * local, local, axis=1)
-    partial, picked, gate_up, shared_gu = expert_forward(
-        rows_all, own_gates, expert_in, expert_out, shared_in, shared_out
-    )
-    output = hidden + gather_sum([partial], group, 2)[0]
-    return output, (norm_back, normed_low, probs, rows_all, own_gates, picked, gate_up, shared_gu)
-
-
-def moe_backward(grad_out, saved, valid, weights):
-    norm_back, normed_low, probs, rows_all, own_gates, picked, gate_up, shared_gu = saved
+    partial, picked, gate_up, shared_gu = expert_forward(rows_all, own_gates, expert_in, expert_out, *weights[1:3])
+    output = hidden + gather_sum([partial], [], group, 2)[0]
+    return output, (norm_back, normed_low, probs, rows_all, own_gates, picked, gate_up, shared_gu, weights)
+
+
+def moe_backward(grad_out, saved, valid):
+    norm_back, normed_low, probs, rows_all, own_gates, picked, gate_up, shared_gu, weights = saved
     router, shared_in, shared_out, expert_in, expert_out = weights
     group = lax.axis_size("expert")
     local, width, inner = expert_in.shape
-    grads_all = spread([grad_out.astype(BRAIN)], group, 3)[0]
+    grads_all = spread([grad_out.astype(BRAIN)], [], group, 3)[0]
     partial, dgates, dgate_up, dresult, middle, dshared, shared_mid = expert_backward(
         grads_all, own_gates, gate_up, shared_gu, expert_in, expert_out, shared_in, shared_out
     )
@@ -745,30 +1237,28 @@
         lax.axis_index("expert") * local,
         axis=1,
     )
-    grad_normed, grad_gates = gather_sum([partial, placed], group, 4)
     rows_of = lambda array: array.reshape(local, -1, array.shape[-1])
     by_expert = lambda left, right: lax.dot_general(
         rows_of(left), rows_of(right), (((1,), (1,)), ((0,), (0,))), preferred_element_type=FLOAT
     ).astype(BRAIN)
-    grad_expert_in = by_expert(picked, dgate_up)
-    grad_expert_out = by_expert(dresult, middle)
     flat = lambda array: array.reshape(-1, array.shape[-1])
-    grad_shared_in = matmul_tn(flat(rows_all), flat(dshared)).astype(BRAIN)
-    grad_shared_out = matmul_tn(flat(grads_all), flat(shared_mid)).astype(BRAIN)
+    shared_grads = [matmul_tn(flat(rows_all), flat(dshared)), matmul_tn(flat(grads_all), flat(shared_mid))]
+    sums = [
+        by_expert(picked, dgate_up),
+        by_expert(dresult, middle),
+        jnp.concatenate(shared_grads, axis=1).astype(BRAIN)[None],
+    ]
+    if lax.axis_size("dp") == 4:
+        grad_normed, grad_gates, *sums = gather_sum([partial, placed], sums, group, 4)
+    else:
+        grad_normed, grad_gates = gather_sum([partial, placed], [], group, 4)
+        sums = [lax.psum_scatter(s, "dp", scatter_dimension=1, tiled=True).astype(FLOAT) for s in sums]
     grad_probs = grad_gates.T * valid[:, None]
     grad_logits = probs * (grad_probs - jnp.sum(probs * grad_probs, axis=1, keepdims=True))
     logits_low = grad_logits.astype(BRAIN)
     grad_router = matmul_tn(normed_low, logits_low).astype(BRAIN)
     grad_hidden, grad_gain = norm_back(grad_normed + matmul_nt(logits_low, router))
-    return (
-        grad_out + grad_hidden,
-        grad_gain,
-        grad_router,
-        grad_shared_in,
-        grad_shared_out,
-        grad_expert_in,
-        grad_expert_out,
-    )
+    return grad_out + grad_hidden, grad_gain, grad_router, sums[2][0].astype(BRAIN), sums[0], sums[1]
 
 
 def attend_scores(query, key_rows):
@@ -871,16 +1361,8 @@
     return lax.all_gather(array, BOTH, axis=0, tiled=True)
 
 
-def gather_expert(array):
-    return lax.all_gather(array, "dp", axis=1, tiled=True)
-
-
 def scatter_dense(array):
     return lax.psum_scatter(array, BOTH, scatter_dimension=0, tiled=True).astype(FLOAT)
-
-
-def scatter_expert(array):
-    return lax.psum_scatter(array, "dp", scatter_dimension=1, tiled=True).astype(FLOAT)
 
 
 def shared_columns(shared):
@@ -894,25 +1376,7 @@
     return jnp.transpose(jnp.concatenate(cut, axis=2), (1, 0, 2))
 
 
-def gather_shared(shared):
-    group = lax.axis_size("expert")
-    mine = lax.all_to_all(shared_columns(shared), "expert", split_axis=0, concat_axis=0, tiled=True)
-    mine = mine.reshape(-1, mine.shape[2])
-    whole = lax.all_gather(mine, "dp", axis=0, tiled=True)
-    part = shared[1].shape[1] // group
-    return [
-        whole[:, 0 : 2 * part],
-        whole[:, 2 * part : 3 * part],
-        whole[:, 3 * part : 5 * part],
-        whole[:, 5 * part :],
-    ]
-
-
-def scatter_shared(grads):
-    group = lax.axis_size("expert")
-    rows = lax.psum_scatter(jnp.concatenate(grads, axis=1), "dp", scatter_dimension=0, tiled=True)
-    rows = rows.reshape(group, -1, rows.shape[1])
-    own = lax.all_to_all(rows, "expert", split_axis=0, concat_axis=0, tiled=True).astype(FLOAT)
+def shared_whole(own):
     part = own.shape[2] // 6
 
     def columns(index):
@@ -925,6 +1389,24 @@
         jnp.concatenate([columns(3), columns(4)], axis=1),
         columns(5),
     ]
+
+
+def exchange(blocks):
+    return lax.all_to_all(blocks, "expert", split_axis=0, concat_axis=0, tiled=True)
+
+
+def first_gather(mixer_in, routers, shared):
+    if lax.axis_size("dp") == 4:
+        mix, routers, shared = head_exchange(mixer_in, routers, shared, 5)
+        return mix.reshape(-1, mix.shape[2]), routers.reshape(-1, routers.shape[2]), shared
+    return gather_dense(mixer_in), gather_dense(routers), exchange(shared)
+
+
+def last_sums(mix, routers, shared, small):
+    if lax.axis_size("dp") == 4:
+        cut = lambda array: array.reshape(4 * lax.axis_size("expert"), -1, array.shape[1])
+        return tail_exchange(cut(mix), cut(routers), shared, small, 6)
+    return scatter_dense(mix), scatter_dense(routers), exchange(shared), lax.psum(small, BOTH)
 
 
 def per_device(
@@ -942,47 +1424,50 @@
         "mixer_gain": mixer_gain,
     }
     assert lengths.shape[0] == 1 and layer_input.shape[0] == SLOT_LEN
+    group = lax.axis_size("expert")
+    experts = router_a.shape[1]
     valid = (jnp.arange(SLOT_LEN) < lengths[0]).astype(FLOAT)
-    w_mixer_in = gather_dense(mixer_in)
+    w_mixer_in, w_routers, w_shared = first_gather(
+        mixer_in,
+        jnp.concatenate([router_a, router_b], axis=1),
+        shared_columns([shared_in_a, shared_out_a, shared_in_b, shared_out_b]),
+    )
+    w_shared = w_shared.reshape(1, -1, w_shared.shape[2])
+    half = w_shared.shape[2] // 2
     w_mixer_out = gather_dense(mixer_out)
-    w_routers = gather_dense(jnp.concatenate([router_a, router_b], axis=1))
-    experts = router_a.shape[1]
-    w_shared = gather_shared([shared_in_a, shared_out_a, shared_in_b, shared_out_b])
-    weights_a = (
-        w_routers[:, :experts], w_shared[0], w_shared[1], gather_expert(expert_in_a), gather_expert(expert_out_a)
-    )
     w_qkv = gather_dense(attn_qkv)
     w_attn_out = gather_dense(attn_out)
-    weights_b = (
-        w_routers[:, experts:], w_shared[2], w_shared[3], gather_expert(expert_in_b), gather_expert(expert_out_b)
-    )
     hidden = layer_input.astype(FLOAT)
     hidden, saved_mix = mixer_forward(hidden, norm_gains[0], w_mixer_in, w_mixer_out, small)
-    hidden, saved_a = moe_forward(hidden, routes_a, valid, norm_gains[1], weights_a)
+    hidden, saved_a = moe_forward(
+        hidden, routes_a, valid, norm_gains[1], w_routers[:, :experts], [expert_in_a, expert_out_a, w_shared[:, :, :half]]
+    )
     hidden, saved_attn = attention_forward(hidden, norm_gains[2], w_qkv, w_attn_out)
-    layer_output, saved_b = moe_forward(hidden, routes_b, valid, norm_gains[3], weights_b)
+    layer_output, saved_b = moe_forward(
+        hidden, routes_b, valid, norm_gains[3], w_routers[:, experts:], [expert_in_b, expert_out_b, w_shared[:, :, half:]]
+    )
     grad = cotangent * valid[:, None]
-    grad, gain_four, d_router_b, d_shared_in_b, d_shared_out_b, d_in_b, d_out_b = moe_backward(
-        grad, saved_b, valid, weights_b
-    )
-    d_in_b, d_out_b = scatter_expert(d_in_b), scatter_expert(d_out_b)
+    grad, gain_four, d_router_b, d_shared_b, d_in_b, d_out_b = moe_backward(grad, saved_b, valid)
     grad, gain_three, d_qkv, d_attn_out = attention_backward(grad, saved_attn, w_qkv, w_attn_out)
+    grad, d_qkv, d_attn_out = lax.optimization_barrier((grad, d_qkv, d_attn_out))
     d_qkv, d_attn_out = scatter_dense(d_qkv), scatter_dense(d_attn_out)
-    grad, gain_two, d_router_a, d_shared_in_a, d_shared_out_a, d_in_a, d_out_a = moe_backward(
-        grad, saved_a, valid, weights_a
-    )
-    d_in_a, d_out_a = scatter_expert(d_in_a), scatter_expert(d_out_a)
-    d_shared = scatter_shared([d_shared_in_a, d_shared_out_a, d_shared_in_b, d_shared_out_b])
-    d_routers = scatter_dense(jnp.concatenate([d_router_a, d_router_b], axis=1))
+    grad, gain_two, d_router_a, d_shared_a, d_in_a, d_out_a = moe_backward(grad, saved_a, valid)
     grad, gain_one, d_mixer_in, d_mixer_out, grad_small = mixer_backward(
         grad, saved_mix, w_mixer_in, w_mixer_out, small
     )
     d_mixer_out = scatter_dense(d_mixer_out)
-    d_mixer_in = scatter_dense(d_mixer_in)
     parts = [jnp.stack([gain_one, gain_two, gain_three, gain_four])] + list(grad_small)
     flat = jnp.concatenate([part.reshape(-1) for part in parts])
     padded = jnp.pad(flat, (0, -flat.shape[0] % 1024)).reshape(-1, 128)
-    summed = swap_sum(padded, 5).reshape(-1)
+    d_shared = jnp.concatenate([d_shared_a, d_shared_b], axis=1)
+    d_mixer_in, d_routers, d_shared, summed = last_sums(
+        d_mixer_in,
+        jnp.concatenate([d_router_a, d_router_b], axis=1),
+        d_shared.reshape(group, -1, d_shared.shape[1]),
+        padded,
+    )
+    d_shared = shared_whole(d_shared.astype(FLOAT))
+    summed = summed.reshape(-1)
     sums = []
     place = 0
     for part in parts:

time: 2000 us -> 1540 us (0.77)
  waiting for transfers between devices: 767 us -> 2.65 us
  Pallas kernels: 858 us -> 1230 us
  blocking collectives: 84.8 us -> 0 us
  local copies, waits for them, and re-layouts: 54.5 us -> 89.5 us
    reduce_scatter x4 -> x3, waiting for transfers between devices: 494 us -> 0.01 us  [scatter_dense(): lax.psum_scatter(array, BOTH, scatter_dimension=0, tiled=True).astype(FLOAT)]
    pallas_call x9 -> x10, Pallas kernels: 675 us -> 1050 us  [the longest x4 390 us: spread(): pl.pallas_call(functools.partial(spread_kernel, n, w, group), out_shape=s...]
    reduce_scatter x5 -> x0, waiting for transfers between devices: 194 us -> none  [the longest x4 194 us: scatter_expert(): lax.psum_scatter(array, 'dp', scatter_dimension=1, tiled=True).astype(FLOAT)]
    all_gather x1 -> x0, blocking collectives: 64.4 us -> none  [gather_dense(): return lax.all_gather(array, BOTH, axis=0, tiled=True)]
    all_gather x4 -> x3, waiting for transfers between devices: 62.5 us -> 0.02 us  [gather_dense(): return lax.all_gather(array, BOTH, axis=0, tiled=True)]
    convert_element_type x0 -> x1, local copies, waits for them, and re-layouts: none -> 25.5 us  [mixer_backward(): grad_mixer_in = matmul_tn(normed_low, grad_proj).astype(BRAIN)]
    all_to_all x1 -> x0, blocking collectives: 20.4 us -> none  [gather_shared(): lax.all_to_all(shared_columns(shared), 'expert', split_axis=0, concat_axi...]
  transfers between devices with their start and end apart: 20 -> 6, of which waited for: 12 -> 0; matrix products, arithmetic and copies ran while one was open for 10% -> 12% of each run, Pallas kernels for 26% -> 57%
where the time goes in v2:
time: 1540 us; the launch traced here: 1530 us
  Pallas kernels  1230 us (80%)
  matrix products  137 us (9%)
  local copies, waits for them, and re-layouts  89.5 us (6%)
  other arithmetic  56.3 us (4%)
  between operations  16.6 us (1%)
    pallas_call x4, Pallas kernels, spread(): pl.pallas_call(functools.partial(spread_kernel, n, w, group), out_shape=s...  390 us
    pallas_call x4, Pallas kernels, gather_sum(): pl.pallas_call(functools.partial(gather_sum_kernel, n, w, group), out_sha...  379 us
    pallas_call x1, Pallas kernels, head_exchange(): pl.pallas_call(functools.partial(head_kernel, group, half_columns(mix.sha...  140 us
    pallas_call x1, Pallas kernels, tail_exchange(): pl.pallas_call(functools.partial(tail_kernel, group, half_columns(mix.sha...  139 us
    pallas_call x2, Pallas kernels, expert_backward(): pl.pallas_call(expert_backward_kernel, grid=(group,), out_shape=[jax.Shap...  79.5 us
    pallas_call x2, Pallas kernels, expert_forward(): pl.pallas_call(expert_forward_kernel, grid=(group,), out_shape=[jax.Shape...  65.8 us
    dot_general x10, matrix products, matmul_tn(): lax.dot_general(left, right, (((0,), (0,)), ((), ())), preferred_element_...  42.6 us
    unnamed x249, local copies, waits for them, and re-layouts  36.2 us
  transfers between devices with their start and end apart: 6, of which 0 were waited for; matrix products, arithmetic and copies ran while one was open for 12% of the time, Pallas kernels for 57%

profile of v2, /device:TPU:16, one launch (start us, length us, event | category | flops | bytes accessed | tf_op | source)
XLA Modules:
  0.0 1532.0 jit_solution(6233148845972765119)
XLA Ops:
  15.2 1.6 slice_reduce_fusion.4
  19.8 100.7 %spread3.2.d_ref = bf16[8,256,1536]{2,1,0:T(8,128)(2,1)} custom-call(bf16[256,1536]{1,0:T(8,128)(2,1)} %multiply_convert_fusion.4.refs_0_), custom_call_target="tpu_custom_call" | custom-call | tf_op jit(solution)/shard_map/spread3/pallas_call | solution.py:196
  122.2 139.8 %head_exchange.1 = (bf16[32,48,6448]{2,1,0:T(8,128)(2,1)}, bf16[32,48,32]{2,1,0:T(8,128)(2,1)}, bf16[8,48,768]{2,1,0:T(8,128)(2,1)}) custom-call(bf16[48,6448]{1,0:T(8,128)(2,1)} %mix_ref.1, bf16[48,32]{1,0:T(8,128)(2,1)} %pad_maximum_fusion.10.router_ref, bf16[8,48,768]{2,1,0:T(8,128)(2,1)} %bitcast.226), custom_call_target="tpu_custom_call" | custom-call | tf_op jit(solution)/shard_map/head_exchange/pallas_call | solution.py:562
  262.1 9.9 fusion.43
  272.2 2.6 copy-done.33
  278.9 4.1 fusion.3
  283.1 9.3 state_forward.1
  292.5 4.1 multiply_reduce_fusion.6
  297.6 6.9 multiply_reduce_fusion.15
  306.9 109.4 %spread1.2 = (bf16[8,256,1536]{2,1,0:T(8,128)(2,1)}, f32[8,16,256]{2,1,0:T(8,128)}, bf16[2,1536,1024]{2,1,0:T(8,128)(2,1)}, bf16[2,1536,512]{2,1,0:T(8,128)(2,1)}, bf16[1,1536,384]{2,1,0:T(8,128)(2,1)}) custom-call(bf16[256,1536]{1,0:T(8,128)(2,1)} %copy-done.46, f32[16,256]{1,0:T(8,128)} %fusion.66.refs_1_, bf16[2,384,1024]{2,1,0:T(8,128)(2,1)} %refs_2_.2, ...), custom_call_target="tpu_custom_call" | custom-call | tf_op jit(solution)/shard_map/spread1/pallas_call | solution.py:196
  419.4 32.9 %expert_forward.2 = (bf16[8,256,1536]{2,1,0:T(8,128)(2,1)}, bf16[2,8,128,1536]{3,2,1,0:T(8,128)(2,1)}, bf16[2,8,128,1024]{3,2,1,0:T(8,128)(2,1)}, bf16[8,256,256]{2,1,0:T(8,128)(2,1)}) custom-call(bf16[8,256,1536]{2,1,0:T(8,128)(2,1)} %get-tuple-element.88.x_ref, f32[8,2,256]{2,1,0:T(2,128)S(1)} %constant_dynamic-slice_fusion.1.g_ref, ...), custom_call_target="tpu_custom_call" | custom-call | tf_op jit(solution)/shard_map/expert_forward/pallas_call | solution.py:1090
  452.3 89.5 %gather_sum2.2 = f32[256,1536]{1,0:T(8,128)S(1)} custom-call(bf16[8,256,1536]{2,1,0:T(8,128)(2,1)} %get-tuple-element.93.refs_0_), custom_call_target="tpu_custom_call" | custom-call | tf_op jit(solution)/shard_map/gather_sum2/pallas_call | solution.py:399
  543.1 6.0 convolution_convert_fusion.6.q_ref.k_ref.v_ref
  549.1 4.6 attention_forward.1
  553.7 4.4 multiply_reduce_fusion.13
  561.7 108.1 %spread1.3 = (bf16[8,256,1536]{2,1,0:T(8,128)(2,1)}, f32[8,16,256]{2,1,0:T(8,128)}, bf16[2,1536,1024]{2,1,0:T(8,128)(2,1)}, bf16[2,1536,512]{2,1,0:T(8,128)(2,1)}, bf16[1,1536,384]{2,1,0:T(8,128)(2,1)}) custom-call(bf16[256,1536]{1,0:T(8,128)(2,1)} %copy-done.48, f32[16,256]{1,0:T(8,128)} %fusion.62.refs_1_, bf16[2,384,1024]{2,1,0:T(8,128)(2,1)} %refs_2_.3, ...), custom_call_target="tpu_custom_call" | custom-call | tf_op jit(solution)/shard_map/spread1/pallas_call | solution.py:196
  672.8 32.9 %expert_forward.3 = (bf16[8,256,1536]{2,1,0:T(8,128)(2,1)}, bf16[2,8,128,1536]{3,2,1,0:T(8,128)(2,1)}, bf16[2,8,128,1024]{3,2,1,0:T(8,128)(2,1)}, bf16[8,256,256]{2,1,0:T(8,128)(2,1)}) custom-call(bf16[8,256,1536]{2,1,0:T(8,128)(2,1)} %get-tuple-element.94.x_ref, f32[8,2,256]{2,1,0:T(2,128)S(1)} %constant_dynamic-slice_fusion.g_ref, ...), custom_call_target="tpu_custom_call" | custom-call | tf_op jit(solution)/shard_map/expert_forward/pallas_call | solution.py:1090
  705.7 80.3 %gather_sum2.3 = f32[256,1536]{1,0:T(8,128)S(1)} custom-call(bf16[8,256,1536]{2,1,0:T(8,128)(2,1)} %get-tuple-element.99.refs_0_), custom_call_target="tpu_custom_call" | custom-call | tf_op jit(solution)/shard_map/gather_sum2/pallas_call | solution.py:399
  786.0 39.6 %expert_backward.2 = (bf16[8,256,1536]{2,1,0:T(8,128)(2,1)}, f32[8,2,256]{2,1,0:T(2,128)S(1)}, bf16[2,8,128,1024]{3,2,1,0:T(8,128)(2,1)}, bf16[2,8,128,1536]{3,2...) custom-call(bf16[8,256,1536]{2,1,0:T(8,128)(2,1)} %spread3.2.d_ref, ...), custom_call_target="tpu_custom_call" | custom-call | tf_op jit(solution)/shard_map/expert_backward/pallas_call | solution.py:1165
  825.6 4.8 fusion.16
  830.4 4.8 fusion.12
  835.4 8.7 convolution_convert_fusion.5.refs_2_
  844.2 6.6 convolution_convert_fusion.8.refs_3_
  850.8 93.1 %gather_sum4.2 = (f32[256,1536]{1,0:T(8,128)}, f32[16,256]{1,0:T(8,128)S(1)}, f32[2,384,1024]{2,1,0:T(8,128)}, f32[2,384,512]{2,1,0:T(8,128)}, f32[1,384,384]{2,1,0:T(8,128)S(1)}) custom-call(bf16[8,256,1536]{2,1,0:T(8,128)(2,1)} %get-tuple-element.102.refs_0_, f32[8,16,256]{2,1,0:T(8,128)S(1)} %constant_dynamic-update-slice_fusion.7.refs_1_, ...), custom_call_target="tpu_custom_call" | custom-call | tf_op jit(solution)/shard_map/gather_sum4/pallas_call | solution.py:399
  944.1 2.5 multiply_reduce_fusion.7
  946.6 1.7 fusion.21
  949.4 3.6 convolution_convert_fusion.3
  953.0 4.2 convolution_convert_fusion.9.d_ref
  957.2 7.1 attention_backward.1
  964.4 5.4 convolution_convert_fusion.2
  969.8 6.2 multiply_reduce_fusion.8
  976.0 1.5 fusion.22
  980.2 2.4 convert_element_type.143.refs_0_
  982.5 71.7 %spread3.3.d_ref = bf16[8,256,1536]{2,1,0:T(8,128)(2,1)} custom-call(bf16[256,1536]{1,0:T(8,128)(2,1)} %convert_element_type.143.refs_0_), custom_call_target="tpu_custom_call" | custom-call | tf_op jit(solution)/shard_map/spread3/pallas_call | solution.py:196
  1054.3 39.9 %expert_backward.3 = (bf16[8,256,1536]{2,1,0:T(8,128)(2,1)}, f32[8,2,256]{2,1,0:T(2,128)S(1)}, bf16[2,8,128,1024]{3,2,1,0:T(8,128)(2,1)}, bf16[2,8,128,1536]{3,2...) custom-call(bf16[8,256,1536]{2,1,0:T(8,128)(2,1)} %spread3.3.d_ref, ...), custom_call_target="tpu_custom_call" | custom-call | tf_op jit(solution)/shard_map/expert_backward/pallas_call | solution.py:1165
  1094.3 1.8 fusion.15
  1096.2 4.8 fusion.11
  1101.1 6.6 convolution_convert_fusion.7.refs_3_
  1107.7 9.1 convolution_convert_fusion.4.refs_2_
  1116.8 115.9 %gather_sum4.3 = (f32[256,1536]{1,0:T(8,128)}, f32[16,256]{1,0:T(8,128)S(1)}, f32[2,384,1024]{2,1,0:T(8,128)}, f32[2,384,512]{2,1,0:T(8,128)}, f32[1,384,384]{2,1,0:T(8,128)S(1)}) custom-call(bf16[8,256,1536]{2,1,0:T(8,128)(2,1)} %get-tuple-element.118.refs_0_, f32[8,16,256]{2,1,0:T(8,128)S(1)} %constant_dynamic-update-slice_fusion.6.refs_1_, ...), custom_call_target="tpu_custom_call" | custom-call | tf_op jit(solution)/shard_map/gather_sum4/pallas_call | solution.py:399
  1232.9 3.3 multiply_reduce_fusion.9
  1238.9 2.4 fusion.23
  1242.5 5.4 convolution_convert_fusion.1
  1247.9 5.8 fusion.30
  1253.7 1.7 multiply_reduce_fusion.4
  1255.8 6.2 fusion.7
  1263.4 1.9 copy-done.6
  1266.8 16.4 %state_backward.1 = (f32[256,3072]{1,0:T(8,128)S(1)}, f32[256,128]{1,0:T(8,128)S(1)}, f32[256,128]{1,0:T(8,128)S(1)}, f32[256,48]{1,0:T(8,128)S(1)}, f32[48,256]{1,0:T(8,128)S(1)}) custom-call(f32[256,3328]{1,0:T(8,128)S(1)} %copy-done.3, f32[256,3328]{1,0:T(8,128)S(1)} %copy-done.3, f32[256,3328]{1,0:T(8,128)S(1)} %copy-done.3, f32[256,48]{1,0:T(8,128)S(1)} %copy-done.10, ...), custom_call_target="tpu_custom_call" | custom-call | tf_op jit(solution)/shard_map/state_backward/pallas_call | solution.py:955
  1283.2 1.7 copy-done.7
  1287.5 1.6 copy.148
  1289.0 1.9 copy-done.8
  1293.1 6.3 multiply_reduce_fusion.2
  1300.9 3.0 broadcast_multiply_fusion
  1305.1 11.9 fusion.20
  1317.0 11.6 convolution_convert_fusion
  1328.6 25.5 %copy.150 = bf16[1536,6448]{1,0:T(8,128)(2,1)} copy(bf16[1536,6448]{0,1:T(8,128)(2,1)} %convolution_convert_fusion) | data formatting | bytes 39616512 | tf_op jit(solution)/shard_map/convert_element_type | solution.py:1040
  1355.9 139.0 %tail_exchange.1 = (f32[48,6448]{1,0:T(8,128)}, f32[48,32]{1,0:T(8,128)}, bf16[8,48,768]{2,1,0:T(8,128)(2,1)}, f32[208,128]{1,0:T(8,128)}) custom-call(bf16[32,48,6448]{2,1,0:T(8,128)(2,1)} %bitcast.218, bf16[32,48,32]{2,1,0:T(8,128)(2,1)} %bitcast.223, bf16[8,48,768]{2,1,0:T(8,128)(2,1)} %pad_maximum_fusion.5.refs_2_, f32[208,128]{1,0:T(8,128)} %pad_bitcast_fusion.refs_3_), custom_call_target="tpu_custom_call" | custom-call | tf_op jit(solution)/shard_map/tail_exchange/pallas_call | solution.py:803
  1508.2 1.6 fusion.24
  1509.8 1.8 convert_element_type.159
  1511.6 1.8 convert_element_type.158
  1513.3 1.8 convert_element_type.156
  1515.1 2.4 copy.221
  1517.6 1.7 copy.222
  1521.2 1.7 copy.224
  (357 shorter events, 68.5 us)
Async XLA Ops:
  7.2 114.0 %copy-start = (bf16[48,1024]{1,0:T(8,128)(2,1)S(1)}, bf16[48,1024]{1,0:T(8,128)(2,1)}, u32[]{:S(2)}) copy-start(bf16[48,1024]{1,0:T(8,128)(2,1)} %param.35) | copy-start | bytes 294916
  7.2 11.5 copy-start.52
  7.2 290.4 %all-gather.4.cloned.1.call-start = ((), (), s32[]{:S(2)}) async-start(), calls=%async_computation.3 | async-start | bytes 9732096 | tf_op jit(solution)/shard_map/all_gather | solution.py:1361
  8.0 535.1 %all-gather.6.cloned.1.call-start = ((), (), s32[]{:S(2)}) async-start(), calls=%async_computation.4 | async-start | bytes 8110080 | tf_op jit(solution)/shard_map/all_gather | solution.py:1361
  8.7 545.0 %all-gather.8.cloned.1.call-start = ((), (), s32[]{:S(2)}) async-start(), calls=%async_computation.5 | async-start | bytes 4866048 | tf_op jit(solution)/shard_map/all_gather | solution.py:1361
  9.4 1500.3 %reduce-scatter.8.cloned.1.call-start = ((), (), s32[]{:S(2)}) async-start(), calls=%async_computation.8 | async-start | bytes 4866048 | tf_op jit(solution)/shard_map/reduce_scatter | solution.py:1365
  10.1 110.4 %copy-start.86 = (f32[256]{0:T(256)}, f32[256]{0:T(256)S(1)}, u32[]{:S(2)}) copy-start(f32[256]{0:T(256)S(1)} %compare_convert_fusion) | copy-start | bytes 3076
  11.5 250.5 %copy-start.84 = (f32[256]{0:T(256)}, f32[256]{0:T(256)S(1)}, u32[]{:S(2)}) copy-start(f32[256]{0:T(256)S(1)} %fusion.71) | copy-start | bytes 3076
  12.7 270.3 %copy-start.24 = (f32[1,48]{1,0:T(1,128)}, f32[1,48]{1,0:T(1,128)S(1)}, u32[]{:S(2)}) copy-start(f32[1,48]{1,0:T(1,128)S(1)} %get-tuple-element.276.rate_ref) | copy-start | bytes 580
  14.4 268.7 %copy-start.15 = (f32[48,1]{1,0:T(8,128)}, f32[48,1]{1,0:T(8,128)S(1)}, u32[]{:S(2)}) copy-start(f32[48,1]{1,0:T(8,128)S(1)} %copy.132.rate_t_ref) | copy-start | bytes 580
  15.2 267.8 %copy-start.21 = (f32[1,3072]{1,0:T(1,128)}, f32[1,3072]{1,0:T(1,128)S(1)}, u32[]{:S(2)}) copy-start(f32[1,3072]{1,0:T(1,128)S(1)} %broadcast_in_dim_reshape.4.skip_ref) | copy-start | bytes 36868
  16.8 245.3 %copy-start.67 = (f32[1536]{0:T(1024)}, f32[1536]{0:T(1024)S(1)}, u32[]{:S(2)}) copy-start(f32[1536]{0:T(1024)S(1)} %get-tuple-element.237) | copy-start | bytes 18436
  19.8 101.6 %copy-start.81 = (bf16[48,1024]{1,0:T(8,128)(2,1)S(1)}, bf16[48,1024]{1,0:T(8,128)(2,1)}, u32[]{:S(2)}) copy-start(bf16[48,1024]{1,0:T(8,128)(2,1)} %param.42) | copy-start | bytes 294916
  19.8 242.3 %copy-start.50 = (bf16[256,1536]{1,0:T(8,128)(2,1)S(1)}, bf16[256,1536]{1,0:T(8,128)(2,1)}, u32[]{:S(2)}) copy-start(bf16[256,1536]{1,0:T(8,128)(2,1)} %param.26) | copy-start | bytes 2359300
  274.7 8.3 copy-start.31
  276.7 6.4 copy-start.13
  283.0 9.4 copy-start.2
  283.1 9.3 copy-start.97
  283.1 9.3 copy-start.98
  296.6 8.0 copy-start.28
  296.6 8.0 copy-start.95
  296.6 957.1 %copy-start.92 = (f32[256]{0:T(256)}, f32[256]{0:T(256)S(1)}, u32[]{:S(2)}) copy-start(f32[256]{0:T(256)S(1)} %fusion.72) | copy-start | bytes 3076
  297.6 8.3 copy-start.54
  452.3 89.5 %copy-start.36 = (f32[256,1536]{1,0:T(8,128)S(1)}, f32[256,1536]{1,0:T(8,128)}, u32[]{:S(2)}) copy-start(f32[256,1536]{1,0:T(8,128)} %copy-done.35) | copy-start | bytes 4718596
  553.7 6.7 copy-start.55
  825.6 9.7 slice-start.2
  835.2 8.9 slice-start.4
  835.4 8.8 slice-start.5
  850.8 93.2 %copy-start.45 = (f32[256,1536]{1,0:T(8,128)S(1)}, f32[256,1536]{1,0:T(8,128)}, u32[]{:S(2)}) copy-start(f32[256,1536]{1,0:T(8,128)} %copy-done.44) | copy-start | bytes 4718596
  850.8 93.2 %copy-start.56 = (bf16[32,48,32]{2,1,0:T(8,128)(2,1)S(1)}, bf16[32,48,32]{2,1,0:T(8,128)(2,1)}, u32[]{:S(2)}) copy-start(bf16[32,48,32]{2,1,0:T(8,128)(2,1)} %get-tuple-element.86) | copy-start | bytes 294916
  957.2 7.2 copy-start.40
  969.8 6.2 copy-start.39
  969.8 6.2 copy-start.41
  977.6 534.0 %reduce-scatter.6.cloned.1.call-start = ((), (), s32[]{:S(2)}) async-start(), calls=%async_computation.7 | async-start | bytes 8110080 | tf_op jit(solution)/shard_map/reduce_scatter | solution.py:1365
  978.2 535.2 %reduce-scatter.4.cloned.1.call-start = ((), (), s32[]{:S(2)}) async-start(), calls=%async_computation.6 | async-start | bytes 9732096 | tf_op jit(solution)/shard_map/reduce_scatter | solution.py:1365
  1054.3 40.0 %copy-start.34 = (bf16[8,256,1536]{2,1,0:T(8,128)(2,1)S(1)}, bf16[8,256,1536]{2,1,0:T(8,128)(2,1)}, u32[]{:S(2)}) copy-start(bf16[8,256,1536]{2,1,0:T(8,128)(2,1)} %spread3.3.d_ref) | copy-start | bytes 18874372
  1096.1 11.6 slice-start
  1101.1 6.6 slice-start.1
  1101.1 6.6 copy-start.104
  1116.8 116.0 %copy-start.37 = (f32[256,1536]{1,0:T(8,128)S(1)}, f32[256,1536]{1,0:T(8,128)}, u32[]{:S(2)}) copy-start(f32[256,1536]{1,0:T(8,128)} %copy-done.35) | copy-start | bytes 4718596
  1116.8 116.0 %copy-start.57 = (bf16[32,48,32]{2,1,0:T(8,128)(2,1)S(1)}, bf16[32,48,32]{2,1,0:T(8,128)(2,1)}, u32[]{:S(2)}) copy-start(bf16[32,48,32]{2,1,0:T(8,128)(2,1)} %get-tuple-element.86) | copy-start | bytes 294916
  1247.9 5.8 copy-start.30
  1247.9 7.5 copy-start.5
  1255.8 7.6 copy-start.10
  1255.8 7.6 copy-start.22
  1255.8 7.6 copy-start.25
  1293.0 6.6 copy-start.27
  1293.0 6.6 copy-start.78
  1293.0 6.6 copy-start.100
  1293.0 6.6 copy-start.102
  1293.0 7.8 copy-start.70
  1293.0 7.8 copy-start.72
  1293.0 7.8 copy-start.74
  1293.1 7.8 copy-start.76
  1305.0 11.9 copy-start.89
  1305.0 11.9 copy-start.90
  1305.1 11.9 copy-start.91
  1328.6 25.5 %copy-start.82 = (f32[48,64]{1,0:T(8,128)S(1)}, f32[48,64]{1,0:T(8,128)}, u32[]{:S(2)}) copy-start(f32[48,64]{1,0:T(8,128)} %reshape.400) | copy-start | bytes 36868
  1328.6 25.6 %copy-start.101 = (f32[48]{0:T(128)S(1)}, f32[48]{0:T(128)}, u32[]{:S(2)}) copy-start(f32[48]{0:T(128)} %param.49) | copy-start | bytes 580
  1328.6 25.6 %copy-start.88 = (f32[3072]{0:T(1024)S(1)}, f32[3072]{0:T(1024)}, u32[]{:S(2)}) copy-start(f32[3072]{0:T(1024)} %get-tuple-element.219) | copy-start | bytes 36868
  1328.6 26.4 %copy-start.63 = (bf16[1,384,384]{2,1,0:T(8,128)(2,1)S(1)}, bf16[1,384,384]{2,1,0:T(8,128)(2,1)}, u32[]{:S(2)}) copy-start(bf16[1,384,384]{2,1,0:T(8,128)(2,1)} %convert_element_type.154) | copy-start | bytes 884740
  1328.6 26.4 %copy-start.64 = (bf16[1,384,384]{2,1,0:T(8,128)(2,1)S(1)}, bf16[1,384,384]{2,1,0:T(8,128)(2,1)}, u32[]{:S(2)}) copy-start(bf16[1,384,384]{2,1,0:T(8,128)(2,1)} %convert_element_type.152) | copy-start | bytes 884740
  1355.9 145.2 %copy-start.94 = (f32[256]{0:T(256)S(1)}, f32[256]{0:T(256)}, u32[]{:S(2)}) copy-start(f32[256]{0:T(256)} %copy-done.93) | copy-start | bytes 3076
  1509.8 7.8 copy-start.59
  (56 other events, 145.5 us)
Sparse Core Ops, SparseCore 0:
  11.0 106.9 all-gather.3
  121.0 106.3 all-gather.5
  230.4 67.9 all-gather.7
  977.7 114.5 reduce-scatter.7
  1098.8 147.2 reduce-scatter.5
  1289.2 182.7 reduce-scatter.3

commit v3 on v2

--- a/solution.py
+++ b/solution.py
@@ -98,15 +98,19 @@
     )
 
 
-def spread_kernel(count, wide, group, *refs):
+def spread_kernel(count, wide, sums, group, *refs):
     total = count + wide
-    ins, outs = refs[:total], refs[total : 2 * total]
-    sems = refs[2 * total :]
+    every = total + sums
+    ins, outs = refs[:every], refs[every : 2 * every]
+    stages = refs[2 * every : 2 * every + wide]
+    sum_bufs = refs[2 * every + wide : 2 * every + wide + 3 * sums]
+    sems = refs[2 * every + wide + 3 * sums :]
+    sum_sems = sems[-5:]
     up_sems, down_sems, cross_sems, recv_sems, own_sems = sems[:5]
     line = group // 2
     y, c, z, x = places(group)
     sibling, opposite = {"dp": 2 * y + 1 - c}, {"dp": 2 * (1 - y) + c}
-    greet(line_peers(z, x, line) + ([(None, sibling), (None, opposite)] if wide else []))
+    greet(line_peers(z, x, line) + ([(None, sibling), (None, opposite)] if wide or sums else []))
 
     def copy(i, src, place, sem, device):
         return remote(src, outs[i].at[place], sem, recv_sems.at[i, place], {"expert": device})
@@ -135,7 +139,7 @@
         return outs[i].at[:, pl.ds(pl.multiple_of(q * rows, rows), rows), :]
 
     def wide_copy(i, kind):
-        wide_send, wide_recv = sems[5:]
+        wide_send, wide_recv = sems[5:7]
         own, other = 2 * y + c, 2 * (1 - y) + c
         k = i - count
         if kind == 0:
@@ -145,8 +149,12 @@
         return remote(block(i, other), block(i, other), wide_send.at[k, 2], wide_recv.at[k, 2], sibling)
 
     def own_copy(i):
-        place = outs[i].at[2 * z + x] if i < count else block(i, 2 * y + c)
-        return pltpu.make_async_copy(ins[i], place, own_sems.at[i])
+        if i < count:
+            return pltpu.make_async_copy(ins[i], outs[i].at[2 * z + x], own_sems.at[i])
+        return pltpu.make_async_copy(ins[i], stages[i - count], own_sems.at[i])
+
+    def own_store(i):
+        return pltpu.make_async_copy(stages[i - count], block(i, 2 * y + c), own_sems.at[i])
 
     def forward(i, s, rising, up, down, cross):
         if s:
@@ -164,12 +172,54 @@
             pl.when(z > 0)(lambda: down().wait_send())
         cross().wait_send()
 
+    def sum_parts(k):
+        kept, landed, arrived = sum_bufs[3 * k : 3 * k + 3]
+        own, core_send, core_recv, side_send, side_recv = sum_sems
+        source = ins[total + k]
+        rows = source.shape[1] // 4
+
+        def piece(q):
+            return source.at[:, pl.ds(pl.multiple_of(q * rows, rows), rows), :]
+
+        def load(h):
+            return pltpu.make_async_copy(piece(2 * h + c), kept.at[h], own.at[k, h])
+
+        def to_sibling(h):
+            return remote(piece(2 * h + 1 - c), landed.at[h], core_send.at[k, h], core_recv.at[k, h], sibling)
+
+        def to_opposite():
+            return remote(kept.at[1 - y], arrived, side_send.at[k], side_recv.at[k], opposite)
+
+        def add(target, lead, sources):
+            for e in range(source.shape[0]):
+                add_blocks((target, lead + (e,), None), [(ref, at + (e,), None) for ref, at in sources], rows)
+
+        return kept, landed, arrived, load, to_sibling, to_opposite, add
+
+    for k in range(sums):
+        load, to_sibling = sum_parts(k)[3:5]
+        for h in (1 - y, y):
+            to_sibling(h).start()
+            load(h).start()
     for i in range(count, total):
         wide_copy(i, 1).start()
         wide_copy(i, 0).start()
     for i in range(total):
         own_copy(i).start()
-    steps(forward)
+    for i in range(count, total):
+        own_copy(i).wait()
+        own_store(i).start()
+    if sums:
+        steps(lambda *move: forward(*move) if move[1] == 0 else None)
+        for k in range(sums):
+            kept, landed, arrived, load, to_sibling, to_opposite, add = sum_parts(k)
+            load(1 - y).wait()
+            to_sibling(1 - y).wait_recv()
+            add(kept, (1 - y,), [(kept, (1 - y,)), (landed, (1 - y,))])
+            to_opposite().start()
+        steps(lambda *move: forward(*move) if move[1] else None)
+    else:
+        steps(forward)
     for i in range(count, total):
         wide_copy(i, 1).wait_recv()
         wide_copy(i, 2).start()
@@ -182,27 +232,48 @@
         wide_copy(i, 0).wait()
         wide_copy(i, 1).wait_send()
         wide_copy(i, 2).wait()
-    for i in range(total):
+    for i in range(count):
         own_copy(i).wait()
-
-
-def spread(arrays, wide, group, number):
-    n, w, line = len(arrays), len(wide), group // 2
+    for i in range(count, total):
+        own_store(i).wait()
+    for k in range(sums):
+        kept, landed, arrived, load, to_sibling, to_opposite, add = sum_parts(k)
+        load(y).wait()
+        to_sibling(y).wait_recv()
+        to_opposite().wait_recv()
+        add(outs[total + k], (), [(kept, (y,)), (landed, (y,)), (arrived, ())])
+        for h in range(2):
+            to_sibling(h).wait_send()
+        to_opposite().wait_send()
+
+
+def spread(arrays, wide, sums, group, number):
+    n, w, s, line = len(arrays), len(wide), len(sums), group // 2
     split = lax.axis_size("dp")
     dma = pltpu.SemaphoreType.DMA
     any_spec = pl.BlockSpec(memory_space=pl.ANY)
+    vmem = pl.BlockSpec(memory_space=pltpu.VMEM)
     shapes = [jax.ShapeDtypeStruct((group,) + a.shape, a.dtype) for a in arrays]
     shapes += [jax.ShapeDtypeStruct((a.shape[0], split * a.shape[1], a.shape[2]), a.dtype) for a in wide]
+    scratch = [pltpu.VMEM(a.shape, a.dtype) for a in wide]
+    for a in sums:
+        part = (a.shape[0], a.shape[1] // 4, a.shape[2])
+        scratch += [pltpu.VMEM((2,) + part, a.dtype)] * 2 + [pltpu.VMEM(part, a.dtype)]
+        shapes.append(jax.ShapeDtypeStruct(part, FLOAT))
+    scratch += [dma((n, line)), dma((n, line)), dma((n, line)), dma((n, group)), dma((n + w,))]
+    if w:
+        scratch += [dma((w, 3)), dma((w, 3))]
+    if s:
+        scratch += [dma((s, 2))] * 3 + [dma((s,))] * 2
     return pl.pallas_call(
-        functools.partial(spread_kernel, n, w, group),
+        functools.partial(spread_kernel, n, w, s, group),
         out_shape=shapes,
-        in_specs=[any_spec] * (n + w),
-        out_specs=[any_spec] * (n + w),
-        scratch_shapes=[dma((n, line)), dma((n, line)), dma((n, line)), dma((n, group)), dma((n + w,))]
-        + ([dma((w, 3)), dma((w, 3))] if w else []),
-        compiler_params=pltpu.CompilerParams(collective_id=number, has_side_effects=True),
+        in_specs=[any_spec] * (n + w + s),
+        out_specs=[any_spec] * (n + w) + [vmem] * s,
+        scratch_shapes=scratch,
+        compiler_params=pltpu.CompilerParams(collective_id=number, has_side_effects=True, vmem_limit_bytes=40 * MIB),
         name="spread%d" % number,
-    )(*arrays, *wide)
+    )(*arrays, *wide, *sums)
 
 
 def add_blocks(target, sources, rows):
@@ -227,187 +298,11 @@
     lax.fori_loop(0, rows // step, body, 0)
 
 
-def gather_sum_kernel(count, wide, group, *refs):
-    total = count + wide
-    ins, outs = refs[:total], refs[total : 2 * total]
-    bufs = refs[2 * total : 2 * total + 4 * count + 3 * wide]
-    own_sems, cross_send, cross_recv, up_send, up_recv, down_send, down_recv = refs[2 * total + 4 * count + 3 * wide :][:7]
-    line = group // 2
-    held = [bufs[4 * i] for i in range(count)]
-    crossed = [bufs[4 * i + 1] for i in range(count)]
-    below = [bufs[4 * i + 2] for i in range(count)]
-    above = [bufs[4 * i + 3] for i in range(count)]
-    y, c, z, x = places(group)
-    sibling, opposite = {"dp": 2 * y + 1 - c}, {"dp": 2 * (1 - y) + c}
-    greet(line_peers(z, x, line) + ([(None, sibling), (None, opposite)] if wide else []))
-
-    def own(i, d):
-        return pltpu.make_async_copy(ins[i].at[2 * d + x], held[i].at[d], own_sems.at[i, d])
-
-    def cross(i, d):
-        return remote(
-            ins[i].at[2 * d + 1 - x], crossed[i].at[d], cross_send.at[i, d], cross_recv.at[i, d],
-            {"expert": 2 * z + 1 - x},
-        )
-
-    def rise(i, d):
-        return remote(held[i].at[d], below[i].at[d], up_send.at[i, d], up_recv.at[i, d], {"expert": 2 * (z + 1) + x})
-
-    def fall(i, d):
-        return remote(held[i].at[d], above[i].at[d], down_send.at[i, d], down_recv.at[i, d], {"expert": 2 * (z - 1) + x})
-
-    def order(act):
-        for k in range(line):
-            pl.when(line - 1 - k > z)(functools.partial(act, line - 1 - k))
-            pl.when(k < z)(functools.partial(act, k))
-        for k in range(line):
-            pl.when(k == z)(functools.partial(act, k))
-
-    def start_all(d):
-        for i in range(count):
-            cross(i, d).start()
-            own(i, d).start()
-
-    order(start_all)
-
-    def wide_parts(i):
-        k = i - count
-        kept, landed, arrived = bufs[4 * count + 3 * k : 4 * count + 3 * k + 3]
-        wide_own, core_send, core_recv, side_send, side_recv = refs[-5:]
-        rows = ins[i].shape[1] // 4
-
-        def block(q):
-            return ins[i].at[:, pl.ds(pl.multiple_of(q * rows, rows), rows), :]
-
-        def load(h):
-            return pltpu.make_async_copy(block(2 * h + c), kept.at[h], wide_own.at[k, h])
-
-        def to_sibling(h):
-            return remote(block(2 * h + 1 - c), landed.at[h], core_send.at[k, h], core_recv.at[k, h], sibling)
-
-        def to_opposite():
-            return remote(kept.at[1 - y], arrived, side_send.at[k], side_recv.at[k], opposite)
-
-        return kept, landed, arrived, load, to_sibling, to_opposite, rows
-
-    for i in range(count, total):
-        load, to_sibling = wide_parts(i)[3:5]
-        for h in (1 - y, y):
-            to_sibling(h).start()
-            load(h).start()
-    for i in range(count, total):
-        kept, landed, arrived, load, to_sibling, to_opposite, rows = wide_parts(i)
-        h = 1 - y
-        load(h).wait()
-        to_sibling(h).wait_recv()
-        for e in range(ins[i].shape[0]):
-            add_blocks((kept, (h, e), None), [(kept, (h, e), None), (landed, (h, e), None)], rows)
-        to_opposite().start()
-
-    def add(i, d, final, sources):
-        target = (outs[i], (), None) if final else (held[i], (d,), None)
-        add_blocks(target, [(held[i], (d,), None)] + [(s[i], (d,), None) for s in sources], held[i].shape[1])
-
-    def ready(i, d):
-        own(i, d).wait()
-        cross(i, d).wait_recv()
-
-    for k in range(line - 1):
-        d = line - 1 - k
-
-        @pl.when(d > z)
-        def _():
-            for i in range(count):
-                ready(i, d)
-
-                @pl.when(z > 0)
-                def _():
-                    rise(i, d).wait_recv()
-                    add(i, d, False, [crossed, below])
-
-                @pl.when(z == 0)
-                def _():
-                    add(i, d, False, [crossed])
-
-                rise(i, d).start()
-
-        d = k
-
-        @pl.when(d < z)
-        def _():
-            for i in range(count):
-                ready(i, d)
-
-                @pl.when(z < line - 1)
-                def _():
-                    fall(i, d).wait_recv()
-                    add(i, d, False, [crossed, above])
-
-                @pl.when(z == line - 1)
-                def _():
-                    add(i, d, False, [crossed])
-
-                fall(i, d).start()
-
-    for i in range(count, total):
-        kept, landed, arrived, load, to_sibling, to_opposite, rows = wide_parts(i)
-        load(y).wait()
-        to_sibling(y).wait_recv()
-        to_opposite().wait_recv()
-        for e in range(ins[i].shape[0]):
-            add_blocks(
-                (outs[i], (e,), None), [(kept, (y, e), None), (landed, (y, e), None), (arrived, (e,), None)], rows
-            )
-    for d in range(line):
-
-        @pl.when(d == z)
-        def _():
-            for i in range(count):
-                ready(i, d)
-                if d < line - 1:
-                    fall(i, d).wait_recv()
-                if d > 0:
-                    rise(i, d).wait_recv()
-                add(i, d, True, [crossed] + ([below] if d > 0 else []) + ([above] if d < line - 1 else []))
-
-    for d in range(line):
-        for i in range(count):
-            cross(i, d).wait_send()
-            pl.when(d > z)(lambda: rise(i, d).wait_send())
-            pl.when(d < z)(lambda: fall(i, d).wait_send())
-    for i in range(count, total):
-        to_sibling, to_opposite = wide_parts(i)[4:6]
-        for h in range(2):
-            to_sibling(h).wait_send()
-        to_opposite().wait_send()
-
-
-def gather_sum(arrays, wide, group, number):
-    n, w, line = len(arrays), len(wide), group // 2
-    dma = pltpu.SemaphoreType.DMA
-    scratch = []
-    for a in arrays:
-        scratch += [pltpu.VMEM((line,) + a.shape[1:], a.dtype)] * 4
-    shapes = [jax.ShapeDtypeStruct(a.shape[1:], FLOAT) for a in arrays]
-    for a in wide:
-        part = (a.shape[0], a.shape[1] // 4, a.shape[2])
-        scratch += [pltpu.VMEM((2,) + part, a.dtype)] * 2 + [pltpu.VMEM(part, a.dtype)]
-        shapes.append(jax.ShapeDtypeStruct(part, FLOAT))
-    scratch += [dma((n, line))] * 7
-    if w:
-        scratch += [dma((w, 2))] * 3 + [dma((w,))] * 2
-    return pl.pallas_call(
-        functools.partial(gather_sum_kernel, n, w, group),
-        out_shape=shapes,
-        in_specs=[pl.BlockSpec(memory_space=pl.ANY)] * (n + w),
-        out_specs=[pl.BlockSpec(memory_space=pltpu.VMEM)] * (n + w),
-        scratch_shapes=scratch,
-        compiler_params=pltpu.CompilerParams(collective_id=number, has_side_effects=True, vmem_limit_bytes=52 * MIB),
-        name="gather_sum%d" % number,
-    )(*arrays, *wide)
-
-
-def head_kernel(group, cut, mix_ref, router_ref, shared_ref, mix_out, router_out, shared_out, own_sems, send_sems, recv_sems, swap_send, swap_recv):
+def head_kernel(group, cut, dense, *refs):
+    ins, outs = refs[: dense + 2], refs[dense + 2 : 2 * dense + 4]
+    own_sems, send_sems, recv_sems, swap_send, swap_recv, row_send, row_recv = refs[2 * dense + 4 :]
+    shared_ref, shared_out = ins[dense], outs[dense]
+    row_ref, row_out = ins[dense + 1], outs[dense + 1]
     line = group // 2
     y, c, z, x = places(group)
     sibling, opposite = {"dp": 2 * y + 1 - c}, {"dp": 2 * (1 - y) + c}
@@ -415,35 +310,33 @@
     me = 2 * z + x
     peers = [(None, {"expert": lax.rem(me + k, group)}) for k in range(1, group)]
     greet(peers + [(None, sibling), (None, opposite)])
-    width = mix_ref.shape[1]
-    pieces = [
-        (mix_ref, mix_out, pl.ds(0, cut)),
-        (mix_ref, mix_out, pl.ds(cut, width - cut)),
-        (router_ref, router_out, pl.ds(0, router_ref.shape[1])),
-    ]
-    first = (0, 2)
-    second = (1,)
+    width = ins[0].shape[1]
+    pieces = [(0, pl.ds(0, cut), True), (0, pl.ds(cut, width - cut), False)]
+    pieces += [(i, pl.ds(0, ins[i].shape[1]), True) for i in range(1, dense)]
+    count = len(pieces)
 
     def copy(p, yy, cc, zz, xx, way, device, own=False):
-        ref, out, columns = pieces[p]
+        i, columns, _ = pieces[p]
         place = (2 * yy + cc) * group + 2 * zz + xx
-        dst = out.at[place, :, columns]
-        src = ref.at[:, columns] if own else dst
+        dst = outs[i].at[place, :, columns]
+        src = ins[i].at[:, columns] if own else dst
         slot = yy * group + 2 * zz + xx
         return remote(src, dst, send_sems.at[p, slot, way], recv_sems.at[p, place], device)
+
+    def row_copy(zz, xx, way, device, own=False):
+        dst = row_out.at[2 * zz + xx]
+        return remote(row_ref if own else dst, dst, row_send.at[zz, way], row_recv.at[2 * zz + xx], device)
 
     def swap(k):
         to = lax.rem(me + k, group)
         return remote(shared_ref.at[to], shared_out.at[me], swap_send.at[k], swap_recv.at[me], {"expert": to})
 
-    def own_copy(i, ref, out):
-        return pltpu.make_async_copy(ref, out, own_sems.at[i])
-
-    owns = [
-        (mix_ref, mix_out.at[(2 * y + c) * group + me]),
-        (router_ref, router_out.at[(2 * y + c) * group + me]),
-        (shared_ref.at[me], shared_out.at[me]),
-    ]
+    def own_copy(i):
+        if i < dense:
+            return pltpu.make_async_copy(ins[i], outs[i].at[(2 * y + c) * group + me], own_sems.at[i])
+        if i == dense:
+            return pltpu.make_async_copy(shared_ref.at[me], shared_out.at[me], own_sems.at[i])
+        return pltpu.make_async_copy(row_ref, row_out.at[me], own_sems.at[i])
 
     def steps(act):
         for s in range(line):
@@ -457,55 +350,58 @@
 
     def column_moves(p, s, up, zz):
         own = s == 0
+        make = functools.partial(row_copy, zz, x) if p is None else functools.partial(copy, p, y, c, zz, x)
         moves = []
         if up:
-            moves.append((z < line - 1, functools.partial(copy, p, y, c, zz, x, 0, rising, own)))
+            moves.append((z < line - 1, functools.partial(make, 0, rising, own)))
         if not up or own:
-            moves.append((z > 0, functools.partial(copy, p, y, c, zz, x, 1, falling, own)))
-        moves.append((None, functools.partial(copy, p, y, c, zz, x, 2, across, own)))
-        moves.append((None, functools.partial(copy, p, y, c, zz, x, 3, opposite, own)))
-        moves.append((None, functools.partial(copy, p, y, c, zz, x, 4, sibling, own)))
+            moves.append((z > 0, functools.partial(make, 1, falling, own)))
+        moves.append((None, functools.partial(make, 2, across, own)))
+        if p is not None:
+            moves.append((None, functools.partial(make, 3, opposite, own)))
+            moves.append((None, functools.partial(make, 4, sibling, own)))
         return moves
 
-    def later_moves(p, zz):
-        if p in first:
+    def run(moves, act):
+        for condition, move in moves:
+            if condition is None:
+                act(move())
+            else:
+                pl.when(condition)(lambda: act(move()))
+
+    def later_moves(p):
+        if pieces[p][2]:
             return [
-                ((y, x, 0), [(3, opposite), (4, sibling)], (y, 1 - x)),
-                ((y, x, 1), [(4, sibling)], (1 - y, x)),
-                ((y, x, 1), [(4, sibling)], (1 - y, 1 - x)),
+                (0, [(3, opposite), (4, sibling)], (y, 1 - x)),
+                (1, [(4, sibling)], (1 - y, x)),
+                (1, [(4, sibling)], (1 - y, 1 - x)),
             ]
         return [
-            ((y, x, 0), [(2, across), (4, sibling)], (1 - y, x)),
-            ((y, x, 1), [(4, sibling)], (y, 1 - x)),
-            ((y, x, 1), [(4, sibling)], (1 - y, 1 - x)),
+            (0, [(2, across), (4, sibling)], (1 - y, x)),
+            (1, [(4, sibling)], (y, 1 - x)),
+            (1, [(4, sibling)], (1 - y, 1 - x)),
         ]
 
-    for p in range(3):
-        for condition, move in column_moves(p, 0, True, z):
-            if condition is None:
-                move().start()
-            else:
-                pl.when(condition)(lambda: move().start())
-    for k in range(1, group):
-        swap(k).start()
-    for i, (ref, out) in enumerate(owns):
-        own_copy(i, ref, out).start()
+    everything = list(range(count)) + [None]
 
     def column(s, up, zz):
+        for p in everything:
+            if s:
+                if p is None:
+                    row_copy(zz, x, 2, across).wait_recv()
+                else:
+                    copy(p, y, c, zz, x, 4, sibling).wait_recv()
+            run(column_moves(p, s, up, zz), lambda item: item.start())
         if s == 0:
-            return
-        for p in range(3):
-            copy(p, y, c, zz, x, 4, sibling).wait_recv()
-            for condition, move in column_moves(p, s, up, zz):
-                if condition is None:
-                    move().start()
-                else:
-                    pl.when(condition)(lambda: move().start())
+            for k in range(1, group):
+                swap(k).start()
+            for i in range(dense + 2):
+                own_copy(i).start()
 
     def later(phase, start):
         def act(s, up, zz):
-            for p in range(3):
-                for (_, _, when), sends, (yy, xx) in later_moves(p, zz):
+            for p in range(count):
+                for when, sends, (yy, xx) in later_moves(p):
                     if when != phase:
                         continue
                     if start:
@@ -519,26 +415,26 @@
 
         return act
 
-    steps(column)
-    steps(later(0, True))
-    steps(later(1, True))
-
     def finish(s, up, zz):
-        for p in range(3):
+        row_copy(zz, 1 - x, 2, across).wait_recv()
+        for p in range(count):
             for yy in range(2):
                 for xx in range(2):
                     copy(p, yy, 1 - c, zz, xx, 4, sibling).wait_recv()
 
+    def settle(s, up, zz):
+        for p in everything:
+            run(column_moves(p, s, up, zz), lambda item: item.wait_send())
+
+    only = lambda act, k: steps(lambda s, up, zz: act(s, up, zz) if s == k else None)
+    for k in range(line + 2):
+        if k < line:
+            only(column, k)
+        if 0 <= k - 1 < line:
+            only(later(0, True), k - 1)
+        if 0 <= k - 2 < line:
+            only(later(1, True), k - 2)
     steps(finish)
-
-    def settle(s, up, zz):
-        for p in range(3):
-            for condition, move in column_moves(p, s, up, zz):
-                if condition is None:
-                    move().wait_send()
-                else:
-                    pl.when(condition)(lambda: move().wait_send())
-
     steps(settle)
     steps(later(0, False))
     steps(later(1, False))
@@ -546,40 +442,58 @@
         source = lax.rem(me + k, group)
         remote(shared_ref.at[source], shared_out.at[source], swap_send.at[k], swap_recv.at[source], across).wait_recv()
         swap(k).wait_send()
-    for i, (ref, out) in enumerate(owns):
-        own_copy(i, ref, out).wait()
-
-
-def half_columns(width):
-    return width // 256 * 128
-
-
-def head_exchange(mix, routers, shared, number):
+    for i in range(dense + 2):
+        own_copy(i).wait()
+
+
+def head_exchange(dense, shared, rows, number):
     group = lax.axis_size("expert")
     total = 4 * group
+    count = len(dense) + 1
     dma = pltpu.SemaphoreType.DMA
     any_spec = pl.BlockSpec(memory_space=pl.ANY)
+    cut = dense[0].shape[1] * 9 // 10 // 128 * 128
     return pl.pallas_call(
-        functools.partial(head_kernel, group, half_columns(mix.shape[1])),
-        out_shape=[
-            jax.ShapeDtypeStruct((total,) + mix.shape, mix.dtype),
-            jax.ShapeDtypeStruct((total,) + routers.shape, routers.dtype),
+        functools.partial(head_kernel, group, cut, len(dense)),
+        out_shape=[jax.ShapeDtypeStruct((total,) + a.shape, a.dtype) for a in dense]
+        + [
             jax.ShapeDtypeStruct(shared.shape, shared.dtype),
+            jax.ShapeDtypeStruct((group,) + rows.shape, rows.dtype),
         ],
-        in_specs=[any_spec] * 3,
-        out_specs=[any_spec] * 3,
-        scratch_shapes=[dma((3,)), dma((3, 2 * group, 5)), dma((3, total)), dma((group,)), dma((group,))],
+        in_specs=[any_spec] * (len(dense) + 2),
+        out_specs=[any_spec] * (len(dense) + 2),
+        scratch_shapes=[
+            dma((len(dense) + 2,)),
+            dma((count, 2 * group, 5)),
+            dma((count, total)),
+            dma((group,)),
+            dma((group,)),
+            dma((group // 2, 3)),
+            dma((group,)),
+        ],
         compiler_params=pltpu.CompilerParams(collective_id=number, has_side_effects=True),
         name="head_exchange",
-    )(mix, routers, shared)
-
-
-def tail_kernel(group, cut, steps, *refs):
-    (mix_ref, router_ref, shared_ref, small_ref, mix_out, router_out, shared_out, small_out) = refs[:8]
-    bufs = refs[8:20]
-    totals, small_landed = refs[20:22]
+    )(*dense, shared, rows)
+
+
+def farthest(z, line, j):
+    table = [sorted(range(line), key=lambda d: (-abs(d - k), d)) for k in range(line)]
+    return sum(
+        jnp.where((z == k) & (j == n), table[k][n], 0) for k in range(line) for n in range(line) if table[k][n]
+    )
+
+
+def tail_kernel(group, sums, steps, *refs):
+    (left_ref, right_ref, router_ref, shared_ref, small_ref) = refs[:5]
+    sum_ins, refs = refs[5 : 5 + sums], refs[5 + sums :]
+    (mix_out, router_out, shared_out, small_out) = refs[:4]
+    sum_outs, refs = refs[4 : 4 + sums], refs[4 + sums :]
+    bufs = refs[:12]
+    made, totals, small_landed = refs[12:15]
+    sum_bufs, refs = refs[15 : 15 + 3 * sums], refs[15 + 3 * sums :]
+    sum_own, sum_core_send, sum_core_recv, sum_side_send, sum_side_recv, sum_store, late_send, late_recv = refs[-8:]
     (own_sems, core_send, core_recv, one_send, one_recv, two_send, two_recv, line_send, line_recv,
-     swap_send, swap_recv, small_send, small_recv, keep_sem) = refs[22:]
+     swap_send, swap_recv, small_send, small_recv, keep_sem) = refs[:-8]
     line = group // 2
     y, c, z, x = places(group)
     sibling, opposite = {"dp": 2 * y + 1 - c}, {"dp": 2 * (1 - y) + c}
@@ -593,24 +507,38 @@
     peers = [(None, {"expert": lax.rem(me + k, group)}) for k in range(1, group)]
     greet(peers + [(None, sibling), (None, opposite)])
 
-    ins, outs = (mix_ref, router_ref), (mix_out, router_out)
+    outs = (mix_out, router_out)
     held, landed, one, two, below, above = (bufs[0:2], bufs[2:4], bufs[4:6], bufs[6:8], bufs[8:10], bufs[10:12])
-    rows = mix_ref.shape[1]
-    width = mix_ref.shape[2]
-    pieces = [(0, pl.ds(0, cut), True), (0, pl.ds(cut, width - cut), False), (1, pl.ds(0, router_ref.shape[2]), True)]
+    rows, width = mix_out.shape
+    pieces = [(0, pl.ds(0, width), False), (1, pl.ds(0, router_ref.shape[2]), True)]
+    count = len(pieces)
 
     def slot(yy, zz, xx):
         return yy * group + 2 * zz + xx
 
-    def load(a, yy, zz, xx):
+    def load(yy, zz, xx):
         s = slot(yy, zz, xx)
-        return pltpu.make_async_copy(ins[a].at[(2 * yy + c) * group + 2 * zz + xx], held[a].at[s], own_sems.at[a, s])
-
-    def to_sibling(a, yy, zz, xx):
+        return pltpu.make_async_copy(router_ref.at[(2 * yy + c) * group + 2 * zz + xx], held[1].at[s], own_sems.at[s])
+
+    def to_sibling(a, yy, zz, xx, turn=0):
         s = slot(yy, zz, xx)
-        return remote(
-            ins[a].at[(2 * yy + 1 - c) * group + 2 * zz + xx], landed[a].at[s], core_send.at[a, s], core_recv.at[a, s], sibling
-        )
+        source = made.at[4 * turn + 2 * yy + xx] if a == 0 else router_ref.at[(2 * yy + 1 - c) * group + 2 * zz + xx]
+        return remote(source, landed[a].at[s], core_send.at[a, s], core_recv.at[a, s], sibling)
+
+    def make(cc, zz, target, place_of):
+        lefts = []
+        for yy in range(2):
+            start = pl.multiple_of(((2 * yy + cc) * group + 2 * zz) * rows, 16)
+            lefts.append(left_ref[pl.ds(start, 2 * rows)])
+        lefts = jnp.concatenate(lefts, axis=0)
+        step = 1664
+        for start in range(0, width, step):
+            columns = slice(start, min(start + step, width))
+            product = jnp.dot(lefts, right_ref[:, columns], preferred_element_type=FLOAT).astype(BRAIN)
+            for yy in range(2):
+                for xx in range(2):
+                    place = (2 * yy + xx) * rows
+                    target[place_of(yy, xx), :, columns] = product[place : place + rows]
 
     def stage_one(p, zz, k):
         a, columns, over_y = pieces[p]
@@ -634,11 +562,6 @@
     def fall(a, zz):
         return remote(held[a].at[slot(y, zz, x)], above[a].at[zz], line_send.at[a, 1, zz], line_recv.at[a, 1, zz], falling)
 
-    table = [sorted(range(line), key=lambda d: (-abs(d - k), d)) for k in range(line)]
-
-    def target(j):
-        return sum(jnp.where(z == k, table[k][j], 0) for k in range(line))
-
     def swap(k):
         to = lax.rem(me + k, group)
         return remote(shared_ref.at[to], shared_out.at[me], swap_send.at[k], swap_recv.at[me], {"expert": to})
@@ -652,11 +575,10 @@
     keep = pltpu.make_async_copy(shared_ref.at[me], shared_out.at[me], keep_sem)
     keep.start()
     corners = [(yy, xx) for yy in range(2) for xx in range(2)]
-    for j in range(line):
-        for a in range(2):
-            for yy, xx in corners:
-                to_sibling(a, yy, target(j), xx).start()
-                load(a, yy, target(j), xx).start()
+    for zz in range(line):
+        for yy, xx in corners:
+            to_sibling(1, yy, zz, xx).start()
+            load(yy, zz, xx).start()
     for k in range(1, group):
         swap(k).start()
     totals[0] = small_ref[...]
@@ -669,14 +591,100 @@
             if step + 1 < len(steps):
                 small(step + 1).start()
 
+    def phase_make(zz, t):
+        turn = lax.rem(t, 2)
+
+        @pl.when(t >= 2)
+        def _():
+            for yy, xx in corners:
+                to_sibling(0, yy, farthest(z, line, t - 2), xx, turn).wait_send()
+
+        make(1 - c, zz, made, lambda yy, xx: 4 * turn + 2 * yy + xx)
+        for yy, xx in corners:
+            to_sibling(0, yy, zz, xx, turn).start()
+        make(c, zz, held[0], lambda yy, xx: slot(yy, zz, xx))
+
+    def sum_parts(k):
+        kept, landed, arrived = sum_bufs[3 * k : 3 * k + 3]
+        source = sum_ins[k]
+        height = source.shape[1] // 4
+
+        def piece(q):
+            return source.at[:, pl.ds(pl.multiple_of(q * height, height), height), :]
+
+        def take(h):
+            return pltpu.make_async_copy(piece(2 * h + c), kept.at[h], sum_own.at[k, h])
+
+        def give(h):
+            return remote(piece(2 * h + 1 - c), landed.at[h], sum_core_send.at[k, h], sum_core_recv.at[k, h], sibling)
+
+        def pass_on():
+            return remote(kept.at[1 - y], arrived, sum_side_send.at[k], sum_side_recv.at[k], opposite)
+
+        def add(h, extra):
+            for e in range(source.shape[0]):
+                items = [(kept, (h, e), None), (landed, (h, e), None)] + ([(arrived, (e,), None)] if extra else [])
+                add_blocks((kept, (h, e), None), items, height)
+
+        def store():
+            return pltpu.make_async_copy(kept.at[y], sum_outs[k], sum_store.at[k])
+
+        return take, give, pass_on, add, store
+
+    def sums_first():
+        for k in range(sums):
+            take, give, pass_on, add, store = sum_parts(k)
+            take(1 - y).wait()
+            give(1 - y).wait_recv()
+            add(1 - y, False)
+            pass_on().start()
+
+    def late(k):
+        to = lax.rem(me + k, group)
+        height = sum_outs[0].shape[1]
+        block = sum_bufs[0].at[y, 0, pl.ds(pl.multiple_of(to * height, 16), height)]
+        if k == 0:
+            return pltpu.make_async_copy(block, sum_outs[0].at[me], late_send.at[k])
+        return remote(block, sum_outs[0].at[me], late_send.at[k], late_recv.at[me], {"expert": to})
+
+    def sums_last(which):
+        for k in which:
+            take, give, pass_on, add, store = sum_parts(k)
+            take(y).wait()
+            give(y).wait_recv()
+            pass_on().wait_recv()
+            add(y, True)
+            if k:
+                store().start()
+            else:
+                for n in range(group):
+                    late(n).start()
+
+    def sums_settle():
+        for k in range(sums):
+            take, give, pass_on, add, store = sum_parts(k)
+            give(y).wait_send()
+            give(1 - y).wait_send()
+            pass_on().wait_send()
+            if k:
+                store().wait()
+        late(0).wait()
+        for n in range(1, group):
+            source = lax.rem(me + n, group)
+            remote(
+                shared_ref.at[source], sum_outs[0].at[source], late_send.at[n], late_recv.at[source], across
+            ).wait_recv()
+            late(n).wait_send()
+
     def phase_a(zz):
         for a in range(2):
             for yy, xx in corners:
                 s = slot(yy, zz, xx)
-                load(a, yy, zz, xx).wait()
+                if a == 1:
+                    load(yy, zz, xx).wait()
                 to_sibling(a, yy, zz, xx).wait_recv()
                 add_blocks((held[a], (s,), None), [(held[a], (s,), None), (landed[a], (s,), None)], rows)
-        for p in range(3):
+        for p in range(count):
             for k in range(2):
                 stage_one(p, zz, k).start()
 
@@ -692,7 +700,7 @@
 
     def phase_c(zz):
         s = slot(y, zz, x)
-        for p in range(3):
+        for p in range(count):
             stage_two(p, zz).wait_recv()
         for a in range(2):
             base = [(held[a], (s,), None), (two[a], (zz,), None)]
@@ -728,7 +736,7 @@
 
     def phase_last():
         s = slot(y, z, x)
-        for p in range(3):
+        for p in range(count):
             stage_two(p, z).wait_recv()
         for a in range(2):
             base = [(held[a], (s,), None), (two[a], (z,), None)]
@@ -752,18 +760,32 @@
                 rise(a, z).wait_recv()
                 add_blocks(final, base + [low, high], rows)
 
-    for t in range(line + 2):
-        if t < line:
-            phase_a(target(t))
-        if 0 <= t - 1 < line:
-            phase_b(target(t - 1))
-        if 0 <= t - 2 < line - 1:
-            phase_c(target(t - 2))
-        if t - 2 == line - 1:
-            phase_last()
-        advance(t)
-    for step in range(line + 2, len(steps)):
-        advance(step)
+    for k in range(sums):
+        take, give = sum_parts(k)[:2]
+        for h in (1 - y, y):
+            take(h).start()
+            give(h).start()
+
+    def body(t, carry):
+        for shift, phase, number in ((0, phase_make, line), (1, phase_a, line), (2, phase_b, line), (3, phase_c, line - 1)):
+
+            @pl.when((t >= shift) & (t - shift < number))
+            def _():
+                phase(farthest(z, line, t - shift), *([t] if shift == 0 else []))
+
+        pl.when(t == 0)(sums_first)
+        pl.when(t == 4)(lambda: sums_last([0]))
+        for step in range(len(steps)):
+            pl.when(t == step + 1)(functools.partial(advance, step))
+        return carry
+
+    lax.fori_loop(0, max(line + 3, len(steps) + 1), body, 0)
+    phase_last()
+    sums_last(range(1, sums))
+    sums_settle()
+    for t in (line - 2, line - 1):
+        for yy, xx in corners:
+            to_sibling(0, yy, farthest(z, line, t), xx, t % 2).wait_send()
     small_out[...] = totals[len(steps)]
     for k in range(1, group):
         source = lax.rem(me + k, group)
@@ -772,17 +794,18 @@
     keep.wait()
     for zz in range(line):
         for a in range(2):
-            for yy, xx in corners:
-                to_sibling(a, yy, zz, xx).wait_send()
+            if a == 1:
+                for yy, xx in corners:
+                    to_sibling(a, yy, zz, xx).wait_send()
             pl.when(zz > z)(lambda: rise(a, zz).wait_send())
             pl.when(zz < z)(lambda: fall(a, zz).wait_send())
-        for p in range(3):
+        for p in range(count):
             for k in range(2):
                 stage_one(p, zz, k).wait_send()
             stage_two(p, zz).wait_send()
 
 
-def tail_exchange(mix, routers, shared, small, number):
+def tail_exchange(left, right, routers, shared, small, sums, number):
     group = lax.axis_size("expert")
     line = group // 2
     steps = []
@@ -794,26 +817,35 @@
     dma = pltpu.SemaphoreType.DMA
     vmem = pl.BlockSpec(memory_space=pltpu.VMEM)
     any_spec = pl.BlockSpec(memory_space=pl.ANY)
+    mix = (left.shape[0] // (4 * group), right.shape[1])
     scratch = []
     for blocks in (2 * group, 2 * group, group, line, line, line):
-        scratch += [pltpu.VMEM((blocks,) + a.shape[1:], a.dtype) for a in (mix, routers)]
+        scratch += [pltpu.VMEM((blocks,) + shape, BRAIN) for shape in (mix, routers.shape[1:])]
+    scratch += [pltpu.VMEM((8,) + mix, BRAIN)]
     scratch += [pltpu.VMEM((len(steps) + 1,) + small.shape, FLOAT), pltpu.VMEM((len(steps),) + small.shape, FLOAT)]
-    scratch += [dma((2, 2 * group))] * 3 + [dma((3, group))] * 2 + [dma((3, line))] * 2 + [dma((2, 2, line))] * 2
+    parts = [(a.shape[0], a.shape[1] // 4, a.shape[2]) for a in sums]
+    for part in parts:
+        scratch += [pltpu.VMEM((2,) + part, BRAIN)] * 2 + [pltpu.VMEM(part, BRAIN)]
+    scratch += [dma((2 * group,))] + [dma((2, 2 * group))] * 2
+    scratch += [dma((2, group))] * 2 + [dma((2, line))] * 2 + [dma((2, 2, line))] * 2
     scratch += [dma((group,))] * 2 + [dma((len(steps),))] * 2 + [dma]
+    scratch += [dma((len(sums), 2))] * 3 + [dma((len(sums),))] * 3 + [dma((group,))] * 2
     return pl.pallas_call(
-        functools.partial(tail_kernel, group, half_columns(mix.shape[2]), steps),
+        functools.partial(tail_kernel, group, len(sums), steps),
         out_shape=[
-            jax.ShapeDtypeStruct(mix.shape[1:], FLOAT),
+            jax.ShapeDtypeStruct(mix, FLOAT),
             jax.ShapeDtypeStruct(routers.shape[1:], FLOAT),
             jax.ShapeDtypeStruct(shared.shape, shared.dtype),
             jax.ShapeDtypeStruct(small.shape, FLOAT),
-        ],
-        in_specs=[any_spec, any_spec, any_spec, vmem],
-        out_specs=[vmem, vmem, any_spec, vmem],
+        ]
+        + [jax.ShapeDtypeStruct(shared.shape, BRAIN)]
+        + [jax.ShapeDtypeStruct(part, BRAIN) for part in parts[1:]],
+        in_specs=[vmem, vmem, any_spec, any_spec, vmem] + [any_spec] * len(sums),
+        out_specs=[vmem, vmem, any_spec, vmem] + [any_spec] * len(sums),
         scratch_shapes=scratch,
-        compiler_params=pltpu.CompilerParams(collective_id=number, has_side_effects=True, vmem_limit_bytes=56 * MIB),
+        compiler_params=pltpu.CompilerParams(collective_id=number, has_side_effects=True, vmem_limit_bytes=62 * MIB),
         name="tail_exchange",
-    )(mix, routers, shared, small)
+    )(left, right, routers, shared, small, *sums)
 
 
 def state_setup(step_ref, rate_ref, step_t_ref, rate_t_ref, b_ref, c_ref, cum, cum_t, cross):
@@ -1037,12 +1069,168 @@
     grad_conv_in, grad_conv_weight, grad_conv_bias = conv_back(jnp.concatenate([dx, db, dc], axis=1))
     grad_step_raw, grad_step_bias = step_back(grad_step)
     grad_proj = jnp.concatenate([grad_gate, grad_conv_in, grad_step_raw], axis=1).astype(BRAIN)
-    grad_mixer_in = matmul_tn(normed_low, grad_proj).astype(BRAIN)
     grad_hidden, grad_gain = norm_back(matmul_nt(grad_proj, mixer_in))
     grad_small = (
         grad_mixer_gain, grad_conv_weight, grad_conv_bias, grad_decay_log, grad_step_bias, grad_skip
     )
-    return grad_out + grad_hidden, grad_gain, grad_mixer_in, grad_mixer_out, grad_small
+    return grad_out + grad_hidden, grad_gain, normed_low, grad_proj, grad_mixer_out, grad_small
+
+
+PARTS = 2
+
+
+def fold(group, held, sent, crossed, below, above, out_ref, sems):
+    cross_send, cross_recv, up_send, up_recv, down_send, down_recv = sems
+    line = group // 2
+    z, x = places(group)[2:]
+    rows = held.shape[1] // PARTS
+
+    def piece(ref, d, p):
+        return ref.at[d, pl.ds(p * rows, rows)]
+
+    def cross(d, p):
+        return remote(
+            piece(sent, d, p), piece(crossed, d, p), cross_send.at[d, p], cross_recv.at[d, p], {"expert": 2 * z + 1 - x}
+        )
+
+    def rise(d, p):
+        return remote(
+            piece(held, d, p), piece(below, d, p), up_send.at[d, p], up_recv.at[d, p], {"expert": 2 * (z + 1) + x}
+        )
+
+    def fall(d, p):
+        return remote(
+            piece(held, d, p), piece(above, d, p), down_send.at[d, p], down_recv.at[d, p], {"expert": 2 * (z - 1) + x}
+        )
+
+    def add(d, p, final, sources):
+        def body(j, carry):
+            at = pl.ds(pl.multiple_of(p * rows + j * 16, 16), 16)
+            total = held[d, at].astype(FLOAT)
+            for source in sources:
+                total = total + source[d, at].astype(FLOAT)
+            if final:
+                out_ref[at] = total
+            else:
+                held[d, at] = total.astype(held.dtype)
+            return carry
+
+        lax.fori_loop(0, rows // 16, body, 0)
+
+    def start_cross(d):
+        for p in range(PARTS):
+            cross(d, p).start()
+
+    def chain(d):
+        for p in range(PARTS):
+            cross(d, p).wait_recv()
+
+            @pl.when(d > z)
+            def _():
+                @pl.when(z > 0)
+                def _():
+                    rise(d, p).wait_recv()
+                    add(d, p, False, [crossed, below])
+
+                @pl.when(z == 0)
+                def _():
+                    add(d, p, False, [crossed])
+
+                rise(d, p).start()
+
+            @pl.when(d < z)
+            def _():
+                @pl.when(z < line - 1)
+                def _():
+                    fall(d, p).wait_recv()
+                    add(d, p, False, [crossed, above])
+
+                @pl.when(z == line - 1)
+                def _():
+                    add(d, p, False, [crossed])
+
+                fall(d, p).start()
+
+    def last():
+        for p in range(PARTS):
+            cross(z, p).wait_recv()
+
+            @pl.when(z == 0)
+            def _():
+                fall(z, p).wait_recv()
+                add(z, p, True, [crossed, above])
+
+            @pl.when(z == line - 1)
+            def _():
+                rise(z, p).wait_recv()
+                add(z, p, True, [crossed, below])
+
+            @pl.when((z > 0) & (z < line - 1))
+            def _():
+                fall(z, p).wait_recv()
+                rise(z, p).wait_recv()
+                add(z, p, True, [crossed, below, above])
+
+    def settle():
+        for d in range(line):
+            for p in range(PARTS):
+                cross(d, p).wait_send()
+                pl.when(d > z)(lambda: rise(d, p).wait_send())
+                pl.when(d < z)(lambda: fall(d, p).wait_send())
+
+    return start_cross, chain, last, settle
+
+
+def fold_scratch(group, tokens, width):
+    line = group // 2
+    dma = pltpu.SemaphoreType.DMA
+    return [pltpu.VMEM((line, tokens, width), BRAIN)] * 5 + [dma((line, PARTS))] * 6
+
+
+def run_blocks(group, compute, held, sent, start_cross, chain, last):
+    line = group // 2
+    z, x = places(group)[2:]
+
+    def body(j, carry):
+        d = farthest(z, line, j // 2)
+        crossing = lax.rem(j, 2) == 0
+
+        @pl.when(j == group - 2)
+        def _():
+            chain(farthest(z, line, 0))
+
+        total = compute(2 * d + jnp.where(crossing, 1 - x, x)).astype(BRAIN)
+
+        @pl.when(crossing)
+        def _():
+            sent[d] = total
+            start_cross(d)
+
+        @pl.when(jnp.logical_not(crossing))
+        def _():
+            held[d] = total
+
+        return carry
+
+    lax.fori_loop(0, group, body, 0)
+    for j in range(1, line - 1):
+        chain(farthest(z, line, j))
+    last()
+
+
+def load_blocks(group, source, target, sems):
+    z, x = places(group)[2:]
+
+    def load(s):
+        return pltpu.make_async_copy(source.at[s], target.at[s], sems.at[s])
+
+    def body(j, carry):
+        d = farthest(z, group // 2, j // 2)
+        load(2 * d + jnp.where(lax.rem(j, 2) == 0, 1 - x, x)).start()
+        return carry
+
+    lax.fori_loop(0, group, body, 0)
+    return lambda s: load(s).wait()
 
 
 def pick_rows(gates):
@@ -1058,59 +1246,60 @@
     return (ranks == place) & (live > 0.0)
 
 
-def expert_forward_kernel(x_ref, g_ref, in_ref, out_ref, sin_ref, sout_ref, y_ref, xe_ref, gu_ref, sgu_ref):
-    rows = x_ref[0]
-    shared_gu = jnp.dot(rows, sin_ref[...], preferred_element_type=FLOAT)
-    half = shared_gu.shape[1] // 2
-    shared_mid = (silu_of(shared_gu[:, :half]) * shared_gu[:, half:]).astype(BRAIN)
-    sgu_ref[0] = shared_gu.astype(sgu_ref.dtype)
-    total = matmul_nt(shared_mid, sout_ref[...])
-    for e in range(in_ref.shape[0]):
-        gates = g_ref[0, e : e + 1, :]
-        hit = pick_rows(gates)
-        picked = jnp.dot(
-            jnp.where(hit, 1.0, 0.0).astype(BRAIN), rows, preferred_element_type=FLOAT
-        ).astype(BRAIN)
-        gate_up = jnp.dot(picked, in_ref[e], preferred_element_type=FLOAT)
-        width = gate_up.shape[1] // 2
-        inner = (silu_of(gate_up[:, :width]) * gate_up[:, width:]).astype(BRAIN)
-        result = matmul_nt(inner, out_ref[e]).astype(BRAIN)
-        total = total + matmul_tn(jnp.where(hit, gates, 0.0).astype(BRAIN), result)
-        xe_ref[e, 0] = picked
-        gu_ref[e, 0] = gate_up.astype(gu_ref.dtype)
-    y_ref[0] = total.astype(y_ref.dtype)
-
-
-def expert_forward(rows, gates, expert_in, expert_out, shared_in, shared_out):
+def expert_forward_kernel(
+    group, x_hbm, g_ref, in_ref, out_ref, sin_ref, sout_ref, y_ref, xe_ref, gu_ref, sgu_ref,
+    rows_ref, held, sent, crossed, below, above, *sems,
+):
+    z, x = places(group)[2:]
+    wait_load = load_blocks(group, x_hbm, rows_ref, sems[6])
+    greet(line_peers(z, x, group // 2))
+    start_cross, chain, last, settle = fold(group, held, sent, crossed, below, above, y_ref, sems[:6])
+
+    def compute(s):
+        wait_load(s)
+        rows = rows_ref[s]
+        shared_gu = jnp.dot(rows, sin_ref[...], preferred_element_type=FLOAT)
+        half = shared_gu.shape[1] // 2
+        shared_mid = (silu_of(shared_gu[:, :half]) * shared_gu[:, half:]).astype(BRAIN)
+        sgu_ref[s] = shared_gu.astype(sgu_ref.dtype)
+        total = matmul_nt(shared_mid, sout_ref[...])
+        for e in range(in_ref.shape[0]):
+            gates = g_ref[s, e : e + 1, :]
+            hit = pick_rows(gates)
+            picked = jnp.dot(
+                jnp.where(hit, 1.0, 0.0).astype(BRAIN), rows, preferred_element_type=FLOAT
+            ).astype(BRAIN)
+            gate_up = jnp.dot(picked, in_ref[e], preferred_element_type=FLOAT)
+            width = gate_up.shape[1] // 2
+            inner = (silu_of(gate_up[:, :width]) * gate_up[:, width:]).astype(BRAIN)
+            result = matmul_nt(inner, out_ref[e]).astype(BRAIN)
+            total = total + matmul_tn(jnp.where(hit, gates, 0.0).astype(BRAIN), result)
+            xe_ref[e, s] = picked
+            gu_ref[e, s] = gate_up.astype(gu_ref.dtype)
+        return total
+
+    run_blocks(group, compute, held, sent, start_cross, chain, last)
+    settle()
+
+
+def expert_forward(rows, gates, expert_in, expert_out, shared_in, shared_out, number):
     group, tokens, width = rows.shape
     local = expert_in.shape[0]
     inner = expert_in.shape[2]
-    by_slot = lambda *shape: pl.BlockSpec((1,) + shape, lambda s: (s,) + (0,) * len(shape))
-    by_pair = lambda *shape: pl.BlockSpec((local, 1) + shape, lambda s: (0, s) + (0,) * len(shape))
+    vmem = pl.BlockSpec(memory_space=pltpu.VMEM)
+    dma = pltpu.SemaphoreType.DMA
     return pl.pallas_call(
-        expert_forward_kernel,
-        grid=(group,),
+        functools.partial(expert_forward_kernel, group),
         out_shape=[
-            jax.ShapeDtypeStruct(rows.shape, BRAIN),
+            jax.ShapeDtypeStruct((tokens, width), FLOAT),
             jax.ShapeDtypeStruct((local, group, PICKED, width), BRAIN),
             jax.ShapeDtypeStruct((local, group, PICKED, inner), BRAIN),
             jax.ShapeDtypeStruct((group, tokens, shared_in.shape[1]), BRAIN),
         ],
-        in_specs=[
-            by_slot(tokens, width),
-            by_slot(local, tokens),
-            whole_spec(expert_in.shape),
-            whole_spec(expert_out.shape),
-            whole_spec(shared_in.shape),
-            whole_spec(shared_out.shape),
-        ],
-        out_specs=[
-            by_slot(tokens, width),
-            by_pair(PICKED, width),
-            by_pair(PICKED, inner),
-            by_slot(tokens, shared_in.shape[1]),
-        ],
-        compiler_params=pltpu.CompilerParams(vmem_limit_bytes=52 * MIB),
+        in_specs=[pl.BlockSpec(memory_space=pl.ANY)] + [vmem] * 5,
+        out_specs=[vmem] * 4,
+        scratch_shapes=[pltpu.VMEM(rows.shape, BRAIN)] + fold_scratch(group, tokens, width) + [dma((group,))],
+        compiler_params=pltpu.CompilerParams(collective_id=number, has_side_effects=True, vmem_limit_bytes=60 * MIB),
         name="expert_forward",
     )(rows, gates, expert_in, expert_out, shared_in, shared_out)
 
@@ -1122,51 +1311,72 @@
 
 
 def expert_backward_kernel(
-    d_ref, g_ref, gu_ref, sgu_ref, in_ref, out_ref, sin_ref, sout_ref,
+    group, d_hbm, g_ref, gu_ref, sgu_ref, in_ref, out_ref, sin_ref, sout_ref,
     dx_ref, dg_ref, dgu_ref, dres_ref, mid_ref, dsgu_ref, smid_ref,
+    rows_ref, dgates, held, sent, crossed, below, above, *sems,
 ):
-    grads = d_ref[0]
-    shared_gu = sgu_ref[0].astype(FLOAT)
-    half = shared_gu.shape[1] // 2
-    dmid = jnp.dot(grads, sout_ref[...], preferred_element_type=FLOAT)
-    dgate, dup, shared_mid = swiglu_back(shared_gu[:, :half], shared_gu[:, half:], dmid)
-    shared_d = jnp.concatenate([dgate, dup], axis=1).astype(BRAIN)
-    dsgu_ref[0] = shared_d
-    smid_ref[0] = shared_mid.astype(BRAIN)
-    total = matmul_nt(shared_d, sin_ref[...])
-    for e in range(in_ref.shape[0]):
-        gates = g_ref[0, e : e + 1, :]
-        hit = pick_rows(gates)
-        chosen = jnp.where(hit, 1.0, 0.0).astype(BRAIN)
-        weight = jnp.sum(jnp.where(hit, gates, 0.0), axis=1, keepdims=True)
-        picked = jnp.dot(chosen, grads, preferred_element_type=FLOAT)
-        dres_ref[e, 0] = (picked * weight).astype(BRAIN)
-        raw = jnp.dot(picked.astype(BRAIN), out_ref[e], preferred_element_type=FLOAT)
-        gate_up = gu_ref[e, 0].astype(FLOAT)
-        width = gate_up.shape[1] // 2
-        dgate, dup, inner = swiglu_back(gate_up[:, :width], gate_up[:, width:], raw * weight)
-        inner_low = inner.astype(BRAIN)
-        mid_ref[e, 0] = inner_low
-        dweight = jnp.sum(raw * inner_low.astype(FLOAT), axis=1, keepdims=True)
-        dg_ref[0, e : e + 1, :] = jnp.sum(jnp.where(hit, dweight, 0.0), axis=0, keepdims=True)
-        dgu = jnp.concatenate([dgate, dup], axis=1).astype(BRAIN)
-        dgu_ref[e, 0] = dgu
-        back = matmul_nt(dgu, in_ref[e]).astype(BRAIN)
-        total = total + matmul_tn(chosen, back)
-    dx_ref[0] = total.astype(dx_ref.dtype)
-
-
-def expert_backward(grads, gates, gate_up, shared_gu, expert_in, expert_out, shared_in, shared_out):
+    z, x = places(group)[2:]
+    me = 2 * z + x
+    gate_send, gate_recv = sems[7:9]
+    wait_load = load_blocks(group, d_hbm, rows_ref, sems[6])
+    greet([(None, {"expert": lax.rem(me + k, group)}) for k in range(1, group)])
+    start_cross, chain, last, settle = fold(group, held, sent, crossed, below, above, dx_ref, sems[:6])
+
+    def give(s):
+        return remote(dgates.at[s], dg_ref.at[me], gate_send.at[s], gate_recv.at[me], {"expert": s})
+
+    def compute(s):
+        wait_load(s)
+        grads = rows_ref[s]
+        shared_gu = sgu_ref[s].astype(FLOAT)
+        half = shared_gu.shape[1] // 2
+        dmid = jnp.dot(grads, sout_ref[...], preferred_element_type=FLOAT)
+        dgate, dup, shared_mid = swiglu_back(shared_gu[:, :half], shared_gu[:, half:], dmid)
+        shared_d = jnp.concatenate([dgate, dup], axis=1).astype(BRAIN)
+        dsgu_ref[s] = shared_d
+        smid_ref[s] = shared_mid.astype(BRAIN)
+        total = matmul_nt(shared_d, sin_ref[...])
+        for e in range(in_ref.shape[0]):
+            gates = g_ref[s, e : e + 1, :]
+            hit = pick_rows(gates)
+            chosen = jnp.where(hit, 1.0, 0.0).astype(BRAIN)
+            weight = jnp.sum(jnp.where(hit, gates, 0.0), axis=1, keepdims=True)
+            picked = jnp.dot(chosen, grads, preferred_element_type=FLOAT)
+            dres_ref[e, s] = (picked * weight).astype(BRAIN)
+            raw = jnp.dot(picked.astype(BRAIN), out_ref[e], preferred_element_type=FLOAT)
+            gate_up = gu_ref[e, s].astype(FLOAT)
+            width = gate_up.shape[1] // 2
+            dgate, dup, inner = swiglu_back(gate_up[:, :width], gate_up[:, width:], raw * weight)
+            inner_low = inner.astype(BRAIN)
+            mid_ref[e, s] = inner_low
+            dweight = jnp.sum(raw * inner_low.astype(FLOAT), axis=1, keepdims=True)
+            dgates[s, e : e + 1, :] = jnp.sum(jnp.where(hit, dweight, 0.0), axis=0, keepdims=True)
+            dgu = jnp.concatenate([dgate, dup], axis=1).astype(BRAIN)
+            dgu_ref[e, s] = dgu
+            back = matmul_nt(dgu, in_ref[e]).astype(BRAIN)
+            total = total + matmul_tn(chosen, back)
+        pl.when(s != me)(lambda: give(s).start())
+        return total
+
+    run_blocks(group, compute, held, sent, start_cross, chain, last)
+    dg_ref[me] = dgates[me]
+    for k in range(1, group):
+        source = lax.rem(me + k, group)
+        remote(dgates.at[source], dg_ref.at[source], gate_send.at[source], gate_recv.at[source], {"expert": source}).wait_recv()
+        give(source).wait_send()
+    settle()
+
+
+def expert_backward(grads, gates, gate_up, shared_gu, expert_in, expert_out, shared_in, shared_out, number):
     group, tokens, width = grads.shape
     local = expert_in.shape[0]
     inner = expert_in.shape[2]
-    by_slot = lambda *shape: pl.BlockSpec((1,) + shape, lambda s: (s,) + (0,) * len(shape))
-    by_pair = lambda *shape: pl.BlockSpec((local, 1) + shape, lambda s: (0, s) + (0,) * len(shape))
+    vmem = pl.BlockSpec(memory_space=pltpu.VMEM)
+    dma = pltpu.SemaphoreType.DMA
     return pl.pallas_call(
-        expert_backward_kernel,
-        grid=(group,),
+        functools.partial(expert_backward_kernel, group),
         out_shape=[
-            jax.ShapeDtypeStruct(grads.shape, BRAIN),
+            jax.ShapeDtypeStruct((tokens, width), FLOAT),
             jax.ShapeDtypeStruct((group, local, tokens), FLOAT),
             jax.ShapeDtypeStruct((local, group, PICKED, inner), BRAIN),
             jax.ShapeDtypeStruct((local, group, PICKED, width), BRAIN),
@@ -1174,26 +1384,12 @@
             jax.ShapeDtypeStruct(shared_gu.shape, BRAIN),
             jax.ShapeDtypeStruct(shared_gu.shape[:2] + (shared_gu.shape[2] // 2,), BRAIN),
         ],
-        in_specs=[
-            by_slot(tokens, width),
-            by_slot(local, tokens),
-            by_pair(PICKED, inner),
-            by_slot(tokens, shared_gu.shape[2]),
-            whole_spec(expert_in.shape),
-            whole_spec(expert_out.shape),
-            whole_spec(shared_in.shape),
-            whole_spec(shared_out.shape),
-        ],
-        out_specs=[
-            by_slot(tokens, width),
-            by_slot(local, tokens),
-            by_pair(PICKED, inner),
-            by_pair(PICKED, width),
-            by_pair(PICKED, inner // 2),
-            by_slot(tokens, shared_gu.shape[2]),
-            by_slot(tokens, shared_gu.shape[2] // 2),
-        ],
-        compiler_params=pltpu.CompilerParams(vmem_limit_bytes=52 * MIB),
+        in_specs=[pl.BlockSpec(memory_space=pl.ANY)] + [vmem] * 7,
+        out_specs=[vmem] * 7,
+        scratch_shapes=[pltpu.VMEM(grads.shape, BRAIN), pltpu.VMEM((group, local, tokens), FLOAT)]
+        + fold_scratch(group, tokens, width)
+        + [dma((group,))] * 3,
+        compiler_params=pltpu.CompilerParams(collective_id=number, has_side_effects=True, vmem_limit_bytes=62 * MIB),
         name="expert_backward",
     )(grads, gates, gate_up, shared_gu, expert_in, expert_out, shared_in, shared_out)
 
@@ -1210,32 +1406,30 @@
     probs = raised / jnp.sum(raised, axis=1, keepdims=True)
     gates = probs * valid[:, None]
     if lax.axis_size("dp") == 4:
-        rows_all, gates_all, expert_in, expert_out, shared = spread([normed_low, gates.T], pieces, group, 1)
+        rows_all, gates_all, expert_in, expert_out, shared = spread([normed_low, gates.T], pieces, [], group, 1)
     else:
-        rows_all, gates_all = spread([normed_low, gates.T], [], group, 1)
+        rows_all, gates_all = spread([normed_low, gates.T], [], [], group, 1)
         expert_in, expert_out, shared = [lax.all_gather(p, "dp", axis=1, tiled=True) for p in pieces]
     part = shared.shape[2] // 3
     weights = (router, shared[0, :, : 2 * part], shared[0, :, 2 * part :], expert_in, expert_out)
     own_gates = lax.dynamic_slice_in_dim(gates_all, lax.axis_index("expert") * local, local, axis=1)
-    partial, picked, gate_up, shared_gu = expert_forward(rows_all, own_gates, expert_in, expert_out, *weights[1:3])
-    output = hidden + gather_sum([partial], [], group, 2)[0]
-    return output, (norm_back, normed_low, probs, rows_all, own_gates, picked, gate_up, shared_gu, weights)
-
-
-def moe_backward(grad_out, saved, valid):
+    routed, picked, gate_up, shared_gu = expert_forward(rows_all, own_gates, expert_in, expert_out, *weights[1:3], 2)
+    return hidden + routed, (norm_back, normed_low, probs, rows_all, own_gates, picked, gate_up, shared_gu, weights)
+
+
+def moe_backward(grad_out, saved, valid, grads_all, earlier):
     norm_back, normed_low, probs, rows_all, own_gates, picked, gate_up, shared_gu, weights = saved
     router, shared_in, shared_out, expert_in, expert_out = weights
     group = lax.axis_size("expert")
     local, width, inner = expert_in.shape
-    grads_all = spread([grad_out.astype(BRAIN)], [], group, 3)[0]
-    partial, dgates, dgate_up, dresult, middle, dshared, shared_mid = expert_backward(
-        grads_all, own_gates, gate_up, shared_gu, expert_in, expert_out, shared_in, shared_out
-    )
-    placed = lax.dynamic_update_slice_in_dim(
-        jnp.zeros((group, probs.shape[1], probs.shape[0]), FLOAT),
-        dgates,
-        lax.axis_index("expert") * local,
-        axis=1,
+    if grads_all is None:
+        if lax.axis_size("dp") == 4:
+            grads_all, *earlier = spread([grad_out.astype(BRAIN)], [], earlier, group, 3)
+        else:
+            grads_all = spread([grad_out.astype(BRAIN)], [], [], group, 3)[0]
+            earlier = [scatter_expert(s) for s in earlier]
+    grad_normed, grad_gates, dgate_up, dresult, middle, dshared, shared_mid = expert_backward(
+        grads_all, own_gates, gate_up, shared_gu, expert_in, expert_out, shared_in, shared_out, 4
     )
     rows_of = lambda array: array.reshape(local, -1, array.shape[-1])
     by_expert = lambda left, right: lax.dot_general(
@@ -1244,21 +1438,16 @@
     flat = lambda array: array.reshape(-1, array.shape[-1])
     shared_grads = [matmul_tn(flat(rows_all), flat(dshared)), matmul_tn(flat(grads_all), flat(shared_mid))]
     sums = [
+        jnp.concatenate(shared_grads, axis=1).astype(BRAIN)[None],
         by_expert(picked, dgate_up),
         by_expert(dresult, middle),
-        jnp.concatenate(shared_grads, axis=1).astype(BRAIN)[None],
     ]
-    if lax.axis_size("dp") == 4:
-        grad_normed, grad_gates, *sums = gather_sum([partial, placed], sums, group, 4)
-    else:
-        grad_normed, grad_gates = gather_sum([partial, placed], [], group, 4)
-        sums = [lax.psum_scatter(s, "dp", scatter_dimension=1, tiled=True).astype(FLOAT) for s in sums]
-    grad_probs = grad_gates.T * valid[:, None]
+    grad_probs = grad_gates.reshape(-1, grad_gates.shape[2]).T * valid[:, None]
     grad_logits = probs * (grad_probs - jnp.sum(probs * grad_probs, axis=1, keepdims=True))
     logits_low = grad_logits.astype(BRAIN)
     grad_router = matmul_tn(normed_low, logits_low).astype(BRAIN)
     grad_hidden, grad_gain = norm_back(grad_normed + matmul_nt(logits_low, router))
-    return grad_out + grad_hidden, grad_gain, grad_router, sums[2][0].astype(BRAIN), sums[0], sums[1]
+    return grad_out + grad_hidden, grad_gain, grad_router, sums, earlier
 
 
 def attend_scores(query, key_rows):
@@ -1365,6 +1554,10 @@
     return lax.psum_scatter(array, BOTH, scatter_dimension=0, tiled=True).astype(FLOAT)
 
 
+def scatter_expert(array):
+    return lax.psum_scatter(array, "dp", scatter_dimension=1, tiled=True).astype(FLOAT)
+
+
 def shared_columns(shared):
     group = lax.axis_size("expert")
     rows = shared[0].shape[0]
@@ -1395,18 +1588,25 @@
     return lax.all_to_all(blocks, "expert", split_axis=0, concat_axis=0, tiled=True)
 
 
-def first_gather(mixer_in, routers, shared):
+def first_gather(dense, shared, rows):
     if lax.axis_size("dp") == 4:
-        mix, routers, shared = head_exchange(mixer_in, routers, shared, 5)
-        return mix.reshape(-1, mix.shape[2]), routers.reshape(-1, routers.shape[2]), shared
-    return gather_dense(mixer_in), gather_dense(routers), exchange(shared)
-
-
-def last_sums(mix, routers, shared, small):
+        *dense, shared, rows = head_exchange(dense, shared, rows, 5)
+        return [array.reshape(-1, array.shape[2]) for array in dense], shared, rows
+    rows = spread([rows], [], [], lax.axis_size("expert"), 3)[0]
+    return [gather_dense(array) for array in dense], exchange(shared), rows
+
+
+def last_sums(left, right, routers, small, sums_a, shared_b):
+    group = lax.axis_size("expert")
+    cut = lambda array: array.reshape(group, -1, array.shape[-1])
+    shared_b = cut(shared_b.astype(BRAIN))
     if lax.axis_size("dp") == 4:
-        cut = lambda array: array.reshape(4 * lax.axis_size("expert"), -1, array.shape[1])
-        return tail_exchange(cut(mix), cut(routers), shared, small, 6)
-    return scatter_dense(mix), scatter_dense(routers), exchange(shared), lax.psum(small, BOTH)
+        routers = routers.reshape(4 * group, -1, routers.shape[1])
+        return tail_exchange(left.T, right, routers, shared_b, small, sums_a, 6)
+    mix = matmul_tn(left, right).astype(BRAIN)
+    shared_a, *sums_a = [scatter_expert(s) for s in sums_a]
+    shared_a = exchange(cut(shared_a.astype(BRAIN)))
+    return scatter_dense(mix), scatter_dense(routers), exchange(shared_b), lax.psum(small, BOTH), shared_a, *sums_a
 
 
 def per_device(
@@ -1427,14 +1627,15 @@
     group = lax.axis_size("expert")
     experts = router_a.shape[1]
     valid = (jnp.arange(SLOT_LEN) < lengths[0]).astype(FLOAT)
-    w_mixer_in, w_routers, w_shared = first_gather(
-        mixer_in,
-        jnp.concatenate([router_a, router_b], axis=1),
+    grad = cotangent * valid[:, None]
+    (w_mixer_in, w_mixer_out, w_routers), w_shared, last_rows = first_gather(
+        [mixer_in, mixer_out, jnp.concatenate([router_a, router_b], axis=1)],
         shared_columns([shared_in_a, shared_out_a, shared_in_b, shared_out_b]),
+        grad.astype(BRAIN),
     )
     w_shared = w_shared.reshape(1, -1, w_shared.shape[2])
     half = w_shared.shape[2] // 2
-    w_mixer_out = gather_dense(mixer_out)
+    attn_qkv, attn_out, w_routers = lax.optimization_barrier((attn_qkv, attn_out, w_routers))
     w_qkv = gather_dense(attn_qkv)
     w_attn_out = gather_dense(attn_out)
     hidden = layer_input.astype(FLOAT)
@@ -1446,27 +1647,24 @@
     layer_output, saved_b = moe_forward(
         hidden, routes_b, valid, norm_gains[3], w_routers[:, experts:], [expert_in_b, expert_out_b, w_shared[:, :, half:]]
     )
-    grad = cotangent * valid[:, None]
-    grad, gain_four, d_router_b, d_shared_b, d_in_b, d_out_b = moe_backward(grad, saved_b, valid)
+    grad, gain_four, d_router_b, sums_b, _ = moe_backward(grad, saved_b, valid, last_rows, [])
     grad, gain_three, d_qkv, d_attn_out = attention_backward(grad, saved_attn, w_qkv, w_attn_out)
     grad, d_qkv, d_attn_out = lax.optimization_barrier((grad, d_qkv, d_attn_out))
     d_qkv, d_attn_out = scatter_dense(d_qkv), scatter_dense(d_attn_out)
-    grad, gain_two, d_router_a, d_shared_a, d_in_a, d_out_a = moe_backward(grad, saved_a, valid)
-    grad, gain_one, d_mixer_in, d_mixer_out, grad_small = mixer_backward(
+    grad, gain_two, d_router_a, sums_a, sums_b = moe_backward(grad, saved_a, valid, None, sums_b)
+    d_shared_b, d_in_b, d_out_b = sums_b
+    grad, gain_one, mix_left, mix_right, d_mixer_out, grad_small = mixer_backward(
         grad, saved_mix, w_mixer_in, w_mixer_out, small
     )
     d_mixer_out = scatter_dense(d_mixer_out)
     parts = [jnp.stack([gain_one, gain_two, gain_three, gain_four])] + list(grad_small)
     flat = jnp.concatenate([part.reshape(-1) for part in parts])
     padded = jnp.pad(flat, (0, -flat.shape[0] % 1024)).reshape(-1, 128)
-    d_shared = jnp.concatenate([d_shared_a, d_shared_b], axis=1)
-    d_mixer_in, d_routers, d_shared, summed = last_sums(
-        d_mixer_in,
-        jnp.concatenate([d_router_a, d_router_b], axis=1),
-        d_shared.reshape(group, -1, d_shared.shape[1]),
-        padded,
+    d_mixer_in, d_routers, d_shared_b, summed, d_shared_a, d_in_a, d_out_a = last_sums(
+        mix_left, mix_right, jnp.concatenate([d_router_a, d_router_b], axis=1), padded, sums_a, d_shared_b
     )
-    d_shared = shared_whole(d_shared.astype(FLOAT))
+    d_in_a, d_out_a = d_in_a.astype(FLOAT), d_out_a.astype(FLOAT)
+    d_shared = shared_whole(jnp.concatenate([d_shared_a, d_shared_b], axis=2).astype(FLOAT))
     summed = summed.reshape(-1)
     sums = []
     place = 0

time: 1540 us -> 1330 us (0.86)
  Pallas kernels: 1230 us -> 1020 us
    pallas_call x14 -> x9, Pallas kernels: 1190 us -> 985 us  [the longest x3 257 us: spread(): pl.pallas_call(functools.partial(spread_kernel, n, w, s, group), out_shap...]
    convert_element_type x1 -> x4, local copies, waits for them, and re-layouts: 25.5 us -> 3.12 us  [the longest x2 1.68 us: moe_forward(): normed_low = normed.astype(BRAIN)]
    unnamed x249 -> x303, local copies, waits for them, and re-layouts: 36.2 us -> 55.1 us
    dot_general x10 -> x9, matrix products: 42.6 us -> 35.7 us  [matmul_tn(): lax.dot_general(left, right, (((0,), (0,)), ((), ())), preferred_element_...]
  transfers between devices with their start and end apart: 6 -> 5, of which waited for: 0 -> 0; matrix products, arithmetic and copies ran while one was open for 12% -> 14% of each run, Pallas kernels for 57% -> 45%
where the time goes in v3:
time: 1330 us; the launch traced here: 1320 us
  Pallas kernels  1020 us (77%)
  matrix products  131 us (10%)
  local copies, waits for them, and re-layouts  91.3 us (7%)
  other arithmetic  57.9 us (4%)
  between operations  16.7 us (1%)
    pallas_call x3, Pallas kernels, spread(): pl.pallas_call(functools.partial(spread_kernel, n, w, s, group), out_shap...  257 us
    pallas_call x2, Pallas kernels, expert_backward(): pl.pallas_call(functools.partial(expert_backward_kernel, group), out_shap...  195 us
    pallas_call x1, Pallas kernels, tail_exchange(): pl.pallas_call(functools.partial(tail_kernel, group, len(sums), steps), o...  188 us
    pallas_call x1, Pallas kernels, head_exchange(): pl.pallas_call(functools.partial(head_kernel, group, cut, len(dense)), ou...  174 us
    pallas_call x2, Pallas kernels, expert_forward(): pl.pallas_call(functools.partial(expert_forward_kernel, group), out_shape...  171 us
    unnamed x303, local copies, waits for them, and re-layouts  55.1 us
    dot_general x9, matrix products, matmul_tn(): lax.dot_general(left, right, (((0,), (0,)), ((), ())), preferred_element_...  35.7 us
    dot_general x6, matrix products, matmul_nt(): lax.dot_general(left, right, (((1,), (1,)), ((), ())), preferred_element_...  33.7 us
  transfers between devices with their start and end apart: 5, of which 0 were waited for; matrix products, arithmetic and copies ran while one was open for 14% of the time, Pallas kernels for 45%

profile of v3, /device:TPU:16, one launch (start us, length us, event | category | flops | bytes accessed | tf_op | source)
XLA Modules:
  0.0 1320.4 jit_solution(10180138978136313844)
XLA Ops:
  11.4 1.9 copy.168
  16.4 173.8 %head_exchange.1 = (bf16[32,48,6448]{2,1,0:T(8,128)(2,1)}, bf16[32,48,3072]{2,1,0:T(8,128)(2,1)}, bf16[32,48,32]{2,1,0:T(8,128)(2,1)}, bf16[8,48,768]{2,1,0:T(8,128)(2,1)}, bf16[8,256,1536]{2,1,0:T(8,128)(2,1)}) custom-call(bf16[48,6448]{1,0:T(8,128)(2,1)} %refs_0_.1, bf16[48,3072]{1,0:T(8,128)(2,1)} %refs_1_.1, bf16[48,32]{1,0:T(8,128)(2,1)} %pad_maximum_fusion.7.refs_2_, ...), custom_call_target="tpu_custom_call" | custom-call | tf_op jit(solution)/shard_map/head_exchange/pallas_call | solution.py:456
  193.9 10.0 fusion.42
  204.2 2.5 copy-done.33
  210.8 3.5 fusion.3
  214.3 9.3 state_forward.1
  223.7 4.1 multiply_reduce_fusion.6
  227.9 3.0 multiply_reduce_fusion.15
  237.0 96.5 %spread1.2 = (bf16[8,256,1536]{2,1,0:T(8,128)(2,1)S(1)}, f32[8,16,256]{2,1,0:T(8,128)S(1)}, bf16[2,1536,1024]{2,1,0:T(8,128)(2,1)}, bf16[2,1536,512]{2,1,0:T(8,128)(2,1)S(1)}, bf16[1,1536,384]{2,1,0:T(8,128)(2,1)S(1)}) custom-call(bf16[256,1536]{1,0:T(8,128)(2,1)S(1)} %copy.176.refs_0_, f32[16,256]{1,0:T(8,128)S(1)} %fusion.65.refs_1_, ...), custom_call_target="tpu_custom_call" | custom-call | tf_op jit(solution)/shard_map/spread1/pallas_call | solution.py:268
  333.5 1.7 copy-done.6
  335.1 2.6 copy-done.9
  340.1 91.0 %expert_forward.2 = (f32[256,1536]{1,0:T(8,128)}, bf16[2,8,128,1536]{3,2,1,0:T(8,128)(2,1)}, bf16[2,8,128,1024]{3,2,1,0:T(8,128)(2,1)}, bf16[8,256,256]{2,1,0:T(8,128)(2,1)}) custom-call(bf16[8,256,1536]{2,1,0:T(8,128)(2,1)} %copy-done.9, f32[8,2,256]{2,1,0:T(2,128)} %constant_dynamic-slice_fusion.1.g_ref, bf16[2,1536,1024]{2,1,0:T(8,128)(2,1)} %get-tuple-element.94.in_ref, ...), custom_call_target="tpu_custom_call" | custom-call | tf_op jit(solution)/shard_map/expert_forward/pallas_call | solution.py:1291
  431.1 2.0 copy.177
  435.2 6.0 convolution_convert_fusion.5.q_ref.k_ref.v_ref
  441.3 4.6 attention_forward.1
  445.9 4.6 multiply_reduce_fusion.13
  459.2 72.6 %spread1.3 = (bf16[8,256,1536]{2,1,0:T(8,128)(2,1)S(1)}, f32[8,16,256]{2,1,0:T(8,128)S(1)}, bf16[2,1536,1024]{2,1,0:T(8,128)(2,1)}, bf16[2,1536,512]{2,1,0:T(8,128)(2,1)S(1)}, bf16[1,1536,384]{2,1,0:T(8,128)(2,1)S(1)}) custom-call(bf16[256,1536]{1,0:T(8,128)(2,1)S(1)} %copy.179.refs_0_, f32[16,256]{1,0:T(8,128)S(1)} %fusion.61.refs_1_, ...), custom_call_target="tpu_custom_call" | custom-call | tf_op jit(solution)/shard_map/spread1/pallas_call | solution.py:268
  533.5 2.6 copy-done.10
  538.4 80.3 %expert_forward.3 = (f32[256,1536]{1,0:T(8,128)}, bf16[2,8,128,1536]{3,2,1,0:T(8,128)(2,1)}, bf16[2,8,128,1024]{3,2,1,0:T(8,128)(2,1)}, bf16[8,256,256]{2,1,0:T(8,128)(2,1)}) custom-call(bf16[8,256,1536]{2,1,0:T(8,128)(2,1)} %copy-done.10, f32[8,2,256]{2,1,0:T(2,128)} %constant_dynamic-slice_fusion.g_ref, bf16[2,1536,1024]{2,1,0:T(8,128)(2,1)} %get-tuple-element.102.in_ref, ...), custom_call_target="tpu_custom_call" | custom-call | tf_op jit(solution)/shard_map/expert_forward/pallas_call | solution.py:1291
  618.7 3.1 copy.180
  621.8 89.5 %expert_backward.2 = (f32[256,1536]{1,0:T(8,128)}, f32[8,2,256]{2,1,0:T(2,128)}, bf16[2,8,128,1024]{3,2,1,0:T(8,128)(2,1)}, bf16[2,8,128,1536]{3,2,1,0:T(8,128)(...) custom-call(bf16[8,256,1536]{2,1,0:T(8,128)(2,1)} %get-tuple-element.106.d_hbm, ...), custom_call_target="tpu_custom_call" | custom-call | tf_op jit(solution)/shard_map/expert_backward/pallas_call | solution.py:1376
  711.3 3.0 copy.181
  714.4 2.8 multiply_reduce_fusion.7
  717.2 4.1 fusion.21
  722.4 3.6 convolution_convert_fusion.2
  726.0 4.2 convolution_convert_fusion.8.d_ref
  730.2 7.1 attention_backward.1
  737.5 5.4 convolution_convert_fusion.1
  742.9 5.8 multiply_reduce_fusion.8
  751.3 4.9 fusion.12
  757.2 4.6 fusion.16
  762.0 7.2 convolution_convert_fusion.7.refs_3_
  769.2 8.7 convolution_convert_fusion.4.refs_2_
  778.0 87.6 %spread3.1 = (bf16[8,256,1536]{2,1,0:T(8,128)(2,1)}, f32[1,384,384]{2,1,0:T(8,128)S(1)}, f32[2,384,1024]{2,1,0:T(8,128)S(1)}, f32[2,384,512]{2,1,0:T(8,128)S(1)}) custom-call(bf16[256,1536]{1,0:T(8,128)(2,1)S(1)} %copy.190.refs_0_, bf16[1,1536,384]{2,1,0:T(8,128)(2,1)S(1)} %pad_maximum_fusion.1.refs_1_, ...), custom_call_target="tpu_custom_call" | custom-call | tf_op jit(solution)/shard_map/spread3/pallas_call | solution.py:268
  865.6 1.7 copy-done.11
  868.5 105.7 %expert_backward.3 = (f32[256,1536]{1,0:T(8,128)}, f32[8,2,256]{2,1,0:T(2,128)}, bf16[2,8,128,1024]{3,2,1,0:T(8,128)(2,1)}, bf16[2,8,128,1536]{3,2,1,0:T(8,128)(...) custom-call(bf16[8,256,1536]{2,1,0:T(8,128)(2,1)} %get-tuple-element.121.d_hbm, ...), custom_call_target="tpu_custom_call" | custom-call | tf_op jit(solution)/shard_map/expert_backward/pallas_call | solution.py:1376
  974.2 3.1 copy.191
  978.2 3.7 multiply_reduce_fusion.9
  985.3 2.4 fusion.23
  988.1 5.4 convolution_convert_fusion
  993.5 5.4 fusion.29
  998.8 1.7 multiply_reduce_fusion.4
  1000.9 5.3 fusion.7
  1006.9 1.9 copy-done.8
  1009.7 16.4 %state_backward.1 = (f32[256,3072]{1,0:T(8,128)S(1)}, f32[256,128]{1,0:T(8,128)S(1)}, f32[256,128]{1,0:T(8,128)S(1)}, f32[256,48]{1,0:T(8,128)S(1)}, f32[48,256]{1,0:T(8,128)S(1)}) custom-call(f32[256,3328]{1,0:T(8,128)S(1)} %copy-done.3, f32[256,3328]{1,0:T(8,128)S(1)} %copy-done.3, f32[256,3328]{1,0:T(8,128)S(1)} %copy-done.3, f32[256,48]{1,0:T(8,128)S(1)} %copy-done.21, ...), custom_call_target="tpu_custom_call" | custom-call | tf_op jit(solution)/shard_map/state_backward/pallas_call | solution.py:987
  1029.9 2.3 constant_dynamic-update-slice_fusion.5
  1032.9 6.6 multiply_reduce_fusion.2
  1041.9 3.0 broadcast_multiply_fusion
  1046.7 13.9 %fusion.20 = (f32[1536]{0:T(1024)S(1)}, f32[256]{0:T(256)S(1)}, f32[256,1536]{0,1:T(8,128)}) fusion(bf16[256,1536]{0,1:T(8,128)(2,1)S(1)} %copy-done.53, f32[256]{0:T(256)S(1)} %copy-done.102, f32[1536]{0:T(1024)S(1)} %copy-done.81, bf16[1536,6448]{1,0:T(8,128)(2,1)} %bitcast.220, bf16[256,48]{1,0:T(8,128)(2,1)S(1)} %get-tuple-element.246, ...), kind=kOutput, calls=%fused_computation.72 | convolution fusion | flops 5083568128 | bytes 25483264 | tf_op jit(solution)/shard_map/dot_general | solution.py:41
  1061.6 5.0 fusion.15
  1066.7 5.1 fusion.11
  1073.6 2.1 fusion.41
  1075.8 6.8 convolution_convert_fusion.6.refs_7_
  1082.6 1.9 pad_maximum_fusion.refs_1_
  1084.4 1.7 copy-done.126
  1086.1 8.7 convolution_convert_fusion.3.refs_6_
  1094.8 188.0 %tail_exchange.1 = (f32[48,6448]{1,0:T(8,128)}, f32[48,32]{1,0:T(8,128)}, bf16[8,48,384]{2,1,0:T(8,128)(2,1)}, f32[208,128]{1,0:T(8,128)}, bf16[8,48,384]{2,1,0:...) custom-call(bf16[1536,256]{1,0:T(8,128)(2,1)} %get-tuple-element.267.refs_0_, ...), custom_call_target="tpu_custom_call" | custom-call | tf_op jit(solution)/shard_map/tail_exchange/pallas_call | solution.py:833
  1288.7 2.5 convert_element_type.147
  1292.8 2.1 convert_element_type.146
  1302.1 1.9 convert_element_type.149
  1304.0 1.8 convert_element_type.148
  1305.7 1.8 convert_element_type.144
  1307.6 2.4 copy.279
  1310.0 1.7 copy.280
  (409 shorter events, 77.9 us)
Async XLA Ops:
  7.2 8.2 copy-start
  7.2 428.0 %all-gather.3.cloned.1.call-start = ((), (), s32[]{:S(2)}) async-start(), calls=%async_computation.3 | async-start | bytes 8110080 | tf_op jit(solution)/shard_map/all_gather | solution.py:1550
  7.9 5.6 copy-start.90
  13.3 177.0 %copy-start.48 = (f32[256,1536]{0,1:T(8,128)}, f32[256,1536]{0,1:T(8,128)S(1)}, u32[]{:S(2)}) copy-start(f32[256,1536]{0,1:T(8,128)S(1)} %copy.168) | copy-start | bytes 4718596
  13.5 177.8 %copy-start.123 = (f32[48]{0:T(128)S(1)}, f32[48]{0:T(128)}, u32[]{:S(2)}) copy-start(f32[48]{0:T(128)} %param.49) | copy-start | bytes 580
  13.5 178.4 %copy-start.122 = (f32[48]{0:T(128)S(1)}, f32[48]{0:T(128)}, u32[]{:S(2)}) copy-start(f32[48]{0:T(128)} %param.51) | copy-start | bytes 580
  13.5 178.5 %copy-start.96 = (f32[4,1536]{1,0:T(4,128)S(1)}, f32[4,1536]{1,0:T(4,128)}, u32[]{:S(2)}) copy-start(f32[4,1536]{1,0:T(4,128)} %param.45) | copy-start | bytes 73732
  14.7 178.0 %copy-start.65 = (bf16[256,1536]{1,0:T(8,128)(2,1)S(1)}, bf16[256,1536]{1,0:T(8,128)(2,1)}, u32[]{:S(2)}) copy-start(bf16[256,1536]{1,0:T(8,128)(2,1)} %param.26) | copy-start | bytes 2359300
  190.3 255.6 %all-gather.5.cloned.1.call-start = ((), (), s32[]{:S(2)}) async-start(), calls=%async_computation.4 | async-start | bytes 4866048 | tf_op jit(solution)/shard_map/all_gather | solution.py:1550
  191.0 1111.0 %reduce-scatter.8.cloned.1.call-start = ((), (), s32[]{:S(2)}) async-start(), calls=%async_computation.7 | async-start | bytes 4866048 | tf_op jit(solution)/shard_map/reduce_scatter | solution.py:1554
  192.1 22.2 %copy-start.29 = (f32[1,3072]{1,0:T(1,128)}, f32[1,3072]{1,0:T(1,128)S(1)}, u32[]{:S(2)}) copy-start(f32[1,3072]{1,0:T(1,128)S(1)} %broadcast_in_dim_reshape.4.skip_ref) | copy-start | bytes 36868
  192.7 11.1 copy-start.80
  192.7 38.2 %copy-start.82 = (f32[1536]{0:T(1024)}, f32[1536]{0:T(1024)S(1)}, u32[]{:S(2)}) copy-start(f32[1536]{0:T(1024)S(1)} %get-tuple-element.240) | copy-start | bytes 18436
  193.3 10.6 copy-start.111
  193.3 10.6 copy-start.101
  203.9 6.9 copy-start.100
  206.7 7.5 copy-start.41
  209.8 4.5 copy-start.72
  214.3 9.3 copy-start.2
  214.3 13.5 %slice-start = ((s8[9437184]{0:T(1024)(128)(4,1)}), s8[4194304]{0:T(1024)(128)(4,1)S(1)}, s32[]{:S(2)}) async-start(s8[9437184]{0:T(1024)(128)(4,1)} %bitcast.222), calls=%async_computation.8 | async-start | bytes 8388608
  214.3 13.5 %slice-start.1 = ((s8[9437184]{0:T(1024)(128)(4,1)}), s8[4194304]{0:T(1024)(128)(4,1)S(1)}, s32[]{:S(2)}) async-start(s8[9437184]{0:T(1024)(128)(4,1)} %bitcast.222), calls=%async_computation.9 | async-start | bytes 8388608
  232.3 101.2 %copy-start.54 = (bf16[256,1536]{0,1:T(8,128)(2,1)}, bf16[256,1536]{0,1:T(8,128)(2,1)S(1)}, u32[]{:S(2)}) copy-start(bf16[256,1536]{0,1:T(8,128)(2,1)S(1)} %multiply_convert_fusion.3) | copy-start | bytes 2359300
  433.8 22.0 %copy-start.70 = (pred[256,16]{0,1:T(8,128)(4,1)}, pred[256,16]{0,1:T(8,128)(4,1)S(1)}, u32[]{:S(2)}) copy-start(pred[256,16]{0,1:T(8,128)(4,1)S(1)} %fusion.51) | copy-start | bytes 12292
  435.2 6.1 copy-start.115
  445.9 4.6 copy-start.14
  445.9 5.8 copy-start.84
  450.5 5.4 copy-start.92
  717.2 5.2 copy-start.15
  730.2 7.2 copy-start.37
  730.2 7.2 copy-start.69
  737.5 5.5 copy-start.38
  742.9 5.8 copy-start.116
  742.9 5.9 copy-start.47
  749.2 554.8 %reduce-scatter.6.cloned.1.call-start = ((), (), s32[]{:S(2)}) async-start(), calls=%async_computation.6 | async-start | bytes 8110080 | tf_op jit(solution)/shard_map/reduce_scatter | solution.py:1554
  756.2 549.6 %reduce-scatter.4.cloned.1.call-start = ((), (), s32[]{:S(2)}) async-start(), calls=%async_computation.5 | async-start | bytes 9732096 | tf_op jit(solution)/shard_map/reduce_scatter | solution.py:1554
  761.8 7.4 slice-start.7
  761.9 7.3 slice-start.8
  762.0 7.3 copy-start.127
  978.1 5.9 copy-start.55
  978.2 7.0 copy-start.119
  978.2 7.0 copy-start.45
  988.1 5.4 copy-start.39
  993.5 5.4 copy-start.36
  993.5 7.1 copy-start.5
  1000.9 6.0 copy-start.30
  1046.6 14.0 %copy-start.97 = (f32[1,1536]{1,0:T(1,128)S(1)}, f32[1,1536]{1,0:T(1,128)}, u32[]{:S(2)}) copy-start(f32[1,1536]{1,0:T(1,128)} %reshape.394) | copy-start | bytes 18436
  1046.6 14.0 %copy-start.98 = (f32[1,1536]{1,0:T(1,128)S(1)}, f32[1,1536]{1,0:T(1,128)}, u32[]{:S(2)}) copy-start(f32[1,1536]{1,0:T(1,128)} %reshape.393) | copy-start | bytes 18436
  1046.6 14.0 %copy-start.99 = (f32[1,1536]{1,0:T(1,128)S(1)}, f32[1,1536]{1,0:T(1,128)}, u32[]{:S(2)}) copy-start(f32[1,1536]{1,0:T(1,128)} %reshape.392) | copy-start | bytes 18436
  1046.7 14.0 %copy-start.88 = (f32[48,64]{1,0:T(8,128)S(1)}, f32[48,64]{1,0:T(8,128)}, u32[]{:S(2)}) copy-start(f32[48,64]{1,0:T(8,128)} %reshape.401) | copy-start | bytes 36868
  1046.7 14.2 %copy-start.124 = (f32[48]{0:T(128)S(1)}, f32[48]{0:T(128)}, u32[]{:S(2)}) copy-start(f32[48]{0:T(128)} %param.49) | copy-start | bytes 580
  1046.7 14.2 %copy-start.93 = (f32[3072]{0:T(1024)S(1)}, f32[3072]{0:T(1024)}, u32[]{:S(2)}) copy-start(f32[3072]{0:T(1024)} %get-tuple-element.223) | copy-start | bytes 36868
  1046.7 14.9 %copy-start.112 = (f32[256]{0:T(256)S(1)}, f32[256]{0:T(256)}, u32[]{:S(2)}) copy-start(f32[256]{0:T(256)} %copy-done.111) | copy-start | bytes 3076
  1046.7 14.9 %copy-start.129 = (bf16[8,256,128]{2,1,0:T(8,128)(2,1)S(1)}, bf16[8,256,128]{2,1,0:T(8,128)(2,1)}, u32[]{:S(2)}) copy-start(bf16[8,256,128]{2,1,0:T(8,128)(2,1)} %get-tuple-element.134) | copy-start | bytes 1572868
  1061.6 5.0 copy-start.128
  1061.6 14.1 %slice-start.5 = ((s8[6291456]{0:T(1024)(128)(4,1)}), s8[4194304]{0:T(1024)(128)(4,1)S(1)}, s32[]{:S(2)}) async-start(s8[6291456]{0:T(1024)(128)(4,1)} %bitcast.237), calls=%async_computation.13 | async-start | bytes 8388608
  1066.6 6.2 copy-start.62
  1066.6 9.1 slice-start.6
  1073.6 10.8 slice-start.3
  1075.8 6.8 copy-start.58
  1075.8 8.6 slice-start.4
  1094.8 189.6 %copy-start.56 = (f32[256,1536]{0,1:T(8,128)S(1)}, f32[256,1536]{0,1:T(8,128)}, u32[]{:S(2)}) copy-start(f32[256,1536]{0,1:T(8,128)} %get-tuple-element.260) | copy-start | bytes 4718596
  1286.0 5.2 copy-start.61
  1286.0 6.8 copy-start.63
  1301.2 8.7 copy-start.12
  (81 other events, 191.9 us)
Sparse Core Ops, SparseCore 0:
  190.4 89.7 all-gather.2
  283.2 72.0 all-gather.4
  749.3 130.3 reduce-scatter.7
  886.2 140.5 reduce-scatter.5
  1039.9 177.2 reduce-scatter.3

commit v4 on v3

--- a/solution.py
+++ b/solution.py
@@ -385,18 +385,20 @@
     everything = list(range(count)) + [None]
 
     def column(s, up, zz):
-        for p in everything:
+        for p in range(count):
             if s:
-                if p is None:
-                    row_copy(zz, x, 2, across).wait_recv()
-                else:
-                    copy(p, y, c, zz, x, 4, sibling).wait_recv()
+                copy(p, y, c, zz, x, 4, sibling).wait_recv()
             run(column_moves(p, s, up, zz), lambda item: item.start())
         if s == 0:
             for k in range(1, group):
                 swap(k).start()
             for i in range(dense + 2):
                 own_copy(i).start()
+
+    def rows(s, up, zz):
+        if s:
+            row_copy(zz, x, 2, across).wait_recv()
+        run(column_moves(None, s, up, zz), lambda item: item.start())
 
     def later(phase, start):
         def act(s, up, zz):
@@ -430,6 +432,7 @@
     for k in range(line + 2):
         if k < line:
             only(column, k)
+            only(rows, k)
         if 0 <= k - 1 < line:
             only(later(0, True), k - 1)
         if 0 <= k - 2 < line:
@@ -1187,7 +1190,7 @@
     return [pltpu.VMEM((line, tokens, width), BRAIN)] * 5 + [dma((line, PARTS))] * 6
 
 
-def run_blocks(group, compute, held, sent, start_cross, chain, last):
+def run_blocks(group, compute, held, sent, start_cross, chain, last, between=None):
     line = group // 2
     z, x = places(group)[2:]
 
@@ -1215,6 +1218,8 @@
     lax.fori_loop(0, group, body, 0)
     for j in range(1, line - 1):
         chain(farthest(z, line, j))
+        if between is not None:
+            between(j - 1, line - 2)
     last()
 
 
@@ -1246,13 +1251,66 @@
     return (ranks == place) & (live > 0.0)
 
 
-def expert_forward_kernel(
-    group, x_hbm, g_ref, in_ref, out_ref, sin_ref, sout_ref, y_ref, xe_ref, gu_ref, sgu_ref,
-    rows_ref, held, sent, crossed, below, above, *sems,
-):
-    z, x = places(group)[2:]
+def wide_flow(ins, outs, stages, sems, group):
+    own_sems, send_sems, recv_sems = sems
+    y, c = places(group)[:2]
+    sibling, opposite = {"dp": 2 * y + 1 - c}, {"dp": 2 * (1 - y) + c}
+    own, other = 2 * y + c, 2 * (1 - y) + c
+    count = len(ins)
+
+    def block(i, q):
+        rows = ins[i].shape[0]
+        return outs[i].at[pl.ds(pl.multiple_of(q * rows, rows), rows)]
+
+    def copy(i, kind):
+        src = block(i, other) if kind == 2 else ins[i]
+        dst = block(i, other if kind == 2 else own)
+        return remote(src, dst, send_sems.at[i, kind], recv_sems.at[i, kind], opposite if kind == 1 else sibling)
+
+    def load(i):
+        return pltpu.make_async_copy(ins[i], stages[i], own_sems.at[i])
+
+    def keep(i):
+        return pltpu.make_async_copy(stages[i], block(i, own), own_sems.at[i])
+
+    def begin():
+        for i in range(count):
+            copy(i, 1).start()
+            copy(i, 0).start()
+            load(i).start()
+
+    def store():
+        for i in range(count):
+            load(i).wait()
+            keep(i).start()
+
+    def forward(i):
+        copy(i, 1).wait_recv()
+        copy(i, 2).start()
+
+    def finish():
+        for i in range(count):
+            copy(i, 0).wait()
+            copy(i, 1).wait_send()
+            copy(i, 2).wait()
+            keep(i).wait()
+
+    return begin, store, forward, finish
+
+
+def expert_forward_kernel(group, wide, x_hbm, g_ref, in_ref, out_ref, sin_ref, sout_ref, *refs):
+    wide_ins, (y_ref, xe_ref, gu_ref, sgu_ref), refs = refs[:wide], refs[wide : wide + 4], refs[wide + 4 :]
+    wide_outs, stages, refs = refs[:wide], refs[wide : 2 * wide], refs[2 * wide :]
+    rows_ref, held, sent, crossed, below, above, *sems = refs
+    y, c, z, x = places(group)
     wait_load = load_blocks(group, x_hbm, rows_ref, sems[6])
-    greet(line_peers(z, x, group // 2))
+    peers = line_peers(z, x, group // 2)
+    if wide:
+        peers += [(None, {"dp": 2 * y + 1 - c}), (None, {"dp": 2 * (1 - y) + c})]
+    greet(peers)
+    if wide:
+        begin, store, forward, finish = wide_flow(wide_ins, wide_outs, stages, sems[7:], group)
+        begin()
     start_cross, chain, last, settle = fold(group, held, sent, crossed, below, above, y_ref, sems[:6])
 
     def compute(s):
@@ -1278,30 +1336,46 @@
             gu_ref[e, s] = gate_up.astype(gu_ref.dtype)
         return total
 
-    run_blocks(group, compute, held, sent, start_cross, chain, last)
+    def between(turn, turns):
+        if wide and turn == 0:
+            store()
+        if wide and turn == turns - 1:
+            for i in range(wide - 1):
+                forward(i)
+
+    run_blocks(group, compute, held, sent, start_cross, chain, last, between)
+    if wide:
+        forward(wide - 1)
+        finish()
     settle()
 
 
-def expert_forward(rows, gates, expert_in, expert_out, shared_in, shared_out, number):
+def expert_forward(rows, gates, expert_in, expert_out, shared_in, shared_out, wide, number):
     group, tokens, width = rows.shape
     local = expert_in.shape[0]
     inner = expert_in.shape[2]
     vmem = pl.BlockSpec(memory_space=pltpu.VMEM)
+    any_spec = pl.BlockSpec(memory_space=pl.ANY)
     dma = pltpu.SemaphoreType.DMA
     return pl.pallas_call(
-        functools.partial(expert_forward_kernel, group),
+        functools.partial(expert_forward_kernel, group, len(wide)),
         out_shape=[
             jax.ShapeDtypeStruct((tokens, width), FLOAT),
             jax.ShapeDtypeStruct((local, group, PICKED, width), BRAIN),
             jax.ShapeDtypeStruct((local, group, PICKED, inner), BRAIN),
             jax.ShapeDtypeStruct((group, tokens, shared_in.shape[1]), BRAIN),
-        ],
-        in_specs=[pl.BlockSpec(memory_space=pl.ANY)] + [vmem] * 5,
-        out_specs=[vmem] * 4,
-        scratch_shapes=[pltpu.VMEM(rows.shape, BRAIN)] + fold_scratch(group, tokens, width) + [dma((group,))],
+        ]
+        + [jax.ShapeDtypeStruct((4 * a.shape[0], a.shape[1]), a.dtype) for a in wide],
+        in_specs=[any_spec] + [vmem] * 5 + [any_spec] * len(wide),
+        out_specs=[vmem] * 4 + [any_spec] * len(wide),
+        scratch_shapes=[pltpu.VMEM(a.shape, a.dtype) for a in wide]
+        + [pltpu.VMEM(rows.shape, BRAIN)]
+        + fold_scratch(group, tokens, width)
+        + [dma((group,))]
+        + ([dma((len(wide),)), dma((len(wide), 3)), dma((len(wide), 3))] if wide else []),
         compiler_params=pltpu.CompilerParams(collective_id=number, has_side_effects=True, vmem_limit_bytes=60 * MIB),
         name="expert_forward",
-    )(rows, gates, expert_in, expert_out, shared_in, shared_out)
+    )(rows, gates, expert_in, expert_out, shared_in, shared_out, *wide)
 
 
 def swiglu_back(gate, up, grad):
@@ -1310,17 +1384,25 @@
     return grad * up * (sig + act * (1.0 - sig)), grad * act, act * up
 
 
+TILE = 256
+
+
 def expert_backward_kernel(
-    group, d_hbm, g_ref, gu_ref, sgu_ref, in_ref, out_ref, sin_ref, sout_ref,
-    dx_ref, dg_ref, dgu_ref, dres_ref, mid_ref, dsgu_ref, smid_ref,
-    rows_ref, dgates, held, sent, crossed, below, above, *sems,
+    group, d_hbm, xe_hbm, gu_hbm, g_ref, sgu_ref, in_ref, out_ref, sin_ref, sout_ref,
+    dx_ref, dg_ref, win_hbm, wout_hbm, dsgu_ref, smid_ref,
+    rows_ref, xe_ref, gu_ref, dres_ref, mid_ref, win_stage, wout_stage, dgates, held, sent, crossed, below, above, *sems,
 ):
     z, x = places(group)[2:]
     me = 2 * z + x
-    gate_send, gate_recv = sems[7:9]
+    gate_send, gate_recv, fetch_sems, stage_sems = sems[7:11]
     wait_load = load_blocks(group, d_hbm, rows_ref, sems[6])
+    fetch_gu = pltpu.make_async_copy(gu_hbm, gu_ref, fetch_sems.at[0])
+    fetch_xe = pltpu.make_async_copy(xe_hbm, xe_ref, fetch_sems.at[1])
+    fetch_gu.start()
+    fetch_xe.start()
     greet([(None, {"expert": lax.rem(me + k, group)}) for k in range(1, group)])
     start_cross, chain, last, settle = fold(group, held, sent, crossed, below, above, dx_ref, sems[:6])
+    fetch_gu.wait()
 
     def give(s):
         return remote(dgates.at[s], dg_ref.at[me], gate_send.at[s], gate_recv.at[me], {"expert": s})
@@ -1352,13 +1434,49 @@
             dweight = jnp.sum(raw * inner_low.astype(FLOAT), axis=1, keepdims=True)
             dgates[s, e : e + 1, :] = jnp.sum(jnp.where(hit, dweight, 0.0), axis=0, keepdims=True)
             dgu = jnp.concatenate([dgate, dup], axis=1).astype(BRAIN)
-            dgu_ref[e, s] = dgu
+            gu_ref[e, s] = dgu
             back = matmul_nt(dgu, in_ref[e]).astype(BRAIN)
             total = total + matmul_tn(chosen, back)
         pl.when(s != me)(lambda: give(s).start())
         return total
 
-    run_blocks(group, compute, held, sent, start_cross, chain, last)
+    local, depth, inner = in_ref.shape
+    tiles = depth // TILE
+
+    def stores(n):
+        e, t, slot = n // tiles, lax.rem(n, tiles), lax.rem(n, 2)
+        at = pl.ds(pl.multiple_of(t * TILE, TILE), TILE)
+        return (
+            pltpu.make_async_copy(win_stage.at[slot], win_hbm.at[e, at], stage_sems.at[0, slot]),
+            pltpu.make_async_copy(wout_stage.at[slot], wout_hbm.at[e, at], stage_sems.at[1, slot]),
+        )
+
+    def weight_tile(n, carry):
+        e, t, slot = n // tiles, lax.rem(n, tiles), lax.rem(n, 2)
+        at = pl.ds(pl.multiple_of(t * TILE, TILE), TILE)
+
+        @pl.when(n >= 2)
+        def _():
+            for store in stores(n - 2):
+                store.wait()
+
+        flat = lambda array: array.reshape(-1, array.shape[-1])
+        win_stage[slot] = matmul_tn(flat(xe_ref[e, :, :, at]), flat(gu_ref[e])).astype(BRAIN)
+        wout_stage[slot] = matmul_tn(flat(dres_ref[e, :, :, at]), flat(mid_ref[e])).astype(BRAIN)
+        for store in stores(n):
+            store.start()
+        return carry
+
+    def between(turn, turns):
+        if turn == 0:
+            fetch_xe.wait()
+        count = local * tiles
+        lax.fori_loop(count * turn // turns, count * (turn + 1) // turns, weight_tile, 0)
+
+    run_blocks(group, compute, held, sent, start_cross, chain, last, between)
+    for n in (local * tiles - 2, local * tiles - 1):
+        for store in stores(n):
+            store.wait()
     dg_ref[me] = dgates[me]
     for k in range(1, group):
         source = lax.rem(me + k, group)
@@ -1367,34 +1485,44 @@
     settle()
 
 
-def expert_backward(grads, gates, gate_up, shared_gu, expert_in, expert_out, shared_in, shared_out, number):
+def expert_backward(grads, picked, gates, gate_up, shared_gu, expert_in, expert_out, shared_in, shared_out, number):
     group, tokens, width = grads.shape
     local = expert_in.shape[0]
     inner = expert_in.shape[2]
     vmem = pl.BlockSpec(memory_space=pltpu.VMEM)
+    any_spec = pl.BlockSpec(memory_space=pl.ANY)
     dma = pltpu.SemaphoreType.DMA
     return pl.pallas_call(
         functools.partial(expert_backward_kernel, group),
         out_shape=[
             jax.ShapeDtypeStruct((tokens, width), FLOAT),
             jax.ShapeDtypeStruct((group, local, tokens), FLOAT),
-            jax.ShapeDtypeStruct((local, group, PICKED, inner), BRAIN),
-            jax.ShapeDtypeStruct((local, group, PICKED, width), BRAIN),
-            jax.ShapeDtypeStruct((local, group, PICKED, inner // 2), BRAIN),
+            jax.ShapeDtypeStruct((local, width, inner), BRAIN),
+            jax.ShapeDtypeStruct((local, width, inner // 2), BRAIN),
             jax.ShapeDtypeStruct(shared_gu.shape, BRAIN),
             jax.ShapeDtypeStruct(shared_gu.shape[:2] + (shared_gu.shape[2] // 2,), BRAIN),
         ],
-        in_specs=[pl.BlockSpec(memory_space=pl.ANY)] + [vmem] * 7,
-        out_specs=[vmem] * 7,
-        scratch_shapes=[pltpu.VMEM(grads.shape, BRAIN), pltpu.VMEM((group, local, tokens), FLOAT)]
+        in_specs=[any_spec] * 3 + [vmem] * 6,
+        out_specs=[vmem] * 2 + [any_spec] * 2 + [vmem] * 2,
+        scratch_shapes=[
+            pltpu.VMEM(grads.shape, BRAIN),
+            pltpu.VMEM(picked.shape, BRAIN),
+            pltpu.VMEM(gate_up.shape, BRAIN),
+            pltpu.VMEM((local, group, PICKED, width), BRAIN),
+            pltpu.VMEM((local, group, PICKED, inner // 2), BRAIN),
+            pltpu.VMEM((2, TILE, inner), BRAIN),
+            pltpu.VMEM((2, TILE, inner // 2), BRAIN),
+            pltpu.VMEM((group, local, tokens), FLOAT),
+        ]
         + fold_scratch(group, tokens, width)
-        + [dma((group,))] * 3,
-        compiler_params=pltpu.CompilerParams(collective_id=number, has_side_effects=True, vmem_limit_bytes=62 * MIB),
+        + [dma((group,))] * 3
+        + [dma((2,)), dma((2, 2))],
+        compiler_params=pltpu.CompilerParams(collective_id=number, has_side_effects=True, vmem_limit_bytes=63 * MIB),
         name="expert_backward",
-    )(grads, gates, gate_up, shared_gu, expert_in, expert_out, shared_in, shared_out)
-
-
-def moe_forward(hidden, routes, valid, norm_gain, router, pieces):
+    )(grads, picked, gate_up, gates, shared_gu, expert_in, expert_out, shared_in, shared_out)
+
+
+def moe_forward(hidden, routes, valid, norm_gain, router, pieces, wide, number):
     group = lax.axis_size("expert")
     local = pieces[0].shape[0]
     normed, norm_back = jax.vjp(rms_norm, hidden, norm_gain)
@@ -1413,34 +1541,34 @@
     part = shared.shape[2] // 3
     weights = (router, shared[0, :, : 2 * part], shared[0, :, 2 * part :], expert_in, expert_out)
     own_gates = lax.dynamic_slice_in_dim(gates_all, lax.axis_index("expert") * local, local, axis=1)
-    routed, picked, gate_up, shared_gu = expert_forward(rows_all, own_gates, expert_in, expert_out, *weights[1:3], 2)
-    return hidden + routed, (norm_back, normed_low, probs, rows_all, own_gates, picked, gate_up, shared_gu, weights)
+    four = lax.axis_size("dp") == 4
+    routed, picked, gate_up, shared_gu, *gathered = expert_forward(
+        rows_all, own_gates, expert_in, expert_out, *weights[1:3], wide if four else [], number
+    )
+    if not four:
+        gathered = [lax.all_gather(array, "dp", axis=0, tiled=True) for array in wide]
+    return hidden + routed, gathered, (norm_back, normed_low, probs, rows_all, own_gates, picked, gate_up, shared_gu, weights)
 
 
 def moe_backward(grad_out, saved, valid, grads_all, earlier):
     norm_back, normed_low, probs, rows_all, own_gates, picked, gate_up, shared_gu, weights = saved
     router, shared_in, shared_out, expert_in, expert_out = weights
     group = lax.axis_size("expert")
-    local, width, inner = expert_in.shape
     if grads_all is None:
         if lax.axis_size("dp") == 4:
             grads_all, *earlier = spread([grad_out.astype(BRAIN)], [], earlier, group, 3)
         else:
             grads_all = spread([grad_out.astype(BRAIN)], [], [], group, 3)[0]
             earlier = [scatter_expert(s) for s in earlier]
-    grad_normed, grad_gates, dgate_up, dresult, middle, dshared, shared_mid = expert_backward(
-        grads_all, own_gates, gate_up, shared_gu, expert_in, expert_out, shared_in, shared_out, 4
+    grad_normed, grad_gates, grad_in, grad_out_weight, dshared, shared_mid = expert_backward(
+        grads_all, picked, own_gates, gate_up, shared_gu, expert_in, expert_out, shared_in, shared_out, 4
     )
-    rows_of = lambda array: array.reshape(local, -1, array.shape[-1])
-    by_expert = lambda left, right: lax.dot_general(
-        rows_of(left), rows_of(right), (((1,), (1,)), ((0,), (0,))), preferred_element_type=FLOAT
-    ).astype(BRAIN)
     flat = lambda array: array.reshape(-1, array.shape[-1])
     shared_grads = [matmul_tn(flat(rows_all), flat(dshared)), matmul_tn(flat(grads_all), flat(shared_mid))]
     sums = [
         jnp.concatenate(shared_grads, axis=1).astype(BRAIN)[None],
-        by_expert(picked, dgate_up),
-        by_expert(dresult, middle),
+        grad_in,
+        grad_out_weight,
     ]
     grad_probs = grad_gates.reshape(-1, grad_gates.shape[2]).T * valid[:, None]
     grad_logits = probs * (grad_probs - jnp.sum(probs * grad_probs, axis=1, keepdims=True))
@@ -1635,17 +1763,30 @@
     )
     w_shared = w_shared.reshape(1, -1, w_shared.shape[2])
     half = w_shared.shape[2] // 2
-    attn_qkv, attn_out, w_routers = lax.optimization_barrier((attn_qkv, attn_out, w_routers))
-    w_qkv = gather_dense(attn_qkv)
-    w_attn_out = gather_dense(attn_out)
+    attn_both, w_routers = lax.optimization_barrier((jnp.concatenate([attn_qkv, attn_out], axis=1), w_routers))
+    attn_part = lax.all_gather(attn_both, "expert", axis=0, tiled=True)
     hidden = layer_input.astype(FLOAT)
     hidden, saved_mix = mixer_forward(hidden, norm_gains[0], w_mixer_in, w_mixer_out, small)
-    hidden, saved_a = moe_forward(
-        hidden, routes_a, valid, norm_gains[1], w_routers[:, :experts], [expert_in_a, expert_out_a, w_shared[:, :, :half]]
+    hidden, (w_qkv, w_attn_out), saved_a = moe_forward(
+        hidden,
+        routes_a,
+        valid,
+        norm_gains[1],
+        w_routers[:, :experts],
+        [expert_in_a, expert_out_a, w_shared[:, :, :half]],
+        [attn_part[:, :QKV], attn_part[:, QKV:]],
+        2,
     )
     hidden, saved_attn = attention_forward(hidden, norm_gains[2], w_qkv, w_attn_out)
-    layer_output, saved_b = moe_forward(
-        hidden, routes_b, valid, norm_gains[3], w_routers[:, experts:], [expert_in_b, expert_out_b, w_shared[:, :, half:]]
+    layer_output, _, saved_b = moe_forward(
+        hidden,
+        routes_b,
+        valid,
+        norm_gains[3],
+        w_routers[:, experts:],
+        [expert_in_b, expert_out_b, w_shared[:, :, half:]],
+        [],
+        7,
     )
     grad, gain_four, d_router_b, sums_b, _ = moe_backward(grad, saved_b, valid, last_rows, [])
     grad, gain_three, d_qkv, d_attn_out = attention_backward(grad, saved_attn, w_qkv, w_attn_out)

time: 1330 us -> 1290 us (0.970)
  matrix products: 131 us -> 91.5 us
    dot_general x4 -> x0, matrix products: 31.4 us -> none  [moe_backward(): lax.dot_general(rows_of(left), rows_of(right), (((1,), (1,)), ((0,), (0,)...]
    pallas_call x3, Pallas kernels: 257 us -> 241 us  [spread(): pl.pallas_call(functools.partial(spread_kernel, n, w, s, group), out_shap...]
    unnamed x303 -> x297, local copies, waits for them, and re-layouts: 55.1 us -> 54 us
  transfers between devices with their start and end apart: 5 -> 4, of which waited for: 0 -> 0; matrix products, arithmetic and copies ran while one was open for 14% -> 12% of each run, Pallas kernels for 45% -> 38%
where the time goes in v4:
time: 1290 us; the launch traced here: 1280 us
  Pallas kernels  1010 us (78%)
  local copies, waits for them, and re-layouts  98.4 us (8%)
  matrix products  91.5 us (7%)
  other arithmetic  66.3 us (5%)
  between operations  16.5 us (1%)
    pallas_call x3, Pallas kernels, spread(): pl.pallas_call(functools.partial(spread_kernel, n, w, s, group), out_shap...  241 us
    pallas_call x2, Pallas kernels, expert_backward(): pl.pallas_call(functools.partial(expert_backward_kernel, group), out_shap...  200 us
    pallas_call x1, Pallas kernels, tail_exchange(): pl.pallas_call(functools.partial(tail_kernel, group, len(sums), steps), o...  185 us
    pallas_call x1, Pallas kernels, head_exchange(): pl.pallas_call(functools.partial(head_kernel, group, cut, len(dense)), ou...  174 us
    pallas_call x2, Pallas kernels, expert_forward(): pl.pallas_call(functools.partial(expert_forward_kernel, group, len(wide))...  171 us
    unnamed x297, local copies, waits for them, and re-layouts  54 us
    dot_general x6, matrix products, matmul_nt(): lax.dot_general(left, right, (((1,), (1,)), ((), ())), preferred_element_...  32.3 us
    dot_general x9, matrix products, matmul_tn(): lax.dot_general(left, right, (((0,), (0,)), ((), ())), preferred_element_...  31.7 us
  transfers between devices with their start and end apart: 4, of which 0 were waited for; matrix products, arithmetic and copies ran while one was open for 12% of the time, Pallas kernels for 38%

profile of v4, /device:TPU:16, one launch (start us, length us, event | category | flops | bytes accessed | tf_op | source)
XLA Modules:
  0.0 1281.6 jit_solution(12606025473373833673)
XLA Ops:
  12.6 1.9 copy.160
  17.4 1.7 pad_maximum_fusion.3
  21.1 173.8 %head_exchange.1 = (bf16[32,48,6448]{2,1,0:T(8,128)(2,1)}, bf16[32,48,3072]{2,1,0:T(8,128)(2,1)}, bf16[32,48,32]{2,1,0:T(8,128)(2,1)}, bf16[8,48,768]{2,1,0:T(8,128)(2,1)}, bf16[8,256,1536]{2,1,0:T(8,128)(2,1)}) custom-call(bf16[48,6448]{1,0:T(8,128)(2,1)} %refs_0_.1, bf16[48,3072]{1,0:T(8,128)(2,1)} %refs_1_.1, bf16[48,32]{1,0:T(8,128)(2,1)} %pad_maximum_fusion.8.refs_2_, ...), custom_call_target="tpu_custom_call" | custom-call | tf_op jit(solution)/shard_map/head_exchange/pallas_call | solution.py:459
  196.6 10.0 fusion.42
  206.8 2.5 copy-done.37
  210.4 3.4 fusion.3
  214.7 1.8 fusion.115
  218.5 9.3 state_forward.1
  227.8 4.1 multiply_reduce_fusion.6
  232.0 3.0 multiply_reduce_fusion.15
  240.4 1.8 fusion.84
  242.2 82.4 %spread1.2 = (bf16[8,256,1536]{2,1,0:T(8,128)(2,1)S(1)}, f32[8,16,256]{2,1,0:T(8,128)S(1)}, bf16[2,1536,1024]{2,1,0:T(8,128)(2,1)}, bf16[2,1536,512]{2,1,0:T(8,128)(2,1)S(1)}, bf16[1,1536,384]{2,1,0:T(8,128)(2,1)S(1)}) custom-call(bf16[256,1536]{1,0:T(8,128)(2,1)S(1)} %copy.168.refs_0_, f32[16,256]{1,0:T(8,128)S(1)} %fusion.65.refs_1_, ...), custom_call_target="tpu_custom_call" | custom-call | tf_op jit(solution)/shard_map/spread1/pallas_call | solution.py:268
  324.6 1.7 copy-done.9
  326.3 2.6 copy-done.12
  331.3 2.4 slice.194.refs_1_
  333.7 2.9 slice.193.refs_0_
  336.6 88.0 %expert_forward.2 = (f32[256,1536]{1,0:T(8,128)}, bf16[2,8,128,1536]{3,2,1,0:T(8,128)(2,1)}, bf16[2,8,128,1024]{3,2,1,0:T(8,128)(2,1)}, bf16[8,256,256]{2,1,0:T(...) custom-call(bf16[8,256,1536]{2,1,0:T(8,128)(2,1)} %copy-done.12, ...), custom_call_target="tpu_custom_call" | custom-call | tf_op jit(solution)/shard_map/expert_forward/pallas_call | solution.py:1360
  424.6 2.0 copy.169
  426.9 6.3 convolution_convert_fusion.3.q_ref.k_ref.v_ref
  433.2 4.6 attention_forward.1
  443.0 1.7 select_reduce_fusion
  446.9 75.5 %spread1.3 = (bf16[8,256,1536]{2,1,0:T(8,128)(2,1)S(1)}, f32[8,16,256]{2,1,0:T(8,128)S(1)}, bf16[2,1536,1024]{2,1,0:T(8,128)(2,1)}, bf16[2,1536,512]{2,1,0:T(8,128)(2,1)S(1)}, bf16[1,1536,384]{2,1,0:T(8,128)(2,1)S(1)}) custom-call(bf16[256,1536]{1,0:T(8,128)(2,1)S(1)} %copy.171.refs_0_, f32[16,256]{1,0:T(8,128)S(1)} %fusion.61.refs_1_, ...), custom_call_target="tpu_custom_call" | custom-call | tf_op jit(solution)/shard_map/spread1/pallas_call | solution.py:268
  524.1 2.7 copy-done.11
  529.1 83.1 %expert_forward.3 = (f32[256,1536]{1,0:T(8,128)}, bf16[2,8,128,1536]{3,2,1,0:T(8,128)(2,1)}, bf16[2,8,128,1024]{3,2,1,0:T(8,128)(2,1)}, bf16[8,256,256]{2,1,0:T(8,128)(2,1)}) custom-call(bf16[8,256,1536]{2,1,0:T(8,128)(2,1)} %copy-done.11, f32[8,2,256]{2,1,0:T(2,128)} %constant_dynamic-slice_fusion.g_ref, bf16[2,1536,1024]{2,1,0:T(8,128)(2,1)} %get-tuple-element.102.in_ref, ...), custom_call_target="tpu_custom_call" | custom-call | tf_op jit(solution)/shard_map/expert_forward/pallas_call | solution.py:1360
  612.2 3.0 copy.172
  615.2 89.2 %expert_backward.2 = (f32[256,1536]{1,0:T(8,128)}, f32[8,2,256]{2,1,0:T(2,128)}, bf16[2,1536,1024]{2,1,0:T(8,128)(2,1)}, bf16[2,1536,512]{2,1,0:T(8,128)(2,1)}, ...) custom-call(bf16[8,256,1536]{2,1,0:T(8,128)(2,1)} %get-tuple-element.106.d_hbm, ...), custom_call_target="tpu_custom_call" | custom-call | tf_op jit(solution)/shard_map/expert_backward/pallas_call | solution.py:1495
  704.4 3.1 copy.173
  707.6 2.9 multiply_reduce_fusion.7
  710.8 1.7 fusion.21
  713.9 3.6 convolution_convert_fusion.2
  717.5 7.0 attention_backward.1
  724.7 6.9 multiply_reduce_fusion.8
  731.6 5.4 convolution_convert_fusion.1
  737.0 2.9 fusion.22
  742.2 2.5 convert_element_type.121
  746.1 5.0 fusion.16
  751.1 1.8 fusion.12
  753.1 82.7 %spread3.1 = (bf16[8,256,1536]{2,1,0:T(8,128)(2,1)}, f32[1,384,384]{2,1,0:T(8,128)S(1)}, f32[2,384,1024]{2,1,0:T(8,128)S(1)}, f32[2,384,512]{2,1,0:T(8,128)S(1)}) custom-call(bf16[256,1536]{1,0:T(8,128)(2,1)S(1)} %copy.180.refs_0_, bf16[1,1536,384]{2,1,0:T(8,128)(2,1)S(1)} %pad_maximum_fusion.1.refs_1_, bf16[2,1536,1024]{2,1,0:T(8,128)(2,1)} %get-tuple-element.118.refs_2_, ...), custom_call_target="tpu_custom_call" | custom-call | tf_op jit(solution)/shard_map/spread3/pallas_call | solution.py:268
  839.4 110.8 %expert_backward.3 = (f32[256,1536]{1,0:T(8,128)}, f32[8,2,256]{2,1,0:T(2,128)}, bf16[2,1536,1024]{2,1,0:T(8,128)(2,1)}, bf16[2,1536,512]{2,1,0:T(8,128)(2,1)}, ...) custom-call(bf16[8,256,1536]{2,1,0:T(8,128)(2,1)} %get-tuple-element.120.d_hbm, ...), custom_call_target="tpu_custom_call" | custom-call | tf_op jit(solution)/shard_map/expert_backward/pallas_call | solution.py:1495
  950.3 3.2 copy.181
  954.3 3.3 multiply_reduce_fusion.9
  959.8 2.4 fusion.23
  962.6 5.3 convolution_convert_fusion
  967.9 5.4 fusion.29
  973.3 1.7 multiply_reduce_fusion.4
  975.4 5.3 fusion.7
  981.4 1.9 copy-done.10
  984.2 16.4 %state_backward.1 = (f32[256,3072]{1,0:T(8,128)S(1)}, f32[256,128]{1,0:T(8,128)S(1)}, f32[256,128]{1,0:T(8,128)S(1)}, f32[256,48]{1,0:T(8,128)S(1)}, f32[48,256]{1,0:T(8,128)S(1)}) custom-call(f32[256,3328]{1,0:T(8,128)S(1)} %copy-done.3, f32[256,3328]{1,0:T(8,128)S(1)} %copy-done.3, f32[256,3328]{1,0:T(8,128)S(1)} %copy-done.3, f32[256,48]{1,0:T(8,128)S(1)} %copy-done.22, ...), custom_call_target="tpu_custom_call" | custom-call | tf_op jit(solution)/shard_map/state_backward/pallas_call | solution.py:990
  1004.3 3.9 constant_dynamic-update-slice_fusion.5
  1010.5 10.4 multiply_reduce_fusion.2
  1022.4 3.0 broadcast_multiply_fusion
  1027.2 14.8 %fusion.20 = (f32[1536]{0:T(1024)S(1)}, f32[256]{0:T(256)S(1)}, f32[256,1536]{0,1:T(8,128)}) fusion(bf16[256,1536]{0,1:T(8,128)(2,1)S(1)} %copy-done.58, f32[256]{0:T(256)S(1)} %copy-done.102, f32[1536]{0:T(1024)S(1)} %copy-done.83, bf16[1536,6448]{1,0:T(8,128)(2,1)} %bitcast.206, bf16[256,48]{1,0:T(8,128)(2,1)S(1)} %get-tuple-element.244, ...), kind=kOutput, calls=%fused_computation.68 | convolution fusion | flops 5083568128 | bytes 25483264 | tf_op jit(solution)/shard_map/dot_general | solution.py:41
  1043.0 5.0 fusion.15
  1048.0 5.0 fusion.11
  1055.0 2.2 fusion.41
  1057.2 1.8 pad_maximum_fusion.refs_1_
  1059.0 185.0 %tail_exchange.1 = (f32[48,6448]{1,0:T(8,128)}, f32[48,32]{1,0:T(8,128)}, bf16[8,48,384]{2,1,0:T(8,128)(2,1)}, f32[208,128]{1,0:T(8,128)}, bf16[8,48,384]{2,1,0:...) custom-call(bf16[1536,256]{1,0:T(8,128)(2,1)} %get-tuple-element.265.refs_0_, ...), custom_call_target="tpu_custom_call" | custom-call | tf_op jit(solution)/shard_map/tail_exchange/pallas_call | solution.py:836
  1249.9 2.5 convert_element_type.131
  1254.0 2.1 convert_element_type.130
  1263.3 1.9 convert_element_type.133
  1265.2 1.8 convert_element_type.132
  1266.9 1.8 convert_element_type.128
  1268.8 2.4 copy.263
  1271.2 1.7 copy.264
  (399 shorter events, 77.4 us)
Async XLA Ops:
  7.2 12.0 copy-start
  7.2 324.1 %all-gather.2.cloned.1.call-start = ((), (), s32[]{:S(2)}) async-start(), calls=%async_computation.3 | async-start | bytes 3538944 | tf_op jit(solution)/shard_map/all_gather | solution.py:1767
  7.9 6.8 copy-start.92
  14.5 180.3 %copy-start.52 = (f32[256,1536]{0,1:T(8,128)}, f32[256,1536]{0,1:T(8,128)S(1)}, u32[]{:S(2)}) copy-start(f32[256,1536]{0,1:T(8,128)S(1)} %copy.160) | copy-start | bytes 4718596
  14.7 180.5 %copy-start.94 = (f32[4,3328]{1,0:T(4,128)S(1)}, f32[4,3328]{1,0:T(4,128)}, u32[]{:S(2)}) copy-start(f32[4,3328]{1,0:T(4,128)} %param.47) | copy-start | bytes 159748
  15.9 179.5 %copy-start.70 = (bf16[256,1536]{1,0:T(8,128)(2,1)S(1)}, bf16[256,1536]{1,0:T(8,128)(2,1)}, u32[]{:S(2)}) copy-start(bf16[256,1536]{1,0:T(8,128)(2,1)} %param.26) | copy-start | bytes 2359300
  19.1 176.0 %copy-start.96 = (f32[4,1536]{1,0:T(4,128)S(1)}, f32[4,1536]{1,0:T(4,128)}, u32[]{:S(2)}) copy-start(f32[4,1536]{1,0:T(4,128)} %param.45) | copy-start | bytes 73732
  194.9 1068.3 %reduce-scatter.8.cloned.1.call-start = ((), (), s32[]{:S(2)}) async-start(), calls=%async_computation.6 | async-start | bytes 4866048 | tf_op jit(solution)/shard_map/reduce_scatter | solution.py:1682
  195.2 11.3 copy-start.82
  195.2 39.8 %copy-start.84 = (f32[1536]{0:T(1024)}, f32[1536]{0:T(1024)S(1)}, u32[]{:S(2)}) copy-start(f32[1536]{0:T(1024)S(1)} %get-tuple-element.238) | copy-start | bytes 18436
  195.3 244.1 %copy-start.86 = (f32[1536]{0:T(1024)}, f32[1536]{0:T(1024)S(1)}, u32[]{:S(2)}) copy-start(f32[1536]{0:T(1024)S(1)} %get-tuple-element.237) | copy-start | bytes 18436
  195.4 13.9 %copy-start.74 = (f32[3328]{0:T(1024)}, f32[3328]{0:T(1024)S(1)}, u32[]{:S(2)}) copy-start(f32[3328]{0:T(1024)S(1)} %get-tuple-element.233) | copy-start | bytes 39940
  195.4 13.9 %copy-start.76 = (f32[3328]{0:T(1024)}, f32[3328]{0:T(1024)S(1)}, u32[]{:S(2)}) copy-start(f32[3328]{0:T(1024)S(1)} %get-tuple-element.234) | copy-start | bytes 39940
  195.4 13.9 %copy-start.78 = (f32[3328]{0:T(1024)}, f32[3328]{0:T(1024)S(1)}, u32[]{:S(2)}) copy-start(f32[3328]{0:T(1024)S(1)} %get-tuple-element.235) | copy-start | bytes 39940
  195.5 13.9 %copy-start.80 = (f32[3328]{0:T(1024)}, f32[3328]{0:T(1024)S(1)}, u32[]{:S(2)}) copy-start(f32[3328]{0:T(1024)S(1)} %get-tuple-element.236) | copy-start | bytes 39940
  195.7 10.8 copy-start.56
  213.9 13.9 %copy-start.2 = (f32[256,3328]{1,0:T(8,128)}, f32[256,3328]{1,0:T(8,128)S(1)}, u32[]{:S(2)}) copy-start(f32[256,3328]{1,0:T(8,128)S(1)} %get-tuple-element.250.x_ref.b_ref.c_ref) | copy-start | bytes 10223620
  214.7 13.1 %copy-start.33 = (f32[1,3072]{1,0:T(1,128)}, f32[1,3072]{1,0:T(1,128)S(1)}, u32[]{:S(2)}) copy-start(f32[1,3072]{1,0:T(1,128)S(1)} %broadcast_in_dim_reshape.4.skip_ref) | copy-start | bytes 36868
  218.4 9.3 copy-start.21
  218.5 13.5 %slice-start.2 = ((s8[9437184]{0:T(1024)(128)(4,1)}), s8[4194304]{0:T(1024)(128)(4,1)S(1)}, s32[]{:S(2)}) async-start(s8[9437184]{0:T(1024)(128)(4,1)} %bitcast.208), calls=%async_computation.9 | async-start | bytes 8388608
  218.5 13.5 %slice-start.3 = ((s8[9437184]{0:T(1024)(128)(4,1)}), s8[4194304]{0:T(1024)(128)(4,1)S(1)}, s32[]{:S(2)}) async-start(s8[9437184]{0:T(1024)(128)(4,1)} %bitcast.208), calls=%async_computation.10 | async-start | bytes 8388608
  231.9 730.3 %copy-start.103 = (f32[256]{0:T(256)}, f32[256]{0:T(256)S(1)}, u32[]{:S(2)}) copy-start(f32[256]{0:T(256)S(1)} %fusion.71) | copy-start | bytes 3076
  236.1 6.1 copy-start.19
  236.1 6.1 copy-start.25
  238.7 90.8 %copy-start.114 = (s32[256,6]{0,1:T(8,128)S(1)}, s32[256,6]{0,1:T(8,128)}, u32[]{:S(2)}) copy-start(s32[256,6]{0,1:T(8,128)} %param.30) | copy-start | bytes 18436
  426.6 11.2 slice-start.5
  426.9 6.3 copy-start.111
  426.9 10.9 copy-start.41
  426.9 10.9 slice-start.6
  433.2 6.1 copy-start.4
  439.3 5.5 copy-start.20
  717.5 7.2 copy-start.42
  731.6 5.4 copy-start.112
  731.6 5.4 copy-start.43
  731.6 5.4 copy-start.51
  740.0 525.2 %reduce-scatter.6.cloned.1.call-start = ((), (), s32[]{:S(2)}) async-start(), calls=%async_computation.5 | async-start | bytes 8110080 | tf_op jit(solution)/shard_map/reduce_scatter | solution.py:1682
  740.7 526.2 %reduce-scatter.4.cloned.1.call-start = ((), (), s32[]{:S(2)}) async-start(), calls=%async_computation.4 | async-start | bytes 9732096 | tf_op jit(solution)/shard_map/reduce_scatter | solution.py:1682
  742.2 8.9 slice-start
  954.3 5.4 copy-start.116
  962.6 5.3 copy-start.44
  967.9 5.4 copy-start.40
  967.9 5.4 copy-start.104
  967.9 7.1 copy-start.7
  975.4 6.0 copy-start.34
  1010.5 10.6 copy-start.23
  1010.5 10.6 copy-start.36
  1010.5 10.7 copy-start.120
  1010.5 10.7 copy-start.124
  1010.5 11.9 copy-start.75
  1010.5 11.9 copy-start.77
  1010.5 11.9 copy-start.79
  1010.5 11.9 copy-start.81
  1027.1 14.9 %copy-start.97 = (f32[1,1536]{1,0:T(1,128)S(1)}, f32[1,1536]{1,0:T(1,128)}, u32[]{:S(2)}) copy-start(f32[1,1536]{1,0:T(1,128)} %reshape.366) | copy-start | bytes 18436
  1027.1 14.9 %copy-start.98 = (f32[1,1536]{1,0:T(1,128)S(1)}, f32[1,1536]{1,0:T(1,128)}, u32[]{:S(2)}) copy-start(f32[1,1536]{1,0:T(1,128)} %reshape.365) | copy-start | bytes 18436
  1027.1 14.9 %copy-start.99 = (f32[1,1536]{1,0:T(1,128)S(1)}, f32[1,1536]{1,0:T(1,128)}, u32[]{:S(2)}) copy-start(f32[1,1536]{1,0:T(1,128)} %reshape.364) | copy-start | bytes 18436
  1027.2 15.0 %copy-start.90 = (f32[48,64]{1,0:T(8,128)S(1)}, f32[48,64]{1,0:T(8,128)}, u32[]{:S(2)}) copy-start(f32[48,64]{1,0:T(8,128)} %reshape.373) | copy-start | bytes 36868
  1027.2 15.1 %copy-start.123 = (f32[48]{0:T(128)S(1)}, f32[48]{0:T(128)}, u32[]{:S(2)}) copy-start(f32[48]{0:T(128)} %param.49) | copy-start | bytes 580
  1027.2 15.1 %copy-start.95 = (f32[3072]{0:T(1024)S(1)}, f32[3072]{0:T(1024)}, u32[]{:S(2)}) copy-start(f32[3072]{0:T(1024)} %get-tuple-element.221) | copy-start | bytes 36868
  1027.2 15.8 %copy-start.108 = (f32[256]{0:T(256)S(1)}, f32[256]{0:T(256)}, u32[]{:S(2)}) copy-start(f32[256]{0:T(256)} %copy-done.107) | copy-start | bytes 3076
  1027.2 15.8 %copy-start.127 = (bf16[8,256,128]{2,1,0:T(8,128)(2,1)S(1)}, bf16[8,256,128]{2,1,0:T(8,128)(2,1)}, u32[]{:S(2)}) copy-start(bf16[8,256,128]{2,1,0:T(8,128)(2,1)} %get-tuple-element.134) | copy-start | bytes 1572868
  1048.0 6.2 copy-start.67
  1059.0 186.6 %copy-start.61 = (f32[256,1536]{0,1:T(8,128)S(1)}, f32[256,1536]{0,1:T(8,128)}, u32[]{:S(2)}) copy-start(f32[256,1536]{0,1:T(8,128)} %get-tuple-element.258) | copy-start | bytes 4718596
  1247.2 6.8 copy-start.68
  1262.4 8.7 copy-start.14
  (77 other events, 210.2 us)
Sparse Core Ops, SparseCore 0:
  195.0 69.0 all-gather.1
  740.1 119.9 reduce-scatter.7
  866.7 133.6 reduce-scatter.5
  1008.3 171.4 reduce-scatter.3

commit v5 on v4

--- a/solution.py
+++ b/solution.py
@@ -1082,7 +1082,7 @@
 PARTS = 2
 
 
-def fold(group, held, sent, crossed, below, above, out_ref, sems):
+def fold(group, held, sent, crossed, passing, out_ref, sems):
     cross_send, cross_recv, up_send, up_recv, down_send, down_recv = sems
     line = group // 2
     z, x = places(group)[2:]
@@ -1098,20 +1098,30 @@
 
     def rise(d, p):
         return remote(
-            piece(held, d, p), piece(below, d, p), up_send.at[d, p], up_recv.at[d, p], {"expert": 2 * (z + 1) + x}
+            piece(held, d, p), piece(passing, d, p), up_send.at[d, p], up_recv.at[d, p], {"expert": 2 * (z + 1) + x}
         )
 
     def fall(d, p):
         return remote(
-            piece(held, d, p), piece(above, d, p), down_send.at[d, p], down_recv.at[d, p], {"expert": 2 * (z - 1) + x}
+            piece(held, d, p),
+            piece(passing, jnp.where(d == z - 1, line, d), p),
+            down_send.at[d, p],
+            down_recv.at[d, p],
+            {"expert": 2 * (z - 1) + x},
+        )
+
+    def fallen(d, p):
+        place = jnp.where(d == z, line, d)
+        return remote(
+            piece(held, d, p), piece(passing, place, p), down_send.at[d, p], down_recv.at[d, p], {"expert": 2 * (z + 1) + x}
         )
 
     def add(d, p, final, sources):
         def body(j, carry):
             at = pl.ds(pl.multiple_of(p * rows + j * 16, 16), 16)
             total = held[d, at].astype(FLOAT)
-            for source in sources:
-                total = total + source[d, at].astype(FLOAT)
+            for source, place in sources:
+                total = total + source[place, at].astype(FLOAT)
             if final:
                 out_ref[at] = total
             else:
@@ -1133,11 +1143,11 @@
                 @pl.when(z > 0)
                 def _():
                     rise(d, p).wait_recv()
-                    add(d, p, False, [crossed, below])
+                    add(d, p, False, [(crossed, d), (passing, d)])
 
                 @pl.when(z == 0)
                 def _():
-                    add(d, p, False, [crossed])
+                    add(d, p, False, [(crossed, d)])
 
                 rise(d, p).start()
 
@@ -1145,12 +1155,12 @@
             def _():
                 @pl.when(z < line - 1)
                 def _():
-                    fall(d, p).wait_recv()
-                    add(d, p, False, [crossed, above])
+                    fallen(d, p).wait_recv()
+                    add(d, p, False, [(crossed, d), (passing, d)])
 
                 @pl.when(z == line - 1)
                 def _():
-                    add(d, p, False, [crossed])
+                    add(d, p, False, [(crossed, d)])
 
                 fall(d, p).start()
 
@@ -1160,19 +1170,19 @@
 
             @pl.when(z == 0)
             def _():
-                fall(z, p).wait_recv()
-                add(z, p, True, [crossed, above])
+                fallen(z, p).wait_recv()
+                add(z, p, True, [(crossed, z), (passing, line)])
 
             @pl.when(z == line - 1)
             def _():
                 rise(z, p).wait_recv()
-                add(z, p, True, [crossed, below])
+                add(z, p, True, [(crossed, z), (passing, z)])
 
             @pl.when((z > 0) & (z < line - 1))
             def _():
-                fall(z, p).wait_recv()
+                fallen(z, p).wait_recv()
                 rise(z, p).wait_recv()
-                add(z, p, True, [crossed, below, above])
+                add(z, p, True, [(crossed, z), (passing, z), (passing, line)])
 
     def settle():
         for d in range(line):
@@ -1187,16 +1197,20 @@
 def fold_scratch(group, tokens, width):
     line = group // 2
     dma = pltpu.SemaphoreType.DMA
-    return [pltpu.VMEM((line, tokens, width), BRAIN)] * 5 + [dma((line, PARTS))] * 6
-
-
-def run_blocks(group, compute, held, sent, start_cross, chain, last, between=None):
+    blocks = [pltpu.VMEM((line, tokens, width), BRAIN)] * 3 + [pltpu.VMEM((line + 1, tokens, width), BRAIN)]
+    return blocks + [dma((line, PARTS))] * 6
+
+
+def run_blocks(group, compute, held, sent, start_cross, chain, last, between=None, early=None):
     line = group // 2
     z, x = places(group)[2:]
 
     def body(j, carry):
         d = farthest(z, line, j // 2)
         crossing = lax.rem(j, 2) == 0
+
+        if early is not None:
+            pl.when(j == 2)(early)
 
         @pl.when(j == group - 2)
         def _():
@@ -1251,6 +1265,88 @@
     return (ranks == place) & (live > 0.0)
 
 
+def sum_flow(ins, outs, bufs, sems, group):
+    own, core_send, core_recv, side_send, side_recv, keep = sems
+    y, c = places(group)[:2]
+    sibling, opposite = {"dp": 2 * y + 1 - c}, {"dp": 2 * (1 - y) + c}
+
+    def parts(k):
+        kept, landed, arrived = bufs[3 * k : 3 * k + 3]
+        source = ins[k]
+        height = source.shape[1] // 4
+
+        def piece(q):
+            return source.at[:, pl.ds(pl.multiple_of(q * height, height), height), :]
+
+        def take(h):
+            return pltpu.make_async_copy(piece(2 * h + c), kept, own.at[k, h])
+
+        def give(h):
+            return remote(piece(2 * h + 1 - c), landed.at[h], core_send.at[k, h], core_recv.at[k, h], sibling)
+
+        def pass_on():
+            return remote(kept, arrived, side_send.at[k], side_recv.at[k], opposite)
+
+        def add(h, extra):
+            for e in range(source.shape[0]):
+                items = [(kept, (e,), None), (landed, (h, e), None)] + ([(arrived, (e,), None)] if extra else [])
+                add_blocks((kept, (e,), None), items, height)
+
+        def store():
+            return pltpu.make_async_copy(kept, outs[k], keep.at[k])
+
+        return take, give, pass_on, add, store
+
+    def begin():
+        for k in range(len(ins)):
+            take, give = parts(k)[:2]
+            take(1 - y).start()
+            for h in (1 - y, y):
+                give(h).start()
+
+    def cross():
+        for k in range(len(ins)):
+            take, give, pass_on, add, store = parts(k)
+            take(1 - y).wait()
+            give(1 - y).wait_recv()
+            add(1 - y, False)
+            pass_on().start()
+
+    def finish():
+        for k in range(len(ins)):
+            take, give, pass_on, add, store = parts(k)
+            pass_on().wait_send()
+            take(y).start()
+            take(y).wait()
+            give(y).wait_recv()
+            pass_on().wait_recv()
+            add(y, True)
+            store().start()
+        for k in range(len(ins)):
+            take, give, pass_on, add, store = parts(k)
+            give(y).wait_send()
+            give(1 - y).wait_send()
+            store().wait()
+
+    return begin, cross, finish
+
+
+def sum_parts_of(sums):
+    return [(a.shape[0], a.shape[1] // 4, a.shape[2]) for a in sums]
+
+
+def sum_scratch(sums):
+    scratch = []
+    for part in sum_parts_of(sums):
+        scratch += [pltpu.VMEM(part, BRAIN), pltpu.VMEM((2,) + part, BRAIN), pltpu.VMEM(part, BRAIN)]
+    return scratch
+
+
+def sum_sems(count):
+    dma = pltpu.SemaphoreType.DMA
+    return [dma((count, 2))] * 3 + [dma((count,))] * 3
+
+
 def wide_flow(ins, outs, stages, sems, group):
     own_sems, send_sems, recv_sems = sems
     y, c = places(group)[:2]
@@ -1301,7 +1397,7 @@
 def expert_forward_kernel(group, wide, x_hbm, g_ref, in_ref, out_ref, sin_ref, sout_ref, *refs):
     wide_ins, (y_ref, xe_ref, gu_ref, sgu_ref), refs = refs[:wide], refs[wide : wide + 4], refs[wide + 4 :]
     wide_outs, stages, refs = refs[:wide], refs[wide : 2 * wide], refs[2 * wide :]
-    rows_ref, held, sent, crossed, below, above, *sems = refs
+    rows_ref, held, sent, crossed, passing, *sems = refs
     y, c, z, x = places(group)
     wait_load = load_blocks(group, x_hbm, rows_ref, sems[6])
     peers = line_peers(z, x, group // 2)
@@ -1311,7 +1407,7 @@
     if wide:
         begin, store, forward, finish = wide_flow(wide_ins, wide_outs, stages, sems[7:], group)
         begin()
-    start_cross, chain, last, settle = fold(group, held, sent, crossed, below, above, y_ref, sems[:6])
+    start_cross, chain, last, settle = fold(group, held, sent, crossed, passing, y_ref, sems[:6])
 
     def compute(s):
         wait_load(s)
@@ -1384,15 +1480,17 @@
     return grad * up * (sig + act * (1.0 - sig)), grad * act, act * up
 
 
-TILE = 256
+TILE = 128
 
 
 def expert_backward_kernel(
-    group, d_hbm, xe_hbm, gu_hbm, g_ref, sgu_ref, in_ref, out_ref, sin_ref, sout_ref,
-    dx_ref, dg_ref, win_hbm, wout_hbm, dsgu_ref, smid_ref,
-    rows_ref, xe_ref, gu_ref, dres_ref, mid_ref, win_stage, wout_stage, dgates, held, sent, crossed, below, above, *sems,
+    group, sums, d_hbm, xe_hbm, gu_hbm, sgu_hbm, g_ref, in_ref, out_ref, sin_ref, sout_ref, *refs
 ):
-    z, x = places(group)[2:]
+    sum_ins, refs = refs[:sums], refs[sums:]
+    (dx_ref, dg_ref, win_hbm, wout_hbm, dsgu_ref, smid_ref), refs = refs[:6], refs[6:]
+    sum_outs, sum_bufs, refs = refs[:sums], refs[sums : 4 * sums], refs[4 * sums :]
+    rows_ref, xe_ref, gu_ref, mid_ref, win_stage, wout_stage, dgates, held, sent, crossed, passing, *sems = refs
+    y, c, z, x = places(group)
     me = 2 * z + x
     gate_send, gate_recv, fetch_sems, stage_sems = sems[7:11]
     wait_load = load_blocks(group, d_hbm, rows_ref, sems[6])
@@ -1400,9 +1498,18 @@
     fetch_xe = pltpu.make_async_copy(xe_hbm, xe_ref, fetch_sems.at[1])
     fetch_gu.start()
     fetch_xe.start()
-    greet([(None, {"expert": lax.rem(me + k, group)}) for k in range(1, group)])
-    start_cross, chain, last, settle = fold(group, held, sent, crossed, below, above, dx_ref, sems[:6])
+    fetch_sgu = pltpu.make_async_copy(sgu_hbm, dsgu_ref, fetch_sems.at[2])
+    fetch_sgu.start()
+    peers = [(None, {"expert": lax.rem(me + k, group)}) for k in range(1, group)]
+    if sums:
+        peers += [(None, {"dp": 2 * y + 1 - c}), (None, {"dp": 2 * (1 - y) + c})]
+    greet(peers)
+    start_cross, chain, last, settle = fold(group, held, sent, crossed, passing, dx_ref, sems[:6])
+    if sums:
+        begin, cross, finish = sum_flow(sum_ins, sum_outs, sum_bufs, sems[11:], group)
+        begin()
     fetch_gu.wait()
+    fetch_sgu.wait()
 
     def give(s):
         return remote(dgates.at[s], dg_ref.at[me], gate_send.at[s], gate_recv.at[me], {"expert": s})
@@ -1410,7 +1517,7 @@
     def compute(s):
         wait_load(s)
         grads = rows_ref[s]
-        shared_gu = sgu_ref[s].astype(FLOAT)
+        shared_gu = dsgu_ref[s].astype(FLOAT)
         half = shared_gu.shape[1] // 2
         dmid = jnp.dot(grads, sout_ref[...], preferred_element_type=FLOAT)
         dgate, dup, shared_mid = swiglu_back(shared_gu[:, :half], shared_gu[:, half:], dmid)
@@ -1418,13 +1525,14 @@
         dsgu_ref[s] = shared_d
         smid_ref[s] = shared_mid.astype(BRAIN)
         total = matmul_nt(shared_d, sin_ref[...])
+        results = []
         for e in range(in_ref.shape[0]):
             gates = g_ref[s, e : e + 1, :]
             hit = pick_rows(gates)
             chosen = jnp.where(hit, 1.0, 0.0).astype(BRAIN)
             weight = jnp.sum(jnp.where(hit, gates, 0.0), axis=1, keepdims=True)
             picked = jnp.dot(chosen, grads, preferred_element_type=FLOAT)
-            dres_ref[e, s] = (picked * weight).astype(BRAIN)
+            results.append((picked * weight).astype(BRAIN))
             raw = jnp.dot(picked.astype(BRAIN), out_ref[e], preferred_element_type=FLOAT)
             gate_up = gu_ref[e, s].astype(FLOAT)
             width = gate_up.shape[1] // 2
@@ -1437,6 +1545,8 @@
             gu_ref[e, s] = dgu
             back = matmul_nt(dgu, in_ref[e]).astype(BRAIN)
             total = total + matmul_tn(chosen, back)
+        for e, result in enumerate(results):
+            rows_ref[s, e * PICKED : (e + 1) * PICKED] = result
         pl.when(s != me)(lambda: give(s).start())
         return total
 
@@ -1462,7 +1572,8 @@
 
         flat = lambda array: array.reshape(-1, array.shape[-1])
         win_stage[slot] = matmul_tn(flat(xe_ref[e, :, :, at]), flat(gu_ref[e])).astype(BRAIN)
-        wout_stage[slot] = matmul_tn(flat(dres_ref[e, :, :, at]), flat(mid_ref[e])).astype(BRAIN)
+        own = pl.ds(pl.multiple_of(e * PICKED, PICKED), PICKED)
+        wout_stage[slot] = matmul_tn(flat(rows_ref[:, own, at]), flat(mid_ref[e])).astype(BRAIN)
         for store in stores(n):
             store.start()
         return carry
@@ -1473,7 +1584,9 @@
         count = local * tiles
         lax.fori_loop(count * turn // turns, count * (turn + 1) // turns, weight_tile, 0)
 
-    run_blocks(group, compute, held, sent, start_cross, chain, last, between)
+    run_blocks(group, compute, held, sent, start_cross, chain, last, between, cross if sums else None)
+    if sums:
+        finish()
     for n in (local * tiles - 2, local * tiles - 1):
         for store in stores(n):
             store.wait()
@@ -1485,7 +1598,12 @@
     settle()
 
 
-def expert_backward(grads, picked, gates, gate_up, shared_gu, expert_in, expert_out, shared_in, shared_out, number):
+def local_rows(expert_in):
+    return expert_in.shape[0] * PICKED
+
+
+def expert_backward(grads, picked, gates, gate_up, shared_gu, expert_in, expert_out, shared_in, shared_out, sums, number):
+    assert local_rows(expert_in) == grads.shape[1]
     group, tokens, width = grads.shape
     local = expert_in.shape[0]
     inner = expert_in.shape[2]
@@ -1493,7 +1611,7 @@
     any_spec = pl.BlockSpec(memory_space=pl.ANY)
     dma = pltpu.SemaphoreType.DMA
     return pl.pallas_call(
-        functools.partial(expert_backward_kernel, group),
+        functools.partial(expert_backward_kernel, group, len(sums)),
         out_shape=[
             jax.ShapeDtypeStruct((tokens, width), FLOAT),
             jax.ShapeDtypeStruct((group, local, tokens), FLOAT),
@@ -1501,14 +1619,15 @@
             jax.ShapeDtypeStruct((local, width, inner // 2), BRAIN),
             jax.ShapeDtypeStruct(shared_gu.shape, BRAIN),
             jax.ShapeDtypeStruct(shared_gu.shape[:2] + (shared_gu.shape[2] // 2,), BRAIN),
-        ],
-        in_specs=[any_spec] * 3 + [vmem] * 6,
-        out_specs=[vmem] * 2 + [any_spec] * 2 + [vmem] * 2,
-        scratch_shapes=[
+        ]
+        + [jax.ShapeDtypeStruct(part, BRAIN) for part in sum_parts_of(sums)],
+        in_specs=[any_spec] * 4 + [vmem] * 5 + [any_spec] * len(sums),
+        out_specs=[vmem] * 2 + [any_spec] * 2 + [vmem] * 2 + [any_spec] * len(sums),
+        scratch_shapes=sum_scratch(sums)
+        + [
             pltpu.VMEM(grads.shape, BRAIN),
             pltpu.VMEM(picked.shape, BRAIN),
             pltpu.VMEM(gate_up.shape, BRAIN),
-            pltpu.VMEM((local, group, PICKED, width), BRAIN),
             pltpu.VMEM((local, group, PICKED, inner // 2), BRAIN),
             pltpu.VMEM((2, TILE, inner), BRAIN),
             pltpu.VMEM((2, TILE, inner // 2), BRAIN),
@@ -1516,10 +1635,11 @@
         ]
         + fold_scratch(group, tokens, width)
         + [dma((group,))] * 3
-        + [dma((2,)), dma((2, 2))],
+        + [dma((3,)), dma((2, 2))]
+        + (sum_sems(len(sums)) if sums else []),
         compiler_params=pltpu.CompilerParams(collective_id=number, has_side_effects=True, vmem_limit_bytes=63 * MIB),
         name="expert_backward",
-    )(grads, picked, gate_up, gates, shared_gu, expert_in, expert_out, shared_in, shared_out)
+    )(grads, picked, gate_up, shared_gu, gates, expert_in, expert_out, shared_in, shared_out, *sums)
 
 
 def moe_forward(hidden, routes, valid, norm_gain, router, pieces, wide, number):
@@ -1550,19 +1670,22 @@
     return hidden + routed, gathered, (norm_back, normed_low, probs, rows_all, own_gates, picked, gate_up, shared_gu, weights)
 
 
-def moe_backward(grad_out, saved, valid, grads_all, earlier):
+def moe_backward(grad_out, saved, valid, grads_all, before, beside, number):
     norm_back, normed_low, probs, rows_all, own_gates, picked, gate_up, shared_gu, weights = saved
     router, shared_in, shared_out, expert_in, expert_out = weights
     group = lax.axis_size("expert")
     if grads_all is None:
         if lax.axis_size("dp") == 4:
-            grads_all, *earlier = spread([grad_out.astype(BRAIN)], [], earlier, group, 3)
+            grads_all, *before = spread([grad_out.astype(BRAIN)], [], before, group, 3)
         else:
             grads_all = spread([grad_out.astype(BRAIN)], [], [], group, 3)[0]
-            earlier = [scatter_expert(s) for s in earlier]
-    grad_normed, grad_gates, grad_in, grad_out_weight, dshared, shared_mid = expert_backward(
-        grads_all, picked, own_gates, gate_up, shared_gu, expert_in, expert_out, shared_in, shared_out, 4
+            before = [scatter_expert(s) for s in before]
+    four = lax.axis_size("dp") == 4
+    grad_normed, grad_gates, grad_in, grad_out_weight, dshared, shared_mid, *summed = expert_backward(
+        grads_all, picked, own_gates, gate_up, shared_gu, expert_in, expert_out, shared_in, shared_out,
+        beside if four else [], number,
     )
+    beside = summed if four else [scatter_expert(s) for s in beside]
     flat = lambda array: array.reshape(-1, array.shape[-1])
     shared_grads = [matmul_tn(flat(rows_all), flat(dshared)), matmul_tn(flat(grads_all), flat(shared_mid))]
     sums = [
@@ -1575,7 +1698,7 @@
     logits_low = grad_logits.astype(BRAIN)
     grad_router = matmul_tn(normed_low, logits_low).astype(BRAIN)
     grad_hidden, grad_gain = norm_back(grad_normed + matmul_nt(logits_low, router))
-    return grad_out + grad_hidden, grad_gain, grad_router, sums, earlier
+    return grad_out + grad_hidden, grad_gain, grad_router, sums, before, beside
 
 
 def attend_scores(query, key_rows):
@@ -1788,12 +1911,15 @@
         [],
         7,
     )
-    grad, gain_four, d_router_b, sums_b, _ = moe_backward(grad, saved_b, valid, last_rows, [])
+    grad, gain_four, d_router_b, sums_b, _, _ = moe_backward(grad, saved_b, valid, last_rows, [], [], 4)
     grad, gain_three, d_qkv, d_attn_out = attention_backward(grad, saved_attn, w_qkv, w_attn_out)
-    grad, d_qkv, d_attn_out = lax.optimization_barrier((grad, d_qkv, d_attn_out))
-    d_qkv, d_attn_out = scatter_dense(d_qkv), scatter_dense(d_attn_out)
-    grad, gain_two, d_router_a, sums_a, sums_b = moe_backward(grad, saved_a, valid, None, sums_b)
-    d_shared_b, d_in_b, d_out_b = sums_b
+    grad, gain_two, d_router_a, sums_a, d_attn, sums_b = moe_backward(
+        grad, saved_a, valid, None, [d_qkv[None], d_attn_out[None]], sums_b, 8
+    )
+    d_attn = jnp.concatenate([part[0].astype(BRAIN) for part in d_attn], axis=1)
+    d_attn = lax.psum_scatter(d_attn, "expert", scatter_dimension=0, tiled=True).astype(FLOAT)
+    d_qkv, d_attn_out = d_attn[:, :QKV], d_attn[:, QKV:]
+    d_shared_b, d_in_b, d_out_b = [part.astype(FLOAT) for part in sums_b]
     grad, gain_one, mix_left, mix_right, d_mixer_out, grad_small = mixer_backward(
         grad, saved_mix, w_mixer_in, w_mixer_out, small
     )

time: 1290 us -> 1280 us (level)
    unnamed x297 -> x285, local copies, waits for them, and re-layouts: 54 us -> 46.1 us
  transfers between devices with their start and end apart: 4 -> 3, of which waited for: 0 -> 0; matrix products, arithmetic and copies ran while one was open for 12% -> 12% of each run, Pallas kernels for 38% -> 32%
where the time goes in v5:
time: 1280 us; the launch traced here: 1270 us
  Pallas kernels  1010 us (79%)
  local copies, waits for them, and re-layouts  94.7 us (7%)
  matrix products  87.3 us (7%)
  other arithmetic  65.2 us (5%)
  between operations  16.7 us (1%)
    pallas_call x3, Pallas kernels, spread(): pl.pallas_call(functools.partial(spread_kernel, n, w, s, group), out_shap...  235 us
    pallas_call x2, Pallas kernels, expert_backward(): pl.pallas_call(functools.partial(expert_backward_kernel, group, len(sums)...  208 us
    pallas_call x1, Pallas kernels, tail_exchange(): pl.pallas_call(functools.partial(tail_kernel, group, len(sums), steps), o...  180 us
    pallas_call x1, Pallas kernels, head_exchange(): pl.pallas_call(functools.partial(head_kernel, group, cut, len(dense)), ou...  174 us
    pallas_call x2, Pallas kernels, expert_forward(): pl.pallas_call(functools.partial(expert_forward_kernel, group, len(wide))...  171 us
    unnamed x285, local copies, waits for them, and re-layouts  46.1 us
    dot_general x9, matrix products, matmul_tn(): lax.dot_general(left, right, (((0,), (0,)), ((), ())), preferred_element_...  31.4 us
    dot_general x6, matrix products, matmul_nt(): lax.dot_general(left, right, (((1,), (1,)), ((), ())), preferred_element_...  28.4 us
  transfers between devices with their start and end apart: 3, of which 0 were waited for; matrix products, arithmetic and copies ran while one was open for 12% of the time, Pallas kernels for 32%

profile of v5, /device:TPU:16, one launch (start us, length us, event | category | flops | bytes accessed | tf_op | source)
XLA Modules:
  0.0 1270.4 jit_solution(3623254147517531834)
XLA Ops:
  11.4 1.9 copy.160
  15.4 1.7 pad_maximum_fusion.4
  19.1 173.8 %head_exchange.1 = (bf16[32,48,6448]{2,1,0:T(8,128)(2,1)}, bf16[32,48,3072]{2,1,0:T(8,128)(2,1)}, bf16[32,48,32]{2,1,0:T(8,128)(2,1)}, bf16[8,48,768]{2,1,0:T(8,128)(2,1)}, bf16[8,256,1536]{2,1,0:T(8,128)(2,1)}) custom-call(bf16[48,6448]{1,0:T(8,128)(2,1)} %refs_0_.1, bf16[48,3072]{1,0:T(8,128)(2,1)} %refs_1_.1, bf16[48,32]{1,0:T(8,128)(2,1)} %pad_maximum_fusion.9.refs_2_, ...), custom_call_target="tpu_custom_call" | custom-call | tf_op jit(solution)/shard_map/head_exchange/pallas_call | solution.py:459
  195.9 10.0 fusion.44
  206.2 2.4 copy-done.31
  208.7 3.4 fusion.5
  213.0 1.8 fusion.119
  216.8 9.3 state_forward.1
  226.1 4.1 multiply_reduce_fusion.6
  230.3 3.0 multiply_reduce_fusion.15
  238.7 1.8 fusion.88
  240.6 82.1 %spread1.2 = (bf16[8,256,1536]{2,1,0:T(8,128)(2,1)S(1)}, f32[8,16,256]{2,1,0:T(8,128)S(1)}, bf16[2,1536,1024]{2,1,0:T(8,128)(2,1)}, bf16[2,1536,512]{2,1,0:T(8,128)(2,1)S(1)}, bf16[1,1536,384]{2,1,0:T(8,128)(2,1)S(1)}) custom-call(bf16[256,1536]{1,0:T(8,128)(2,1)S(1)} %copy.168.refs_0_, f32[16,256]{1,0:T(8,128)S(1)} %fusion.67.refs_1_, ...), custom_call_target="tpu_custom_call" | custom-call | tf_op jit(solution)/shard_map/spread1/pallas_call | solution.py:268
  322.6 1.7 copy-done.10
  324.3 2.6 copy-done.13
  329.2 2.4 slice.202.refs_1_
  331.6 2.9 slice.201.refs_0_
  334.5 88.2 %expert_forward.2 = (f32[256,1536]{1,0:T(8,128)}, bf16[2,8,128,1536]{3,2,1,0:T(8,128)(2,1)}, bf16[2,8,128,1024]{3,2,1,0:T(8,128)(2,1)}, bf16[8,256,256]{2,1,0:T(...) custom-call(bf16[8,256,1536]{2,1,0:T(8,128)(2,1)} %copy-done.13, ...), custom_call_target="tpu_custom_call" | custom-call | tf_op jit(solution)/shard_map/expert_forward/pallas_call | solution.py:1456
  422.7 2.0 copy.169
  425.1 6.3 convolution_convert_fusion.3.q_ref.k_ref.v_ref
  431.4 4.6 attention_forward.1
  441.2 1.7 select_reduce_fusion
  445.1 76.3 %spread1.3 = (bf16[8,256,1536]{2,1,0:T(8,128)(2,1)S(1)}, f32[8,16,256]{2,1,0:T(8,128)S(1)}, bf16[2,1536,1024]{2,1,0:T(8,128)(2,1)}, bf16[2,1536,512]{2,1,0:T(8,128)(2,1)S(1)}, bf16[1,1536,384]{2,1,0:T(8,128)(2,1)S(1)}) custom-call(bf16[256,1536]{1,0:T(8,128)(2,1)S(1)} %copy.171.refs_0_, f32[16,256]{1,0:T(8,128)S(1)} %fusion.63.refs_1_, ...), custom_call_target="tpu_custom_call" | custom-call | tf_op jit(solution)/shard_map/spread1/pallas_call | solution.py:268
  521.4 1.7 copy-done.9
  523.1 2.6 copy-done.12
  528.0 82.9 %expert_forward.3 = (f32[256,1536]{1,0:T(8,128)}, bf16[2,8,128,1536]{3,2,1,0:T(8,128)(2,1)}, bf16[2,8,128,1024]{3,2,1,0:T(8,128)(2,1)}, bf16[8,256,256]{2,1,0:T(8,128)(2,1)}) custom-call(bf16[8,256,1536]{2,1,0:T(8,128)(2,1)} %copy-done.12, f32[8,2,256]{2,1,0:T(2,128)} %constant_dynamic-slice_fusion.g_ref, bf16[2,1536,1024]{2,1,0:T(8,128)(2,1)} %get-tuple-element.101.in_ref, ...), custom_call_target="tpu_custom_call" | custom-call | tf_op jit(solution)/shard_map/expert_forward/pallas_call | solution.py:1456
  610.9 3.1 copy.172
  613.9 92.0 %expert_backward.2 = (f32[256,1536]{1,0:T(8,128)}, f32[8,2,256]{2,1,0:T(2,128)}, bf16[2,1536,1024]{2,1,0:T(8,128)(2,1)}, bf16[2,1536,512]{2,1,0:T(8,128)(2,1)}, ...) custom-call(bf16[8,256,1536]{2,1,0:T(8,128)(2,1)} %get-tuple-element.105.d_hbm, ...), custom_call_target="tpu_custom_call" | custom-call | tf_op jit(solution)/shard_map/expert_backward/pallas_call | solution.py:1613
  706.0 3.1 copy.173
  710.0 3.2 multiply_reduce_fusion.7
  713.3 1.7 fusion.23
  716.4 3.6 fusion.1.refs_2_
  720.0 7.5 attention_backward.1
  727.7 2.6 multiply_reduce_fusion.8
  730.3 5.4 fusion.refs_1_
  735.8 1.9 fusion.14
  739.5 2.3 copy-done.8
  741.9 76.6 %spread3.1 = (bf16[8,256,1536]{2,1,0:T(8,128)(2,1)}, f32[1,384,2560]{2,1,0:T(8,128)S(1)}, f32[1,384,1536]{2,1,0:T(8,128)S(1)}) custom-call(bf16[256,1536]{1,0:T(8,128)(2,1)S(1)} %copy.176.refs_0_, bf16[1,1536,2560]{2,1,0:T(8,128)(2,1)} %fusion.refs_1_, bf16[1,1536,1536]{2,1,0:T(8,128)(2,1)S(1)} %copy-done.8), custom_call_target="tpu_custom_call" | custom-call | tf_op jit(solution)/shard_map/spread3/pallas_call | solution.py:268
  818.8 2.2 pad_maximum_fusion.1
  822.0 4.6 fusion.18
  829.0 116.5 %expert_backward.3 = (f32[256,1536]{1,0:T(8,128)}, f32[8,2,256]{2,1,0:T(2,128)}, bf16[2,1536,1024]{2,1,0:T(8,128)(2,1)}, bf16[2,1536,512]{2,1,0:T(8,128)(2,1)}, ...) custom-call(bf16[8,256,1536]{2,1,0:T(8,128)(2,1)} %get-tuple-element, ...), custom_call_target="tpu_custom_call" | custom-call | tf_op jit(solution)/shard_map/expert_backward/pallas_call | solution.py:1613
  945.5 3.1 copy.181
  948.8 3.3 multiply_reduce_fusion.9
  954.3 2.4 fusion.25
  957.1 5.2 convolution_convert_fusion
  962.3 5.3 fusion.31
  967.7 1.7 multiply_reduce_fusion.4
  969.7 5.3 fusion.9
  975.7 1.9 copy-done.11
  978.5 16.4 %state_backward.1 = (f32[256,3072]{1,0:T(8,128)S(1)}, f32[256,128]{1,0:T(8,128)S(1)}, f32[256,128]{1,0:T(8,128)S(1)}, f32[256,48]{1,0:T(8,128)S(1)}, f32[48,256]{1,0:T(8,128)S(1)}) custom-call(f32[256,3328]{1,0:T(8,128)S(1)} %copy-done.3, f32[256,3328]{1,0:T(8,128)S(1)} %copy-done.3, f32[256,3328]{1,0:T(8,128)S(1)} %copy-done.3, f32[256,48]{1,0:T(8,128)S(1)} %copy-done.18, ...), custom_call_target="tpu_custom_call" | custom-call | tf_op jit(solution)/shard_map/state_backward/pallas_call | solution.py:990
  994.9 1.7 copy-done.14
  998.6 4.0 constant_dynamic-update-slice_fusion.5
  1004.9 10.5 multiply_reduce_fusion.2
  1016.8 3.2 broadcast_multiply_fusion
  1021.8 14.8 %fusion.22 = (f32[1536]{0:T(1024)S(1)}, f32[256]{0:T(256)S(1)}, f32[256,1536]{0,1:T(8,128)}) fusion(bf16[256,1536]{0,1:T(8,128)(2,1)S(1)} %copy-done.49, f32[256]{0:T(256)S(1)} %copy-done.87, f32[1536]{0:T(1024)S(1)} %copy-done.77, bf16[1536,6448]{1,0:T(8,128)(2,1)} %bitcast.216, bf16[256,48]{1,0:T(8,128)(2,1)S(1)} %get-tuple-element.242, ...), kind=kOutput, calls=%fused_computation.72 | convolution fusion | flops 5083568128 | bytes 25483264 | tf_op jit(solution)/shard_map/dot_general | solution.py:41
  1037.6 5.0 fusion.17
  1042.7 5.0 fusion.13
  1049.6 2.2 fusion.43
  1051.8 1.8 pad_maximum_fusion.refs_1_
  1053.6 180.2 %tail_exchange.1 = (f32[48,6448]{1,0:T(8,128)}, f32[48,32]{1,0:T(8,128)}, bf16[8,48,384]{2,1,0:T(8,128)(2,1)}, f32[208,128]{1,0:T(8,128)}, bf16[8,48,384]{2,1,0:...) custom-call(bf16[1536,256]{1,0:T(8,128)(2,1)} %get-tuple-element.265.refs_0_, ...), custom_call_target="tpu_custom_call" | custom-call | tf_op jit(solution)/shard_map/tail_exchange/pallas_call | solution.py:836
  1239.0 2.1 convert_element_type.150
  1243.8 2.5 convert_element_type.144
  1247.9 2.1 convert_element_type.143
  1258.8 1.8 slice.208
  1260.6 1.8 convert_element_type.141
  (388 shorter events, 73.3 us)
Async XLA Ops:
  7.2 10.0 copy-start
  7.2 322.0 %all-gather.2.cloned.1.call-start = ((), (), s32[]{:S(2)}) async-start(), calls=%async_computation.2 | async-start | bytes 3538944 | tf_op jit(solution)/shard_map/all_gather | solution.py:1890
  13.3 179.5 %copy-start.43 = (f32[256,1536]{0,1:T(8,128)}, f32[256,1536]{0,1:T(8,128)S(1)}, u32[]{:S(2)}) copy-start(f32[256,1536]{0,1:T(8,128)S(1)} %copy.160) | copy-start | bytes 4718596
  14.7 180.5 %copy-start.63 = (bf16[256,1536]{1,0:T(8,128)(2,1)S(1)}, bf16[256,1536]{1,0:T(8,128)(2,1)}, u32[]{:S(2)}) copy-start(bf16[256,1536]{1,0:T(8,128)(2,1)} %param.26) | copy-start | bytes 2359300
  192.9 1064.3 %reduce-scatter.5.cloned.1.call-start = ((), (), s32[]{:S(2)}) async-start(), calls=%async_computation.4 | async-start | bytes 3538944 | tf_op jit(solution)/shard_map/reduce_scatter | solution.py:1920
  194.1 11.8 copy-start.76
  195.3 13.4 %copy-start.68 = (f32[3328]{0:T(1024)}, f32[3328]{0:T(1024)S(1)}, u32[]{:S(2)}) copy-start(f32[3328]{0:T(1024)S(1)} %get-tuple-element.231) | copy-start | bytes 39940
  195.3 13.4 %copy-start.70 = (f32[3328]{0:T(1024)}, f32[3328]{0:T(1024)S(1)}, u32[]{:S(2)}) copy-start(f32[3328]{0:T(1024)S(1)} %get-tuple-element.232) | copy-start | bytes 39940
  195.3 13.4 %copy-start.72 = (f32[3328]{0:T(1024)}, f32[3328]{0:T(1024)S(1)}, u32[]{:S(2)}) copy-start(f32[3328]{0:T(1024)S(1)} %get-tuple-element.233) | copy-start | bytes 39940
  195.3 13.4 %copy-start.74 = (f32[3328]{0:T(1024)}, f32[3328]{0:T(1024)S(1)}, u32[]{:S(2)}) copy-start(f32[3328]{0:T(1024)S(1)} %get-tuple-element.234) | copy-start | bytes 39940
  195.6 10.3 copy-start.47
  195.9 10.1 copy-start.99
  195.9 10.1 copy-start.86
  212.2 13.9 %copy-start.2 = (f32[256,3328]{1,0:T(8,128)}, f32[256,3328]{1,0:T(8,128)S(1)}, u32[]{:S(2)}) copy-start(f32[256,3328]{1,0:T(8,128)S(1)} %get-tuple-element.250.x_ref.b_ref.c_ref) | copy-start | bytes 10223620
  213.0 13.1 %copy-start.27 = (f32[1,3072]{1,0:T(1,128)}, f32[1,3072]{1,0:T(1,128)S(1)}, u32[]{:S(2)}) copy-start(f32[1,3072]{1,0:T(1,128)S(1)} %broadcast_in_dim_reshape.4.skip_ref) | copy-start | bytes 36868
  216.8 9.3 copy-start.17
  216.8 13.5 %slice-start.4 = ((s8[9437184]{0:T(1024)(128)(4,1)}), s8[4194304]{0:T(1024)(128)(4,1)S(1)}, s32[]{:S(2)}) async-start(s8[9437184]{0:T(1024)(128)(4,1)} %bitcast.218), calls=%async_computation.9 | async-start | bytes 8388608
  216.8 13.5 %slice-start.5 = ((s8[9437184]{0:T(1024)(128)(4,1)}), s8[4194304]{0:T(1024)(128)(4,1)S(1)}, s32[]{:S(2)}) async-start(s8[9437184]{0:T(1024)(128)(4,1)} %bitcast.218), calls=%async_computation.10 | async-start | bytes 8388608
  234.5 6.1 copy-start.15
  234.5 6.1 copy-start.21
  237.1 90.4 %copy-start.106 = (s32[256,6]{0,1:T(8,128)S(1)}, s32[256,6]{0,1:T(8,128)}, u32[]{:S(2)}) copy-start(s32[256,6]{0,1:T(8,128)} %param.30) | copy-start | bytes 18436
  238.7 90.5 %copy-start.94 = (f32[256]{0:T(256)}, f32[256]{0:T(256)S(1)}, u32[]{:S(2)}) copy-start(f32[256]{0:T(256)S(1)} %fusion.69) | copy-start | bytes 3076
  424.7 11.2 slice-start.7
  425.0 6.3 copy-start.103
  425.0 10.9 copy-start.35
  425.1 10.9 slice-start.8
  431.4 6.1 copy-start.4
  437.5 5.4 copy-start.109
  437.5 5.5 copy-start.16
  437.5 83.9 %copy-start.92 = (f32[256]{0:T(256)}, f32[256]{0:T(256)S(1)}, u32[]{:S(2)}) copy-start(f32[256]{0:T(256)S(1)} %fusion.76) | copy-start | bytes 3076
  443.0 266.1 %copy-start.96 = (f32[256]{0:T(256)}, f32[256]{0:T(256)S(1)}, u32[]{:S(2)}) copy-start(f32[256]{0:T(256)S(1)} %fusion.71) | copy-start | bytes 3076
  715.0 12.6 slice-start.2
  716.4 11.2 slice-start.3
  720.0 7.6 copy-start.36
  727.5 8.3 slice-start
  727.6 8.1 slice-start.1
  730.3 5.5 copy-start.118
  821.0 439.6 %reduce-scatter.3.cloned.1.call-start = ((), (), s32[]{:S(2)}) async-start(), calls=%async_computation.3 | async-start | bytes 9732096 | tf_op jit(solution)/shard_map/reduce_scatter | solution.py:1805
  948.8 5.5 copy-start.108
  962.3 5.3 copy-start.34
  962.3 7.1 copy-start.7
  969.7 6.0 copy-start.28
  1004.8 10.7 copy-start.19
  1004.8 10.7 copy-start.30
  1004.8 10.7 copy-start.112
  1004.8 10.7 copy-start.116
  1004.8 11.9 copy-start.69
  1004.8 11.9 copy-start.71
  1004.9 11.9 copy-start.73
  1004.9 11.9 copy-start.75
  1021.8 14.9 %copy-start.82 = (f32[1,1536]{1,0:T(1,128)S(1)}, f32[1,1536]{1,0:T(1,128)}, u32[]{:S(2)}) copy-start(f32[1,1536]{1,0:T(1,128)} %reshape.368) | copy-start | bytes 18436
  1021.8 14.9 %copy-start.83 = (f32[1,1536]{1,0:T(1,128)S(1)}, f32[1,1536]{1,0:T(1,128)}, u32[]{:S(2)}) copy-start(f32[1,1536]{1,0:T(1,128)} %reshape.367) | copy-start | bytes 18436
  1021.8 14.9 %copy-start.84 = (f32[1,1536]{1,0:T(1,128)S(1)}, f32[1,1536]{1,0:T(1,128)}, u32[]{:S(2)}) copy-start(f32[1,1536]{1,0:T(1,128)} %reshape.366) | copy-start | bytes 18436
  1021.8 14.9 %copy-start.79 = (f32[48,64]{1,0:T(8,128)S(1)}, f32[48,64]{1,0:T(8,128)}, u32[]{:S(2)}) copy-start(f32[48,64]{1,0:T(8,128)} %reshape.375) | copy-start | bytes 36868
  1021.8 15.0 %copy-start.115 = (f32[48]{0:T(128)S(1)}, f32[48]{0:T(128)}, u32[]{:S(2)}) copy-start(f32[48]{0:T(128)} %param.49) | copy-start | bytes 580
  1021.8 15.1 %copy-start.81 = (f32[3072]{0:T(1024)S(1)}, f32[3072]{0:T(1024)}, u32[]{:S(2)}) copy-start(f32[3072]{0:T(1024)} %get-tuple-element.219) | copy-start | bytes 36868
  1021.8 15.8 %copy-start.100 = (f32[256]{0:T(256)S(1)}, f32[256]{0:T(256)}, u32[]{:S(2)}) copy-start(f32[256]{0:T(256)} %copy-done.99) | copy-start | bytes 3076
  1021.8 15.8 %copy-start.119 = (bf16[8,256,128]{2,1,0:T(8,128)(2,1)S(1)}, bf16[8,256,128]{2,1,0:T(8,128)(2,1)}, u32[]{:S(2)}) copy-start(bf16[8,256,128]{2,1,0:T(8,128)(2,1)} %get-tuple-element.132) | copy-start | bytes 1572868
  1042.6 6.2 copy-start.59
  1053.6 181.8 %copy-start.52 = (f32[256,1536]{0,1:T(8,128)S(1)}, f32[256,1536]{0,1:T(8,128)}, u32[]{:S(2)}) copy-start(f32[256,1536]{0,1:T(8,128)} %get-tuple-element.258) | copy-start | bytes 4718596
  1239.0 7.2 copy-start.57
  1241.1 6.8 copy-start.60
  1254.2 8.2 copy-start.61
  1256.4 7.1 copy-start.1
  (71 other events, 197.8 us)
Sparse Core Ops, SparseCore 0:
  193.0 69.0 all-gather.1
  821.1 100.4 reduce-scatter.4
  1002.7 167.4 reduce-scatter.2
